TPU v7x, 256 devices: a whole 4x4x8 slice. The times are simulated.
256 devices in a mesh: dp: 32 (over y_hi, z, core), mp: 8 (over x, y_lo).
Axes of the slice: x: 4, y: 4 (y_hi: 2, y_lo: 2; y = y_hi * 2 + y_lo), z: 8, core: 2. Of those that a mesh axis runs over, the one named last changes fastest.
Arguments:
- features: bfloat16 [32768, 4096], P('dp'), may hold values from -13 to 13
- out_grads: bfloat16 [32768, 4096], P('dp', 'mp'), may hold values from -6 to 6
- counts: int32 [32], P('dp'), may hold values from 341 to 1024, as said below
- factor_old: float32 [8, 32, 2, 512, 512], P('mp', 'dp'), may hold values from -1 to 3, as said below
- inverse_old: float32 [8, 32, 2, 512, 512], P('mp', 'dp'), may hold values from -1 to 3, as said below
- old_owner: int32 [8, 2], replicated, may hold values from 0 to 31, as said below
- new_owner: int32 [8, 2], replicated, may hold values from 0 to 31, as said below
Outputs:
- factor_new: float32 [8, 32, 512, 512], P('mp', 'dp')
- inverse_new: float32 [8, 32, 512, 512], P('mp', 'dp')
- update: float32 [4096, 4096], P('dp', 'mp')
Inputs may be any that keep to these rules, and one draw needn't show every extreme that they name: `counts`: some dp index has all 1024 rows valid. `factor_old`: Symmetric. `inverse_old`: Symmetric. `old_owner`: A dp index holds at most both blocks of one mp index; in every draw some mp index has both blocks at one dp index. `new_owner`: the two blocks of one mp index have different new owners.
All inputs are finite; a program needn't handle non-finite values.
Results may differ from a plain program's by a relative error of at most 0.0057.
Values may be sent and summed in bfloat16 or wider, within the bound.
No kernel may reach another device: no remote copies, remote signals or barrier semaphores. Data moves between devices by JAX's collectives and lax.ppermute only.
A program may use at most 128 MiB of HBM per device.

v0:
```python
import jax
import jax.numpy as jnp
from jax import lax
from jax.sharding import PartitionSpec as P

DECAY = 0.9
DAMPING = 0.01


def from_root(block, axis, owner):
    block = jnp.where(lax.axis_index(axis) == owner, block, jnp.zeros_like(block))
    return lax.psum(block, axis)


def contract_rows(first_rows, second_rows):
    return lax.dot_general(
        first_rows, second_rows, (((0,), (0,)), ((), ())), preferred_element_type=jnp.float32
    )


def refresh(stale_factor, stale_inverse, covariance, token_total):
    block_width = stale_factor.shape[0]
    factor = DECAY * stale_factor + (1.0 - DECAY) * covariance / token_total
    damped = factor + DAMPING * jnp.eye(block_width, dtype=jnp.float32)
    inner_prod = jnp.dot(damped, stale_inverse, precision=lax.Precision.HIGHEST)
    inverse = 2.0 * stale_inverse - jnp.dot(
        stale_inverse, inner_prod, precision=lax.Precision.HIGHEST
    )
    return (factor, inverse)


def local(features, out_grads, counts, factor_old, inverse_old, old_owner, new_owner):
    block_width = out_grads.shape[1]
    tok_rows = features.shape[0]
    feature_count = features.shape[1]
    column = lax.axis_index("mp")
    member = lax.axis_index("dp")
    members = lax.axis_size("dp")
    valid_rows = (jnp.arange(tok_rows, dtype=jnp.int32) < counts[0])[:, None]
    grads_kept = jnp.where(valid_rows, out_grads, jnp.zeros_like(out_grads))
    own_block = lax.dynamic_slice_in_dim(features, column * block_width, block_width, 1)
    block_kept = jnp.where(valid_rows, own_block, jnp.zeros_like(own_block))
    partials = jnp.stack(
        [contract_rows(block_kept, own_block), contract_rows(grads_kept, out_grads)]
    )
    summed, totals = lax.psum((partials, counts.astype(jnp.float32)), "dp")
    token_total = totals[0]
    stale_owner = lax.dynamic_index_in_dim(old_owner, column, 0, keepdims=False)
    fresh_owner = lax.dynamic_index_in_dim(new_owner, column, 0, keepdims=False)
    shared_slot = (stale_owner[1] == stale_owner[0]).astype(jnp.int32)
    slot_index = (jnp.zeros((), jnp.int32), shared_slot)
    held_factors = factor_old[0, 0]
    held_inverses = inverse_old[0, 0]
    blank_block = jnp.zeros((block_width, block_width), jnp.float32)
    factor_out = blank_block
    inverse_out = blank_block
    rounded = []
    for which_block in range(2):
        stale_factor = lax.dynamic_index_in_dim(
            held_factors, slot_index[which_block], 0, keepdims=False
        )
        stale_inverse = lax.dynamic_index_in_dim(
            held_inverses, slot_index[which_block], 0, keepdims=False
        )
        covariance = summed[which_block]
        factor, inverse = lax.cond(
            member == stale_owner[which_block],
            lambda: refresh(stale_factor, stale_inverse, covariance, token_total),
            lambda: (blank_block, blank_block),
        )
        both_blocks = from_root(jnp.stack([factor, inverse]), "dp", stale_owner[which_block])
        factor = both_blocks[0]
        inverse = both_blocks[1]
        rounded.append(inverse.astype(jnp.bfloat16))
        keeper = member == fresh_owner[which_block]
        factor_out = jnp.where(keeper, factor, factor_out)
        inverse_out = jnp.where(keeper, inverse, inverse_out)
    right_inverse = rounded[1]
    left_inverses = lax.all_gather(rounded[0][None], "mp", axis=0, tiled=True)
    share_rows = block_width // members
    summed_grad = lax.psum_scatter(
        contract_rows(grads_kept, features), "dp", scatter_dimension=0, tiled=True
    )
    grad_round = summed_grad.astype(jnp.bfloat16)
    stacked = grad_round.reshape(share_rows, -1, block_width)
    half_step = jnp.einsum(
        "hck,cik->hci", stacked, left_inverses, preferred_element_type=jnp.float32
    )
    half_step = half_step.reshape(share_rows, feature_count).astype(jnp.bfloat16)
    half_moved, grad_moved = (
        lax.all_to_all(half_step, "dp", split_axis=1, concat_axis=0, tiled=True),
        lax.all_to_all(grad_round, "dp", split_axis=1, concat_axis=0, tiled=True),
    )
    result_turned = contract_rows(right_inverse, half_moved)
    curvature = jnp.sum(result_turned * grad_moved.astype(jnp.float32))
    result = result_turned.T
    curvature = lax.psum(curvature, ("dp", "mp"))
    entries = float(feature_count * block_width * lax.axis_size("mp"))
    clip_scale = jnp.minimum(1.0, jnp.sqrt(entries / jnp.abs(curvature)))
    return (factor_out[None, None], inverse_out[None, None], clip_scale * result)


def solution(mesh):
    return jax.shard_map(
        local,
        mesh=mesh,
        in_specs=(
            P("dp", None),
            P("dp", "mp"),
            P("dp"),
            P("mp", "dp", None, None, None),
            P("mp", "dp", None, None, None),
            P(),
            P(),
        ),
        out_specs=(P("mp", "dp", None, None), P("mp", "dp", None, None), P("dp", "mp")),
        check_vma=False,
    )
```

profile of v0, /device:TPU:1, one launch (start us, length us, event | category | flops | bytes accessed | tf_op | source)
XLA Modules:
  0.0 955.9 jit_solution(16445997575437055482)
XLA Ops:
  7.2 0.0 all-reduce.4.cloned.1.call-start
  7.9 2.4 fusion.39
  10.3 2.4 fusion.42
  12.7 1.6 pad_maximum_fusion
  14.3 0.0 all-reduce.4.cloned.1.call-update
  14.3 0.0 all-reduce.6.cloned.1.call-start
  14.3 70.3 %psum.36 = f32[]{:T(128)} all-reduce(f32[]{:T(128)} %bitcast.12), channel_id=1, replica_groups=mesh['dp'=32,'mp'=8] {'dp'}, use_global_device_ids=true, to_apply=%region_1.2 | all-reduce | flops 1 | bytes 8 | tf_op jit(solution)/shard_map/psum | solution.py:46
  84.6 0.0 copy-done.5
  84.6 0.0 copy-done.6
  84.6 0.1 constant_dynamic-slice_fusion
  84.7 0.5 fusion.66
  87.8 201.8 %all-reduce.4.cloned.1.call-done = f32[2,512,512]{2,1,0:T(8,128)} async-done(((f32[2,512,512]{2,1,0:T(8,128)}), f32[2,512,512]{2,1,0:T(8,128)}) %all-reduce.4.cloned.1.call-update) | async-done | bytes 2097168 | tf_op jit(solution)/shard_map/psum | solution.py:46
  289.6 0.0 copy-done
  289.6 1.2 conditional.3
  289.6 0.1 stack.31
  289.7 1.1 stack.31.clone
  290.8 2.8 maximum_select_fusion.1
  293.6 1.2 conditional.2
  293.6 0.1 stack.29
  293.8 1.1 stack.29.clone
  294.9 2.8 maximum_select_fusion
  297.7 0.0 all-reduce.6.cloned.1.call-update
  297.7 0.2 reduce-scatter.2.cloned.1.call-start
  297.9 1.0 copy-done.4
  298.9 10.3 %fusion.35 = f32[512,4096]{1,0:T(8,128)} fusion(bf16[1024,4096]{1,0:T(8,128)(2,1)} %param.11, bf16[1024,512]{1,0:T(8,128)(2,1)S(1)} %copy-done.4, pred[1024]{0:T(1024)(128)(4,1)S(1)} %iota_compare_fusion.4), kind=kOutput, calls=%fused_computation.50 | convolution fusion | flops 4295491584 | bytes 17826816 | tf_op jit(solution)/shard_map/dot_general | solution.py:16
  309.2 0.0 reduce-scatter.2.cloned.1.call-update
  309.2 0.0 all-gather.2.cloned.1.call-start
  309.3 286.3 %all-reduce.6.cloned.1.call-done = (f32[2,512,512]{2,1,0:T(8,128)}, f32[2,512,512]{2,1,0:T(8,128)}) async-done(((f32[2,512,512]{2,1,0:T(8,128)}, f32[2,512,512]{2,1,0:T(8,128)}), (f32[2,512,512]{2,1,0:T(8,128)}, f32[2,512,512]{2,1,0:T(8,128)})) %all-reduce.6.cloned.1.call-update) | async-done | bytes 4194320 | tf_op jit(solution)/shard_map/psum | solution.py:12
  595.6 2.1 slice.84
  597.7 0.0 all-gather.2.cloned.1.call-update
  597.7 0.5 fusion.65
  599.5 149.4 %reduce-scatter.2.cloned.1.call-done = f32[16,4096]{1,0:T(8,128)} async-done(((f32[512,4096]{1,0:T(8,128)}), f32[16,4096]{1,0:T(8,128)}) %reduce-scatter.2.cloned.1.call-update) | async-done | bytes 262160 | tf_op jit(solution)/shard_map/reduce_scatter | solution.py:81
  748.9 1.6 copy_bitcast_fusion
  750.5 10.9 %all-to-all-start.1 = ((bf16[16,32,128]{2,0,1:T(8,128)(2,1)}), bf16[16,32,128]{2,0,1:T(8,128)(2,1)S(1)}, u32[]{:S(2)}, u32[]{:S(2)}) async-start(bf16[16,32,128]{2,0,1:T(8,128)(2,1)} %copy_bitcast_fusion), calls=%async_computation.2 | async-start | bytes 262144 | tf_op jit(solution)/shard_map/all_to_all | solution.py:92
  761.5 1.0 convert_element_type.53
  762.4 84.6 %all-gather.2.cloned.1.call-done = bf16[8,512,512]{2,1,0:T(8,128)(2,1)} async-done(((bf16[1,512,512]{2,1,0:T(8,128)(2,1)}), bf16[8,512,512]{2,1,0:T(8,128)(2,1)}) %all-gather.2.cloned.1.call-update) | async-done | bytes 4194320 | tf_op jit(solution)/shard_map/all_gather | solution.py:79
  847.0 3.5 fusion.45
  850.5 0.1 copy.28
  850.6 0.1 convert_element_type.56
  850.7 0.7 copy.29
  851.4 0.0 all-to-all-done.1
  851.5 9.2 all-to-all-start
  860.7 0.0 copy-done.2
  860.7 3.4 select_bitcast_fusion
  864.1 7.2 all-to-all-done
  871.3 0.9 fusion.58
  872.2 75.6 %psum.39 = f32[]{:T(128)} all-reduce(f32[]{:T(128)} %get-tuple-element.140), channel_id=1, replica_groups=mesh['dp'=32,'mp'=8] {'dp','mp'}, use_global_device_ids=true, to_apply=%region_10.11 | all-reduce | flops 1 | bytes 8 | tf_op jit(solution)/shard_map/psum | solution.py:97
  948.6 0.8 copy.31
  (7 shorter events, 0.0 us)
Async XLA Ops:
  7.2 282.4 %all-reduce.4.cloned.1.call-start = ((), (), s32[]{:S(2)}) async-start(), calls=%async_computation.3 | async-start | bytes 4194304 | tf_op jit(solution)/shard_map/psum | solution.py:46
  14.3 70.3 %copy-start.5 = (s32[8,2]{0,1:T(2,128)S(1)}, s32[8,2]{0,1:T(2,128)}, u32[]{:S(2)}) copy-start(s32[8,2]{0,1:T(2,128)} %param.16) | copy-start | bytes 196
  14.3 70.3 %copy-start.6 = (s32[8,2]{0,1:T(2,128)S(1)}, s32[8,2]{0,1:T(2,128)}, u32[]{:S(2)}) copy-start(s32[8,2]{0,1:T(2,128)} %param.17) | copy-start | bytes 196
  14.3 275.3 %copy-start = (f32[1,1,2,512,512]{4,3,2,1,0:T(8,128)S(1)}, f32[1,1,2,512,512]{4,3,2,1,0:T(8,128)}, u32[]{:S(2)}) copy-start(f32[1,1,2,512,512]{4,3,2,1,0:T(8,128)} %param.15) | copy-start | bytes 6291460
  14.3 581.3 %all-reduce.6.cloned.1.call-start = ((), (), s32[]{:S(2)}) async-start(), calls=%async_computation.6 | async-start | bytes 8388608 | tf_op jit(solution)/shard_map/psum | solution.py:12
  297.7 1.2 copy-start.4
  297.7 451.2 %reduce-scatter.2.cloned.1.call-start = ((), (), s32[]{:S(2)}) async-start(), calls=%async_computation.5 | async-start | bytes 8650752 | tf_op jit(solution)/shard_map/reduce_scatter | solution.py:81
  309.2 537.8 %all-gather.2.cloned.1.call-start = ((), (), s32[]{:S(2)}) async-start(), calls=%async_computation.4 | async-start | bytes 4718592 | tf_op jit(solution)/shard_map/all_gather | solution.py:79
  750.5 100.9 %all-to-all-start.1 = ((bf16[16,32,128]{2,0,1:T(8,128)(2,1)}), bf16[16,32,128]{2,0,1:T(8,128)(2,1)S(1)}, u32[]{:S(2)}, u32[]{:S(2)}) async-start(bf16[16,32,128]{2,0,1:T(8,128)(2,1)} %copy_bitcast_fusion), calls=%async_computation.2 | async-start | bytes 262144 | tf_op jit(solution)/shard_map/all_to_all | solution.py:92
  847.0 13.7 %copy-start.2 = (f32[2,512,512]{2,1,0:T(8,128)S(1)}, f32[2,512,512]{2,1,0:T(8,128)}, u32[]{:S(2)}) copy-start(f32[2,512,512]{2,1,0:T(8,128)} %get-tuple-element.133) | copy-start | bytes 6291460
  851.5 19.8 %all-to-all-start = ((bf16[16,32,128]{2,0,1:T(8,128)(2,1)}), bf16[16,32,128]{2,0,1:T(8,128)(2,1)S(1)}, u32[]{:S(2)}, u32[]{:S(2)}) async-start(bf16[16,32,128]{2,0,1:T(8,128)(2,1)} %copy.29), calls=%async_computation.1 | async-start | bytes 262144 | tf_op jit(solution)/shard_map/all_to_all | solution.py:91
Sparse Core Ops, SparseCore 0:
  14.4 275.1 all-reduce.3
  297.8 297.7 all-reduce.5
  600.6 148.2 reduce-scatter.1
  751.3 95.7 all-gather.1
where the time goes:
time: 957 us; the launch traced here: 956 us
  waiting for transfers between devices  729 us (76%)
  blocking collectives  146 us (15%)
  starting transfers between devices  20.5 us (2%)
  matrix products  19.6 us (2%)
  between operations  19.1 us (2%)
  other arithmetic  13.1 us (1%)
    psum x1, waiting for transfers between devices, from_root(): return lax.psum(block, axis)  286 us
    psum x1, waiting for transfers between devices, local(): summed, totals = lax.psum((partials, counts.astype(jnp.float32)), 'dp')  202 us
    reduce_scatter x1, waiting for transfers between devices, local(): lax.psum_scatter(contract_rows(grads_kept, features), 'dp', scatter_dimen...  149 us
    all_gather x1, waiting for transfers between devices, local(): left_inverses = lax.all_gather(rounded[0][None], 'mp', axis=0, tiled=True)  84.6 us
    psum x1, blocking collectives, local(): curvature = lax.psum(curvature, ('dp', 'mp'))  75.6 us
    psum x1, blocking collectives, local(): summed, totals = lax.psum((partials, counts.astype(jnp.float32)), 'dp')  70.3 us
  transfers between devices with their start and end apart: 6, of which 5 were waited for; matrix products, arithmetic and copies ran while one was open for 2% of the time, Pallas kernels for 0%

commit v1 on v0

v1 whole, which is shorter than its diff:
```python
import jax
import jax.numpy as jnp
import numpy as np
from jax import lax
from jax.sharding import PartitionSpec as P

DECAY = 0.9
DAMPING = 0.01
TILE = 128
BF16 = jnp.bfloat16
F32 = jnp.float32


def contract_rows(first_rows, second_rows):
    return lax.dot_general(
        first_rows, second_rows, (((0,), (0,)), ((), ())), preferred_element_type=F32
    )


def upper_pairs(tiles):
    return [(a, b) for a in range(tiles) for b in range(a, tiles)]


def pack_upper(block):
    tiles = block.shape[0] // TILE
    return jnp.concatenate(
        [
            block[a * TILE : (a + 1) * TILE, b * TILE : (b + 1) * TILE]
            for a, b in upper_pairs(tiles)
        ],
        axis=0,
    )


def unpack_upper(packed, width):
    tiles = width // TILE
    at = {pair: n for n, pair in enumerate(upper_pairs(tiles))}

    def tile(a, b):
        n = at[(min(a, b), max(a, b))]
        piece = packed[n * TILE : (n + 1) * TILE]
        return piece if a <= b else piece.T

    return jnp.concatenate(
        [jnp.concatenate([tile(a, b) for b in range(tiles)], axis=1) for a in range(tiles)], axis=0
    )


def split_words(value):
    high = lax.reduce_precision(value, 8, 7)
    return high.astype(BF16), (value - high).astype(BF16)


def local(features, out_grads, counts, factor_old, inverse_old, old_owner, new_owner):
    width = out_grads.shape[1]
    tok_rows = features.shape[0]
    feature_count = features.shape[1]
    column = lax.axis_index("mp")
    member = lax.axis_index("dp")
    members = lax.axis_size("dp")
    columns = lax.axis_size("mp")
    chips = members // 2
    core = member % 2
    swap = [(i, i ^ 1) for i in range(members)]
    same_core = [[2 * q + c for q in range(chips)] for c in range(2)]

    def pair_split(parts):
        paired = parts.reshape((chips, 2) + parts.shape[1:])
        mine = lax.dynamic_index_in_dim(paired, core, 1, keepdims=False)
        other = lax.dynamic_index_in_dim(paired, 1 - core, 1, keepdims=False)
        return mine, lax.ppermute(other, "dp", swap)

    def across_chips(parts):
        return lax.all_to_all(parts, "dp", 0, 0, tiled=True, axis_index_groups=same_core)

    def reduce_scatter(parts):
        mine, received = pair_split(parts)
        pair_sum = (mine.astype(F32) + received.astype(F32)).astype(BF16)
        return jnp.sum(across_chips(pair_sum).astype(F32), axis=0)

    stale_owner = lax.dynamic_index_in_dim(old_owner, column, 0, keepdims=False)
    fresh_owner = lax.dynamic_index_in_dim(new_owner, column, 0, keepdims=False)
    shared_slot = (stale_owner[1] == stale_owner[0]).astype(jnp.int32)

    stale = [
        held[0, 0, 0] if k == 0 else lax.dynamic_index_in_dim(held[0, 0], shared_slot, 0, keepdims=False)
        for held in (factor_old, inverse_old)
        for k in range(2)
    ]
    eye = jnp.eye(width, dtype=F32)
    share = width * (width + TILE) // 2 // TILE // members
    diagonals = jnp.stack([jnp.sum(block * eye, axis=0) for block in stale])
    diag_high, diag_low = split_words(diagonals.reshape(-1, TILE))
    diag_rows = jnp.concatenate([diag_high, diag_low], axis=0)
    packed = jnp.stack(
        [pack_upper((block * (1.0 - eye)).astype(BF16)).reshape(members, share, TILE) for block in stale],
        axis=1,
    ).reshape(members, 4 * share, TILE)
    packed = jnp.concatenate(
        [packed, jnp.broadcast_to(diag_rows, (members,) + diag_rows.shape)], axis=1
    )
    lanes = width // TILE
    row_kind = np.concatenate(
        [np.repeat([0, 1, 0, 1], share), np.tile(np.repeat([0, 1, 0, 1], lanes), 2)]
    )[:, None]
    owner_core = stale_owner % 2
    owner_chip = stale_owner // 2
    mine, received = pair_split(packed)
    from_mine = jnp.where(row_kind == 0, owner_core[0] == core, owner_core[1] == core)
    chosen = across_chips(jnp.where(from_mine, mine, received))
    scattered = jnp.where(
        row_kind == 0,
        lax.dynamic_index_in_dim(chosen, owner_chip[0], 0, keepdims=False),
        lax.dynamic_index_in_dim(chosen, owner_chip[1], 0, keepdims=False),
    )
    diag_rows = scattered[4 * share :].astype(F32)
    diagonals = (diag_rows[: 4 * lanes] + diag_rows[4 * lanes :]).reshape(4, width)
    factor_share = scattered[: 2 * share].astype(F32)
    inverse_share = scattered[2 * share : 4 * share]

    valid_rows = (jnp.arange(tok_rows, dtype=jnp.int32) < counts[0])[:, None]
    grads_kept = jnp.where(valid_rows, out_grads, jnp.zeros_like(out_grads))
    own_block = lax.dynamic_slice_in_dim(features, column * width, width, 1)
    block_kept = jnp.where(valid_rows, own_block, jnp.zeros_like(own_block))
    covariances = [contract_rows(block_kept, own_block), contract_rows(grads_kept, out_grads)]
    digits = jnp.concatenate(
        [jnp.full((4, TILE), (counts[0] >> (3 * d)) & 7).astype(BF16) for d in range(4)], axis=0
    )
    cov_parts = jnp.concatenate(
        [pack_upper(cov.astype(BF16)).reshape(members, share, TILE) for cov in covariances]
        + [jnp.broadcast_to(digits, (members,) + digits.shape)],
        axis=1,
    )
    cov_share = reduce_scatter(cov_parts)
    total = sum(cov_share[2 * share + 4 * d, 0] * float(8**d) for d in range(4))
    factor_share = DECAY * factor_share + (1.0 - DECAY) * cov_share[: 2 * share] / total

    shares = jnp.concatenate([factor_share.astype(BF16), inverse_share], axis=0)
    gathered = across_chips(jnp.broadcast_to(shares, (chips,) + shares.shape))
    gathered_other = lax.ppermute(gathered, "dp", swap)
    gathered = jnp.where(
        core == 0,
        jnp.stack([gathered, gathered_other], axis=1),
        jnp.stack([gathered_other, gathered], axis=1),
    )
    gathered = gathered.reshape(members, 4, share, TILE).transpose(1, 0, 2, 3)
    gathered = gathered.reshape(4, members * share, TILE).astype(F32)
    factors = [unpack_upper(gathered[k], width) + DECAY * eye * diagonals[k] for k in range(2)]
    stales = [unpack_upper(gathered[2 + k], width) + eye * diagonals[2 + k] for k in range(2)]
    inverses = []
    for factor, inverse in zip(factors, stales):
        inner = jnp.dot(factor + DAMPING * eye, inverse, precision=lax.Precision.HIGHEST)
        inverses.append(
            2.0 * inverse - jnp.dot(inverse, inner, precision=lax.Precision.HIGHEST)
        )
    keeps = [member == fresh_owner[k] for k in range(2)]
    factor_out = jnp.where(keeps[0], factors[0], jnp.where(keeps[1], factors[1], 0.0))
    inverse_out = jnp.where(keeps[0], inverses[0], jnp.where(keeps[1], inverses[1], 0.0))
    right_inverse = inverses[1].astype(BF16)

    holders = members // columns
    share_rows = feature_count // members
    left_rows = lax.dynamic_slice_in_dim(
        inverses[0].astype(BF16), (member % holders) * share_rows, share_rows, 0
    )
    left_rows = lax.all_to_all(
        jnp.broadcast_to(left_rows, (columns,) + left_rows.shape), "mp", 0, 0, tiled=True
    )
    left_rows = lax.dynamic_index_in_dim(left_rows, member // holders, 0, keepdims=False)

    grad_parts = contract_rows(features, grads_kept).astype(BF16)
    grad_rows = reduce_scatter(grad_parts.reshape(members, share_rows, width)).astype(BF16)
    neighbours = [[holders * c + r for r in range(holders)] for c in range(columns)]
    grad_block = lax.all_gather(
        grad_rows, "dp", axis=0, tiled=True, axis_index_groups=neighbours
    )
    half = jnp.dot(left_rows, grad_block, preferred_element_type=F32).astype(BF16)
    result = jnp.dot(half, right_inverse, preferred_element_type=F32)

    curvature = jnp.full((8, TILE), jnp.sum(result * grad_rows.astype(F32)))
    curvature = curvature + lax.ppermute(curvature, "dp", swap)
    curvature = jnp.sum(across_chips(jnp.broadcast_to(curvature, (chips, 8, TILE))), axis=0)
    curvature = lax.all_to_all(
        jnp.broadcast_to(curvature, (columns, 8, TILE)), "mp", 0, 0, tiled=True
    )
    curvature = jnp.sum(curvature, axis=0)[0, 0]
    entries = float(feature_count * width * columns)
    clip_scale = jnp.minimum(1.0, jnp.sqrt(entries / jnp.abs(curvature)))
    return (factor_out[None, None], inverse_out[None, None], clip_scale * result)


def solution(mesh):
    return jax.shard_map(
        local,
        mesh=mesh,
        in_specs=(
            P("dp", None),
            P("dp", "mp"),
            P("dp"),
            P("mp", "dp", None, None, None),
            P("mp", "dp", None, None, None),
            P(),
            P(),
        ),
        out_specs=(P("mp", "dp", None, None), P("mp", "dp", None, None), P("dp", "mp")),
        check_vma=False,
    )
```

time: 957 us -> 234 us (0.24)
  waiting for transfers between devices: 729 us -> 35.8 us
  blocking collectives: 146 us -> 9.9 us
  local copies, waits for them, and re-layouts: 8.34 us -> 68.4 us
  starting transfers between devices: 20.5 us -> 52 us
  other arithmetic: 13.1 us -> 22.8 us
    psum x2 -> x0, waiting for transfers between devices: 488 us -> none  [the longest x1 286 us: from_root(): return lax.psum(block, axis)]
    reduce_scatter x1 -> x0, waiting for transfers between devices: 149 us -> none  [local(): lax.psum_scatter(contract_rows(grads_kept, features), 'dp', scatter_dimen...]
    psum x2 -> x0, blocking collectives: 146 us -> none  [the longest x1 75.6 us: local(): curvature = lax.psum(curvature, ('dp', 'mp'))]
    all_gather x1 -> x0, waiting for transfers between devices: 84.6 us -> none  [local(): left_inverses = lax.all_gather(rounded[0][None], 'mp', axis=0, tiled=True)]
    all_to_all x2 -> x7, waiting for transfers between devices: 7.21 us -> 34.1 us  [the longest x5 31.3 us: across_chips(): lax.all_to_all(parts, 'dp', 0, 0, tiled=True, axis_index_groups=same_core)]
    all_to_all x2 -> x7, starting transfers between devices: 20.2 us -> 45.9 us  [the longest x5 38.5 us: across_chips(): lax.all_to_all(parts, 'dp', 0, 0, tiled=True, axis_index_groups=same_core)]
    unnamed x11 -> x189, local copies, waits for them, and re-layouts: 1.82 us -> 22.8 us
    transpose x0 -> x12, local copies, waits for them, and re-layouts: none -> 13.4 us  [tile(): return piece if a <= b else piece.T]
  transfers between devices with their start and end apart: 6 -> 12, of which waited for: 5 -> 6; matrix products, arithmetic and copies ran while one was open for 2% -> 46% of each run, Pallas kernels for 0% -> 0%
where the time goes in v1:
time: 234 us; the launch traced here: 231 us
  local copies, waits for them, and re-layouts  68.4 us (29%)
  starting transfers between devices  52 us (22%)
  waiting for transfers between devices  35.8 us (15%)
  matrix products  27.7 us (12%)
  other arithmetic  22.8 us (10%)
  between operations  14.1 us (6%)
  blocking collectives  9.9 us (4%)
    all_to_all x5, starting transfers between devices, across_chips(): lax.all_to_all(parts, 'dp', 0, 0, tiled=True, axis_index_groups=same_core)  38.5 us
    all_to_all x5, waiting for transfers between devices, across_chips(): lax.all_to_all(parts, 'dp', 0, 0, tiled=True, axis_index_groups=same_core)  31.3 us
    unnamed x189, local copies, waits for them, and re-layouts  22.8 us
    transpose x12, local copies, waits for them, and re-layouts, tile(): return piece if a <= b else piece.T  13.4 us
    dot_general x3, matrix products, contract_rows(): lax.dot_general(first_rows, second_rows, (((0,), (0,)), ((), ())), prefer...  13.2 us
    dynamic_slice x1, local copies, waits for them, and re-layouts, pair_split(): mine = lax.dynamic_index_in_dim(paired, core, 1, keepdims=False)  11.3 us
    all_gather x1, blocking collectives, local(): lax.all_gather(grad_rows, 'dp', axis=0, tiled=True, axis_index_groups=nei...  9.9 us
    another operation x1, local copies, waits for them, and re-layouts, pair_split(): paired = parts.reshape((chips, 2) + parts.shape[1:])  7.78 us
  transfers between devices with their start and end apart: 12, of which 6 were waited for; matrix products, arithmetic and copies ran while one was open for 46% of the time, Pallas kernels for 0%

profile of v1, /device:TPU:1, one launch (start us, length us, event | category | flops | bytes accessed | tf_op | source)
XLA Modules:
  0.0 230.8 jit_solution(6324827446191217854)
XLA Ops:
  1.3 2.6 %fusion.10 = bf16[512,512]{1,0:T(8,128)(2,1)S(1)} fusion(bf16[1024,4096]{1,0:T(8,128)(2,1)} %param.9, s32[]{:T(128)S(6)} %select_n.154, pred[1024]{0:T(1024)(128)(4,1)S(1)} %iota_compare_fusion.4), kind=kOutput, calls=%fused_computation.25 | convolution fusion | flops 537657344 | bytes 2623488 | tf_op jit(solution)/shard_map/dot_general | solution.py:15
  6.4 3.2 %collective-permute-start.1 = (bf16[16,96,128]{2,1,0:T(8,128)(2,1)}, bf16[16,96,128]{2,1,0:T(8,128)(2,1)S(1)}, u32[]{:S(2)}, u32[]{:S(2)}) collective-permute-start(bf16[16,96,128]{2,1,0:T(8,128)(2,1)} %dynamic-slice_bitcast_fusion), channel_id=1, source_target_pairs={{0,8},{8,0},{16,24},{24,16},{32,40},{40,32},{48,56},{56,48},{64,72... | collective-permute-start | bytes 1179656 | tf_op jit(solution)/shard_map/ppermute | solution.py:71
  11.7 1.9 fusion.75
  15.8 9.2 %all-to-all-start.1 = ((bf16[16,96,128]{2,1,0:T(8,128)(2,1)}), bf16[16,96,128]{2,1,0:T(8,128)(2,1)S(1)}, u32[]{:S(2)}, u32[]{:S(2)}) async-start(bf16[16,96,128]{2,1,0:T(8,128)(2,1)} %fusion.89), calls=%async_computation.1 | async-start | bytes 786432 | tf_op jit(solution)/shard_map/all_to_all | solution.py:74
  27.0 2.4 %fusion.88 = bf16[16,192,128]{2,1,0:T(8,128)(2,1)} fusion(bf16[16,192,128]{2,1,0:T(8,128)(2,1)} %collective-permute-done, s32[]{:T(128)S(6)} %select_n.147, bf16[16,2,160,128]{3,2,1,0:T(8,128)(2,1)S(1)} %bitcast.263, bf16[16,2,32,128]{3,2,1,0:T(8,128)(2,1)S(1)} %broadcast_in_dim.83, pred[192]{0:T(512)(128)(4,1)S(1)} %select_reduce_fusion), kind=kLoop, calls=%fused_computation.116 | loop fusion | flops 1966080 | bytes 3145924 | tf_op jit(solution)/shard_map/jit(_where)/select_n | solution.py:110
  29.4 8.1 %all-to-all-done.1 = bf16[16,96,128]{2,1,0:T(8,128)(2,1)S(1)} async-done(((bf16[16,96,128]{2,1,0:T(8,128)(2,1)}), bf16[16,96,128]{2,1,0:T(8,128)(2,1)S(1)}, u32[]{:S(2)}, u32[]{:S(2)}) %all-to-all-start.1) | async-done | bytes 393248 | tf_op jit(solution)/shard_map/all_to_all | solution.py:74
  37.5 6.1 %all-to-all-start = ((bf16[16,192,128]{2,1,0:T(8,128)(2,1)}), bf16[16,192,128]{2,1,0:T(8,128)(2,1)S(1)}, u32[]{:S(2)}, u32[]{:S(2)}) async-start(bf16[16,192,128]{2,1,0:T(8,128)(2,1)} %fusion.88), calls=%async_computation | async-start | bytes 1572864 | tf_op jit(solution)/shard_map/all_to_all | solution.py:74
  43.7 9.7 %fusion = bf16[4096,512]{0,1:T(8,128)(2,1)} fusion(bf16[1024,4096]{1,0:T(8,128)(2,1)} %param.9, bf16[1024,512]{1,0:T(8,128)(2,1)S(1)} %copy-done.62, pred[1024]{0:T(1024)(128)(4,1)S(1)} %iota_compare_fusion.4), kind=kOutput, calls=%fused_computation.1 | convolution fusion | flops 4297588736 | bytes 13632512 | tf_op jit(solution)/shard_map/dot_general | solution.py:15
  53.4 7.8 %reshape_reshape.3 = bf16[16,2,128,512]{2,1,0,3:T(2,128)(2,1)} reshape(bf16[4096,512]{0,1:T(8,128)(2,1)} %fusion) | data formatting | bytes 8388608 | tf_op jit(solution)/shard_map/reshape;reshape | solution.py:68
  61.2 11.3 %constant_dynamic-slice_fusion.1 = (bf16[16,1,128,512]{2,1,0,3:T(2,128)(2,1)}, bf16[16,1,128,512]{2,1,0,3:T(2,128)(2,1)}) fusion(bf16[16,2,128,512]{2,1,0,3:T(2,128)(2,1)} %reshape_reshape.3, s32[]{:T(128)S(6)} %select_n.147, s32[]{:T(128)S(6)} %select_n.148), kind=kLoop, calls=%fused_computation.259 | loop fusion | bytes 8388616 | tf_op jit(solution)/shard_map/jit(dynamic_index_in_dim)/dynamic_slice | solution.py:69
  72.5 10.5 %copy.133 = bf16[16,1,128,512]{3,2,0,1:T(8,128)(2,1)} copy(bf16[16,1,128,512]{2,1,0,3:T(2,128)(2,1)} %get-tuple-element.10) | data formatting | bytes 4194304
  82.9 1.3 collective-permute-start.3
  93.0 9.3 %all-to-all-start.2 = ((bf16[16,160,128]{2,1,0:T(8,128)(2,1)}), bf16[16,160,128]{2,1,0:T(8,128)(2,1)S(1)}, u32[]{:S(2)}, u32[]{:S(2)}) async-start(bf16[16,160,128]{2,1,0:T(8,128)(2,1)} %broadcast_in_dim.90), calls=%async_computation.2 | async-start | bytes 1310720 | tf_op jit(solution)/shard_map/all_to_all | solution.py:74
  104.2 9.0 %copy.132 = bf16[16,1,128,512]{3,2,0,1:T(8,128)(2,1)S(1)} copy(bf16[16,1,128,512]{2,1,0,3:T(2,128)(2,1)} %get-tuple-element.9) | data formatting | bytes 4194304
  113.2 3.6 %fusion.1 = bf16[16,128,512]{2,1,0:T(8,128)(2,1)} fusion(bf16[16,128,512]{2,1,0:T(8,128)(2,1)} %collective-permute-done.3, bf16[16,1,128,512]{3,2,0,1:T(8,128)(2,1)S(1)} %copy.132), kind=kLoop, calls=%fused_computation.3 | loop fusion | flops 4194304 | bytes 6291456 | tf_op jit(solution)/shard_map/convert_element_type | solution.py:78
  116.8 4.2 %all-to-all-done.2 = bf16[16,160,128]{2,1,0:T(8,128)(2,1)S(1)} async-done(((bf16[16,160,128]{2,1,0:T(8,128)(2,1)}), bf16[16,160,128]{2,1,0:T(8,128)(2,1)S(1)}, u32[]{:S(2)}, u32[]{:S(2)}) %all-to-all-start.2) | async-done | bytes 655392 | tf_op jit(solution)/shard_map/all_to_all | solution.py:74
  121.0 6.1 %all-to-all-start.4 = ((bf16[16,128,512]{2,1,0:T(8,128)(2,1)}), bf16[16,128,512]{2,1,0:T(8,128)(2,1)}, u32[]{:S(2)}, u32[]{:S(2)}) async-start(bf16[16,128,512]{2,1,0:T(8,128)(2,1)} %fusion.1), calls=%async_computation.4 | async-start | bytes 4194304 | tf_op jit(solution)/shard_map/all_to_all | solution.py:74
  127.1 1.2 collective-permute-start.2
  128.4 1.7 collective-permute-done.2
  130.7 1.0 slice_bitcast_fusion.1
  135.4 1.0 copy.89
  136.4 1.0 copy.90
  137.4 1.0 copy.91
  138.4 1.6 copy.97
  139.9 1.6 copy.98
  141.5 1.6 copy.99
  143.0 0.9 copy.104
  144.0 1.0 copy.105
  145.0 1.0 copy.106
  145.9 1.6 copy.112
  151.4 2.0 fusion.20
  153.6 3.2 %convolution_subtract_fusion.1 = f32[512,512]{1,0:T(8,128)S(1)} fusion(f32[512,512]{1,0:T(8,128)S(1)} %fusion.20, f32[512]{0:T(512)S(1)} %get-tuple-element.79, f32[128,128]{1,0:T(8,128)S(1)} %copy-done.41, f32[128,128]{1,0:T(8,128)} %copy-done.56, f32[128,128]{1,0:T(8,128)} %bitcast.301, f32[128,128]{1,0:T(8,128)} %copy-done.55, ...), kind=kOutput, calls=%fused_computation.21 | convolution fusion | flops 1619001344 | bytes 3147776 | tf_op jit(solution)/shard_map/dot_general | solution.py:154
  159.2 3.8 %fusion.21 = f32[512,512]{1,0:T(8,128)} fusion(f32[128,128]{1,0:T(8,128)S(1)} %copy-done.17, f32[128,128]{1,0:T(8,128)S(1)} %copy-done.32, f32[128,128]{1,0:T(8,128)S(1)} %copy-done.31, f32[128,128]{1,0:T(8,128)S(1)} %bitcast.278, f32[128,128]{1,0:T(8,128)S(1)} %copy-done.18, f32[128,128]{1,0:T(8,128)S(1)} %copy-done.11, f32[128,128]{1,0:T(8,128)S(1)} %copy-done.30, ...), kind=kOutput, calls=%fused_computation.35 | convolution fusion | flops 1619263488 | bytes 3149824 | tf_op jit(solution)/shard_map/dot_general | solution.py:152
  163.0 13.3 %all-to-all-done.4 = bf16[16,128,512]{2,1,0:T(8,128)(2,1)} async-done(((bf16[16,128,512]{2,1,0:T(8,128)(2,1)}), bf16[16,128,512]{2,1,0:T(8,128)(2,1)}, u32[]{:S(2)}, u32[]{:S(2)}) %all-to-all-start.4) | async-done | bytes 2097184 | tf_op jit(solution)/shard_map/all_to_all | solution.py:74
  176.3 1.1 broadcast_in_dim.92
  177.4 4.1 %all-to-all-start.3 = ((bf16[8,128,512]{2,1,0:T(8,128)(2,1)}), bf16[8,128,512]{2,1,0:T(8,128)(2,1)S(1)}, u32[]{:S(2)}, u32[]{:S(2)}) async-start(bf16[8,128,512]{2,1,0:T(8,128)(2,1)} %broadcast_in_dim.92), calls=%async_computation.3 | async-start | bytes 2097152 | tf_op jit(solution)/shard_map/all_to_all | solution.py:166
  181.5 3.8 %convolution_subtract_fusion = f32[512,512]{1,0:T(8,128)S(1)} fusion(f32[512,512]{1,0:T(8,128)} %fusion.21, f32[512]{0:T(512)S(1)} %get-tuple-element.78, f32[128,128]{1,0:T(8,128)} %get-tuple-element.60, f32[128,128]{1,0:T(8,128)} %copy.114, f32[128,128]{1,0:T(8,128)} %bitcast.290, f32[128,128]{1,0:T(8,128)} %copy.113, f32[128,128]{1,0:T(8,128)} %get-tuple-element.59, ...), kind=kOutput, calls=%fused_computation.20 | convolution fusion | flops 1619001344 | bytes 3147776 | tf_op jit(solution)/shard_map/dot_general | solution.py:154
  185.3 1.2 select_bitcast_fusion
  186.5 1.9 reduce_sum.89
  188.4 9.9 %all_gather.3 = bf16[512,512]{1,0:T(8,128)(2,1)S(1)} all-gather(bf16[128,512]{1,0:T(8,128)(2,1)S(1)} %reduce_sum.89), channel_id=1, replica_groups={{0,8,16,24},{32,40,48,56},{64,72,80,88},{96,104,112,120},{128,136,144,1..., dimensions={0}, use_global_device_ids=true | all-gather | bytes 655360 | tf_op jit(solution)/shard_map/all_gather | solution.py:174
  198.3 1.7 multiply_reduce_fusion
  200.9 1.0 maximum_bitcast_fusion.2
  203.2 7.7 %all-to-all-start.5 = ((f32[16,8,128]{2,1,0:T(8,128)}), f32[16,8,128]{2,1,0:T(8,128)S(1)}, u32[]{:S(2)}, u32[]{:S(2)}) async-start(f32[16,8,128]{2,1,0:T(8,128)} %broadcast_in_dim.94), calls=%async_computation.5 | async-start | bytes 131072 | tf_op jit(solution)/shard_map/all_to_all | solution.py:74
  212.0 1.1 copy.100
  214.1 5.7 %all-to-all-done.5 = f32[16,8,128]{2,1,0:T(8,128)S(1)} async-done(((f32[16,8,128]{2,1,0:T(8,128)}), f32[16,8,128]{2,1,0:T(8,128)S(1)}, u32[]{:S(2)}, u32[]{:S(2)}) %all-to-all-start.5) | async-done | bytes 65568 | tf_op jit(solution)/shard_map/all_to_all | solution.py:74
  220.5 3.3 %all-to-all-start.6 = ((f32[8,8,128]{2,1,0:T(8,128)}), f32[8,8,128]{2,1,0:T(8,128)S(1)}, u32[]{:S(2)}, u32[]{:S(2)}) async-start(f32[8,8,128]{2,1,0:T(8,128)} %broadcast_in_dim.95), calls=%async_computation.6 | async-start | bytes 65536 | tf_op jit(solution)/shard_map/all_to_all | solution.py:183
  223.8 2.3 fusion.15
  226.1 2.7 %all-to-all-done.6 = f32[8,8,128]{2,1,0:T(8,128)S(1)} async-done(((f32[8,8,128]{2,1,0:T(8,128)}), f32[8,8,128]{2,1,0:T(8,128)S(1)}, u32[]{:S(2)}, u32[]{:S(2)}) %all-to-all-start.6) | async-done | bytes 32800 | tf_op jit(solution)/shard_map/all_to_all | solution.py:183
  (267 shorter events, 24.6 us)
Async XLA Ops:
  5.0 4.7 %copy-start.57 = (s32[8,2]{0,1:T(2,128)S(1)}, s32[8,2]{0,1:T(2,128)}, u32[]{:S(2)}) copy-start(s32[8,2]{0,1:T(2,128)} %param.14) | copy-start | bytes 196
  5.0 4.7 %copy-start.58 = (s32[8,2]{0,1:T(2,128)S(1)}, s32[8,2]{0,1:T(2,128)}, u32[]{:S(2)}) copy-start(s32[8,2]{0,1:T(2,128)} %param.15) | copy-start | bytes 196
  6.4 8.5 %collective-permute-start.1 = (bf16[16,96,128]{2,1,0:T(8,128)(2,1)}, bf16[16,96,128]{2,1,0:T(8,128)(2,1)S(1)}, u32[]{:S(2)}, u32[]{:S(2)}) collective-permute-start(bf16[16,96,128]{2,1,0:T(8,128)(2,1)} %dynamic-slice_bitcast_fusion), channel_id=1, source_target_pairs={{0,8},{8,0},{16,24},{24,16},{32,40},{40,32},{48,56},{56,48},{64,72... | collective-permute-start | bytes 1179656 | tf_op jit(solution)/shard_map/ppermute | solution.py:71
  14.8 12.2 %copy-start.59 = (pred[192,1]{0,1:T(4,128)(4,1)S(1)}, pred[192,1]{0,1:T(4,128)(4,1)}, u32[]{:S(2)}) copy-start(pred[192,1]{0,1:T(4,128)(4,1)} %constant.162.clone) | copy-start | bytes 580
  14.9 12.1 %collective-permute-start = (bf16[16,192,128]{2,1,0:T(8,128)(2,1)S(1)}, bf16[16,192,128]{2,1,0:T(8,128)(2,1)}, u32[]{:S(2)}, u32[]{:S(2)}) collective-permute-start(bf16[16,192,128]{2,1,0:T(8,128)(2,1)S(1)} %fusion.85), channel_id=1, source_target_pairs={{0,8},{8,0},{16,24},{24,16},{32,40},{40,32},{48,56},{56,48},{64,72... | collective-permute-start | bytes 2359304 | tf_op jit(solution)/shard_map/ppermute | solution.py:71
  15.8 21.7 %all-to-all-start.1 = ((bf16[16,96,128]{2,1,0:T(8,128)(2,1)}), bf16[16,96,128]{2,1,0:T(8,128)(2,1)S(1)}, u32[]{:S(2)}, u32[]{:S(2)}) async-start(bf16[16,96,128]{2,1,0:T(8,128)(2,1)} %fusion.89), calls=%async_computation.1 | async-start | bytes 786432 | tf_op jit(solution)/shard_map/all_to_all | solution.py:74
  27.0 16.7 %copy-start.62 = (bf16[1024,512]{1,0:T(8,128)(2,1)S(1)}, bf16[1024,512]{1,0:T(8,128)(2,1)}, u32[]{:S(2)}) copy-start(bf16[1024,512]{1,0:T(8,128)(2,1)} %param.10) | copy-start | bytes 3145732
  37.5 54.4 %all-to-all-start = ((bf16[16,192,128]{2,1,0:T(8,128)(2,1)}), bf16[16,192,128]{2,1,0:T(8,128)(2,1)S(1)}, u32[]{:S(2)}, u32[]{:S(2)}) async-start(bf16[16,192,128]{2,1,0:T(8,128)(2,1)} %fusion.88), calls=%async_computation | async-start | bytes 1572864 | tf_op jit(solution)/shard_map/all_to_all | solution.py:74
  72.4 19.4 %copy-start.60 = (pred[192]{0:T(512)(128)(4,1)S(1)}, pred[192]{0:T(512)(128)(4,1)}, u32[]{:S(2)}) copy-start(pred[192]{0:T(512)(128)(4,1)} %constant.166) | copy-start | bytes 580
  82.9 30.2 %collective-permute-start.3 = (bf16[16,128,512]{2,1,0:T(8,128)(2,1)}, bf16[16,128,512]{2,1,0:T(8,128)(2,1)}, u32[]{:S(2)}, u32[]{:S(2)}) collective-permute-start(bf16[16,128,512]{2,1,0:T(8,128)(2,1)} %bitcast.119), channel_id=1, source_target_pairs={{0,8},{8,0},{16,24},{24,16},{32,40},{40,32},{48,56},{56,48},{64,72... | collective-permute-start | bytes 6291464 | tf_op jit(solution)/shard_map/ppermute | solution.py:71
  93.0 28.0 %all-to-all-start.2 = ((bf16[16,160,128]{2,1,0:T(8,128)(2,1)}), bf16[16,160,128]{2,1,0:T(8,128)(2,1)S(1)}, u32[]{:S(2)}, u32[]{:S(2)}) async-start(bf16[16,160,128]{2,1,0:T(8,128)(2,1)} %broadcast_in_dim.90), calls=%async_computation.2 | async-start | bytes 1310720 | tf_op jit(solution)/shard_map/all_to_all | solution.py:74
  121.0 55.4 %all-to-all-start.4 = ((bf16[16,128,512]{2,1,0:T(8,128)(2,1)}), bf16[16,128,512]{2,1,0:T(8,128)(2,1)}, u32[]{:S(2)}, u32[]{:S(2)}) async-start(bf16[16,128,512]{2,1,0:T(8,128)(2,1)} %fusion.1), calls=%async_computation.4 | async-start | bytes 4194304 | tf_op jit(solution)/shard_map/all_to_all | solution.py:74
  127.1 3.0 %collective-permute-start.2 = (bf16[16,160,128]{2,1,0:T(8,128)(2,1)S(1)}, bf16[16,160,128]{2,1,0:T(8,128)(2,1)S(1)}, u32[]{:S(2)}, u32[]{:S(2)}) collective-permute-start(bf16[16,160,128]{2,1,0:T(8,128)(2,1)S(1)} %all-to-all-done.2), channel_id=1, source_target_pairs={{0,8},{8,0},{16,24},{24,16},{32,40},{40,32},{48,56},{56,48},{64,72... | collective-permute-start | bytes 1966088 | tf_op jit(solution)/shard_map/ppermute | solution.py:140
  134.4 16.7 %copy-start.3 = (f32[1,128,128]{1,2,0:T(8,128)}, f32[1,128,128]{1,2,0:T(8,128)S(1)}, u32[]{:S(2)}) copy-start(f32[1,128,128]{1,2,0:T(8,128)S(1)} %copy.121) | copy-start | bytes 196612
  135.4 14.1 %copy-start.20 = (f32[128,128]{0,1:T(8,128)S(1)}, f32[128,128]{0,1:T(8,128)}, u32[]{:S(2)}) copy-start(f32[128,128]{0,1:T(8,128)} %get-tuple-element.23) | copy-start | bytes 196612
  135.4 14.1 %copy-start.22 = (f32[1,128,128]{1,2,0:T(8,128)S(1)}, f32[1,128,128]{1,2,0:T(8,128)}, u32[]{:S(2)}) copy-start(f32[1,128,128]{1,2,0:T(8,128)} %copy.131) | copy-start | bytes 196612
  135.4 14.5 %copy-start.19 = (f32[128,128]{0,1:T(8,128)S(1)}, f32[128,128]{0,1:T(8,128)}, u32[]{:S(2)}) copy-start(f32[128,128]{0,1:T(8,128)} %get-tuple-element.19) | copy-start | bytes 196612
  135.4 14.5 %copy-start.26 = (f32[1,128,128]{1,2,0:T(8,128)S(1)}, f32[1,128,128]{1,2,0:T(8,128)}, u32[]{:S(2)}) copy-start(f32[1,128,128]{1,2,0:T(8,128)} %copy.127) | copy-start | bytes 196612
  136.4 14.7 %copy-start.21 = (f32[128,128]{1,0:T(8,128)}, f32[128,128]{1,0:T(8,128)S(1)}, u32[]{:S(2)}) copy-start(f32[128,128]{1,0:T(8,128)S(1)} %copy.89) | copy-start | bytes 196612
  137.4 13.8 %copy-start.24 = (f32[128,128]{1,0:T(8,128)}, f32[128,128]{1,0:T(8,128)S(1)}, u32[]{:S(2)}) copy-start(f32[128,128]{1,0:T(8,128)S(1)} %copy.90) | copy-start | bytes 196612
  138.3 12.8 %copy-start.25 = (f32[128,128]{1,0:T(8,128)}, f32[128,128]{1,0:T(8,128)S(1)}, u32[]{:S(2)}) copy-start(f32[128,128]{1,0:T(8,128)S(1)} %copy.91) | copy-start | bytes 196612
  144.0 7.2 %copy-start.54 = (f32[128,128]{1,0:T(8,128)}, f32[128,128]{1,0:T(8,128)S(1)}, u32[]{:S(2)}) copy-start(f32[128,128]{1,0:T(8,128)S(1)} %copy.104) | copy-start | bytes 196612
  144.9 6.2 %copy-start.55 = (f32[128,128]{1,0:T(8,128)}, f32[128,128]{1,0:T(8,128)S(1)}, u32[]{:S(2)}) copy-start(f32[128,128]{1,0:T(8,128)S(1)} %copy.105) | copy-start | bytes 196612
  145.9 5.3 %copy-start.56 = (f32[128,128]{1,0:T(8,128)}, f32[128,128]{1,0:T(8,128)S(1)}, u32[]{:S(2)}) copy-start(f32[128,128]{1,0:T(8,128)S(1)} %copy.106) | copy-start | bytes 196612
  149.9 9.2 %copy-start.4 = (f32[128,512]{1,0:T(8,128)}, f32[128,512]{1,0:T(8,128)S(1)}, u32[]{:S(2)}) copy-start(f32[128,512]{1,0:T(8,128)S(1)} %copy.115) | copy-start | bytes 786436
  153.5 4.2 %copy-start.17 = (f32[128,128]{1,0:T(8,128)S(1)}, f32[128,128]{1,0:T(8,128)}, u32[]{:S(2)}) copy-start(f32[128,128]{1,0:T(8,128)} %get-tuple-element.47) | copy-start | bytes 196612
  153.5 4.2 %copy-start.31 = (f32[128,128]{1,0:T(8,128)S(1)}, f32[128,128]{1,0:T(8,128)}, u32[]{:S(2)}) copy-start(f32[128,128]{1,0:T(8,128)} %copy.98) | copy-start | bytes 196612
  153.5 4.9 %copy-start.11 = (f32[128,128]{1,0:T(8,128)S(1)}, f32[128,128]{1,0:T(8,128)}, u32[]{:S(2)}) copy-start(f32[128,128]{1,0:T(8,128)} %get-tuple-element.50) | copy-start | bytes 196612
  153.5 4.9 %copy-start.18 = (f32[128,128]{1,0:T(8,128)S(1)}, f32[128,128]{1,0:T(8,128)}, u32[]{:S(2)}) copy-start(f32[128,128]{1,0:T(8,128)} %get-tuple-element.48) | copy-start | bytes 196612
  153.5 4.9 %copy-start.30 = (f32[128,128]{1,0:T(8,128)S(1)}, f32[128,128]{1,0:T(8,128)}, u32[]{:S(2)}) copy-start(f32[128,128]{1,0:T(8,128)} %copy.97) | copy-start | bytes 196612
  153.5 5.6 %copy-start.5 = (f32[128,128]{1,0:T(8,128)S(1)}, f32[128,128]{1,0:T(8,128)}, u32[]{:S(2)}) copy-start(f32[128,128]{1,0:T(8,128)} %get-tuple-element.51) | copy-start | bytes 196612
  153.5 5.6 %copy-start.6 = (f32[128,128]{1,0:T(8,128)S(1)}, f32[128,128]{1,0:T(8,128)}, u32[]{:S(2)}) copy-start(f32[128,128]{1,0:T(8,128)} %get-tuple-element.52) | copy-start | bytes 196612
  153.5 5.6 %copy-start.7 = (f32[128,128]{1,0:T(8,128)S(1)}, f32[128,128]{1,0:T(8,128)}, u32[]{:S(2)}) copy-start(f32[128,128]{1,0:T(8,128)} %get-tuple-element.53) | copy-start | bytes 196612
  153.6 5.6 %copy-start.23 = (f32[1,128,128]{1,2,0:T(8,128)S(1)}, f32[1,128,128]{1,2,0:T(8,128)}, u32[]{:S(2)}) copy-start(f32[1,128,128]{1,2,0:T(8,128)} %copy.131) | copy-start | bytes 196612
  153.6 5.6 %copy-start.29 = (f32[1,128,128]{1,2,0:T(8,128)S(1)}, f32[1,128,128]{1,2,0:T(8,128)}, u32[]{:S(2)}) copy-start(f32[1,128,128]{1,2,0:T(8,128)} %copy-done.28) | copy-start | bytes 196612
  153.6 5.6 %copy-start.34 = (f32[128,128]{1,0:T(8,128)S(1)}, f32[128,128]{1,0:T(8,128)}, u32[]{:S(2)}) copy-start(f32[128,128]{1,0:T(8,128)} %get-tuple-element.49) | copy-start | bytes 196612
  153.6 5.6 %copy-start.35 = (f32[128,128]{1,0:T(8,128)S(1)}, f32[128,128]{1,0:T(8,128)}, u32[]{:S(2)}) copy-start(f32[128,128]{1,0:T(8,128)} %get-tuple-element.59) | copy-start | bytes 196612
  153.6 5.6 %copy-start.36 = (f32[128,128]{1,0:T(8,128)S(1)}, f32[128,128]{1,0:T(8,128)}, u32[]{:S(2)}) copy-start(f32[128,128]{1,0:T(8,128)} %get-tuple-element.60) | copy-start | bytes 196612
  153.6 5.6 %copy-start.37 = (f32[128,128]{1,0:T(8,128)S(1)}, f32[128,128]{1,0:T(8,128)}, u32[]{:S(2)}) copy-start(f32[128,128]{1,0:T(8,128)} %get-tuple-element.30) | copy-start | bytes 196612
  153.6 5.6 %copy-start.38 = (f32[128,128]{1,0:T(8,128)S(1)}, f32[128,128]{1,0:T(8,128)}, u32[]{:S(2)}) copy-start(f32[128,128]{1,0:T(8,128)} %get-tuple-element.41) | copy-start | bytes 196612
  153.6 5.6 %copy-start.39 = (f32[128,128]{1,0:T(8,128)S(1)}, f32[128,128]{1,0:T(8,128)}, u32[]{:S(2)}) copy-start(f32[128,128]{1,0:T(8,128)} %get-tuple-element.42) | copy-start | bytes 196612
  153.6 5.6 %copy-start.44 = (f32[128,128]{1,0:T(8,128)S(1)}, f32[128,128]{1,0:T(8,128)}, u32[]{:S(2)}) copy-start(f32[128,128]{1,0:T(8,128)} %get-tuple-element.11) | copy-start | bytes 196612
  177.4 20.9 %all-to-all-start.3 = ((bf16[8,128,512]{2,1,0:T(8,128)(2,1)}), bf16[8,128,512]{2,1,0:T(8,128)(2,1)S(1)}, u32[]{:S(2)}, u32[]{:S(2)}) async-start(bf16[8,128,512]{2,1,0:T(8,128)(2,1)} %broadcast_in_dim.92), calls=%async_computation.3 | async-start | bytes 2097152 | tf_op jit(solution)/shard_map/all_to_all | solution.py:166
  198.3 25.5 %copy-start.1 = (f32[1,1,128,512]{3,2,1,0:T(8,128)S(1)}, f32[1,1,128,512]{3,2,1,0:T(8,128)}, u32[]{:S(2)}) copy-start(f32[1,1,128,512]{3,2,1,0:T(8,128)} %maximum_bitcast_fusion) | copy-start | bytes 786436
  200.7 1.3 collective-permute-start.4
  203.2 16.6 %all-to-all-start.5 = ((f32[16,8,128]{2,1,0:T(8,128)}), f32[16,8,128]{2,1,0:T(8,128)S(1)}, u32[]{:S(2)}, u32[]{:S(2)}) async-start(f32[16,8,128]{2,1,0:T(8,128)} %broadcast_in_dim.94), calls=%async_computation.5 | async-start | bytes 131072 | tf_op jit(solution)/shard_map/all_to_all | solution.py:74
  212.0 18.0 %copy-start.2 = (f32[128,512]{1,0:T(8,128)S(1)}, f32[128,512]{1,0:T(8,128)}, u32[]{:S(2)}) copy-start(f32[128,512]{1,0:T(8,128)} %get-tuple-element.95) | copy-start | bytes 786436
  220.5 8.3 %all-to-all-start.6 = ((f32[8,8,128]{2,1,0:T(8,128)}), f32[8,8,128]{2,1,0:T(8,128)S(1)}, u32[]{:S(2)}, u32[]{:S(2)}) async-start(f32[8,8,128]{2,1,0:T(8,128)} %broadcast_in_dim.95), calls=%async_computation.6 | async-start | bytes 65536 | tf_op jit(solution)/shard_map/all_to_all | solution.py:183
  (27 other events, 53.3 us)

commit v2 on v0

v2 whole, which is shorter than its diff:
```python
import jax
import jax.numpy as jnp
from jax import lax
from jax.experimental import pallas as pl
from jax.experimental.pallas import tpu as pltpu
from jax.sharding import PartitionSpec as P

DECAY = 0.9
DAMPING = 0.01
TILE = 128
ROWS = 16
VMEM_BYTES = 48 * 1024 * 1024
BF16 = jnp.bfloat16
F32 = jnp.float32
HIGHEST = lax.Precision.HIGHEST
PARAMS = pltpu.CompilerParams(vmem_limit_bytes=VMEM_BYTES)
SCALARS = pl.BlockSpec(memory_space=pltpu.SMEM)
WHOLE = pl.BlockSpec(memory_space=pltpu.VMEM)


def upper_pairs(tiles):
    return [(a, b) for a in range(tiles) for b in range(a, tiles)]


def diagonal_mask():
    rows = lax.broadcasted_iota(jnp.int32, (TILE, TILE), 0)
    return rows == lax.broadcasted_iota(jnp.int32, (TILE, TILE), 1)


def tile_of(a, b):
    return (slice(a * TILE, (a + 1) * TILE), slice(b * TILE, (b + 1) * TILE))


def pack_old(scalars, factors, inverses, keep, send, packed, diag):
    core, shared = scalars[0], scalars[1]
    tiles = factors.shape[1] // TILE
    on_diagonal = diagonal_mask()
    for which, held in enumerate((factors, inverses)):
        for kind in range(2):
            slot = 0 if kind == 0 else shared
            for n, (a, b) in enumerate(upper_pairs(tiles)):
                piece = held[(slot,) + tile_of(a, b)]
                if a == b:
                    row = (which * 2 + kind) * tiles + a
                    diag[row : row + 1, :] = jnp.sum(
                        jnp.where(on_diagonal, piece, 0.0), axis=0, keepdims=True
                    )
                    piece = jnp.where(on_diagonal, 0.0, piece)
                packed[kind, which, n * TILE : (n + 1) * TILE, :] = piece.astype(BF16)
    high = diag[...].astype(BF16)
    low = (diag[...] - high.astype(F32)).astype(BF16)
    words = jnp.concatenate([high, low], axis=0)
    chips = keep.shape[0]
    share = (keep.shape[1] - words.shape[0]) // 2
    for q in range(chips):
        kind, pair = divmod(q, chips // 2)
        for ref, parity in ((keep, core), (send, 1 - core)):
            start = pl.multiple_of((2 * pair + parity) * share, ROWS)
            for which in range(2):
                ref[q, which * share : (which + 1) * share, :] = packed[
                    kind, which, pl.ds(start, share), :
                ]
            ref[q, 2 * share :, :] = words


def covariance_parts(scalars, own, grads, keep, send, kept, packed):
    core, count = scalars[0], scalars[1]
    rows, width = own.shape
    tiles = width // TILE
    valid = lax.broadcasted_iota(jnp.int32, (rows, width), 0) < count
    for kind, block in enumerate((own, grads)):
        masked = jnp.where(valid, block[...].astype(F32), 0.0)
        kept[...] = masked.T.astype(BF16)
        for n, (a, b) in enumerate(upper_pairs(tiles)):
            if b % 2 == 0 and a % 2 == 0:
                square = jnp.dot(
                    kept[a * TILE : (a + 2) * TILE, :],
                    block[:, b * TILE : (b + 2) * TILE],
                    preferred_element_type=F32,
                ).astype(BF16)
                for i in range(2):
                    for j in range(2):
                        if a + i <= b + j:
                            at = upper_pairs(tiles).index((a + i, b + j))
                            packed[kind, at * TILE : (at + 1) * TILE, :] = square[tile_of(i, j)]
    quarter = lax.broadcasted_iota(jnp.int32, (ROWS, TILE), 0) // 4
    digits = lax.shift_right_logical(jnp.full((ROWS, TILE), count), 3 * quarter) & 7
    digits = digits.astype(F32).astype(BF16)
    chips = keep.shape[0]
    share = keep.shape[1] - ROWS
    for q in range(chips):
        kind, pair = divmod(q, chips // 2)
        for ref, parity in ((keep, core), (send, 1 - core)):
            start = pl.multiple_of((2 * pair + parity) * share, ROWS)
            ref[q, :share, :] = packed[kind, pl.ds(start, share), :]
            ref[q, share:, :] = digits


def gradient_parts(scalars, features, grads, keep, send, turned, product):
    core, count = scalars[0], scalars[1]

    @pl.when(pl.program_id(0) == 0)
    def _():
        valid = lax.broadcasted_iota(jnp.int32, grads.shape, 0) < count
        turned[...] = jnp.where(valid, grads[...].astype(F32), 0.0).T.astype(BF16)

    product[...] = jnp.dot(turned[...], features[...], preferred_element_type=F32).astype(BF16)
    for ref, parity in ((keep, core), (send, 1 - core)):
        start = pl.multiple_of(parity * TILE, TILE)
        ref[0] = product[:, pl.ds(start, TILE)]


def unpack(mine, other, core, kind, packed):
    chips = mine.shape[0]
    share = mine.shape[1] // 2
    for pair in range(chips // 2):
        q = kind * (chips // 2) + pair
        for ref, parity in ((mine, core), (other, 1 - core)):
            start = pl.multiple_of((2 * pair + parity) * share, ROWS)
            for which in range(2):
                packed[which, pl.ds(start, share), :] = ref[
                    q, which * share : (which + 1) * share, :
                ]


def spread(packed, which, diag, row, scale, block):
    tiles = block.shape[0] // TILE
    on_diagonal = diagonal_mask()
    for n, (a, b) in enumerate(upper_pairs(tiles)):
        piece = packed[which, n * TILE : (n + 1) * TILE, :].astype(F32)
        if a == b:
            piece = piece + jnp.where(on_diagonal, scale * diag[row + a : row + a + 1, :], 0.0)
        else:
            block[tile_of(b, a)] = piece.T
        block[tile_of(a, b)] = piece


def load_blocks(mine, other, core, kind, packed, diag, factor, inverse):
    tiles = factor.shape[0] // TILE
    unpack(mine, other, core, kind, packed)
    spread(packed, 0, diag, kind * tiles, DECAY, factor)
    spread(packed, 1, diag, (2 + kind) * tiles, 1.0, inverse)


def refine(factor, inverse, part):
    inner = jnp.dot(factor[...], part, precision=HIGHEST, preferred_element_type=F32)
    inner = inner + DAMPING * part
    return 2.0 * part - jnp.dot(inverse[...], inner, precision=HIGHEST, preferred_element_type=F32)


def left_columns(scalars, mine, other, diag, left, packed, factor, inverse):
    core, place = scalars[0], scalars[1]
    load_blocks(mine, other, core, 0, packed, diag, factor, inverse)
    start = pl.multiple_of(place * TILE, TILE)
    left[...] = refine(factor, inverse, inverse[:, pl.ds(start, TILE)]).astype(BF16)


def new_blocks(scalars, mine, other, diag, right, factor_out, inverse_out, packed, factor, inverse):
    core, first, second = scalars[0], scalars[2], scalars[3]
    load_blocks(mine, other, core, 1, packed, diag, factor, inverse)
    fresh = refine(factor, inverse, inverse[...])
    right[...] = fresh.astype(BF16)

    @pl.when(second == 1)
    def _():
        factor_out[...] = factor[...]
        inverse_out[...] = fresh

    @pl.when(second == 0)
    def _():
        factor_out[...] = jnp.zeros_like(factor_out)
        inverse_out[...] = jnp.zeros_like(inverse_out)

    @pl.when(first == 1)
    def _():
        load_blocks(mine, other, core, 0, packed, diag, factor, inverse)
        factor_out[...] = factor[...]
        inverse_out[...] = refine(factor, inverse, inverse[...])


def precondition(scalars, grad, lefts, right, result, curvature):
    own, block = scalars[0], scalars[1]
    left = lefts[block]
    half = sum(
        jnp.dot(grad[p], left[p * TILE : (p + 1) * TILE, :], preferred_element_type=F32)
        for p in range(grad.shape[0])
    )
    product = jnp.dot(half.T.astype(BF16), right[...], preferred_element_type=F32)
    result[...] = product
    curvature[...] = jnp.full(curvature.shape, jnp.sum(product * grad[own].astype(F32).T))


def local(features, out_grads, counts, factor_old, inverse_old, old_owner, new_owner):
    tok_rows, width = out_grads.shape
    feature_count = features.shape[1]
    column = lax.axis_index("mp")
    member = lax.axis_index("dp")
    members = lax.axis_size("dp")
    columns = lax.axis_size("mp")
    chips = members // 2
    core = member % 2
    swap = [(i, i ^ 1) for i in range(members)]
    same_core = [[2 * q + c for q in range(chips)] for c in range(2)]
    packed_rows = width * (width + TILE) // 2 // TILE
    share = 2 * packed_rows // members
    lanes = width // TILE
    shape = jax.ShapeDtypeStruct

    def across_chips(parts):
        return lax.all_to_all(parts, "dp", 0, 0, tiled=True, axis_index_groups=same_core)

    def pair_sum(keep, send):
        received = lax.ppermute(send, "dp", swap)
        return (keep.astype(F32) + received.astype(F32)).astype(BF16)

    stale_owner = lax.dynamic_index_in_dim(old_owner, column, 0, keepdims=False)
    fresh_owner = lax.dynamic_index_in_dim(new_owner, column, 0, keepdims=False)
    shared_slot = (stale_owner[1] == stale_owner[0]).astype(jnp.int32)

    message = shape((chips, 2 * share + 8 * lanes, TILE), BF16)
    keep, send = pl.pallas_call(
        pack_old,
        out_shape=(message, message),
        in_specs=[SCALARS, WHOLE, WHOLE],
        out_specs=(WHOLE, WHOLE),
        scratch_shapes=[
            pltpu.VMEM((2, 2, packed_rows, TILE), BF16),
            pltpu.VMEM((4 * lanes, TILE), F32),
        ],
        compiler_params=PARAMS,
        name="pack_old",
    )(jnp.stack([core, shared_slot]), factor_old[0, 0], inverse_old[0, 0])
    received = lax.ppermute(send, "dp", swap)
    row = lax.broadcasted_iota(jnp.int32, message.shape, 1) - 2 * share
    chip = lax.broadcasted_iota(jnp.int32, message.shape, 0)
    row_kind = jnp.where(row < 0, chip // (chips // 2), (row // lanes) % 2)
    owner_core = jnp.where(row_kind == 0, stale_owner[0] % 2, stale_owner[1] % 2)
    chosen = across_chips(jnp.where(owner_core == core, keep, received))
    from_first = lax.dynamic_index_in_dim(chosen, stale_owner[0] // 2, 0, keepdims=False)
    from_second = lax.dynamic_index_in_dim(chosen, stale_owner[1] // 2, 0, keepdims=False)
    own_kind = member // chips
    scattered = jnp.where(own_kind == 0, from_first, from_second)
    row = lax.broadcasted_iota(jnp.int32, (8 * lanes, TILE), 0)
    words = jnp.where((row // lanes) % 2 == 0, from_first[2 * share :], from_second[2 * share :])
    words = words.astype(F32)
    diag = words[: 4 * lanes] + words[4 * lanes :]

    message = shape((chips, share + ROWS, TILE), BF16)
    grads_spec = pl.BlockSpec((tok_rows, width), lambda i, s: (0, 0))
    message_spec = pl.BlockSpec(message.shape, lambda i, s: (0, 0, 0))
    keep, send = pl.pallas_call(
        covariance_parts,
        out_shape=(message, message),
        grid_spec=pltpu.PrefetchScalarGridSpec(
            num_scalar_prefetch=1,
            grid=(1,),
            in_specs=[pl.BlockSpec((tok_rows, width), lambda i, s: (0, s[2])), grads_spec],
            out_specs=(message_spec, message_spec),
            scratch_shapes=[
                pltpu.VMEM((width, tok_rows), BF16),
                pltpu.VMEM((2, packed_rows, TILE), BF16),
            ],
        ),
        compiler_params=PARAMS,
        name="covariance_parts",
    )(jnp.stack([core, counts[0], column]), features, out_grads)
    cov_share = jnp.sum(across_chips(pair_sum(keep, send)).astype(F32), axis=0)
    total = sum(cov_share[share + 4 * d, 0] * float(8**d) for d in range(4))
    factor_share = DECAY * scattered[:share].astype(F32) + (1.0 - DECAY) * cov_share[:share] / total

    shares = jnp.concatenate([factor_share.astype(BF16), scattered[share : 2 * share]], axis=0)
    mine = across_chips(jnp.broadcast_to(shares, (chips,) + shares.shape))
    other = lax.ppermute(mine, "dp", swap)
    holders = members // columns
    place = member % holders
    scalars = jnp.stack(
        [core, place, (member == fresh_owner[0]).astype(jnp.int32), (member == fresh_owner[1]).astype(jnp.int32)]
    )
    unpacked = [
        pltpu.VMEM((2, packed_rows, TILE), BF16),
        pltpu.VMEM((width, width), F32),
        pltpu.VMEM((width, width), F32),
    ]
    left = pl.pallas_call(
        left_columns,
        out_shape=shape((width, TILE), BF16),
        in_specs=[SCALARS, WHOLE, WHOLE, WHOLE],
        out_specs=WHOLE,
        scratch_shapes=unpacked,
        compiler_params=PARAMS,
        name="left_columns",
    )(scalars, mine, other, diag)
    lefts = lax.all_to_all(
        jnp.broadcast_to(left, (columns,) + left.shape), "mp", 0, 0, tiled=True
    )
    right, factor_out, inverse_out = pl.pallas_call(
        new_blocks,
        out_shape=(
            shape((width, width), BF16),
            shape((width, width), F32),
            shape((width, width), F32),
        ),
        in_specs=[SCALARS, WHOLE, WHOLE, WHOLE],
        out_specs=(WHOLE, WHOLE, WHOLE),
        scratch_shapes=unpacked,
        compiler_params=PARAMS,
        name="new_blocks",
    )(scalars, mine, other, diag)

    message = shape((chips, width, TILE), BF16)
    message_spec = pl.BlockSpec((1, width, TILE), lambda i, s: (i, 0, 0))
    keep, send = pl.pallas_call(
        gradient_parts,
        out_shape=(message, message),
        grid_spec=pltpu.PrefetchScalarGridSpec(
            num_scalar_prefetch=1,
            grid=(chips,),
            in_specs=[pl.BlockSpec((tok_rows, 2 * TILE), lambda i, s: (0, i)), grads_spec],
            out_specs=(message_spec, message_spec),
            scratch_shapes=[
                pltpu.VMEM((width, tok_rows), BF16),
                pltpu.VMEM((width, 2 * TILE), BF16),
            ],
        ),
        compiler_params=PARAMS,
        name="gradient_parts",
    )(jnp.stack([core, counts[0]]), features, out_grads)
    grad = jnp.sum(across_chips(pair_sum(keep, send)).astype(F32), axis=0).astype(BF16)
    neighbours = [[holders * c + r for r in range(holders)] for c in range(columns)]
    grads = lax.all_gather(grad, "dp", axis=0, axis_index_groups=neighbours)

    result, curvature = pl.pallas_call(
        precondition,
        out_shape=(shape((TILE, width), F32), shape((8, TILE), F32)),
        in_specs=[SCALARS, WHOLE, WHOLE, WHOLE],
        out_specs=(WHOLE, WHOLE),
        compiler_params=PARAMS,
        name="precondition",
    )(jnp.stack([place, member // holders]), grads, lefts, right)

    curvature = curvature + lax.ppermute(curvature, "dp", swap)
    curvature = jnp.sum(across_chips(jnp.broadcast_to(curvature, (chips, 8, TILE))), axis=0)
    curvature = lax.all_to_all(
        jnp.broadcast_to(curvature, (columns, 8, TILE)), "mp", 0, 0, tiled=True
    )
    curvature = jnp.sum(curvature, axis=0)[0, 0]
    entries = float(feature_count * width * columns)
    clip_scale = jnp.minimum(1.0, jnp.sqrt(entries / jnp.abs(curvature)))
    return (factor_out[None, None], inverse_out[None, None], clip_scale * result)


def solution(mesh):
    return jax.shard_map(
        local,
        mesh=mesh,
        in_specs=(
            P("dp", None),
            P("dp", "mp"),
            P("dp"),
            P("mp", "dp", None, None, None),
            P("mp", "dp", None, None, None),
            P(),
            P(),
        ),
        out_specs=(P("mp", "dp", None, None), P("mp", "dp", None, None), P("dp", "mp")),
        check_vma=False,
    )
```

time: 957 us -> 210 us (0.22)
  waiting for transfers between devices: 729 us -> 68.1 us
  blocking collectives: 146 us -> 36.6 us
  Pallas kernels: 0 us -> 31.9 us
  starting transfers between devices: 20.5 us -> 40.8 us
  matrix products: 19.6 us -> 0 us
    psum x2 -> x0, waiting for transfers between devices: 488 us -> none  [the longest x1 286 us: from_root(): return lax.psum(block, axis)]
    reduce_scatter x1 -> x0, waiting for transfers between devices: 149 us -> none  [local(): lax.psum_scatter(contract_rows(grads_kept, features), 'dp', scatter_dimen...]
    psum x2 -> x0, blocking collectives: 146 us -> none  [the longest x1 75.6 us: local(): curvature = lax.psum(curvature, ('dp', 'mp'))]
    all_gather x1 -> x0, waiting for transfers between devices: 84.6 us -> none  [local(): left_inverses = lax.all_gather(rounded[0][None], 'mp', axis=0, tiled=True)]
    all_to_all x2 -> x5, waiting for transfers between devices: 7.21 us -> 66.3 us  [the longest x4 66.3 us: across_chips(): lax.all_to_all(parts, 'dp', 0, 0, tiled=True, axis_index_groups=same_core)]
    pallas_call x0 -> x6, Pallas kernels: none -> 31.9 us  [the longest x1 15.1 us: local(): pl.pallas_call(gradient_parts, out_shape=(message, message), grid_spec=pl...]
    all_to_all x0 -> x2, blocking collectives: none -> 26.7 us  [the longest x1 15.3 us: across_chips(): lax.all_to_all(parts, 'dp', 0, 0, tiled=True, axis_index_groups=same_core)]
    dot_general x5 -> x0, matrix products: 19.6 us -> none  [the longest x4 16.1 us: contract_rows(): lax.dot_general(first_rows, second_rows, (((0,), (0,)), ((), ())), prefer...]
  transfers between devices with their start and end apart: 6 -> 10, of which waited for: 5 -> 5; matrix products, arithmetic and copies ran while one was open for 2% -> 7% of each run, Pallas kernels for 0% -> 13%
where the time goes in v2:
time: 210 us; the launch traced here: 209 us
  waiting for transfers between devices  68.1 us (32%)
  starting transfers between devices  40.8 us (19%)
  blocking collectives  36.6 us (17%)
  Pallas kernels  31.9 us (15%)
  between operations  12.3 us (6%)
  other arithmetic  11.7 us (6%)
  local copies, waits for them, and re-layouts  7.14 us (3%)
    all_to_all x4, waiting for transfers between devices, across_chips(): lax.all_to_all(parts, 'dp', 0, 0, tiled=True, axis_index_groups=same_core)  66.3 us
    all_to_all x4, starting transfers between devices, across_chips(): lax.all_to_all(parts, 'dp', 0, 0, tiled=True, axis_index_groups=same_core)  30.8 us
    all_to_all x1, blocking collectives, across_chips(): lax.all_to_all(parts, 'dp', 0, 0, tiled=True, axis_index_groups=same_core)  15.3 us
    pallas_call x1, Pallas kernels, local(): pl.pallas_call(gradient_parts, out_shape=(message, message), grid_spec=pl...  15.1 us
    all_to_all x1, blocking collectives, local(): lax.all_to_all(jnp.broadcast_to(curvature, (columns, 8, TILE)), 'mp', 0,...  11.4 us
    all_gather x1, blocking collectives, local(): grads = lax.all_gather(grad, 'dp', axis=0, axis_index_groups=neighbours)  9.91 us
    pallas_call x1, Pallas kernels, local(): pl.pallas_call(new_blocks, out_shape=(shape((width, width), BF16), shape(...  5.84 us
    convert_element_type x2, other arithmetic, pair_sum(): return (keep.astype(F32) + received.astype(F32)).astype(BF16)  5.29 us
  transfers between devices with their start and end apart: 10, of which 5 were waited for; matrix products, arithmetic and copies ran while one was open for 7% of the time, Pallas kernels for 13%

profile of v2, /device:TPU:1, one launch (start us, length us, event | category | flops | bytes accessed | tf_op | source)
XLA Modules:
  0.0 208.6 jit_solution(5316511655537940694)
XLA Ops:
  1.3 0.1 pad_add_fusion.2.scalars
  1.4 1.2 copy-done
  2.6 3.8 %covariance_parts.1 = (bf16[16,96,128]{2,1,0:T(8,128)(2,1)S(1)}, bf16[16,96,128]{2,1,0:T(8,128)(2,1)}) custom-call(s32[3]{0:T(128)S(1)} %pad_add_fusion.2.scalars, bf16[1024,4096]{1,0:T(8,128)(2,1)} %features.1, bf16[1024,512]{1,0:T(8,128)(2,1)S(1)} %copy-done), custom_call_target="tpu_custom_call" | custom-call | tf_op jit(solution)/shard_map/covariance_parts/pallas_call | solution.py:251
  6.4 3.2 %collective-permute-start.1 = (bf16[16,96,128]{2,1,0:T(8,128)(2,1)}, bf16[16,96,128]{2,1,0:T(8,128)(2,1)}, u32[]{:S(2)}, u32[]{:S(2)}) collective-permute-start(bf16[16,96,128]{2,1,0:T(8,128)(2,1)} %get-tuple-element.17), channel_id=1, source_target_pairs={{0,8},{8,0},{16,24},{24,16},{32,40},{40,32},{48,56},{56,48},{64,72... | collective-permute-start | bytes 1179656 | tf_op jit(solution)/shard_map/ppermute | solution.py:213
  9.6 0.1 constant_dynamic-slice_fusion
  9.7 0.5 fusion.13
  11.4 0.1 pad_add_fusion.1.scalars
  11.5 1.6 copy-done.3
  13.1 1.7 pack_old.1
  14.8 0.0 collective-permute-start
  18.6 1.8 add_convert_fusion.1
  20.4 9.2 %all-to-all-start.1 = ((bf16[16,96,128]{2,1,0:T(8,128)(2,1)}), bf16[16,96,128]{2,1,0:T(8,128)(2,1)S(1)}, u32[]{:S(2)}, u32[]{:S(2)}) async-start(bf16[16,96,128]{2,1,0:T(8,128)(2,1)} %add_convert_fusion.1), calls=%async_computation.1 | async-start | bytes 786432 | tf_op jit(solution)/shard_map/all_to_all | solution.py:210
  29.6 0.0 collective-permute-done
  29.6 0.0 copy-start.1
  29.6 1.7 fusion.3
  31.3 10.7 %all-to-all-done.1 = bf16[16,96,128]{2,1,0:T(8,128)(2,1)S(1)} async-done(((bf16[16,96,128]{2,1,0:T(8,128)(2,1)}), bf16[16,96,128]{2,1,0:T(8,128)(2,1)S(1)}, u32[]{:S(2)}, u32[]{:S(2)}) %all-to-all-start.1) | async-done | bytes 393248 | tf_op jit(solution)/shard_map/all_to_all | solution.py:210
  42.0 6.2 %all-to-all-start = ((bf16[16,192,128]{2,1,0:T(8,128)(2,1)}), bf16[16,192,128]{2,1,0:T(8,128)(2,1)}, u32[]{:S(2)}, u32[]{:S(2)}) async-start(bf16[16,192,128]{2,1,0:T(8,128)(2,1)} %fusion.3), calls=%async_computation | async-start | bytes 1572864 | tf_op jit(solution)/shard_map/all_to_all | solution.py:210
  48.2 0.1 pad_add_fusion.4.scalars
  48.3 15.1 %gradient_parts.1 = (bf16[16,512,128]{2,1,0:T(8,128)(2,1)S(1)}, bf16[16,512,128]{2,1,0:T(8,128)(2,1)}) custom-call(s32[2]{0:T(128)S(1)} %pad_add_fusion.4.scalars, bf16[1024,4096]{1,0:T(8,128)(2,1)} %features.1, bf16[1024,512]{1,0:T(8,128)(2,1)S(1)} %copy-done.1), custom_call_target="tpu_custom_call" | custom-call | tf_op jit(solution)/shard_map/gradient_parts/pallas_call | solution.py:312
  63.4 1.3 collective-permute-start.3
  66.0 0.1 convert_reduce_fusion
  66.0 0.6 fusion.12
  69.2 0.8 dynamic-slice_select_fusion
  70.1 0.9 broadcast_in_dim.28
  71.0 9.3 %all-to-all-start.2 = ((bf16[16,160,128]{2,1,0:T(8,128)(2,1)}), bf16[16,160,128]{2,1,0:T(8,128)(2,1)S(1)}, u32[]{:S(2)}, u32[]{:S(2)}) async-start(bf16[16,160,128]{2,1,0:T(8,128)(2,1)} %broadcast_in_dim.28), calls=%async_computation.2 | async-start | bytes 1310720 | tf_op jit(solution)/shard_map/all_to_all | solution.py:210
  80.4 3.4 %add_convert_fusion = bf16[16,512,128]{2,1,0:T(8,128)(2,1)} fusion(bf16[16,512,128]{2,1,0:T(8,128)(2,1)} %collective-permute-done.3, bf16[16,512,128]{2,1,0:T(8,128)(2,1)S(1)} %get-tuple-element.20), kind=kLoop, calls=%fused_computation | loop fusion | flops 4194304 | bytes 6291456 | tf_op jit(solution)/shard_map/convert_element_type | solution.py:214
  83.8 15.2 %all-to-all-done.2.mine = bf16[16,160,128]{2,1,0:T(8,128)(2,1)S(1)} async-done(((bf16[16,160,128]{2,1,0:T(8,128)(2,1)}), bf16[16,160,128]{2,1,0:T(8,128)(2,1)S(1)}, u32[]{:S(2)}, u32[]{:S(2)}) %all-to-all-start.2) | async-done | bytes 655392 | tf_op jit(solution)/shard_map/all_to_all | solution.py:210
  99.0 6.1 %all-to-all-start.3 = ((bf16[16,512,128]{2,1,0:T(8,128)(2,1)}), bf16[16,512,128]{2,1,0:T(8,128)(2,1)}, u32[]{:S(2)}, u32[]{:S(2)}) async-start(bf16[16,512,128]{2,1,0:T(8,128)(2,1)} %add_convert_fusion), calls=%async_computation.3 | async-start | bytes 4194304 | tf_op jit(solution)/shard_map/all_to_all | solution.py:210
  105.1 0.5 fusion.14
  107.0 1.1 collective-permute-start.2
  108.1 0.1 pad_add_fusion.scalars
  108.1 0.8 fusion.10
  109.0 0.8 collective-permute-done.2.other
  109.8 4.2 %left_columns.1 = bf16[512,128]{1,0:T(8,128)(2,1)S(1)} custom-call(s32[4]{0:T(128)S(1)} %pad_add_fusion.scalars, bf16[16,160,128]{2,1,0:T(8,128)(2,1)S(1)} %all-to-all-done.2.mine, bf16[16,160,128]{2,1,0:T(8,128)(2,1)S(1)} %collective-permute-done.2.other, f32[16,128]{1,0:T(8,128)S(1)} %slice_add_fusion.diag), custom_call_target="tpu_custom_call" | custom-call | tf_op jit(solution)/shard_map/left_columns/pallas_call | solution.py:284
  114.0 40.4 %all-to-all-done.3 = bf16[16,512,128]{2,1,0:T(8,128)(2,1)} async-done(((bf16[16,512,128]{2,1,0:T(8,128)(2,1)}), bf16[16,512,128]{2,1,0:T(8,128)(2,1)}, u32[]{:S(2)}, u32[]{:S(2)}) %all-to-all-start.3) | async-done | bytes 2097184 | tf_op jit(solution)/shard_map/all_to_all | solution.py:210
  154.4 1.1 broadcast_in_dim.31
  155.5 4.1 %all-to-all-start.4 = ((bf16[8,512,128]{2,1,0:T(8,128)(2,1)}), bf16[8,512,128]{2,1,0:T(8,128)(2,1)S(1)}, u32[]{:S(2)}, u32[]{:S(2)}) async-start(bf16[8,512,128]{2,1,0:T(8,128)(2,1)} %broadcast_in_dim.31), calls=%async_computation.4 | async-start | bytes 2097152 | tf_op jit(solution)/shard_map/all_to_all | solution.py:293
  159.6 0.1 pad_add_fusion.3.scalars
  159.7 5.8 %new_blocks.1 = (bf16[512,512]{1,0:T(8,128)(2,1)S(1)}, f32[512,512]{1,0:T(8,128)}, f32[512,512]{1,0:T(8,128)}) custom-call(s32[4]{0:T(128)S(1)} %pad_add_fusion.scalars, bf16[16,160,128]{2,1,0:T(8,128)(2,1)S(1)} %all-to-all-done.2.mine, bf16[16,160,128]{2,1,0:T(8,128)(2,1)S(1)} %collective-permute-done.2.other, f32[16,128]{1,0:T(8,128)S(1)} %slice_add_fusion.diag), custom_call_target="tpu_custom_call" | custom-call | tf_op jit(solution)/shard_map/new_blocks/pallas_call | solution.py:296
  165.5 1.9 reduce_sum.40
  167.4 9.9 %all-gather = bf16[2048,128]{1,0:T(8,128)(2,1)S(1)} all-gather(bf16[512,128]{1,0:T(8,128)(2,1)S(1)} %reduce_sum.40), channel_id=2, replica_groups={{0,8,16,24},{32,40,48,56},{64,72,80,88},{96,104,112,120},{128,136,144,1..., dimensions={0}, use_global_device_ids=true | all-gather | bytes 655360 | tf_op jit(solution)/shard_map/all_gather | solution.py:330
  177.3 1.3 precondition.1
  178.7 0.2 collective-permute-start.4
  178.9 1.0 collective-permute-done.4
  179.9 15.3 %all_to_all.35 = f32[16,8,128]{2,1,0:T(8,128)S(1)} all-to-all(f32[16,8,128]{2,1,0:T(8,128)S(1)} %broadcast_in_dim.32), channel_id=1, replica_groups={{0,16,32,48,64,80,96,112,128,144,160,176,192,208,224,240},{8,24,40,56,7..., dimensions={0} | all-to-all | bytes 131072 | tf_op jit(solution)/shard_map/all_to_all | solution.py:210
  195.2 11.4 %all_to_all.36 = f32[8,8,128]{2,1,0:T(8,128)S(1)} all-to-all(f32[8,8,128]{2,1,0:T(8,128)S(1)} %broadcast_in_dim.33), channel_id=1, replica_groups=mesh['dp'=32,'mp'=8] {'mp'}, dimensions={0} | all-to-all | bytes 65536 | tf_op jit(solution)/shard_map/all_to_all | solution.py:343
  206.6 0.5 slice.84
  207.9 0.7 broadcast_multiply_fusion
  (28 shorter events, 0.1 us)
Async XLA Ops:
  1.4 1.2 copy-start
  2.6 7.0 %copy-start.4 = (s32[8,2]{0,1:T(2,128)S(1)}, s32[8,2]{0,1:T(2,128)}, u32[]{:S(2)}) copy-start(s32[8,2]{0,1:T(2,128)} %param.12) | copy-start | bytes 196
  2.6 7.0 %copy-start.5 = (s32[8,2]{0,1:T(2,128)S(1)}, s32[8,2]{0,1:T(2,128)}, u32[]{:S(2)}) copy-start(s32[8,2]{0,1:T(2,128)} %param.13) | copy-start | bytes 196
  2.6 8.9 %copy-start.2 = (f32[1,1,2,512,512]{4,3,2,1,0:T(8,128)S(1)}, f32[1,1,2,512,512]{4,3,2,1,0:T(8,128)}, u32[]{:S(2)}) copy-start(f32[1,1,2,512,512]{4,3,2,1,0:T(8,128)} %param.10) | copy-start | bytes 6291460
  6.4 12.2 %collective-permute-start.1 = (bf16[16,96,128]{2,1,0:T(8,128)(2,1)}, bf16[16,96,128]{2,1,0:T(8,128)(2,1)}, u32[]{:S(2)}, u32[]{:S(2)}) collective-permute-start(bf16[16,96,128]{2,1,0:T(8,128)(2,1)} %get-tuple-element.17), channel_id=1, source_target_pairs={{0,8},{8,0},{16,24},{24,16},{32,40},{40,32},{48,56},{56,48},{64,72... | collective-permute-start | bytes 1179656 | tf_op jit(solution)/shard_map/ppermute | solution.py:213
  11.5 1.6 copy-start.3
  14.8 14.8 %collective-permute-start = (bf16[16,192,128]{2,1,0:T(8,128)(2,1)}, bf16[16,192,128]{2,1,0:T(8,128)(2,1)S(1)}, u32[]{:S(2)}, u32[]{:S(2)}) collective-permute-start(bf16[16,192,128]{2,1,0:T(8,128)(2,1)} %get-tuple-element.15), channel_id=1, source_target_pairs={{0,8},{8,0},{16,24},{24,16},{32,40},{40,32},{48,56},{56,48},{64,72... | collective-permute-start | bytes 2359304 | tf_op jit(solution)/shard_map/ppermute | solution.py:233
  20.4 21.6 %all-to-all-start.1 = ((bf16[16,96,128]{2,1,0:T(8,128)(2,1)}), bf16[16,96,128]{2,1,0:T(8,128)(2,1)S(1)}, u32[]{:S(2)}, u32[]{:S(2)}) async-start(bf16[16,96,128]{2,1,0:T(8,128)(2,1)} %add_convert_fusion.1), calls=%async_computation.1 | async-start | bytes 786432 | tf_op jit(solution)/shard_map/all_to_all | solution.py:210
  29.6 18.7 %copy-start.1 = (bf16[1024,512]{1,0:T(8,128)(2,1)S(1)}, bf16[1024,512]{1,0:T(8,128)(2,1)}, u32[]{:S(2)}) copy-start(bf16[1024,512]{1,0:T(8,128)(2,1)} %grads.3) | copy-start | bytes 3145732
  42.0 27.2 %all-to-all-start = ((bf16[16,192,128]{2,1,0:T(8,128)(2,1)}), bf16[16,192,128]{2,1,0:T(8,128)(2,1)}, u32[]{:S(2)}, u32[]{:S(2)}) async-start(bf16[16,192,128]{2,1,0:T(8,128)(2,1)} %fusion.3), calls=%async_computation | async-start | bytes 1572864 | tf_op jit(solution)/shard_map/all_to_all | solution.py:210
  63.4 17.0 %collective-permute-start.3 = (bf16[16,512,128]{2,1,0:T(8,128)(2,1)}, bf16[16,512,128]{2,1,0:T(8,128)(2,1)}, u32[]{:S(2)}, u32[]{:S(2)}) collective-permute-start(bf16[16,512,128]{2,1,0:T(8,128)(2,1)} %get-tuple-element.21), channel_id=1, source_target_pairs={{0,8},{8,0},{16,24},{24,16},{32,40},{40,32},{48,56},{56,48},{64,72... | collective-permute-start | bytes 6291464 | tf_op jit(solution)/shard_map/ppermute | solution.py:213
  71.0 27.9 %all-to-all-start.2 = ((bf16[16,160,128]{2,1,0:T(8,128)(2,1)}), bf16[16,160,128]{2,1,0:T(8,128)(2,1)S(1)}, u32[]{:S(2)}, u32[]{:S(2)}) async-start(bf16[16,160,128]{2,1,0:T(8,128)(2,1)} %broadcast_in_dim.28), calls=%async_computation.2 | async-start | bytes 1310720 | tf_op jit(solution)/shard_map/all_to_all | solution.py:210
  99.0 55.4 %all-to-all-start.3 = ((bf16[16,512,128]{2,1,0:T(8,128)(2,1)}), bf16[16,512,128]{2,1,0:T(8,128)(2,1)}, u32[]{:S(2)}, u32[]{:S(2)}) async-start(bf16[16,512,128]{2,1,0:T(8,128)(2,1)} %add_convert_fusion), calls=%async_computation.3 | async-start | bytes 4194304 | tf_op jit(solution)/shard_map/all_to_all | solution.py:210
  107.0 2.8 %collective-permute-start.2 = (bf16[16,160,128]{2,1,0:T(8,128)(2,1)S(1)}, bf16[16,160,128]{2,1,0:T(8,128)(2,1)S(1)}, u32[]{:S(2)}, u32[]{:S(2)}) collective-permute-start(bf16[16,160,128]{2,1,0:T(8,128)(2,1)S(1)} %all-to-all-done.2.mine), channel_id=1, source_target_pairs={{0,8},{8,0},{16,24},{24,16},{32,40},{40,32},{48,56},{56,48},{64,72... | collective-permute-start | bytes 1966088 | tf_op jit(solution)/shard_map/ppermute | solution.py:273
  155.5 21.8 %all-to-all-start.4 = ((bf16[8,512,128]{2,1,0:T(8,128)(2,1)}), bf16[8,512,128]{2,1,0:T(8,128)(2,1)S(1)}, u32[]{:S(2)}, u32[]{:S(2)}) async-start(bf16[8,512,128]{2,1,0:T(8,128)(2,1)} %broadcast_in_dim.31), calls=%async_computation.4 | async-start | bytes 2097152 | tf_op jit(solution)/shard_map/all_to_all | solution.py:293
  178.7 1.3 collective-permute-start.4

commit v3 on v2

--- a/solution.py
+++ b/solution.py
@@ -32,7 +32,7 @@
 
 
 def pack_old(scalars, factors, inverses, keep, send, packed, diag):
-    core, shared = scalars[0], scalars[1]
+    core, shared, flip = scalars[0], scalars[1], scalars[2]
     tiles = factors.shape[1] // TILE
     on_diagonal = diagonal_mask()
     for which, held in enumerate((factors, inverses)):
@@ -53,7 +53,8 @@
     chips = keep.shape[0]
     share = (keep.shape[1] - words.shape[0]) // 2
     for q in range(chips):
-        kind, pair = divmod(q, chips // 2)
+        plane, pair = divmod(q, chips // 2)
+        kind = flip if plane == 0 else 1 - flip
         for ref, parity in ((keep, core), (send, 1 - core)):
             start = pl.multiple_of((2 * pair + parity) * share, ROWS)
             for which in range(2):
@@ -64,7 +65,7 @@
 
 
 def covariance_parts(scalars, own, grads, keep, send, kept, packed):
-    core, count = scalars[0], scalars[1]
+    core, count, flip = scalars[0], scalars[1], scalars[3]
     rows, width = own.shape
     tiles = width // TILE
     valid = lax.broadcasted_iota(jnp.int32, (rows, width), 0) < count
@@ -89,7 +90,8 @@
     chips = keep.shape[0]
     share = keep.shape[1] - ROWS
     for q in range(chips):
-        kind, pair = divmod(q, chips // 2)
+        plane, pair = divmod(q, chips // 2)
+        kind = flip if plane == 0 else 1 - flip
         for ref, parity in ((keep, core), (send, 1 - core)):
             start = pl.multiple_of((2 * pair + parity) * share, ROWS)
             ref[q, :share, :] = packed[kind, pl.ds(start, share), :]
@@ -105,21 +107,20 @@
         turned[...] = jnp.where(valid, grads[...].astype(F32), 0.0).T.astype(BF16)
 
     product[...] = jnp.dot(turned[...], features[...], preferred_element_type=F32).astype(BF16)
-    for ref, parity in ((keep, core), (send, 1 - core)):
-        start = pl.multiple_of(parity * TILE, TILE)
-        ref[0] = product[:, pl.ds(start, TILE)]
-
-
-def unpack(mine, other, core, kind, packed):
-    chips = mine.shape[0]
+    for q in range(keep.shape[0]):
+        for ref, parity in ((keep, core), (send, 1 - core)):
+            start = pl.multiple_of((2 * q + parity) * TILE, TILE)
+            ref[q] = product[:, pl.ds(start, TILE)]
+
+
+def unpack(mine, other, core, packed):
     share = mine.shape[1] // 2
-    for pair in range(chips // 2):
-        q = kind * (chips // 2) + pair
+    for pair in range(mine.shape[0]):
         for ref, parity in ((mine, core), (other, 1 - core)):
             start = pl.multiple_of((2 * pair + parity) * share, ROWS)
             for which in range(2):
                 packed[which, pl.ds(start, share), :] = ref[
-                    q, which * share : (which + 1) * share, :
+                    pair, which * share : (which + 1) * share, :
                 ]
 
 
@@ -135,9 +136,8 @@
         block[tile_of(a, b)] = piece
 
 
-def load_blocks(mine, other, core, kind, packed, diag, factor, inverse):
+def fill_blocks(kind, packed, diag, factor, inverse):
     tiles = factor.shape[0] // TILE
-    unpack(mine, other, core, kind, packed)
     spread(packed, 0, diag, kind * tiles, DECAY, factor)
     spread(packed, 1, diag, (2 + kind) * tiles, 1.0, inverse)
 
@@ -150,14 +150,29 @@
 
 def left_columns(scalars, mine, other, diag, left, packed, factor, inverse):
     core, place = scalars[0], scalars[1]
-    load_blocks(mine, other, core, 0, packed, diag, factor, inverse)
+    unpack(mine, other, core, packed)
+    fill_blocks(0, packed, diag, factor, inverse)
     start = pl.multiple_of(place * TILE, TILE)
     left[...] = refine(factor, inverse, inverse[:, pl.ds(start, TILE)]).astype(BF16)
 
 
-def new_blocks(scalars, mine, other, diag, right, factor_out, inverse_out, packed, factor, inverse):
-    core, first, second = scalars[0], scalars[2], scalars[3]
-    load_blocks(mine, other, core, 1, packed, diag, factor, inverse)
+def new_blocks(
+    scalars, mine, other, far_mine, far_other, diag, right, factor_out, inverse_out, packed, factor, inverse
+):
+    core, first, second, own_kind = scalars[0], scalars[2], scalars[3], scalars[4]
+
+    def load_blocks(kind):
+        @pl.when(own_kind == kind)
+        def _():
+            unpack(mine, other, core, packed)
+
+        @pl.when(own_kind != kind)
+        def _():
+            unpack(far_mine, far_other, core, packed)
+
+        fill_blocks(kind, packed, diag, factor, inverse)
+
+    load_blocks(1)
     fresh = refine(factor, inverse, inverse[...])
     right[...] = fresh.astype(BF16)
 
@@ -173,14 +188,13 @@
 
     @pl.when(first == 1)
     def _():
-        load_blocks(mine, other, core, 0, packed, diag, factor, inverse)
+        load_blocks(0)
         factor_out[...] = factor[...]
         inverse_out[...] = refine(factor, inverse, inverse[...])
 
 
-def precondition(scalars, grad, lefts, right, result, curvature):
-    own, block = scalars[0], scalars[1]
-    left = lefts[block]
+def precondition(scalars, grad, left, right, result, curvature):
+    own = scalars[0]
     half = sum(
         jnp.dot(grad[p], left[p * TILE : (p + 1) * TILE, :], preferred_element_type=F32)
         for p in range(grad.shape[0])
@@ -198,24 +212,43 @@
     members = lax.axis_size("dp")
     columns = lax.axis_size("mp")
     chips = members // 2
+    ring = chips // 2
     core = member % 2
-    swap = [(i, i ^ 1) for i in range(members)]
-    same_core = [[2 * q + c for q in range(chips)] for c in range(2)]
+    plane = member // chips
+    core_swap = [(i, i ^ 1) for i in range(members)]
+    plane_swap = [(i, (i + chips) % members) for i in range(members)]
+    rings = [[y * chips + 2 * z + c for z in range(ring)] for y in range(2) for c in range(2)]
     packed_rows = width * (width + TILE) // 2 // TILE
     share = 2 * packed_rows // members
     lanes = width // TILE
+    holders = members // columns
+    place = member % holders
     shape = jax.ShapeDtypeStruct
 
-    def across_chips(parts):
-        return lax.all_to_all(parts, "dp", 0, 0, tiled=True, axis_index_groups=same_core)
-
-    def pair_sum(keep, send):
-        received = lax.ppermute(send, "dp", swap)
-        return (keep.astype(F32) + received.astype(F32)).astype(BF16)
+    def across_ring(parts):
+        return lax.all_to_all(parts, "dp", 0, 0, tiled=True, axis_index_groups=rings)
+
+    def swap_cores(send):
+        return lax.ppermute(send, "dp", core_swap)
+
+    def swap_planes(send):
+        return lax.ppermute(send, "dp", plane_swap)
+
+    def plane_of(parts, which):
+        return lax.dynamic_slice_in_dim(parts, which * ring, ring, 0)
+
+    def sum_planes(keep, received):
+        def pair(which):
+            return plane_of(keep, which).astype(F32) + plane_of(received, which).astype(F32)
+
+        arrived = swap_planes(pair(1 - plane).astype(BF16))
+        return (pair(plane) + arrived.astype(F32)).astype(BF16)
 
     stale_owner = lax.dynamic_index_in_dim(old_owner, column, 0, keepdims=False)
     fresh_owner = lax.dynamic_index_in_dim(new_owner, column, 0, keepdims=False)
     shared_slot = (stale_owner[1] == stale_owner[0]).astype(jnp.int32)
+    flip = column // (columns // 2)
+    own_kind = plane ^ flip
 
     message = shape((chips, 2 * share + 8 * lanes, TILE), BF16)
     keep, send = pl.pallas_call(
@@ -229,21 +262,19 @@
         ],
         compiler_params=PARAMS,
         name="pack_old",
-    )(jnp.stack([core, shared_slot]), factor_old[0, 0], inverse_old[0, 0])
-    received = lax.ppermute(send, "dp", swap)
+    )(jnp.stack([core, shared_slot, flip]), factor_old[0, 0], inverse_old[0, 0])
     row = lax.broadcasted_iota(jnp.int32, message.shape, 1) - 2 * share
     chip = lax.broadcasted_iota(jnp.int32, message.shape, 0)
-    row_kind = jnp.where(row < 0, chip // (chips // 2), (row // lanes) % 2)
-    owner_core = jnp.where(row_kind == 0, stale_owner[0] % 2, stale_owner[1] % 2)
-    chosen = across_chips(jnp.where(owner_core == core, keep, received))
-    from_first = lax.dynamic_index_in_dim(chosen, stale_owner[0] // 2, 0, keepdims=False)
-    from_second = lax.dynamic_index_in_dim(chosen, stale_owner[1] // 2, 0, keepdims=False)
-    own_kind = member // chips
-    scattered = jnp.where(own_kind == 0, from_first, from_second)
-    row = lax.broadcasted_iota(jnp.int32, (8 * lanes, TILE), 0)
-    words = jnp.where((row // lanes) % 2 == 0, from_first[2 * share :], from_second[2 * share :])
-    words = words.astype(F32)
-    diag = words[: 4 * lanes] + words[4 * lanes :]
+
+    def from_owner(kinds, place_of_owner, here, one, two):
+        owner = jnp.where(kinds == 0, place_of_owner[0], place_of_owner[1])
+        return jnp.where(owner == here, one, two)
+
+    kinds = jnp.where(row < 0, (chip // ring) ^ flip, (row // lanes) % 2)
+    chosen = from_owner(kinds, stale_owner % 2, core, keep, swap_cores(send))
+    arrived = swap_planes(plane_of(chosen, 1 - plane))
+    kinds = plane_of(kinds, plane)
+    chosen = from_owner(kinds, stale_owner // chips, plane, plane_of(chosen, plane), arrived)
 
     message = shape((chips, share + ROWS, TILE), BF16)
     grads_spec = pl.BlockSpec((tok_rows, width), lambda i, s: (0, 0))
@@ -263,18 +294,35 @@
         ),
         compiler_params=PARAMS,
         name="covariance_parts",
-    )(jnp.stack([core, counts[0], column]), features, out_grads)
-    cov_share = jnp.sum(across_chips(pair_sum(keep, send)).astype(F32), axis=0)
+    )(jnp.stack([core, counts[0], column, flip]), features, out_grads)
+    covariances = sum_planes(keep, swap_cores(send))
+
+    arrived = across_ring(jnp.concatenate([chosen, covariances], axis=1))
+    owner_at = (stale_owner // 2) % ring
+    from_first = lax.dynamic_index_in_dim(arrived, owner_at[0], 0, keepdims=False)
+    from_second = lax.dynamic_index_in_dim(arrived, owner_at[1], 0, keepdims=False)
+    scattered = jnp.where(own_kind == 0, from_first, from_second)
+    at = slice(2 * share, 2 * share + 8 * lanes)
+    row = lax.broadcasted_iota(jnp.int32, (8 * lanes, TILE), 0)
+    words = jnp.where((row // lanes) % 2 == 0, from_first[at], from_second[at]).astype(F32)
+    diag = words[: 4 * lanes] + words[4 * lanes :]
+    cov_share = jnp.sum(arrived[:, 2 * share + 8 * lanes :].astype(F32), axis=0)
     total = sum(cov_share[share + 4 * d, 0] * float(8**d) for d in range(4))
     factor_share = DECAY * scattered[:share].astype(F32) + (1.0 - DECAY) * cov_share[:share] / total
 
     shares = jnp.concatenate([factor_share.astype(BF16), scattered[share : 2 * share]], axis=0)
-    mine = across_chips(jnp.broadcast_to(shares, (chips,) + shares.shape))
-    other = lax.ppermute(mine, "dp", swap)
-    holders = members // columns
-    place = member % holders
+    mine = across_ring(jnp.broadcast_to(shares, (ring,) + shares.shape))
+    other = swap_cores(mine)
+    far_mine = swap_planes(mine)
+    far_other = swap_cores(far_mine)
     scalars = jnp.stack(
-        [core, place, (member == fresh_owner[0]).astype(jnp.int32), (member == fresh_owner[1]).astype(jnp.int32)]
+        [
+            core,
+            place,
+            (member == fresh_owner[0]).astype(jnp.int32),
+            (member == fresh_owner[1]).astype(jnp.int32),
+            own_kind,
+        ]
     )
     unpacked = [
         pltpu.VMEM((2, packed_rows, TILE), BF16),
@@ -290,8 +338,27 @@
         compiler_params=PARAMS,
         name="left_columns",
     )(scalars, mine, other, diag)
-    lefts = lax.all_to_all(
-        jnp.broadcast_to(left, (columns,) + left.shape), "mp", 0, 0, tiled=True
+    gates = [(i, i // holders) for i in range(members)]
+    near = lax.ppermute(
+        left, ("dp", "mp"), [(i * columns + g, i * columns + (g ^ 1)) for i, g in gates]
+    )
+    gate = member // holders
+    left = jnp.where(column == gate, left, near)
+    left = jnp.where(
+        column // 2 == gate // 2,
+        left,
+        sum(
+            lax.ppermute(
+                left,
+                ("dp", "mp"),
+                [
+                    (i * columns + g, i * columns + (g + 2 * step) % columns)
+                    for i, at in gates
+                    for g in (at, at ^ 1)
+                ],
+            )
+            for step in range(1, columns // 2)
+        ),
     )
     right, factor_out, inverse_out = pl.pallas_call(
         new_blocks,
@@ -300,32 +367,34 @@
             shape((width, width), F32),
             shape((width, width), F32),
         ),
-        in_specs=[SCALARS, WHOLE, WHOLE, WHOLE],
+        in_specs=[SCALARS, WHOLE, WHOLE, WHOLE, WHOLE, WHOLE],
         out_specs=(WHOLE, WHOLE, WHOLE),
         scratch_shapes=unpacked,
         compiler_params=PARAMS,
         name="new_blocks",
-    )(scalars, mine, other, diag)
+    )(scalars, mine, other, far_mine, far_other, diag)
 
     message = shape((chips, width, TILE), BF16)
-    message_spec = pl.BlockSpec((1, width, TILE), lambda i, s: (i, 0, 0))
+    step = 8
+    message_spec = pl.BlockSpec((step // 2, width, TILE), lambda i, s: (i, 0, 0))
     keep, send = pl.pallas_call(
         gradient_parts,
         out_shape=(message, message),
         grid_spec=pltpu.PrefetchScalarGridSpec(
             num_scalar_prefetch=1,
-            grid=(chips,),
-            in_specs=[pl.BlockSpec((tok_rows, 2 * TILE), lambda i, s: (0, i)), grads_spec],
+            grid=(members // step,),
+            in_specs=[pl.BlockSpec((tok_rows, step * TILE), lambda i, s: (0, i)), grads_spec],
             out_specs=(message_spec, message_spec),
             scratch_shapes=[
                 pltpu.VMEM((width, tok_rows), BF16),
-                pltpu.VMEM((width, 2 * TILE), BF16),
+                pltpu.VMEM((width, step * TILE), BF16),
             ],
         ),
         compiler_params=PARAMS,
         name="gradient_parts",
     )(jnp.stack([core, counts[0]]), features, out_grads)
-    grad = jnp.sum(across_chips(pair_sum(keep, send)).astype(F32), axis=0).astype(BF16)
+    grad = across_ring(sum_planes(keep, swap_cores(send)))
+    grad = jnp.sum(grad.astype(F32), axis=0).astype(BF16)
     neighbours = [[holders * c + r for r in range(holders)] for c in range(columns)]
     grads = lax.all_gather(grad, "dp", axis=0, axis_index_groups=neighbours)
 
@@ -336,10 +405,11 @@
         out_specs=(WHOLE, WHOLE),
         compiler_params=PARAMS,
         name="precondition",
-    )(jnp.stack([place, member // holders]), grads, lefts, right)
-
-    curvature = curvature + lax.ppermute(curvature, "dp", swap)
-    curvature = jnp.sum(across_chips(jnp.broadcast_to(curvature, (chips, 8, TILE))), axis=0)
+    )(place[None], grads, left, right)
+
+    curvature = curvature + swap_cores(curvature)
+    curvature = curvature + swap_planes(curvature)
+    curvature = jnp.sum(across_ring(jnp.broadcast_to(curvature, (ring, 8, TILE))), axis=0)
     curvature = lax.all_to_all(
         jnp.broadcast_to(curvature, (columns, 8, TILE)), "mp", 0, 0, tiled=True
     )

time: 210 us -> 175 us (0.83)
  waiting for transfers between devices: 68.1 us -> 35.7 us
  other arithmetic: 11.7 us -> 17.6 us
  Pallas kernels: 31.9 us -> 26 us
  blocking collectives: 36.6 us -> 31.8 us
  local copies, waits for them, and re-layouts: 7.14 us -> 10.5 us
    all_to_all x5 -> x3, waiting for transfers between devices: 66.3 us -> 13.2 us  [across_ring(): lax.all_to_all(parts, 'dp', 0, 0, tiled=True, axis_index_groups=rings)]
    ppermute x5 -> x15, waiting for transfers between devices: 1.84 us -> 22.5 us  [the longest x5 16.8 us: swap_planes(): return lax.ppermute(send, 'dp', plane_swap)]
    all_to_all x5 -> x3, starting transfers between devices: 34.9 us -> 16.1 us  [across_ring(): lax.all_to_all(parts, 'dp', 0, 0, tiled=True, axis_index_groups=rings)]
    ppermute x5 -> x15, starting transfers between devices: 5.88 us -> 22.6 us  [the longest x6 8.65 us: swap_cores(): return lax.ppermute(send, 'dp', core_swap)]
    select_n x1 -> x6, other arithmetic: 1.67 us -> 7.33 us  [the longest x2 5.78 us: from_owner(): return jnp.where(owner == here, one, two)]
    pallas_call x1, Pallas kernels: 15.1 us -> 9.76 us  [local(): pl.pallas_call(gradient_parts, out_shape=(message, message), grid_spec=pl...]
    all_to_all x1, blocking collectives: 11.4 us -> 7.43 us  [local(): lax.all_to_all(jnp.broadcast_to(curvature, (columns, 8, TILE)), 'mp', 0,...]
    convert_element_type x3 -> x5, other arithmetic: 6.09 us -> 8.14 us  [the longest x2 4.13 us: sum_planes(): arrived = swap_planes(pair(1 - plane).astype(BF16))]
  transfers between devices with their start and end apart: 10 -> 18, of which waited for: 5 -> 10; matrix products, arithmetic and copies ran while one was open for 7% -> 12% of each run, Pallas kernels for 13% -> 14%
where the time goes in v3:
time: 175 us; the launch traced here: 172 us
  starting transfers between devices  38.7 us (22%)
  waiting for transfers between devices  35.7 us (20%)
  blocking collectives  31.8 us (18%)
  Pallas kernels  26 us (15%)
  other arithmetic  17.6 us (10%)
  between operations  11.3 us (6%)
  local copies, waits for them, and re-layouts  10.5 us (6%)
    ppermute x5, waiting for transfers between devices, swap_planes(): return lax.ppermute(send, 'dp', plane_swap)  16.8 us
    all_to_all x1, blocking collectives, across_ring(): lax.all_to_all(parts, 'dp', 0, 0, tiled=True, axis_index_groups=rings)  16.4 us
    all_to_all x3, starting transfers between devices, across_ring(): lax.all_to_all(parts, 'dp', 0, 0, tiled=True, axis_index_groups=rings)  16.1 us
    all_to_all x3, waiting for transfers between devices, across_ring(): lax.all_to_all(parts, 'dp', 0, 0, tiled=True, axis_index_groups=rings)  13.2 us
    pallas_call x1, Pallas kernels, local(): pl.pallas_call(gradient_parts, out_shape=(message, message), grid_spec=pl...  9.76 us
    ppermute x6, starting transfers between devices, swap_cores(): return lax.ppermute(send, 'dp', core_swap)  8.65 us
    all_gather x1, blocking collectives, local(): grads = lax.all_gather(grad, 'dp', axis=0, axis_index_groups=neighbours)  7.91 us
    all_to_all x1, blocking collectives, local(): lax.all_to_all(jnp.broadcast_to(curvature, (columns, 8, TILE)), 'mp', 0,...  7.43 us
  transfers between devices with their start and end apart: 18, of which 10 were waited for; matrix products, arithmetic and copies ran while one was open for 12% of the time, Pallas kernels for 14%

profile of v3, /device:TPU:1, one launch (start us, length us, event | category | flops | bytes accessed | tf_op | source)
XLA Modules:
  0.0 171.5 jit_solution(7350574724886796486)
XLA Ops:
  0.6 0.9 fusion.13
  3.5 1.6 copy-done.1
  5.0 1.6 copy-done.2
  6.6 1.7 %pack_old.1 = (bf16[16,192,128]{2,1,0:T(8,128)(2,1)S(1)}, bf16[16,192,128]{2,1,0:T(8,128)(2,1)}) custom-call(s32[3]{0:T(128)S(1)} %pad_add_fusion.scalars, f32[2,512,512]{2,1,0:T(8,128)S(1)} %bitcast.38, f32[2,512,512]{2,1,0:T(8,128)S(1)} %bitcast.39), custom_call_target="tpu_custom_call" | custom-call | tf_op jit(solution)/shard_map/pack_old/pallas_call | solution.py:254
  8.4 3.2 %collective-permute-start = (bf16[16,192,128]{2,1,0:T(8,128)(2,1)}, bf16[16,192,128]{2,1,0:T(8,128)(2,1)}, u32[]{:S(2)}, u32[]{:S(2)}) collective-permute-start(bf16[16,192,128]{2,1,0:T(8,128)(2,1)} %get-tuple-element.15), channel_id=1, source_target_pairs={{0,8},{8,0},{16,24},{24,16},{32,40},{40,32},{48,56},{56,48},{64,72... | collective-permute-start | bytes 2359304 | tf_op jit(solution)/shard_map/ppermute | solution.py:232
  12.3 3.7 %covariance_parts.1 = (bf16[16,96,128]{2,1,0:T(8,128)(2,1)S(1)}, bf16[16,96,128]{2,1,0:T(8,128)(2,1)}) custom-call(s32[4]{0:T(128)S(1)} %pad_add_fusion.1.scalars, bf16[1024,4096]{1,0:T(8,128)(2,1)} %features.1, bf16[1024,512]{1,0:T(8,128)(2,1)S(1)} %copy-done), custom_call_target="tpu_custom_call" | custom-call | tf_op jit(solution)/shard_map/covariance_parts/pallas_call | solution.py:282
  16.1 9.8 %gradient_parts.1 = (bf16[16,512,128]{2,1,0:T(8,128)(2,1)S(1)}, bf16[16,512,128]{2,1,0:T(8,128)(2,1)}) custom-call(s32[2]{0:T(128)S(1)} %pad_add_fusion.2.scalars, bf16[1024,4096]{1,0:T(8,128)(2,1)} %features.1, bf16[1024,512]{1,0:T(8,128)(2,1)S(1)} %copy-done), custom_call_target="tpu_custom_call" | custom-call | tf_op jit(solution)/shard_map/gradient_parts/pallas_call | solution.py:380
  27.0 1.7 add_convert_fusion.3
  28.7 1.2 collective-permute-start.3
  29.8 3.1 %fusion.2 = bf16[16,192,128]{2,1,0:T(8,128)(2,1)S(1)} fusion(bf16[16,192,128]{2,1,0:T(8,128)(2,1)S(1)} %get-tuple-element.14, bf16[16,192,128]{2,1,0:T(8,128)(2,1)} %collective-permute-done, s32[]{:T(128)} %select_n.143, s32[]{:T(128)} %bitcast.10, s32[]{:T(128)} %bitcast.9, s32[192]{0:T(256)S(1)} %get-tuple-element.46, s32[192]{0:T(256)S(1)} %get-tuple-element.47, ...), kind=kLoop, calls=%fused_computation.10 | loop fusion | flops 7471104 | bytes 2361376 | tf_op jit(solution)/shard_map/jit(_where)/select_n | solution.py:271
  33.0 0.9 copy-done.3
  33.8 0.8 constant_dynamic-slice_fusion
  34.6 1.8 %collective-permute-start.1 = (bf16[8,192,128]{2,1,0:T(8,128)(2,1)}, bf16[8,192,128]{2,1,0:T(8,128)(2,1)}, u32[]{:S(2)}, u32[]{:S(2)}) collective-permute-start(bf16[8,192,128]{2,1,0:T(8,128)(2,1)} %constant_dynamic-slice_fusion), channel_id=1, source_target_pairs={{0,128},{8,136},{16,144},{24,152},{32,160},{40,168},{48,176},{56,1... | collective-permute-start | bytes 1179656 | tf_op jit(solution)/shard_map/ppermute | solution.py:235
  36.4 1.5 fusion
  37.9 0.6 fusion.18
  38.5 1.0 add_convert_fusion.2
  39.5 7.3 %collective-permute-done.1 = bf16[8,192,128]{2,1,0:T(8,128)(2,1)} collective-permute-done((bf16[8,192,128]{2,1,0:T(8,128)(2,1)}, bf16[8,192,128]{2,1,0:T(8,128)(2,1)}, u32[]{:S(2)}, u32[]{:S(2)}) %collective-permute-start.1) | collective-permute-done | bytes 393248 | tf_op jit(solution)/shard_map/ppermute | solution.py:235
  46.8 2.7 %fusion.3 = bf16[8,192,128]{2,1,0:T(8,128)(2,1)S(1)} fusion(bf16[8,192,128]{2,1,0:T(8,128)(2,1)} %collective-permute-done.1, s32[16,192,128]{2,1,0:T(8,128)} %fusion, s32[]{:T(128)S(6)} %select_n.153, bf16[16,192,128]{2,1,0:T(8,128)(2,1)S(1)} %copy-done.4, s32[]{:T(128)S(6)} %select_n.146, s32[]{:T(128)} %bitcast.8, s32[]{:T(128)} %bitcast.7), kind=kLoop, calls=%fused_computation.13 | loop fusion | flops 786432 | bytes 1966096 | tf_op jit(solution)/shard_map/jit(_where)/select_n | solution.py:271
  49.5 0.9 pad_maximum_fusion
  50.4 8.2 %all-to-all-start = ((bf16[8,288,128]{2,1,0:T(8,128)(2,1)}), bf16[8,288,128]{2,1,0:T(8,128)(2,1)S(1)}, u32[]{:S(2)}, u32[]{:S(2)}) async-start(bf16[8,288,128]{2,1,0:T(8,128)(2,1)} %pad_maximum_fusion), calls=%async_computation | async-start | bytes 1179648 | tf_op jit(solution)/shard_map/all_to_all | solution.py:229
  63.1 2.5 %add_convert_fusion.1 = bf16[8,512,128]{2,1,0:T(8,128)(2,1)} fusion(bf16[16,512,128]{2,1,0:T(8,128)(2,1)} %collective-permute-done.7, s32[]{:T(128)S(6)} %select_n.159, bf16[16,512,128]{2,1,0:T(8,128)(2,1)S(1)} %get-tuple-element.20), kind=kLoop, calls=%fused_computation.6 | loop fusion | flops 2097152 | bytes 3145732 | tf_op jit(solution)/shard_map/convert_element_type | solution.py:244
  65.6 11.4 %all-to-all-done = bf16[8,288,128]{2,1,0:T(8,128)(2,1)S(1)} async-done(((bf16[8,288,128]{2,1,0:T(8,128)(2,1)}), bf16[8,288,128]{2,1,0:T(8,128)(2,1)S(1)}, u32[]{:S(2)}, u32[]{:S(2)}) %all-to-all-start) | async-done | bytes 589856 | tf_op jit(solution)/shard_map/all_to_all | solution.py:229
  80.1 0.8 broadcast_in_dim.36
  80.9 3.4 %all-to-all-start.1 = ((bf16[8,160,128]{2,1,0:T(8,128)(2,1)}), bf16[8,160,128]{2,1,0:T(8,128)(2,1)S(1)}, u32[]{:S(2)}, u32[]{:S(2)}) async-start(bf16[8,160,128]{2,1,0:T(8,128)(2,1)} %broadcast_in_dim.36), calls=%async_computation.1 | async-start | bytes 655360 | tf_op jit(solution)/shard_map/all_to_all | solution.py:229
  84.3 6.3 %collective-permute-done.8 = bf16[8,512,128]{2,1,0:T(8,128)(2,1)} collective-permute-done((bf16[8,512,128]{2,1,0:T(8,128)(2,1)}, bf16[8,512,128]{2,1,0:T(8,128)(2,1)}, u32[]{:S(2)}, u32[]{:S(2)}) %collective-permute-start.8) | collective-permute-done | bytes 1048608 | tf_op jit(solution)/shard_map/ppermute | solution.py:235
  90.6 2.9 %add_convert_fusion = bf16[8,512,128]{2,1,0:T(8,128)(2,1)} fusion(bf16[8,512,128]{2,1,0:T(8,128)(2,1)} %collective-permute-done.8, bf16[16,512,128]{2,1,0:T(8,128)(2,1)} %collective-permute-done.7, s32[]{:T(128)S(6)} %select_n.153, bf16[16,512,128]{2,1,0:T(8,128)(2,1)S(1)} %get-tuple-element.20), kind=kLoop, calls=%fused_computation.5 | loop fusion | flops 3145728 | bytes 4194308 | tf_op jit(solution)/shard_map/convert_element_type | solution.py:245
  93.5 1.9 %all-to-all-done.1.mine = bf16[8,160,128]{2,1,0:T(8,128)(2,1)S(1)} async-done(((bf16[8,160,128]{2,1,0:T(8,128)(2,1)}), bf16[8,160,128]{2,1,0:T(8,128)(2,1)S(1)}, u32[]{:S(2)}, u32[]{:S(2)}) %all-to-all-start.1) | async-done | bytes 327712 | tf_op jit(solution)/shard_map/all_to_all | solution.py:229
  95.4 4.5 %all-to-all-start.2 = ((bf16[8,512,128]{2,1,0:T(8,128)(2,1)}), bf16[8,512,128]{2,1,0:T(8,128)(2,1)S(1)}, u32[]{:S(2)}, u32[]{:S(2)}) async-start(bf16[8,512,128]{2,1,0:T(8,128)(2,1)} %add_convert_fusion), calls=%async_computation.2 | async-start | bytes 2097152 | tf_op jit(solution)/shard_map/all_to_all | solution.py:229
  101.8 3.1 %collective-permute-start.4 = (bf16[8,160,128]{2,1,0:T(8,128)(2,1)S(1)}, bf16[8,160,128]{2,1,0:T(8,128)(2,1)S(1)}, u32[]{:S(2)}, u32[]{:S(2)}) collective-permute-start(bf16[8,160,128]{2,1,0:T(8,128)(2,1)S(1)} %all-to-all-done.1.mine), channel_id=1, source_target_pairs={{0,8},{8,0},{16,24},{24,16},{32,40},{40,32},{48,56},{56,48},{64,72... | collective-permute-start | bytes 983048 | tf_op jit(solution)/shard_map/ppermute | solution.py:232
  105.1 1.2 collective-permute-done.4.other
  106.2 4.2 %left_columns.1 = bf16[512,128]{1,0:T(8,128)(2,1)S(1)} custom-call(s32[5]{0:T(128)S(1)} %stack.56.scalars, bf16[8,160,128]{2,1,0:T(8,128)(2,1)S(1)} %all-to-all-done.1.mine, bf16[8,160,128]{2,1,0:T(8,128)(2,1)S(1)} %collective-permute-done.4.other, f32[16,128]{1,0:T(8,128)S(1)} %slice_add_fusion.diag), custom_call_target="tpu_custom_call" | custom-call | tf_op jit(solution)/shard_map/left_columns/pallas_call | solution.py:332
  110.4 2.3 %collective-permute-start.9 = (bf16[512,128]{1,0:T(8,128)(2,1)S(1)}, bf16[512,128]{1,0:T(8,128)(2,1)S(1)}, u32[]{:S(2)}, u32[]{:S(2)}) collective-permute-start(bf16[512,128]{1,0:T(8,128)(2,1)S(1)} %left_columns.1), channel_id=1, source_target_pairs={{0,1},{8,9},{16,17},{24,25},{33,32},{41,40},{49,48},{57,56},{66,67... | collective-permute-start | bytes 393224 | tf_op jit(solution)/shard_map/ppermute | solution.py:342
  112.9 2.4 %collective-permute-done.9 = bf16[512,128]{1,0:T(8,128)(2,1)S(1)} collective-permute-done((bf16[512,128]{1,0:T(8,128)(2,1)S(1)}, bf16[512,128]{1,0:T(8,128)(2,1)S(1)}, u32[]{:S(2)}, u32[]{:S(2)}) %collective-permute-start.9) | collective-permute-done | bytes 131104 | tf_op jit(solution)/shard_map/ppermute | solution.py:342
  115.3 1.3 collective-permute-start.10
  116.6 3.2 %collective-permute-start.11 = (bf16[512,128]{1,0:T(8,128)(2,1)S(1)}, bf16[512,128]{1,0:T(8,128)(2,1)S(1)}, u32[]{:S(2)}, u32[]{:S(2)}) collective-permute-start(bf16[512,128]{1,0:T(8,128)(2,1)S(1)} %broadcast_select_fusion), channel_id=1, source_target_pairs={{0,4},{1,5},{8,12},{9,13},{16,20},{17,21},{24,28},{25,29},{33,37},... | collective-permute-start | bytes 393224 | tf_op jit(solution)/shard_map/ppermute | solution.py:351
  119.8 1.3 collective-permute-start.12
  121.1 1.9 %collective-permute-done.5.far_mine = bf16[8,160,128]{2,1,0:T(8,128)(2,1)S(1)} collective-permute-done((bf16[8,160,128]{2,1,0:T(8,128)(2,1)S(1)}, bf16[8,160,128]{2,1,0:T(8,128)(2,1)S(1)}, u32[]{:S(2)}, u32[]{:S(2)}) %collective-permute-start.5) | collective-permute-done | bytes 327712 | tf_op jit(solution)/shard_map/ppermute | solution.py:235
  122.9 1.5 collective-permute-start.6
  124.5 1.2 collective-permute-done.6.far_other
  125.7 5.8 %new_blocks.1 = (bf16[512,512]{1,0:T(8,128)(2,1)S(1)}, f32[512,512]{1,0:T(8,128)}, f32[512,512]{1,0:T(8,128)}) custom-call(s32[5]{0:T(128)S(1)} %stack.56.scalars, bf16[8,160,128]{2,1,0:T(8,128)(2,1)S(1)} %all-to-all-done.1.mine, bf16[8,160,128]{2,1,0:T(8,128)(2,1)S(1)} %collective-permute-done.4.other, ...), custom_call_target="tpu_custom_call" | custom-call | tf_op jit(solution)/shard_map/new_blocks/pallas_call | solution.py:363
  131.7 7.9 %all-gather = bf16[2048,128]{1,0:T(8,128)(2,1)S(1)} all-gather(bf16[512,128]{1,0:T(8,128)(2,1)S(1)} %reduce_sum.40), channel_id=2, replica_groups={{0,8,16,24},{32,40,48,56},{64,72,80,88},{96,104,112,120},{128,136,144,1..., dimensions={0}, use_global_device_ids=true | all-gather | bytes 655360 | tf_op jit(solution)/shard_map/all_gather | solution.py:399
  139.6 0.8 precondition.1
  140.7 1.0 collective-permute-done.13
  141.7 2.7 %collective-permute-start.14 = (f32[8,128]{1,0:T(8,128)S(1)}, f32[8,128]{1,0:T(8,128)S(1)}, u32[]{:S(2)}, u32[]{:S(2)}) collective-permute-start(f32[8,128]{1,0:T(8,128)S(1)} %add.146), channel_id=1, source_target_pairs={{0,128},{8,136},{16,144},{24,152},{32,160},{40,168},{48,176},{56,1... | collective-permute-start | bytes 12296 | tf_op jit(solution)/shard_map/ppermute | solution.py:235
  144.4 1.3 collective-permute-done.14
  145.6 16.4 %all_to_all.25 = f32[8,8,128]{2,1,0:T(8,128)S(1)} all-to-all(f32[8,8,128]{2,1,0:T(8,128)S(1)} %broadcast_in_dim.39), channel_id=1, replica_groups={{0,16,32,48,64,80,96,112},{8,24,40,56,72,88,104,120},{128,144,160,176,1..., dimensions={0} | all-to-all | bytes 65536 | tf_op jit(solution)/shard_map/all_to_all | solution.py:229
  162.1 7.4 %all_to_all.26 = f32[8,8,128]{2,1,0:T(8,128)S(1)} all-to-all(f32[8,8,128]{2,1,0:T(8,128)S(1)} %broadcast_in_dim.40), channel_id=1, replica_groups=mesh['dp'=32,'mp'=8] {'mp'}, dimensions={0} | all-to-all | bytes 65536 | tf_op jit(solution)/shard_map/all_to_all | solution.py:413
  170.8 0.7 broadcast_multiply_fusion
  (53 shorter events, 5.0 us)
Async XLA Ops:
  3.4 1.6 copy-start.1
  5.0 1.6 copy-start.2
  6.6 5.7 %copy-start = (bf16[1024,512]{1,0:T(8,128)(2,1)S(1)}, bf16[1024,512]{1,0:T(8,128)(2,1)}, u32[]{:S(2)}) copy-start(bf16[1024,512]{1,0:T(8,128)(2,1)} %grads.3) | copy-start | bytes 3145732
  8.4 21.5 %collective-permute-start = (bf16[16,192,128]{2,1,0:T(8,128)(2,1)}, bf16[16,192,128]{2,1,0:T(8,128)(2,1)}, u32[]{:S(2)}, u32[]{:S(2)}) collective-permute-start(bf16[16,192,128]{2,1,0:T(8,128)(2,1)} %get-tuple-element.15), channel_id=1, source_target_pairs={{0,8},{8,0},{16,24},{24,16},{32,40},{40,32},{48,56},{56,48},{64,72... | collective-permute-start | bytes 2359304 | tf_op jit(solution)/shard_map/ppermute | solution.py:232
  16.0 11.0 %collective-permute-start.2 = (bf16[16,96,128]{2,1,0:T(8,128)(2,1)}, bf16[16,96,128]{2,1,0:T(8,128)(2,1)}, u32[]{:S(2)}, u32[]{:S(2)}) collective-permute-start(bf16[16,96,128]{2,1,0:T(8,128)(2,1)} %get-tuple-element.17), channel_id=1, source_target_pairs={{0,8},{8,0},{16,24},{24,16},{32,40},{40,32},{48,56},{56,48},{64,72... | collective-permute-start | bytes 1179656 | tf_op jit(solution)/shard_map/ppermute | solution.py:232
  25.8 37.2 %collective-permute-start.7 = (bf16[16,512,128]{2,1,0:T(8,128)(2,1)}, bf16[16,512,128]{2,1,0:T(8,128)(2,1)}, u32[]{:S(2)}, u32[]{:S(2)}) collective-permute-start(bf16[16,512,128]{2,1,0:T(8,128)(2,1)} %get-tuple-element.21), channel_id=1, source_target_pairs={{0,8},{8,0},{16,24},{24,16},{32,40},{40,32},{48,56},{56,48},{64,72... | collective-permute-start | bytes 6291464 | tf_op jit(solution)/shard_map/ppermute | solution.py:232
  28.7 9.8 %collective-permute-start.3 = (bf16[8,96,128]{2,1,0:T(8,128)(2,1)}, bf16[8,96,128]{2,1,0:T(8,128)(2,1)S(1)}, u32[]{:S(2)}, u32[]{:S(2)}) collective-permute-start(bf16[8,96,128]{2,1,0:T(8,128)(2,1)} %add_convert_fusion.3), channel_id=1, source_target_pairs={{0,128},{8,136},{16,144},{24,152},{32,160},{40,168},{48,176},{56,1... | collective-permute-start | bytes 589832 | tf_op jit(solution)/shard_map/ppermute | solution.py:235
  32.9 0.9 copy-start.3
  34.6 12.3 %copy-start.4 = (bf16[16,192,128]{2,1,0:T(8,128)(2,1)S(1)}, bf16[16,192,128]{2,1,0:T(8,128)(2,1)}, u32[]{:S(2)}) copy-start(bf16[16,192,128]{2,1,0:T(8,128)(2,1)} %copy-done.3) | copy-start | bytes 2359300
  34.6 12.2 %collective-permute-start.1 = (bf16[8,192,128]{2,1,0:T(8,128)(2,1)}, bf16[8,192,128]{2,1,0:T(8,128)(2,1)}, u32[]{:S(2)}, u32[]{:S(2)}) collective-permute-start(bf16[8,192,128]{2,1,0:T(8,128)(2,1)} %constant_dynamic-slice_fusion), channel_id=1, source_target_pairs={{0,128},{8,136},{16,144},{24,152},{32,160},{40,168},{48,176},{56,1... | collective-permute-start | bytes 1179656 | tf_op jit(solution)/shard_map/ppermute | solution.py:235
  50.4 26.6 %all-to-all-start = ((bf16[8,288,128]{2,1,0:T(8,128)(2,1)}), bf16[8,288,128]{2,1,0:T(8,128)(2,1)S(1)}, u32[]{:S(2)}, u32[]{:S(2)}) async-start(bf16[8,288,128]{2,1,0:T(8,128)(2,1)} %pad_maximum_fusion), calls=%async_computation | async-start | bytes 1179648 | tf_op jit(solution)/shard_map/all_to_all | solution.py:229
  65.5 25.1 %collective-permute-start.8 = (bf16[8,512,128]{2,1,0:T(8,128)(2,1)}, bf16[8,512,128]{2,1,0:T(8,128)(2,1)}, u32[]{:S(2)}, u32[]{:S(2)}) collective-permute-start(bf16[8,512,128]{2,1,0:T(8,128)(2,1)} %add_convert_fusion.1), channel_id=1, source_target_pairs={{0,128},{8,136},{16,144},{24,152},{32,160},{40,168},{48,176},{56,1... | collective-permute-start | bytes 3145736 | tf_op jit(solution)/shard_map/ppermute | solution.py:235
  80.9 14.5 %all-to-all-start.1 = ((bf16[8,160,128]{2,1,0:T(8,128)(2,1)}), bf16[8,160,128]{2,1,0:T(8,128)(2,1)S(1)}, u32[]{:S(2)}, u32[]{:S(2)}) async-start(bf16[8,160,128]{2,1,0:T(8,128)(2,1)} %broadcast_in_dim.36), calls=%async_computation.1 | async-start | bytes 655360 | tf_op jit(solution)/shard_map/all_to_all | solution.py:229
  95.4 36.2 %all-to-all-start.2 = ((bf16[8,512,128]{2,1,0:T(8,128)(2,1)}), bf16[8,512,128]{2,1,0:T(8,128)(2,1)S(1)}, u32[]{:S(2)}, u32[]{:S(2)}) async-start(bf16[8,512,128]{2,1,0:T(8,128)(2,1)} %add_convert_fusion), calls=%async_computation.2 | async-start | bytes 2097152 | tf_op jit(solution)/shard_map/all_to_all | solution.py:229
  101.8 4.4 %collective-permute-start.4 = (bf16[8,160,128]{2,1,0:T(8,128)(2,1)S(1)}, bf16[8,160,128]{2,1,0:T(8,128)(2,1)S(1)}, u32[]{:S(2)}, u32[]{:S(2)}) collective-permute-start(bf16[8,160,128]{2,1,0:T(8,128)(2,1)S(1)} %all-to-all-done.1.mine), channel_id=1, source_target_pairs={{0,8},{8,0},{16,24},{24,16},{32,40},{40,32},{48,56},{56,48},{64,72... | collective-permute-start | bytes 983048 | tf_op jit(solution)/shard_map/ppermute | solution.py:232
  110.4 4.8 %collective-permute-start.9 = (bf16[512,128]{1,0:T(8,128)(2,1)S(1)}, bf16[512,128]{1,0:T(8,128)(2,1)S(1)}, u32[]{:S(2)}, u32[]{:S(2)}) collective-permute-start(bf16[512,128]{1,0:T(8,128)(2,1)S(1)} %left_columns.1), channel_id=1, source_target_pairs={{0,1},{8,9},{16,17},{24,25},{33,32},{41,40},{49,48},{57,56},{66,67... | collective-permute-start | bytes 393224 | tf_op jit(solution)/shard_map/ppermute | solution.py:342
  112.7 10.2 %collective-permute-start.5 = (bf16[8,160,128]{2,1,0:T(8,128)(2,1)S(1)}, bf16[8,160,128]{2,1,0:T(8,128)(2,1)S(1)}, u32[]{:S(2)}, u32[]{:S(2)}) collective-permute-start(bf16[8,160,128]{2,1,0:T(8,128)(2,1)S(1)} %all-to-all-done.1.mine), channel_id=1, source_target_pairs={{0,128},{8,136},{16,144},{24,152},{32,160},{40,168},{48,176},{56,1... | collective-permute-start | bytes 983048 | tf_op jit(solution)/shard_map/ppermute | solution.py:235
  115.3 9.2 %collective-permute-start.10 = (bf16[512,128]{1,0:T(8,128)(2,1)S(1)}, bf16[512,128]{1,0:T(8,128)(2,1)S(1)}, u32[]{:S(2)}, u32[]{:S(2)}) collective-permute-start(bf16[512,128]{1,0:T(8,128)(2,1)S(1)} %broadcast_select_fusion), channel_id=1, source_target_pairs={{0,2},{1,3},{8,10},{9,11},{16,18},{17,19},{24,26},{25,27},{33,35},... | collective-permute-start | bytes 393224 | tf_op jit(solution)/shard_map/ppermute | solution.py:351
  116.6 7.9 %collective-permute-start.11 = (bf16[512,128]{1,0:T(8,128)(2,1)S(1)}, bf16[512,128]{1,0:T(8,128)(2,1)S(1)}, u32[]{:S(2)}, u32[]{:S(2)}) collective-permute-start(bf16[512,128]{1,0:T(8,128)(2,1)S(1)} %broadcast_select_fusion), channel_id=1, source_target_pairs={{0,4},{1,5},{8,12},{9,13},{16,20},{17,21},{24,28},{25,29},{33,37},... | collective-permute-start | bytes 393224 | tf_op jit(solution)/shard_map/ppermute | solution.py:351
  119.8 4.7 %collective-permute-start.12 = (bf16[512,128]{1,0:T(8,128)(2,1)S(1)}, bf16[512,128]{1,0:T(8,128)(2,1)S(1)}, u32[]{:S(2)}, u32[]{:S(2)}) collective-permute-start(bf16[512,128]{1,0:T(8,128)(2,1)S(1)} %broadcast_select_fusion), channel_id=1, source_target_pairs={{0,6},{1,7},{8,14},{9,15},{16,22},{17,23},{24,30},{25,31},{33,39},... | collective-permute-start | bytes 393224 | tf_op jit(solution)/shard_map/ppermute | solution.py:351
  122.9 2.8 %collective-permute-start.6 = (bf16[8,160,128]{2,1,0:T(8,128)(2,1)S(1)}, bf16[8,160,128]{2,1,0:T(8,128)(2,1)S(1)}, u32[]{:S(2)}, u32[]{:S(2)}) collective-permute-start(bf16[8,160,128]{2,1,0:T(8,128)(2,1)S(1)} %collective-permute-done.5.far_mine), channel_id=1, source_target_pairs={{0,8},{8,0},{16,24},{24,16},{32,40},{40,32},{48,56},{56,48},{64,72... | collective-permute-start | bytes 983048 | tf_op jit(solution)/shard_map/ppermute | solution.py:232
  140.4 1.3 collective-permute-start.13
  141.7 4.0 %collective-permute-start.14 = (f32[8,128]{1,0:T(8,128)S(1)}, f32[8,128]{1,0:T(8,128)S(1)}, u32[]{:S(2)}, u32[]{:S(2)}) collective-permute-start(f32[8,128]{1,0:T(8,128)S(1)} %add.146), channel_id=1, source_target_pairs={{0,128},{8,136},{16,144},{24,152},{32,160},{40,168},{48,176},{56,1... | collective-permute-start | bytes 12296 | tf_op jit(solution)/shard_map/ppermute | solution.py:235

commit v4 on v3

--- a/solution.py
+++ b/solution.py
@@ -12,7 +12,6 @@
 VMEM_BYTES = 48 * 1024 * 1024
 BF16 = jnp.bfloat16
 F32 = jnp.float32
-HIGHEST = lax.Precision.HIGHEST
 PARAMS = pltpu.CompilerParams(vmem_limit_bytes=VMEM_BYTES)
 SCALARS = pl.BlockSpec(memory_space=pltpu.SMEM)
 WHOLE = pl.BlockSpec(memory_space=pltpu.VMEM)
@@ -64,26 +63,24 @@
             ref[q, 2 * share :, :] = words
 
 
-def covariance_parts(scalars, own, grads, keep, send, kept, packed):
+def covariance_parts(scalars, own, grads, keep, send, turned, kept, packed):
     core, count, flip = scalars[0], scalars[1], scalars[3]
     rows, width = own.shape
     tiles = width // TILE
     valid = lax.broadcasted_iota(jnp.int32, (rows, width), 0) < count
-    for kind, block in enumerate((own, grads)):
-        masked = jnp.where(valid, block[...].astype(F32), 0.0)
-        kept[...] = masked.T.astype(BF16)
-        for n, (a, b) in enumerate(upper_pairs(tiles)):
-            if b % 2 == 0 and a % 2 == 0:
-                square = jnp.dot(
-                    kept[a * TILE : (a + 2) * TILE, :],
-                    block[:, b * TILE : (b + 2) * TILE],
-                    preferred_element_type=F32,
-                ).astype(BF16)
-                for i in range(2):
-                    for j in range(2):
-                        if a + i <= b + j:
-                            at = upper_pairs(tiles).index((a + i, b + j))
-                            packed[kind, at * TILE : (at + 1) * TILE, :] = square[tile_of(i, j)]
+    for kind, (block, left) in enumerate(((own, kept), (grads, turned))):
+        left[...] = jnp.where(valid, block[...].astype(F32), 0.0).T.astype(BF16)
+        for a, b in upper_pairs(tiles // 2):
+            square = jnp.dot(
+                left[2 * a * TILE : 2 * (a + 1) * TILE, :],
+                block[:, 2 * b * TILE : 2 * (b + 1) * TILE],
+                preferred_element_type=F32,
+            ).astype(BF16)
+            for i in range(2):
+                for j in range(2):
+                    if 2 * a + i <= 2 * b + j:
+                        at = upper_pairs(tiles).index((2 * a + i, 2 * b + j))
+                        packed[kind, at * TILE : (at + 1) * TILE, :] = square[tile_of(i, j)]
     quarter = lax.broadcasted_iota(jnp.int32, (ROWS, TILE), 0) // 4
     digits = lax.shift_right_logical(jnp.full((ROWS, TILE), count), 3 * quarter) & 7
     digits = digits.astype(F32).astype(BF16)
@@ -98,19 +95,98 @@
             ref[q, share:, :] = digits
 
 
-def gradient_parts(scalars, features, grads, keep, send, turned, product):
-    core, count = scalars[0], scalars[1]
-
-    @pl.when(pl.program_id(0) == 0)
+def merge_words(first_flag, second_flag, one, two):
+    lanes = one.shape[0] // 8
+    kinds = (lax.broadcasted_iota(jnp.int32, one.shape, 0) // lanes) % 2
+    flags = jnp.where(kinds == 0, first_flag, second_flag)
+    return jnp.where(flags == 1, one.astype(F32), two.astype(F32))
+
+
+def choose_core(scalars, keep, received, near, far):
+    first, second, plane, own_kind = scalars[0], scalars[1], scalars[2], scalars[3]
+    ring, rows = near.shape[0], near.shape[1]
+    data = rows // 6 * 5
+    words = merge_words(first, second, keep[0, data:, :], received[0, data:, :]).astype(BF16)
+    for ref, at, kind in ((near, plane, own_kind), (far, 1 - plane, 1 - own_kind)):
+        flag = jnp.where(kind == 0, first, second)
+
+        @pl.when(flag == 1)
+        def _():
+            ref[:, :data, :] = keep[pl.ds(at * ring, ring), :data, :]
+
+        @pl.when(flag == 0)
+        def _():
+            ref[:, :data, :] = received[pl.ds(at * ring, ring), :data, :]
+
+        for z in range(ring):
+            ref[z, data:, :] = words
+
+
+def add_core(scalars, keep, received, near, far):
+    plane = scalars[2]
+    ring = near.shape[0]
+    for ref, at in ((near, plane), (far, 1 - plane)):
+        chips = pl.ds(at * ring, ring)
+        total = keep[chips].astype(F32) + received[chips].astype(F32)
+        ref[...] = total.astype(ref.dtype)
+
+
+def join_planes(scalars, near, arrived, near_sum, arrived_sum, out):
+    first, second, own_kind = scalars[4], scalars[5], scalars[3]
+    ring, rows = near.shape[0], near.shape[1]
+    data = rows // 6 * 5
+    flag = jnp.where(own_kind == 0, first, second)
+
+    @pl.when(flag == 1)
     def _():
-        valid = lax.broadcasted_iota(jnp.int32, grads.shape, 0) < count
-        turned[...] = jnp.where(valid, grads[...].astype(F32), 0.0).T.astype(BF16)
-
-    product[...] = jnp.dot(turned[...], features[...], preferred_element_type=F32).astype(BF16)
-    for q in range(keep.shape[0]):
-        for ref, parity in ((keep, core), (send, 1 - core)):
-            start = pl.multiple_of((2 * q + parity) * TILE, TILE)
-            ref[q] = product[:, pl.ds(start, TILE)]
+        out[:, :data, :] = near[:, :data, :]
+
+    @pl.when(flag == 0)
+    def _():
+        out[:, :data, :] = arrived[:, :data, :]
+
+    words = merge_words(first, second, near[0, data:, :], arrived[0, data:, :]).astype(BF16)
+    for z in range(ring):
+        out[z, data:rows, :] = words
+    out[:, rows:, :] = (near_sum[...] + arrived_sum[...].astype(F32)).astype(BF16)
+
+
+def make_shares(scalars, arrived, shares, diag):
+    own_kind, first, second = scalars[3], scalars[6], scalars[7]
+    ring, rows = shares.shape[0], shares.shape[1]
+    share = rows // 2
+    words = rows // 5 + rows
+    owner = jnp.where(own_kind == 0, first, second)
+    both = merge_words(1, 0, arrived[first, rows:words, :], arrived[second, rows:words, :])
+    diag[...] = both[: diag.shape[0]] + both[diag.shape[0] :]
+    summed = sum(arrived[z, words:, :].astype(F32) for z in range(ring))
+    total = sum(summed[share + 4 * d : share + 4 * d + 1, :] * float(8**d) for d in range(4))
+    factor = DECAY * arrived[owner, :share, :].astype(F32) + (1.0 - DECAY) * summed[:share] / total
+    factor = factor.astype(BF16)
+    inverse = arrived[owner, share:rows, :]
+    for z in range(ring):
+        shares[z, :share, :] = factor
+        shares[z, share:, :] = inverse
+
+
+def gradient_tiles(turned, tiles):
+    block = jnp.concatenate([tile[...] for tile in tiles], axis=1)
+    return jnp.dot(turned[...], block, preferred_element_type=F32)
+
+
+def gradient_send(scalars, turned, *refs):
+    tiles, send = refs[:4], refs[-1]
+    product = gradient_tiles(turned, tiles)
+    for n in range(4):
+        send[n] = product[:, n * TILE : (n + 1) * TILE].astype(send.dtype)
+
+
+def gradient_add(scalars, turned, *refs):
+    tiles, received, out = refs[:4], refs[4], refs[-1]
+    product = gradient_tiles(turned, tiles)
+    for n in range(4):
+        total = product[:, n * TILE : (n + 1) * TILE] + received[n].astype(F32)
+        out[n] = total.astype(out.dtype)
 
 
 def unpack(mine, other, core, packed):
@@ -124,42 +200,66 @@
                 ]
 
 
-def spread(packed, which, diag, row, scale, block):
-    tiles = block.shape[0] // TILE
+def spread(packed, which, diag, row, scale, high, low):
+    tiles = high.shape[0] // TILE
     on_diagonal = diagonal_mask()
     for n, (a, b) in enumerate(upper_pairs(tiles)):
         piece = packed[which, n * TILE : (n + 1) * TILE, :].astype(F32)
         if a == b:
-            piece = piece + jnp.where(on_diagonal, scale * diag[row + a : row + a + 1, :], 0.0)
+            exact = piece + jnp.where(on_diagonal, scale * diag[row + a : row + a + 1, :], 0.0)
+            rounded = exact.astype(BF16)
+            high[tile_of(a, a)] = rounded
+            rest = jnp.sum(exact - rounded.astype(F32), axis=1, keepdims=True)
+            low[a * TILE : (a + 1) * TILE, :] = jnp.broadcast_to(rest, (TILE, TILE))
         else:
-            block[tile_of(b, a)] = piece.T
-        block[tile_of(a, b)] = piece
-
-
-def fill_blocks(kind, packed, diag, factor, inverse):
+            high[tile_of(a, b)] = packed[which, n * TILE : (n + 1) * TILE, :]
+            high[tile_of(b, a)] = piece.T.astype(BF16)
+
+
+def fill_blocks(kind, packed, diag, factor, factor_low, inverse, inverse_low):
     tiles = factor.shape[0] // TILE
-    spread(packed, 0, diag, kind * tiles, DECAY, factor)
-    spread(packed, 1, diag, (2 + kind) * tiles, 1.0, inverse)
-
-
-def refine(factor, inverse, part):
-    inner = jnp.dot(factor[...], part, precision=HIGHEST, preferred_element_type=F32)
-    inner = inner + DAMPING * part
-    return 2.0 * part - jnp.dot(inverse[...], inner, precision=HIGHEST, preferred_element_type=F32)
-
-
-def left_columns(scalars, mine, other, diag, left, packed, factor, inverse):
+    spread(packed, 0, diag, kind * tiles, DECAY, factor, factor_low)
+    spread(packed, 1, diag, (2 + kind) * tiles, 1.0, inverse, inverse_low)
+
+
+def times(high, low, right):
+    width = right.shape[1]
+    first = right.astype(BF16)
+    second = (right - first.astype(F32)).astype(BF16)
+    both = jnp.dot(high[...], jnp.concatenate([first, second], axis=1), preferred_element_type=F32)
+    return both[:, :width] + both[:, width:] + low * right
+
+
+def refine(factor, factor_low, inverse, inverse_low, part):
+    inner = times(factor, factor_low[:, :1] + DAMPING, part)
+    return 2.0 * part - times(inverse, inverse_low[:, :1], inner)
+
+
+def exact_block(high, low):
+    rows = lax.broadcasted_iota(jnp.int32, high.shape, 0)
+    columns = lax.broadcasted_iota(jnp.int32, high.shape, 1)
+    return high[...].astype(F32) + jnp.where(rows == columns, low[:, :1], 0.0)
+
+
+def left_columns(scalars, mine, other, diag, left, packed, factor, factor_low, inverse, inverse_low):
     core, place = scalars[0], scalars[1]
     unpack(mine, other, core, packed)
-    fill_blocks(0, packed, diag, factor, inverse)
+    fill_blocks(0, packed, diag, factor, factor_low, inverse, inverse_low)
     start = pl.multiple_of(place * TILE, TILE)
-    left[...] = refine(factor, inverse, inverse[:, pl.ds(start, TILE)]).astype(BF16)
+    part = inverse[:, pl.ds(start, TILE)].astype(F32)
+    rows = lax.broadcasted_iota(jnp.int32, part.shape, 0) - start
+    part = part + jnp.where(
+        rows == lax.broadcasted_iota(jnp.int32, part.shape, 1), inverse_low[...], 0.0
+    )
+    left[...] = refine(factor, factor_low, inverse, inverse_low, part).astype(BF16)
 
 
 def new_blocks(
-    scalars, mine, other, far_mine, far_other, diag, right, factor_out, inverse_out, packed, factor, inverse
+    scalars, mine, other, far_mine, far_other, diag, right, factor_out, inverse_out,
+    packed, factor, factor_low, inverse, inverse_low,
 ):
     core, first, second, own_kind = scalars[0], scalars[2], scalars[3], scalars[4]
+    blocks = (factor, factor_low, inverse, inverse_low)
 
     def load_blocks(kind):
         @pl.when(own_kind == kind)
@@ -170,15 +270,15 @@
         def _():
             unpack(far_mine, far_other, core, packed)
 
-        fill_blocks(kind, packed, diag, factor, inverse)
+        fill_blocks(kind, packed, diag, *blocks)
 
     load_blocks(1)
-    fresh = refine(factor, inverse, inverse[...])
+    fresh = refine(*blocks, exact_block(inverse, inverse_low))
     right[...] = fresh.astype(BF16)
 
     @pl.when(second == 1)
     def _():
-        factor_out[...] = factor[...]
+        factor_out[...] = exact_block(factor, factor_low)
         inverse_out[...] = fresh
 
     @pl.when(second == 0)
@@ -189,8 +289,8 @@
     @pl.when(first == 1)
     def _():
         load_blocks(0)
-        factor_out[...] = factor[...]
-        inverse_out[...] = refine(factor, inverse, inverse[...])
+        factor_out[...] = exact_block(factor, factor_low)
+        inverse_out[...] = refine(*blocks, exact_block(inverse, inverse_low))
 
 
 def precondition(scalars, grad, left, right, result, curvature):
@@ -234,16 +334,6 @@
     def swap_planes(send):
         return lax.ppermute(send, "dp", plane_swap)
 
-    def plane_of(parts, which):
-        return lax.dynamic_slice_in_dim(parts, which * ring, ring, 0)
-
-    def sum_planes(keep, received):
-        def pair(which):
-            return plane_of(keep, which).astype(F32) + plane_of(received, which).astype(F32)
-
-        arrived = swap_planes(pair(1 - plane).astype(BF16))
-        return (pair(plane) + arrived.astype(F32)).astype(BF16)
-
     stale_owner = lax.dynamic_index_in_dim(old_owner, column, 0, keepdims=False)
     fresh_owner = lax.dynamic_index_in_dim(new_owner, column, 0, keepdims=False)
     shared_slot = (stale_owner[1] == stale_owner[0]).astype(jnp.int32)
@@ -263,30 +353,43 @@
         compiler_params=PARAMS,
         name="pack_old",
     )(jnp.stack([core, shared_slot, flip]), factor_old[0, 0], inverse_old[0, 0])
-    row = lax.broadcasted_iota(jnp.int32, message.shape, 1) - 2 * share
-    chip = lax.broadcasted_iota(jnp.int32, message.shape, 0)
-
-    def from_owner(kinds, place_of_owner, here, one, two):
-        owner = jnp.where(kinds == 0, place_of_owner[0], place_of_owner[1])
-        return jnp.where(owner == here, one, two)
-
-    kinds = jnp.where(row < 0, (chip // ring) ^ flip, (row // lanes) % 2)
-    chosen = from_owner(kinds, stale_owner % 2, core, keep, swap_cores(send))
-    arrived = swap_planes(plane_of(chosen, 1 - plane))
-    kinds = plane_of(kinds, plane)
-    chosen = from_owner(kinds, stale_owner // chips, plane, plane_of(chosen, plane), arrived)
+    owner_at = (stale_owner // 2) % ring
+    scalars = jnp.concatenate(
+        [
+            (stale_owner % 2 == core).astype(jnp.int32),
+            jnp.stack([plane, own_kind]),
+            (stale_owner // chips == plane).astype(jnp.int32),
+            owner_at,
+        ]
+    )
+    half_message = shape((ring,) + message.shape[1:], BF16)
+    near_old, far_old = pl.pallas_call(
+        choose_core,
+        out_shape=(half_message, half_message),
+        in_specs=[SCALARS, WHOLE, WHOLE],
+        out_specs=(WHOLE, WHOLE),
+        compiler_params=PARAMS,
+        name="choose_core",
+    )(scalars, keep, swap_cores(send))
+    arrived_old = swap_planes(far_old)
 
     message = shape((chips, share + ROWS, TILE), BF16)
-    grads_spec = pl.BlockSpec((tok_rows, width), lambda i, s: (0, 0))
     message_spec = pl.BlockSpec(message.shape, lambda i, s: (0, 0, 0))
-    keep, send = pl.pallas_call(
+    keep, send, turned = pl.pallas_call(
         covariance_parts,
-        out_shape=(message, message),
+        out_shape=(message, message, shape((width, tok_rows), BF16)),
         grid_spec=pltpu.PrefetchScalarGridSpec(
             num_scalar_prefetch=1,
             grid=(1,),
-            in_specs=[pl.BlockSpec((tok_rows, width), lambda i, s: (0, s[2])), grads_spec],
-            out_specs=(message_spec, message_spec),
+            in_specs=[
+                pl.BlockSpec((tok_rows, width), lambda i, s: (0, s[2])),
+                pl.BlockSpec((tok_rows, width), lambda i, s: (0, 0)),
+            ],
+            out_specs=(
+                message_spec,
+                message_spec,
+                pl.BlockSpec((width, tok_rows), lambda i, s: (0, 0)),
+            ),
             scratch_shapes=[
                 pltpu.VMEM((width, tok_rows), BF16),
                 pltpu.VMEM((2, packed_rows, TILE), BF16),
@@ -295,23 +398,68 @@
         compiler_params=PARAMS,
         name="covariance_parts",
     )(jnp.stack([core, counts[0], column, flip]), features, out_grads)
-    covariances = sum_planes(keep, swap_cores(send))
-
-    arrived = across_ring(jnp.concatenate([chosen, covariances], axis=1))
-    owner_at = (stale_owner // 2) % ring
-    from_first = lax.dynamic_index_in_dim(arrived, owner_at[0], 0, keepdims=False)
-    from_second = lax.dynamic_index_in_dim(arrived, owner_at[1], 0, keepdims=False)
-    scattered = jnp.where(own_kind == 0, from_first, from_second)
-    at = slice(2 * share, 2 * share + 8 * lanes)
-    row = lax.broadcasted_iota(jnp.int32, (8 * lanes, TILE), 0)
-    words = jnp.where((row // lanes) % 2 == 0, from_first[at], from_second[at]).astype(F32)
-    diag = words[: 4 * lanes] + words[4 * lanes :]
-    cov_share = jnp.sum(arrived[:, 2 * share + 8 * lanes :].astype(F32), axis=0)
-    total = sum(cov_share[share + 4 * d, 0] * float(8**d) for d in range(4))
-    factor_share = DECAY * scattered[:share].astype(F32) + (1.0 - DECAY) * cov_share[:share] / total
-
-    shares = jnp.concatenate([factor_share.astype(BF16), scattered[share : 2 * share]], axis=0)
-    mine = across_ring(jnp.broadcast_to(shares, (ring,) + shares.shape))
+    half_shape = (ring,) + message.shape[1:]
+    near_sum, far_sum = pl.pallas_call(
+        add_core,
+        out_shape=(shape(half_shape, F32), shape(half_shape, BF16)),
+        in_specs=[SCALARS, WHOLE, WHOLE],
+        out_specs=(WHOLE, WHOLE),
+        compiler_params=PARAMS,
+        name="add_core",
+    )(scalars, keep, swap_cores(send))
+    arrived_sum = swap_planes(far_sum)
+
+    def gradient(kernel, tile_at, count, dtype, name, *others):
+        def tile_spec(n):
+            return pl.BlockSpec((tok_rows, TILE), lambda i, s: (0, 2 * tile_at(4 * i + n, s) + s[0]))
+
+        message_spec = pl.BlockSpec((4, width, TILE), lambda i, s: (i, 0, 0))
+        received_spec = pl.BlockSpec((4, width, TILE), lambda i, s: (tile_at(4 * i, s) // 4, 0, 0))
+        other_specs = [received_spec] if len(others) == 1 else [pl.BlockSpec(memory_space=pl.ANY)] * 2
+        parity = 1 - core if len(others) == 2 else core
+        return pl.pallas_call(
+            kernel,
+            out_shape=shape((count, width, TILE), dtype),
+            grid_spec=pltpu.PrefetchScalarGridSpec(
+                num_scalar_prefetch=1,
+                grid=(count // 4,),
+                in_specs=[pl.BlockSpec((width, tok_rows), lambda i, s: (0, 0))]
+                + [tile_spec(n) for n in range(4)]
+                + other_specs,
+                out_specs=message_spec,
+            ),
+            compiler_params=PARAMS,
+            name=name,
+        )(jnp.stack([parity, plane]), turned, features, features, features, features, *others)
+
+    send = gradient(gradient_send, lambda q, s: q, chips, BF16, "gradient_send", far_old, far_sum)
+    received = swap_cores(send)
+    far_grad = gradient(
+        gradient_add, lambda q, s: (1 - s[1]) * ring + q, ring, BF16, "gradient_far", received
+    )
+    arrived_grad = swap_planes(far_grad)
+    near_grad = gradient(
+        gradient_add, lambda q, s: s[1] * ring + q, ring, F32, "gradient_near", received
+    )
+
+    joined = pl.pallas_call(
+        join_planes,
+        out_shape=shape((ring, near_old.shape[1] + near_sum.shape[1], TILE), BF16),
+        in_specs=[SCALARS] + [WHOLE] * 4,
+        out_specs=WHOLE,
+        compiler_params=PARAMS,
+        name="join_planes",
+    )(scalars, near_old, arrived_old, near_sum, arrived_sum)
+    shares, diag = pl.pallas_call(
+        make_shares,
+        out_shape=(shape((ring, 2 * share, TILE), BF16), shape((4 * lanes, TILE), F32)),
+        in_specs=[SCALARS, WHOLE],
+        out_specs=(WHOLE, WHOLE),
+        compiler_params=PARAMS,
+        name="make_shares",
+    )(scalars, across_ring(joined))
+
+    mine = across_ring(shares)
     other = swap_cores(mine)
     far_mine = swap_planes(mine)
     far_other = swap_cores(far_mine)
@@ -326,8 +474,10 @@
     )
     unpacked = [
         pltpu.VMEM((2, packed_rows, TILE), BF16),
-        pltpu.VMEM((width, width), F32),
-        pltpu.VMEM((width, width), F32),
+        pltpu.VMEM((width, width), BF16),
+        pltpu.VMEM((width, TILE), F32),
+        pltpu.VMEM((width, width), BF16),
+        pltpu.VMEM((width, TILE), F32),
     ]
     left = pl.pallas_call(
         left_columns,
@@ -374,26 +524,7 @@
         name="new_blocks",
     )(scalars, mine, other, far_mine, far_other, diag)
 
-    message = shape((chips, width, TILE), BF16)
-    step = 8
-    message_spec = pl.BlockSpec((step // 2, width, TILE), lambda i, s: (i, 0, 0))
-    keep, send = pl.pallas_call(
-        gradient_parts,
-        out_shape=(message, message),
-        grid_spec=pltpu.PrefetchScalarGridSpec(
-            num_scalar_prefetch=1,
-            grid=(members // step,),
-            in_specs=[pl.BlockSpec((tok_rows, step * TILE), lambda i, s: (0, i)), grads_spec],
-            out_specs=(message_spec, message_spec),
-            scratch_shapes=[
-                pltpu.VMEM((width, tok_rows), BF16),
-                pltpu.VMEM((width, step * TILE), BF16),
-            ],
-        ),
-        compiler_params=PARAMS,
-        name="gradient_parts",
-    )(jnp.stack([core, counts[0]]), features, out_grads)
-    grad = across_ring(sum_planes(keep, swap_cores(send)))
+    grad = across_ring((near_grad + arrived_grad.astype(F32)).astype(BF16))
     grad = jnp.sum(grad.astype(F32), axis=0).astype(BF16)
     neighbours = [[holders * c + r for r in range(holders)] for c in range(columns)]
     grads = lax.all_gather(grad, "dp", axis=0, axis_index_groups=neighbours)
@@ -407,9 +538,10 @@
         name="precondition",
     )(place[None], grads, left, right)
 
-    curvature = curvature + swap_cores(curvature)
-    curvature = curvature + swap_planes(curvature)
-    curvature = jnp.sum(across_ring(jnp.broadcast_to(curvature, (ring, 8, TILE))), axis=0)
+    curvature = lax.all_to_all(
+        jnp.broadcast_to(curvature, (members, 8, TILE)), "dp", 0, 0, tiled=True
+    )
+    curvature = jnp.sum(curvature, axis=0)
     curvature = lax.all_to_all(
         jnp.broadcast_to(curvature, (columns, 8, TILE)), "mp", 0, 0, tiled=True
     )

time: 175 us -> 158 us (0.903); the launches traced: 172 us -> 157 us
  other arithmetic: 17.6 us -> 3.73 us
  blocking collectives: 31.8 us -> 39.1 us
  between operations: 11.3 us -> 4.86 us
  local copies, waits for them, and re-layouts: 10.5 us -> 7.33 us
  Pallas kernels: 26 us -> 28.8 us
    pallas_call x2 -> x8, Pallas kernels: 13.4 us -> 20.8 us  [the longest x3 13.7 us: gradient(): pl.pallas_call(kernel, out_shape=shape((count, width, TILE), dtype), grid...]
    select_n x4 -> x0, other arithmetic: 7.28 us -> none  [the longest x2 5.78 us: from_owner(): return jnp.where(owner == here, one, two)]
    convert_element_type x6 -> x2, other arithmetic: 8.15 us -> 2.44 us  [the longest x1 2.43 us: local(): grad = across_ring((near_grad + arrived_grad.astype(F32)).astype(BF16))]
    all_to_all x1, blocking collectives: 7.43 us -> 12.3 us  [local(): lax.all_to_all(jnp.broadcast_to(curvature, (columns, 8, TILE)), 'mp', 0,...]
    all_to_all x3, starting transfers between devices: 16.1 us -> 13.4 us  [across_ring(): lax.all_to_all(parts, 'dp', 0, 0, tiled=True, axis_index_groups=rings)]
    pallas_call x1, Pallas kernels: 4.2 us -> 1.6 us  [local(): pl.pallas_call(left_columns, out_shape=shape((width, TILE), BF16), in_spe...]
    slice x5 -> x0, local copies, waits for them, and re-layouts: 2.35 us -> none  [the longest x2 1.18 us: from_owner(): owner = jnp.where(kinds == 0, place_of_owner[0], place_of_owner[1])]
    pallas_call x1, Pallas kernels: 5.84 us -> 3.94 us  [local(): pl.pallas_call(new_blocks, out_shape=(shape((width, width), BF16), shape(...]
  transfers between devices with their start and end apart: 18 -> 16, of which waited for: 10 -> 8; matrix products, arithmetic and copies ran while one was open for 12% -> 2% of each run, Pallas kernels for 14% -> 12%
where the time goes in v4:
time: 158 us; the launch traced here: 157 us
  blocking collectives  39.1 us (25%)
  starting transfers between devices  37.2 us (24%)
  waiting for transfers between devices  36.2 us (23%)
  Pallas kernels  28.8 us (18%)
  local copies, waits for them, and re-layouts  7.33 us (5%)
  between operations  4.86 us (3%)
  other arithmetic  3.73 us (2%)
    all_to_all x1, blocking collectives, local(): lax.all_to_all(jnp.broadcast_to(curvature, (members, 8, TILE)), 'dp', 0,...  17.7 us
    ppermute x4, waiting for transfers between devices, swap_planes(): return lax.ppermute(send, 'dp', plane_swap)  16.6 us
    all_to_all x3, waiting for transfers between devices, across_ring(): lax.all_to_all(parts, 'dp', 0, 0, tiled=True, axis_index_groups=rings)  14 us
    pallas_call x3, Pallas kernels, gradient(): pl.pallas_call(kernel, out_shape=shape((count, width, TILE), dtype), grid...  13.7 us
    all_to_all x3, starting transfers between devices, across_ring(): lax.all_to_all(parts, 'dp', 0, 0, tiled=True, axis_index_groups=rings)  13.4 us
    all_to_all x1, blocking collectives, local(): lax.all_to_all(jnp.broadcast_to(curvature, (columns, 8, TILE)), 'mp', 0,...  12.3 us
    all_gather x1, blocking collectives, local(): grads = lax.all_gather(grad, 'dp', axis=0, axis_index_groups=neighbours)  9.07 us
    ppermute x5, starting transfers between devices, swap_cores(): return lax.ppermute(send, 'dp', core_swap)  7.75 us
  transfers between devices with their start and end apart: 16, of which 8 were waited for; matrix products, arithmetic and copies ran while one was open for 2% of the time, Pallas kernels for 12%

profile of v4, /device:TPU:1, one launch (start us, length us, event | category | flops | bytes accessed | tf_op | source)
XLA Modules:
  0.0 157.3 jit_solution(17007037394569426911)
XLA Ops:
  0.6 0.9 fusion.1
  1.5 0.5 fusion.2
  3.5 1.6 %copy-done.1 = f32[1,1,2,512,512]{4,3,2,1,0:T(8,128)S(1)} copy-done((f32[1,1,2,512,512]{4,3,2,1,0:T(8,128)S(1)}, f32[1,1,2,512,512]{4,3,2,1,0:T(8,128)}, u32[]{:S(2)}) %copy-start.1) | copy-done | bytes 2097176
  5.0 1.6 %copy-done.2 = f32[1,1,2,512,512]{4,3,2,1,0:T(8,128)S(1)} copy-done((f32[1,1,2,512,512]{4,3,2,1,0:T(8,128)S(1)}, f32[1,1,2,512,512]{4,3,2,1,0:T(8,128)}, u32[]{:S(2)}) %copy-start.2) | copy-done | bytes 2097176
  6.6 1.7 %pack_old.1 = (bf16[16,192,128]{2,1,0:T(8,128)(2,1)S(1)}, bf16[16,192,128]{2,1,0:T(8,128)(2,1)}) custom-call(s32[3]{0:T(128)S(1)} %pad_add_fusion.scalars, f32[2,512,512]{2,1,0:T(8,128)S(1)} %bitcast.19, f32[2,512,512]{2,1,0:T(8,128)S(1)} %bitcast.20), custom_call_target="tpu_custom_call" | custom-call | tf_op jit(solution)/shard_map/pack_old/pallas_call | solution.py:344
  8.3 3.2 %collective-permute-start = (bf16[16,192,128]{2,1,0:T(8,128)(2,1)}, bf16[16,192,128]{2,1,0:T(8,128)(2,1)S(1)}, u32[]{:S(2)}, u32[]{:S(2)}) collective-permute-start(bf16[16,192,128]{2,1,0:T(8,128)(2,1)} %get-tuple-element.20), channel_id=1, source_target_pairs={{0,8},{8,0},{16,24},{24,16},{32,40},{40,32},{48,56},{56,48},{64,72... | collective-permute-start | bytes 2359304 | tf_op jit(solution)/shard_map/ppermute | solution.py:332
  12.3 3.7 %covariance_parts.1 = (bf16[16,96,128]{2,1,0:T(8,128)(2,1)S(1)}, bf16[16,96,128]{2,1,0:T(8,128)(2,1)}, bf16[512,1024]{1,0:T(8,128)(2,1)S(1)}) custom-call(s32[4]{0:T(128)S(1)} %pad_add_fusion.1.scalars, bf16[1024,4096]{1,0:T(8,128)(2,1)} %refs_3_.5, bf16[1024,512]{1,0:T(8,128)(2,1)S(1)} %copy-done.3), custom_call_target="tpu_custom_call" | custom-call | tf_op jit(solution)/shard_map/covariance_parts/pallas_call | solution.py:378
  16.2 1.9 %collective-permute-done.2.received = bf16[16,96,128]{2,1,0:T(8,128)(2,1)} collective-permute-done((bf16[16,96,128]{2,1,0:T(8,128)(2,1)}, bf16[16,96,128]{2,1,0:T(8,128)(2,1)}, u32[]{:S(2)}, u32[]{:S(2)}) %collective-permute-start.2) | collective-permute-done | bytes 393248 | tf_op jit(solution)/shard_map/ppermute | solution.py:332
  18.1 1.1 add_core.1
  19.2 0.6 choose_core.1
  19.8 6.3 %gradient_send.1 = bf16[16,512,128]{2,1,0:T(8,128)(2,1)} custom-call(s32[2]{0:T(128)S(1)} %pad_add_fusion.3.scalars, bf16[512,1024]{1,0:T(8,128)(2,1)S(1)} %get-tuple-element.31.turned, bf16[1024,4096]{1,0:T(8,128)(2,1)} %refs_3_.5, bf16[1024,4096]{1,0:T(8,128)(2,1)} %refs_3_.5, bf16[1024,4096]{1,0:T(8,128)(2,1)} %refs_3_.5, bf16[1024,4096]{1,0:T(8,128)(2,1)} %refs_3_.5, ...), custom_call_target="tpu_custom_call" | custom-call | tf_op jit(solution)/shard_map/gradient_send/pallas_call | solution.py:420
  26.2 1.2 collective-permute-start.1
  27.4 1.8 %collective-permute-start.3 = (bf16[8,96,128]{2,1,0:T(8,128)(2,1)S(1)}, bf16[8,96,128]{2,1,0:T(8,128)(2,1)S(1)}, u32[]{:S(2)}, u32[]{:S(2)}) collective-permute-start(bf16[8,96,128]{2,1,0:T(8,128)(2,1)S(1)} %get-tuple-element.26.refs_5_), channel_id=1, source_target_pairs={{0,128},{8,136},{16,144},{24,152},{32,160},{40,168},{48,176},{56,1... | collective-permute-start | bytes 589832 | tf_op jit(solution)/shard_map/ppermute | solution.py:335
  29.2 13.1 %collective-permute-done.3.arrived_sum = bf16[8,96,128]{2,1,0:T(8,128)(2,1)S(1)} collective-permute-done((bf16[8,96,128]{2,1,0:T(8,128)(2,1)S(1)}, bf16[8,96,128]{2,1,0:T(8,128)(2,1)S(1)}, u32[]{:S(2)}, u32[]{:S(2)}) %collective-permute-start.3) | collective-permute-done | bytes 196640 | tf_op jit(solution)/shard_map/ppermute | solution.py:335
  42.3 0.6 join_planes.1
  42.9 0.8 copy-done
  43.7 6.4 %all-to-all-start = ((bf16[8,288,128]{2,1,0:T(8,128)(2,1)}), bf16[8,288,128]{2,1,0:T(8,128)(2,1)}, u32[]{:S(2)}, u32[]{:S(2)}) async-start(bf16[8,288,128]{2,1,0:T(8,128)(2,1)} %copy-done), calls=%async_computation | async-start | bytes 1179648 | tf_op jit(solution)/shard_map/all_to_all | solution.py:329
  50.2 4.1 %gradient_far.1 = bf16[8,512,128]{2,1,0:T(8,128)(2,1)} custom-call(s32[2]{0:T(128)S(1)} %pad_add_fusion.2.scalars, bf16[512,1024]{1,0:T(8,128)(2,1)S(1)} %get-tuple-element.31.turned, bf16[1024,4096]{1,0:T(8,128)(2,1)} %refs_3_.5, bf16[1024,4096]{1,0:T(8,128)(2,1)} %refs_3_.5, bf16[1024,4096]{1,0:T(8,128)(2,1)} %refs_3_.5, bf16[1024,4096]{1,0:T(8,128)(2,1)} %refs_3_.5, ...), custom_call_target="tpu_custom_call" | custom-call | tf_op jit(solution)/shard_map/gradient_far/pallas_call | solution.py:420
  54.3 2.9 %collective-permute-start.8 = (bf16[8,512,128]{2,1,0:T(8,128)(2,1)}, bf16[8,512,128]{2,1,0:T(8,128)(2,1)}, u32[]{:S(2)}, u32[]{:S(2)}) collective-permute-start(bf16[8,512,128]{2,1,0:T(8,128)(2,1)} %gradient_far.1), channel_id=1, source_target_pairs={{0,128},{8,136},{16,144},{24,152},{32,160},{40,168},{48,176},{56,1... | collective-permute-start | bytes 3145736 | tf_op jit(solution)/shard_map/ppermute | solution.py:335
  57.2 11.1 %all-to-all-done.arrived = bf16[8,288,128]{2,1,0:T(8,128)(2,1)} async-done(((bf16[8,288,128]{2,1,0:T(8,128)(2,1)}), bf16[8,288,128]{2,1,0:T(8,128)(2,1)}, u32[]{:S(2)}, u32[]{:S(2)}) %all-to-all-start) | async-done | bytes 589856 | tf_op jit(solution)/shard_map/all_to_all | solution.py:329
  68.4 1.1 make_shares.1
  69.5 0.7 copy-done.4
  70.2 3.4 %all-to-all-start.1 = ((bf16[8,160,128]{2,1,0:T(8,128)(2,1)}), bf16[8,160,128]{2,1,0:T(8,128)(2,1)S(1)}, u32[]{:S(2)}, u32[]{:S(2)}) async-start(bf16[8,160,128]{2,1,0:T(8,128)(2,1)} %copy-done.4), calls=%async_computation.1 | async-start | bytes 655360 | tf_op jit(solution)/shard_map/all_to_all | solution.py:329
  73.7 3.3 %gradient_near.1 = f32[8,512,128]{2,1,0:T(8,128)S(1)} custom-call(s32[2]{0:T(128)S(1)} %pad_add_fusion.2.scalars, bf16[512,1024]{1,0:T(8,128)(2,1)S(1)} %get-tuple-element.31.turned, bf16[1024,4096]{1,0:T(8,128)(2,1)} %refs_3_.5, bf16[1024,4096]{1,0:T(8,128)(2,1)} %refs_3_.5, bf16[1024,4096]{1,0:T(8,128)(2,1)} %refs_3_.5, bf16[1024,4096]{1,0:T(8,128)(2,1)} %refs_3_.5, ...), custom_call_target="tpu_custom_call" | custom-call | tf_op jit(solution)/shard_map/gradient_near/pallas_call | solution.py:420
  77.0 2.3 %collective-permute-done.8 = bf16[8,512,128]{2,1,0:T(8,128)(2,1)} collective-permute-done((bf16[8,512,128]{2,1,0:T(8,128)(2,1)}, bf16[8,512,128]{2,1,0:T(8,128)(2,1)}, u32[]{:S(2)}, u32[]{:S(2)}) %collective-permute-start.8) | collective-permute-done | bytes 1048608 | tf_op jit(solution)/shard_map/ppermute | solution.py:335
  79.3 2.4 %add_convert_fusion = bf16[8,512,128]{2,1,0:T(8,128)(2,1)} fusion(f32[8,512,128]{2,1,0:T(8,128)S(1)} %gradient_near.1, bf16[8,512,128]{2,1,0:T(8,128)(2,1)} %collective-permute-done.8), kind=kLoop, calls=%fused_computation | loop fusion | flops 1572864 | bytes 4194304 | tf_op jit(solution)/shard_map/convert_element_type | solution.py:527
  81.7 2.9 %all-to-all-done.1.mine = bf16[8,160,128]{2,1,0:T(8,128)(2,1)S(1)} async-done(((bf16[8,160,128]{2,1,0:T(8,128)(2,1)}), bf16[8,160,128]{2,1,0:T(8,128)(2,1)S(1)}, u32[]{:S(2)}, u32[]{:S(2)}) %all-to-all-start.1) | async-done | bytes 327712 | tf_op jit(solution)/shard_map/all_to_all | solution.py:329
  84.6 3.6 %all-to-all-start.2 = ((bf16[8,512,128]{2,1,0:T(8,128)(2,1)}), bf16[8,512,128]{2,1,0:T(8,128)(2,1)S(1)}, u32[]{:S(2)}, u32[]{:S(2)}) async-start(bf16[8,512,128]{2,1,0:T(8,128)(2,1)} %add_convert_fusion), calls=%async_computation.2 | async-start | bytes 2097152 | tf_op jit(solution)/shard_map/all_to_all | solution.py:329
  88.2 3.2 %collective-permute-start.4 = (bf16[8,160,128]{2,1,0:T(8,128)(2,1)S(1)}, bf16[8,160,128]{2,1,0:T(8,128)(2,1)S(1)}, u32[]{:S(2)}, u32[]{:S(2)}) collective-permute-start(bf16[8,160,128]{2,1,0:T(8,128)(2,1)S(1)} %all-to-all-done.1.mine), channel_id=1, source_target_pairs={{0,8},{8,0},{16,24},{24,16},{32,40},{40,32},{48,56},{56,48},{64,72... | collective-permute-start | bytes 983048 | tf_op jit(solution)/shard_map/ppermute | solution.py:332
  91.5 0.5 fusion.3
  93.4 1.6 %left_columns.1 = bf16[512,128]{1,0:T(8,128)(2,1)S(1)} custom-call(s32[5]{0:T(128)S(1)} %stack.71.scalars, bf16[8,160,128]{2,1,0:T(8,128)(2,1)S(1)} %all-to-all-done.1.mine, bf16[8,160,128]{2,1,0:T(8,128)(2,1)S(1)} %collective-permute-done.4.other, f32[16,128]{1,0:T(8,128)S(1)} %get-tuple-element.28.diag), custom_call_target="tpu_custom_call" | custom-call | tf_op jit(solution)/shard_map/left_columns/pallas_call | solution.py:482
  95.0 3.2 %collective-permute-start.9 = (bf16[512,128]{1,0:T(8,128)(2,1)S(1)}, bf16[512,128]{1,0:T(8,128)(2,1)S(1)}, u32[]{:S(2)}, u32[]{:S(2)}) collective-permute-start(bf16[512,128]{1,0:T(8,128)(2,1)S(1)} %left_columns.1), channel_id=1, source_target_pairs={{0,1},{8,9},{16,17},{24,25},{33,32},{41,40},{49,48},{57,56},{66,67... | collective-permute-start | bytes 393224 | tf_op jit(solution)/shard_map/ppermute | solution.py:492
  98.2 0.4 collective-permute-start.5
  98.7 2.4 %collective-permute-done.9 = bf16[512,128]{1,0:T(8,128)(2,1)S(1)} collective-permute-done((bf16[512,128]{1,0:T(8,128)(2,1)S(1)}, bf16[512,128]{1,0:T(8,128)(2,1)S(1)}, u32[]{:S(2)}, u32[]{:S(2)}) %collective-permute-start.9) | collective-permute-done | bytes 131104 | tf_op jit(solution)/shard_map/ppermute | solution.py:492
  101.1 1.3 collective-permute-start.10
  102.4 3.8 %collective-permute-start.11 = (bf16[512,128]{1,0:T(8,128)(2,1)S(1)}, bf16[512,128]{1,0:T(8,128)(2,1)S(1)}, u32[]{:S(2)}, u32[]{:S(2)}) collective-permute-start(bf16[512,128]{1,0:T(8,128)(2,1)S(1)} %broadcast_select_fusion), channel_id=1, source_target_pairs={{0,4},{1,5},{8,12},{9,13},{16,20},{17,21},{24,28},{25,29},{33,37},... | collective-permute-start | bytes 393224 | tf_op jit(solution)/shard_map/ppermute | solution.py:501
  106.3 1.3 collective-permute-start.12
  107.6 1.2 collective-permute-done.5.far_mine
  108.8 1.1 collective-permute-start.6
  110.0 1.2 collective-permute-done.6.far_other
  111.2 3.9 %new_blocks.1 = (bf16[512,512]{1,0:T(8,128)(2,1)S(1)}, f32[512,512]{1,0:T(8,128)}, f32[512,512]{1,0:T(8,128)}) custom-call(s32[5]{0:T(128)S(1)} %stack.71.scalars, bf16[8,160,128]{2,1,0:T(8,128)(2,1)S(1)} %all-to-all-done.1.mine, bf16[8,160,128]{2,1,0:T(8,128)(2,1)S(1)} %collective-permute-done.4.other, ...), custom_call_target="tpu_custom_call" | custom-call | tf_op jit(solution)/shard_map/new_blocks/pallas_call | solution.py:513
  115.1 0.1 reduce_sum.30
  115.3 9.1 %all-gather = bf16[2048,128]{1,0:T(8,128)(2,1)S(1)} all-gather(bf16[512,128]{1,0:T(8,128)(2,1)S(1)} %reduce_sum.30), channel_id=2, replica_groups={{0,8,16,24},{32,40,48,56},{64,72,80,88},{96,104,112,120},{128,136,144,1..., dimensions={0}, use_global_device_ids=true | all-gather | bytes 655360 | tf_op jit(solution)/shard_map/all_gather | solution.py:530
  124.4 0.8 precondition.1
  125.2 17.7 %all_to_all.25 = f32[32,8,128]{2,1,0:T(8,128)S(1)} all-to-all(f32[32,8,128]{2,1,0:T(8,128)S(1)} %broadcast_in_dim.15), channel_id=1, replica_groups=mesh['dp'=32,'mp'=8] {'dp'}, dimensions={0} | all-to-all | bytes 262144 | tf_op jit(solution)/shard_map/all_to_all | solution.py:541
  142.9 12.3 %all_to_all.26 = f32[8,8,128]{2,1,0:T(8,128)S(1)} all-to-all(f32[8,8,128]{2,1,0:T(8,128)S(1)} %broadcast_in_dim.16), channel_id=1, replica_groups=mesh['dp'=32,'mp'=8] {'mp'}, dimensions={0} | all-to-all | bytes 65536 | tf_op jit(solution)/shard_map/all_to_all | solution.py:545
  155.3 0.5 slice.23
  156.5 0.7 broadcast_multiply_fusion
  (30 shorter events, 0.8 us)
Async XLA Ops:
  3.5 1.6 %copy-start.1 = (f32[1,1,2,512,512]{4,3,2,1,0:T(8,128)S(1)}, f32[1,1,2,512,512]{4,3,2,1,0:T(8,128)}, u32[]{:S(2)}) copy-start(f32[1,1,2,512,512]{4,3,2,1,0:T(8,128)} %param.10) | copy-start | bytes 6291460
  5.0 1.6 %copy-start.2 = (f32[1,1,2,512,512]{4,3,2,1,0:T(8,128)S(1)}, f32[1,1,2,512,512]{4,3,2,1,0:T(8,128)}, u32[]{:S(2)}) copy-start(f32[1,1,2,512,512]{4,3,2,1,0:T(8,128)} %param.11) | copy-start | bytes 6291460
  6.6 5.7 %copy-start.3 = (bf16[1024,512]{1,0:T(8,128)(2,1)S(1)}, bf16[1024,512]{1,0:T(8,128)(2,1)}, u32[]{:S(2)}) copy-start(bf16[1024,512]{1,0:T(8,128)(2,1)} %grads.1) | copy-start | bytes 3145732
  8.3 10.8 %collective-permute-start = (bf16[16,192,128]{2,1,0:T(8,128)(2,1)}, bf16[16,192,128]{2,1,0:T(8,128)(2,1)S(1)}, u32[]{:S(2)}, u32[]{:S(2)}) collective-permute-start(bf16[16,192,128]{2,1,0:T(8,128)(2,1)} %get-tuple-element.20), channel_id=1, source_target_pairs={{0,8},{8,0},{16,24},{24,16},{32,40},{40,32},{48,56},{56,48},{64,72... | collective-permute-start | bytes 2359304 | tf_op jit(solution)/shard_map/ppermute | solution.py:332
  16.0 2.1 %collective-permute-start.2 = (bf16[16,96,128]{2,1,0:T(8,128)(2,1)}, bf16[16,96,128]{2,1,0:T(8,128)(2,1)}, u32[]{:S(2)}, u32[]{:S(2)}) collective-permute-start(bf16[16,96,128]{2,1,0:T(8,128)(2,1)} %get-tuple-element.24), channel_id=1, source_target_pairs={{0,8},{8,0},{16,24},{24,16},{32,40},{40,32},{48,56},{56,48},{64,72... | collective-permute-start | bytes 1179656 | tf_op jit(solution)/shard_map/ppermute | solution.py:332
  26.1 24.1 %collective-permute-start.7 = (bf16[16,512,128]{2,1,0:T(8,128)(2,1)}, bf16[16,512,128]{2,1,0:T(8,128)(2,1)S(1)}, u32[]{:S(2)}, u32[]{:S(2)}) collective-permute-start(bf16[16,512,128]{2,1,0:T(8,128)(2,1)} %gradient_send.1), channel_id=1, source_target_pairs={{0,8},{8,0},{16,24},{24,16},{32,40},{40,32},{48,56},{56,48},{64,72... | collective-permute-start | bytes 6291464 | tf_op jit(solution)/shard_map/ppermute | solution.py:332
  26.2 16.0 %collective-permute-start.1 = (bf16[8,192,128]{2,1,0:T(8,128)(2,1)S(1)}, bf16[8,192,128]{2,1,0:T(8,128)(2,1)S(1)}, u32[]{:S(2)}, u32[]{:S(2)}) collective-permute-start(bf16[8,192,128]{2,1,0:T(8,128)(2,1)S(1)} %get-tuple-element.22.refs_4_), channel_id=1, source_target_pairs={{0,128},{8,136},{16,144},{24,152},{32,160},{40,168},{48,176},{56,1... | collective-permute-start | bytes 1179656 | tf_op jit(solution)/shard_map/ppermute | solution.py:335
  27.4 14.9 %collective-permute-start.3 = (bf16[8,96,128]{2,1,0:T(8,128)(2,1)S(1)}, bf16[8,96,128]{2,1,0:T(8,128)(2,1)S(1)}, u32[]{:S(2)}, u32[]{:S(2)}) collective-permute-start(bf16[8,96,128]{2,1,0:T(8,128)(2,1)S(1)} %get-tuple-element.26.refs_5_), channel_id=1, source_target_pairs={{0,128},{8,136},{16,144},{24,152},{32,160},{40,168},{48,176},{56,1... | collective-permute-start | bytes 589832 | tf_op jit(solution)/shard_map/ppermute | solution.py:335
  42.9 0.8 copy-start
  43.7 24.6 %all-to-all-start = ((bf16[8,288,128]{2,1,0:T(8,128)(2,1)}), bf16[8,288,128]{2,1,0:T(8,128)(2,1)}, u32[]{:S(2)}, u32[]{:S(2)}) async-start(bf16[8,288,128]{2,1,0:T(8,128)(2,1)} %copy-done), calls=%async_computation | async-start | bytes 1179648 | tf_op jit(solution)/shard_map/all_to_all | solution.py:329
  54.3 25.0 %collective-permute-start.8 = (bf16[8,512,128]{2,1,0:T(8,128)(2,1)}, bf16[8,512,128]{2,1,0:T(8,128)(2,1)}, u32[]{:S(2)}, u32[]{:S(2)}) collective-permute-start(bf16[8,512,128]{2,1,0:T(8,128)(2,1)} %gradient_far.1), channel_id=1, source_target_pairs={{0,128},{8,136},{16,144},{24,152},{32,160},{40,168},{48,176},{56,1... | collective-permute-start | bytes 3145736 | tf_op jit(solution)/shard_map/ppermute | solution.py:335
  69.5 0.7 copy-start.4
  70.2 14.4 %all-to-all-start.1 = ((bf16[8,160,128]{2,1,0:T(8,128)(2,1)}), bf16[8,160,128]{2,1,0:T(8,128)(2,1)S(1)}, u32[]{:S(2)}, u32[]{:S(2)}) async-start(bf16[8,160,128]{2,1,0:T(8,128)(2,1)} %copy-done.4), calls=%async_computation.1 | async-start | bytes 655360 | tf_op jit(solution)/shard_map/all_to_all | solution.py:329
  84.6 30.5 %all-to-all-start.2 = ((bf16[8,512,128]{2,1,0:T(8,128)(2,1)}), bf16[8,512,128]{2,1,0:T(8,128)(2,1)S(1)}, u32[]{:S(2)}, u32[]{:S(2)}) async-start(bf16[8,512,128]{2,1,0:T(8,128)(2,1)} %add_convert_fusion), calls=%async_computation.2 | async-start | bytes 2097152 | tf_op jit(solution)/shard_map/all_to_all | solution.py:329
  88.2 5.2 %collective-permute-start.4 = (bf16[8,160,128]{2,1,0:T(8,128)(2,1)S(1)}, bf16[8,160,128]{2,1,0:T(8,128)(2,1)S(1)}, u32[]{:S(2)}, u32[]{:S(2)}) collective-permute-start(bf16[8,160,128]{2,1,0:T(8,128)(2,1)S(1)} %all-to-all-done.1.mine), channel_id=1, source_target_pairs={{0,8},{8,0},{16,24},{24,16},{32,40},{40,32},{48,56},{56,48},{64,72... | collective-permute-start | bytes 983048 | tf_op jit(solution)/shard_map/ppermute | solution.py:332
  95.0 6.1 %collective-permute-start.9 = (bf16[512,128]{1,0:T(8,128)(2,1)S(1)}, bf16[512,128]{1,0:T(8,128)(2,1)S(1)}, u32[]{:S(2)}, u32[]{:S(2)}) collective-permute-start(bf16[512,128]{1,0:T(8,128)(2,1)S(1)} %left_columns.1), channel_id=1, source_target_pairs={{0,1},{8,9},{16,17},{24,25},{33,32},{41,40},{49,48},{57,56},{66,67... | collective-permute-start | bytes 393224 | tf_op jit(solution)/shard_map/ppermute | solution.py:492
  98.2 10.6 %collective-permute-start.5 = (bf16[8,160,128]{2,1,0:T(8,128)(2,1)S(1)}, bf16[8,160,128]{2,1,0:T(8,128)(2,1)S(1)}, u32[]{:S(2)}, u32[]{:S(2)}) collective-permute-start(bf16[8,160,128]{2,1,0:T(8,128)(2,1)S(1)} %all-to-all-done.1.mine), channel_id=1, source_target_pairs={{0,128},{8,136},{16,144},{24,152},{32,160},{40,168},{48,176},{56,1... | collective-permute-start | bytes 983048 | tf_op jit(solution)/shard_map/ppermute | solution.py:335
  101.1 8.8 %collective-permute-start.10 = (bf16[512,128]{1,0:T(8,128)(2,1)S(1)}, bf16[512,128]{1,0:T(8,128)(2,1)S(1)}, u32[]{:S(2)}, u32[]{:S(2)}) collective-permute-start(bf16[512,128]{1,0:T(8,128)(2,1)S(1)} %broadcast_select_fusion), channel_id=1, source_target_pairs={{0,2},{1,3},{8,10},{9,11},{16,18},{17,19},{24,26},{25,27},{33,35},... | collective-permute-start | bytes 393224 | tf_op jit(solution)/shard_map/ppermute | solution.py:501
  102.4 7.5 %collective-permute-start.11 = (bf16[512,128]{1,0:T(8,128)(2,1)S(1)}, bf16[512,128]{1,0:T(8,128)(2,1)S(1)}, u32[]{:S(2)}, u32[]{:S(2)}) collective-permute-start(bf16[512,128]{1,0:T(8,128)(2,1)S(1)} %broadcast_select_fusion), channel_id=1, source_target_pairs={{0,4},{1,5},{8,12},{9,13},{16,20},{17,21},{24,28},{25,29},{33,37},... | collective-permute-start | bytes 393224 | tf_op jit(solution)/shard_map/ppermute | solution.py:501
  106.3 3.7 %collective-permute-start.12 = (bf16[512,128]{1,0:T(8,128)(2,1)S(1)}, bf16[512,128]{1,0:T(8,128)(2,1)S(1)}, u32[]{:S(2)}, u32[]{:S(2)}) collective-permute-start(bf16[512,128]{1,0:T(8,128)(2,1)S(1)} %broadcast_select_fusion), channel_id=1, source_target_pairs={{0,6},{1,7},{8,14},{9,15},{16,22},{17,23},{24,30},{25,31},{33,39},... | collective-permute-start | bytes 393224 | tf_op jit(solution)/shard_map/ppermute | solution.py:501
  108.8 2.4 %collective-permute-start.6 = (bf16[8,160,128]{2,1,0:T(8,128)(2,1)S(1)}, bf16[8,160,128]{2,1,0:T(8,128)(2,1)S(1)}, u32[]{:S(2)}, u32[]{:S(2)}) collective-permute-start(bf16[8,160,128]{2,1,0:T(8,128)(2,1)S(1)} %collective-permute-done.5.far_mine), channel_id=1, source_target_pairs={{0,8},{8,0},{16,24},{24,16},{32,40},{40,32},{48,56},{56,48},{64,72... | collective-permute-start | bytes 983048 | tf_op jit(solution)/shard_map/ppermute | solution.py:332

commit v5 on v4

--- a/solution.py
+++ b/solution.py
@@ -15,6 +15,7 @@
 PARAMS = pltpu.CompilerParams(vmem_limit_bytes=VMEM_BYTES)
 SCALARS = pl.BlockSpec(memory_space=pltpu.SMEM)
 WHOLE = pl.BlockSpec(memory_space=pltpu.VMEM)
+ANYWHERE = pl.BlockSpec(memory_space=pltpu.HBM)
 
 
 def upper_pairs(tiles):
@@ -30,15 +31,49 @@
     return (slice(a * TILE, (a + 1) * TILE), slice(b * TILE, (b + 1) * TILE))
 
 
-def pack_old(scalars, factors, inverses, keep, send, packed, diag):
-    core, shared, flip = scalars[0], scalars[1], scalars[2]
-    tiles = factors.shape[1] // TILE
+class Facts:
+    def __init__(self, old_owner=None, new_owner=None):
+        member = lax.axis_index("dp")
+        self.column = lax.axis_index("mp")
+        chips = lax.axis_size("dp") // 2
+        self.core = member & 1
+        self.plane = jnp.where(member >= chips, 1, 0)
+        self.place = member & (lax.axis_size("dp") // lax.axis_size("mp") - 1)
+        self.flip = jnp.where(self.column >= lax.axis_size("mp") // 2, 1, 0)
+        self.own_kind = self.plane ^ self.flip
+        if old_owner is not None:
+            owners = [old_owner[self.column, kind] for kind in range(2)]
+            self.shared = jnp.where(owners[0] == owners[1], 1, 0)
+            self.same_core = [jnp.where((o & 1) == self.core, 1, 0) for o in owners]
+            self.same_plane = [
+                jnp.where(jnp.where(o >= chips, 1, 0) == self.plane, 1, 0) for o in owners
+            ]
+            self.ring_at = [lax.shift_right_logical(o & (chips - 1), 1) for o in owners]
+        if new_owner is not None:
+            self.keeps = [
+                jnp.where(new_owner[self.column, kind] == member, 1, 0) for kind in range(2)
+            ]
+
+
+def pack_old(owners, factors, inverses, keep, send, held, packed, diag, arrived):
+    facts = Facts(owners)
+    core, flip = facts.core, facts.flip
+    tiles = held.shape[1] // TILE
     on_diagonal = diagonal_mask()
-    for which, held in enumerate((factors, inverses)):
+    loads = [
+        pltpu.make_async_copy(
+            source.at[facts.shared if kind else 0], held.at[which * 2 + kind], arrived.at[which * 2 + kind]
+        )
+        for which, source in enumerate((factors, inverses))
+        for kind in range(2)
+    ]
+    for load in loads:
+        load.start()
+    for which in range(2):
         for kind in range(2):
-            slot = 0 if kind == 0 else shared
+            loads[which * 2 + kind].wait()
             for n, (a, b) in enumerate(upper_pairs(tiles)):
-                piece = held[(slot,) + tile_of(a, b)]
+                piece = held[(which * 2 + kind,) + tile_of(a, b)]
                 if a == b:
                     row = (which * 2 + kind) * tiles + a
                     diag[row : row + 1, :] = jnp.sum(
@@ -63,12 +98,21 @@
             ref[q, 2 * share :, :] = words
 
 
-def covariance_parts(scalars, own, grads, keep, send, turned, kept, packed):
-    core, count, flip = scalars[0], scalars[1], scalars[3]
+def covariance_parts(counts, features, out_grads, keep, send, turned, own, grads, kept, packed, arrived):
+    facts = Facts()
+    core, flip, count = facts.core, facts.flip, counts[0]
     rows, width = own.shape
+    start = pl.multiple_of(facts.column * width, width)
+    loads = [
+        pltpu.make_async_copy(features.at[:, pl.ds(start, width)], own, arrived.at[0]),
+        pltpu.make_async_copy(out_grads, grads, arrived.at[1]),
+    ]
+    for load in loads:
+        load.start()
     tiles = width // TILE
     valid = lax.broadcasted_iota(jnp.int32, (rows, width), 0) < count
     for kind, (block, left) in enumerate(((own, kept), (grads, turned))):
+        loads[kind].wait()
         left[...] = jnp.where(valid, block[...].astype(F32), 0.0).T.astype(BF16)
         for a, b in upper_pairs(tiles // 2):
             square = jnp.dot(
@@ -102,8 +146,10 @@
     return jnp.where(flags == 1, one.astype(F32), two.astype(F32))
 
 
-def choose_core(scalars, keep, received, near, far):
-    first, second, plane, own_kind = scalars[0], scalars[1], scalars[2], scalars[3]
+def choose_core(owners, keep, received, near, far):
+    facts = Facts(owners)
+    first, second = facts.same_core
+    plane, own_kind = facts.plane, facts.own_kind
     ring, rows = near.shape[0], near.shape[1]
     data = rows // 6 * 5
     words = merge_words(first, second, keep[0, data:, :], received[0, data:, :]).astype(BF16)
@@ -122,8 +168,8 @@
             ref[z, data:, :] = words
 
 
-def add_core(scalars, keep, received, near, far):
-    plane = scalars[2]
+def add_core(keep, received, near, far):
+    plane = Facts().plane
     ring = near.shape[0]
     for ref, at in ((near, plane), (far, 1 - plane)):
         chips = pl.ds(at * ring, ring)
@@ -131,8 +177,10 @@
         ref[...] = total.astype(ref.dtype)
 
 
-def join_planes(scalars, near, arrived, near_sum, arrived_sum, out):
-    first, second, own_kind = scalars[4], scalars[5], scalars[3]
+def join_planes(owners, near, arrived, near_sum, arrived_sum, unread, out, untouched):
+    facts = Facts(owners)
+    first, second = facts.same_plane
+    own_kind = facts.own_kind
     ring, rows = near.shape[0], near.shape[1]
     data = rows // 6 * 5
     flag = jnp.where(own_kind == 0, first, second)
@@ -151,8 +199,10 @@
     out[:, rows:, :] = (near_sum[...] + arrived_sum[...].astype(F32)).astype(BF16)
 
 
-def make_shares(scalars, arrived, shares, diag):
-    own_kind, first, second = scalars[3], scalars[6], scalars[7]
+def make_shares(owners, arrived, shares, diag):
+    facts = Facts(owners)
+    own_kind = facts.own_kind
+    first, second = facts.ring_at
     ring, rows = shares.shape[0], shares.shape[1]
     share = rows // 2
     words = rows // 5 + rows
@@ -241,8 +291,9 @@
     return high[...].astype(F32) + jnp.where(rows == columns, low[:, :1], 0.0)
 
 
-def left_columns(scalars, mine, other, diag, left, packed, factor, factor_low, inverse, inverse_low):
-    core, place = scalars[0], scalars[1]
+def left_columns(mine, other, diag, left, packed, factor, factor_low, inverse, inverse_low):
+    facts = Facts()
+    core, place = facts.core, facts.place
     unpack(mine, other, core, packed)
     fill_blocks(0, packed, diag, factor, factor_low, inverse, inverse_low)
     start = pl.multiple_of(place * TILE, TILE)
@@ -255,10 +306,12 @@
 
 
 def new_blocks(
-    scalars, mine, other, far_mine, far_other, diag, right, factor_out, inverse_out,
+    owners, mine, other, far_mine, far_other, diag, right, factor_out, inverse_out,
     packed, factor, factor_low, inverse, inverse_low,
 ):
-    core, first, second, own_kind = scalars[0], scalars[2], scalars[3], scalars[4]
+    facts = Facts(new_owner=owners)
+    core, own_kind = facts.core, facts.own_kind
+    first, second = facts.keeps
     blocks = (factor, factor_low, inverse, inverse_low)
 
     def load_blocks(kind):
@@ -293,8 +346,8 @@
         inverse_out[...] = refine(*blocks, exact_block(inverse, inverse_low))
 
 
-def precondition(scalars, grad, left, right, result, curvature):
-    own = scalars[0]
+def precondition(grad, left, right, result, curvature):
+    own = Facts().place
     half = sum(
         jnp.dot(grad[p], left[p * TILE : (p + 1) * TILE, :], preferred_element_type=F32)
         for p in range(grad.shape[0])
@@ -302,6 +355,22 @@
     product = jnp.dot(half.T.astype(BF16), right[...], preferred_element_type=F32)
     result[...] = product
     curvature[...] = jnp.full(curvature.shape, jnp.sum(product * grad[own].astype(F32).T))
+
+
+def kernel_call(body, out_shape, in_specs, scratch=(), out_specs=None, aliases=None, flops=0, moved=0):
+    if out_specs is None:
+        out_specs = (WHOLE,) * len(out_shape) if isinstance(out_shape, tuple) else WHOLE
+    return pl.pallas_call(
+        body,
+        out_shape=out_shape,
+        in_specs=in_specs,
+        out_specs=out_specs,
+        input_output_aliases=aliases or {},
+        scratch_shapes=list(scratch),
+        compiler_params=PARAMS,
+        cost_estimate=pl.CostEstimate(flops=flops, bytes_accessed=moved, transcendentals=0),
+        name=body.__name__,
+    )
 
 
 def local(features, out_grads, counts, factor_old, inverse_old, old_owner, new_owner):
@@ -313,8 +382,7 @@
     columns = lax.axis_size("mp")
     chips = members // 2
     ring = chips // 2
-    core = member % 2
-    plane = member // chips
+    core = member & 1
     core_swap = [(i, i ^ 1) for i in range(members)]
     plane_swap = [(i, (i + chips) % members) for i in range(members)]
     rings = [[y * chips + 2 * z + c for z in range(ring)] for y in range(2) for c in range(2)]
@@ -322,8 +390,8 @@
     share = 2 * packed_rows // members
     lanes = width // TILE
     holders = members // columns
-    place = member % holders
     shape = jax.ShapeDtypeStruct
+    megabyte = 2 * width * width * 2
 
     def across_ring(parts):
         return lax.all_to_all(parts, "dp", 0, 0, tiled=True, axis_index_groups=rings)
@@ -334,91 +402,56 @@
     def swap_planes(send):
         return lax.ppermute(send, "dp", plane_swap)
 
-    stale_owner = lax.dynamic_index_in_dim(old_owner, column, 0, keepdims=False)
-    fresh_owner = lax.dynamic_index_in_dim(new_owner, column, 0, keepdims=False)
-    shared_slot = (stale_owner[1] == stale_owner[0]).astype(jnp.int32)
-    flip = column // (columns // 2)
-    own_kind = plane ^ flip
-
     message = shape((chips, 2 * share + 8 * lanes, TILE), BF16)
-    keep, send = pl.pallas_call(
+    keep, send = kernel_call(
         pack_old,
-        out_shape=(message, message),
-        in_specs=[SCALARS, WHOLE, WHOLE],
-        out_specs=(WHOLE, WHOLE),
-        scratch_shapes=[
+        (message, message),
+        [SCALARS, ANYWHERE, ANYWHERE],
+        [
+            pltpu.VMEM((4, width, width), F32),
             pltpu.VMEM((2, 2, packed_rows, TILE), BF16),
             pltpu.VMEM((4 * lanes, TILE), F32),
+            pltpu.SemaphoreType.DMA((4,)),
         ],
-        compiler_params=PARAMS,
-        name="pack_old",
-    )(jnp.stack([core, shared_slot, flip]), factor_old[0, 0], inverse_old[0, 0])
-    owner_at = (stale_owner // 2) % ring
-    scalars = jnp.concatenate(
+        moved=6 * megabyte,
+    )(old_owner, factor_old[0, 0], inverse_old[0, 0])
+    half_message = shape((ring,) + message.shape[1:], BF16)
+    near_old, far_old = kernel_call(
+        choose_core, (half_message, half_message), [SCALARS, WHOLE, WHOLE], moved=megabyte
+    )(old_owner, keep, swap_cores(send))
+    arrived_old = swap_planes(far_old)
+
+    message = shape((chips, share + ROWS, TILE), BF16)
+    keep, send, turned = kernel_call(
+        covariance_parts,
+        (message, message, shape((width, tok_rows), BF16)),
+        [SCALARS, ANYWHERE, ANYWHERE],
         [
-            (stale_owner % 2 == core).astype(jnp.int32),
-            jnp.stack([plane, own_kind]),
-            (stale_owner // chips == plane).astype(jnp.int32),
-            owner_at,
-        ]
-    )
-    half_message = shape((ring,) + message.shape[1:], BF16)
-    near_old, far_old = pl.pallas_call(
-        choose_core,
-        out_shape=(half_message, half_message),
-        in_specs=[SCALARS, WHOLE, WHOLE],
-        out_specs=(WHOLE, WHOLE),
-        compiler_params=PARAMS,
-        name="choose_core",
-    )(scalars, keep, swap_cores(send))
-    arrived_old = swap_planes(far_old)
-
-    message = shape((chips, share + ROWS, TILE), BF16)
-    message_spec = pl.BlockSpec(message.shape, lambda i, s: (0, 0, 0))
-    keep, send, turned = pl.pallas_call(
-        covariance_parts,
-        out_shape=(message, message, shape((width, tok_rows), BF16)),
-        grid_spec=pltpu.PrefetchScalarGridSpec(
-            num_scalar_prefetch=1,
-            grid=(1,),
-            in_specs=[
-                pl.BlockSpec((tok_rows, width), lambda i, s: (0, s[2])),
-                pl.BlockSpec((tok_rows, width), lambda i, s: (0, 0)),
-            ],
-            out_specs=(
-                message_spec,
-                message_spec,
-                pl.BlockSpec((width, tok_rows), lambda i, s: (0, 0)),
-            ),
-            scratch_shapes=[
-                pltpu.VMEM((width, tok_rows), BF16),
-                pltpu.VMEM((2, packed_rows, TILE), BF16),
-            ],
-        ),
-        compiler_params=PARAMS,
-        name="covariance_parts",
-    )(jnp.stack([core, counts[0], column, flip]), features, out_grads)
+            pltpu.VMEM((tok_rows, width), BF16),
+            pltpu.VMEM((tok_rows, width), BF16),
+            pltpu.VMEM((width, tok_rows), BF16),
+            pltpu.VMEM((2, packed_rows, TILE), BF16),
+            pltpu.SemaphoreType.DMA((2,)),
+        ],
+        flops=4 * tok_rows * width * width,
+        moved=6 * megabyte,
+    )(counts, features, out_grads)
     half_shape = (ring,) + message.shape[1:]
-    near_sum, far_sum = pl.pallas_call(
-        add_core,
-        out_shape=(shape(half_shape, F32), shape(half_shape, BF16)),
-        in_specs=[SCALARS, WHOLE, WHOLE],
-        out_specs=(WHOLE, WHOLE),
-        compiler_params=PARAMS,
-        name="add_core",
-    )(scalars, keep, swap_cores(send))
+    near_sum, far_sum = kernel_call(
+        add_core, (shape(half_shape, F32), shape(half_shape, BF16)), [WHOLE, WHOLE], moved=megabyte
+    )(keep, swap_cores(send))
     arrived_sum = swap_planes(far_sum)
 
-    def gradient(kernel, tile_at, count, dtype, name, *others):
+    def gradient(body, tile_at, count, dtype, name, *others):
         def tile_spec(n):
             return pl.BlockSpec((tok_rows, TILE), lambda i, s: (0, 2 * tile_at(4 * i + n, s) + s[0]))
 
         message_spec = pl.BlockSpec((4, width, TILE), lambda i, s: (i, 0, 0))
         received_spec = pl.BlockSpec((4, width, TILE), lambda i, s: (tile_at(4 * i, s) // 4, 0, 0))
-        other_specs = [received_spec] if len(others) == 1 else [pl.BlockSpec(memory_space=pl.ANY)] * 2
+        other_specs = [received_spec] if len(others) == 1 else [ANYWHERE] * 2
         parity = 1 - core if len(others) == 2 else core
         return pl.pallas_call(
-            kernel,
+            body,
             out_shape=shape((count, width, TILE), dtype),
             grid_spec=pltpu.PrefetchScalarGridSpec(
                 num_scalar_prefetch=1,
@@ -429,10 +462,29 @@
                 out_specs=message_spec,
             ),
             compiler_params=PARAMS,
+            cost_estimate=pl.CostEstimate(
+                flops=2 * tok_rows * width * TILE * count,
+                bytes_accessed=(count // 2) * megabyte,
+                transcendentals=0,
+            ),
             name=name,
-        )(jnp.stack([parity, plane]), turned, features, features, features, features, *others)
+        )(
+            jnp.stack([parity, jnp.where(member >= chips, 1, 0)]),
+            turned, features, features, features, features, *others,
+        )
 
     send = gradient(gradient_send, lambda q, s: q, chips, BF16, "gradient_send", far_old, far_sum)
+    joined, send = kernel_call(
+        join_planes,
+        (
+            shape((ring, near_old.shape[1] + near_sum.shape[1], TILE), BF16),
+            shape(send.shape, send.dtype),
+        ),
+        [SCALARS] + [WHOLE] * 4 + [ANYWHERE],
+        out_specs=(WHOLE, ANYWHERE),
+        aliases={5: 1},
+        moved=megabyte,
+    )(old_owner, near_old, arrived_old, near_sum, arrived_sum, send)
     received = swap_cores(send)
     far_grad = gradient(
         gradient_add, lambda q, s: (1 - s[1]) * ring + q, ring, BF16, "gradient_far", received
@@ -442,36 +494,17 @@
         gradient_add, lambda q, s: s[1] * ring + q, ring, F32, "gradient_near", received
     )
 
-    joined = pl.pallas_call(
-        join_planes,
-        out_shape=shape((ring, near_old.shape[1] + near_sum.shape[1], TILE), BF16),
-        in_specs=[SCALARS] + [WHOLE] * 4,
-        out_specs=WHOLE,
-        compiler_params=PARAMS,
-        name="join_planes",
-    )(scalars, near_old, arrived_old, near_sum, arrived_sum)
-    shares, diag = pl.pallas_call(
+    shares, diag = kernel_call(
         make_shares,
-        out_shape=(shape((ring, 2 * share, TILE), BF16), shape((4 * lanes, TILE), F32)),
-        in_specs=[SCALARS, WHOLE],
-        out_specs=(WHOLE, WHOLE),
-        compiler_params=PARAMS,
-        name="make_shares",
-    )(scalars, across_ring(joined))
+        (shape((ring, 2 * share, TILE), BF16), shape((4 * lanes, TILE), F32)),
+        [SCALARS, WHOLE],
+        moved=megabyte,
+    )(old_owner, across_ring(joined))
 
     mine = across_ring(shares)
     other = swap_cores(mine)
     far_mine = swap_planes(mine)
     far_other = swap_cores(far_mine)
-    scalars = jnp.stack(
-        [
-            core,
-            place,
-            (member == fresh_owner[0]).astype(jnp.int32),
-            (member == fresh_owner[1]).astype(jnp.int32),
-            own_kind,
-        ]
-    )
     unpacked = [
         pltpu.VMEM((2, packed_rows, TILE), BF16),
         pltpu.VMEM((width, width), BF16),
@@ -479,23 +512,22 @@
         pltpu.VMEM((width, width), BF16),
         pltpu.VMEM((width, TILE), F32),
     ]
-    left = pl.pallas_call(
+    left = kernel_call(
         left_columns,
-        out_shape=shape((width, TILE), BF16),
-        in_specs=[SCALARS, WHOLE, WHOLE, WHOLE],
-        out_specs=WHOLE,
-        scratch_shapes=unpacked,
-        compiler_params=PARAMS,
-        name="left_columns",
-    )(scalars, mine, other, diag)
+        shape((width, TILE), BF16),
+        [WHOLE] * 3,
+        unpacked,
+        flops=8 * width * width * TILE,
+        moved=2 * megabyte,
+    )(mine, other, diag)
     gates = [(i, i // holders) for i in range(members)]
     near = lax.ppermute(
         left, ("dp", "mp"), [(i * columns + g, i * columns + (g ^ 1)) for i, g in gates]
     )
-    gate = member // holders
+    gate = lax.shift_right_logical(member, holders.bit_length() - 1)
     left = jnp.where(column == gate, left, near)
     left = jnp.where(
-        column // 2 == gate // 2,
+        (column ^ gate) <= 1,
         left,
         sum(
             lax.ppermute(
@@ -510,40 +542,40 @@
             for step in range(1, columns // 2)
         ),
     )
-    right, factor_out, inverse_out = pl.pallas_call(
+    square = shape((width, width), F32)
+    right, factor_out, inverse_out = kernel_call(
         new_blocks,
-        out_shape=(
-            shape((width, width), BF16),
-            shape((width, width), F32),
-            shape((width, width), F32),
-        ),
-        in_specs=[SCALARS, WHOLE, WHOLE, WHOLE, WHOLE, WHOLE],
-        out_specs=(WHOLE, WHOLE, WHOLE),
-        scratch_shapes=unpacked,
-        compiler_params=PARAMS,
-        name="new_blocks",
-    )(scalars, mine, other, far_mine, far_other, diag)
+        (shape((width, width), BF16), square, square),
+        [SCALARS] + [WHOLE] * 5,
+        unpacked,
+        flops=8 * width * width * width,
+        moved=6 * megabyte,
+    )(new_owner, mine, other, far_mine, far_other, diag)
 
     grad = across_ring((near_grad + arrived_grad.astype(F32)).astype(BF16))
     grad = jnp.sum(grad.astype(F32), axis=0).astype(BF16)
     neighbours = [[holders * c + r for r in range(holders)] for c in range(columns)]
     grads = lax.all_gather(grad, "dp", axis=0, axis_index_groups=neighbours)
-
-    result, curvature = pl.pallas_call(
+    result, curvature = kernel_call(
         precondition,
-        out_shape=(shape((TILE, width), F32), shape((8, TILE), F32)),
-        in_specs=[SCALARS, WHOLE, WHOLE, WHOLE],
-        out_specs=(WHOLE, WHOLE),
-        compiler_params=PARAMS,
-        name="precondition",
-    )(place[None], grads, left, right)
-
+        (shape((TILE, width), F32), shape((8, TILE), F32)),
+        [WHOLE] * 3,
+        flops=4 * width * width * TILE,
+        moved=megabyte,
+    )(grads, left, right)
+
+    planes = [[y * chips + i for i in range(chips)] for y in range(2)]
     curvature = lax.all_to_all(
-        jnp.broadcast_to(curvature, (members, 8, TILE)), "dp", 0, 0, tiled=True
+        jnp.broadcast_to(curvature, (chips, 8, TILE)),
+        "dp", 0, 0, tiled=True, axis_index_groups=planes,
     )
     curvature = jnp.sum(curvature, axis=0)
+    rings = [
+        [(y * chips + i) * columns + c for y in range(2) for c in range(columns)] for i in range(chips)
+    ]
     curvature = lax.all_to_all(
-        jnp.broadcast_to(curvature, (columns, 8, TILE)), "mp", 0, 0, tiled=True
+        jnp.broadcast_to(curvature, (2 * columns, 8, TILE)),
+        ("dp", "mp"), 0, 0, tiled=True, axis_index_groups=rings,
     )
     curvature = jnp.sum(curvature, axis=0)[0, 0]
     entries = float(feature_count * width * columns)

time: 158 us -> 145 us (0.918)
  blocking collectives: 39.1 us -> 30.8 us
  between operations: 4.86 us -> 2.21 us
  Pallas kernels: 28.8 us -> 26.5 us
  waiting for transfers between devices: 36.2 us -> 37.9 us
    all_to_all x3, waiting for transfers between devices: 14 us -> 24 us  [across_ring(): lax.all_to_all(parts, 'dp', 0, 0, tiled=True, axis_index_groups=rings)]
    ppermute x4, waiting for transfers between devices: 16.6 us -> 9.49 us  [swap_planes(): return lax.ppermute(send, 'dp', plane_swap)]
    all_to_all x2, blocking collectives: 30.1 us -> 23.5 us  [the longest x1 12.7 us: local(): lax.all_to_all(jnp.broadcast_to(curvature, (2 * columns, 8, TILE)), ('dp'...]
    pallas_call x12, Pallas kernels: 28.8 us -> 26.5 us  [the longest x3 13.7 us: gradient(): pl.pallas_call(body, out_shape=shape((count, width, TILE), dtype), grid_s...]
    all_gather x1, blocking collectives: 9.07 us -> 7.29 us  [local(): grads = lax.all_gather(grad, 'dp', axis=0, axis_index_groups=neighbours)]
    unnamed x10 -> x14, local copies, waits for them, and re-layouts: 4.72 us -> 5.55 us
  transfers between devices with their start and end apart: 16 -> 16, of which waited for: 8 -> 9; matrix products, arithmetic and copies ran while one was open for 2% -> 2% of each run, Pallas kernels for 12% -> 16%
where the time goes in v5:
time: 145 us; the launch traced here: 144 us
  waiting for transfers between devices  37.9 us (26%)
  starting transfers between devices  36.9 us (25%)
  blocking collectives  30.8 us (21%)
  Pallas kernels  26.5 us (18%)
  local copies, waits for them, and re-layouts  6.08 us (4%)
  other arithmetic  3.51 us (2%)
  between operations  2.21 us (2%)
    all_to_all x3, waiting for transfers between devices, across_ring(): lax.all_to_all(parts, 'dp', 0, 0, tiled=True, axis_index_groups=rings)  24 us
    pallas_call x3, Pallas kernels, gradient(): pl.pallas_call(body, out_shape=shape((count, width, TILE), dtype), grid_s...  13.7 us
    all_to_all x3, starting transfers between devices, across_ring(): lax.all_to_all(parts, 'dp', 0, 0, tiled=True, axis_index_groups=rings)  13.4 us
    all_to_all x1, blocking collectives, local(): lax.all_to_all(jnp.broadcast_to(curvature, (2 * columns, 8, TILE)), ('dp'...  12.7 us
    all_to_all x1, blocking collectives, local(): lax.all_to_all(jnp.broadcast_to(curvature, (chips, 8, TILE)), 'dp', 0, 0,...  10.7 us
    ppermute x4, waiting for transfers between devices, swap_planes(): return lax.ppermute(send, 'dp', plane_swap)  9.49 us
    all_gather x1, blocking collectives, local(): grads = lax.all_gather(grad, 'dp', axis=0, axis_index_groups=neighbours)  7.29 us
    ppermute x3, starting transfers between devices, local(): lax.ppermute(left, ('dp', 'mp'), [(i * columns + g, i * columns + (g + 2...  6.88 us
  transfers between devices with their start and end apart: 16, of which 9 were waited for; matrix products, arithmetic and copies ran while one was open for 2% of the time, Pallas kernels for 16%

profile of v5, /device:TPU:1, one launch (start us, length us, event | category | flops | bytes accessed | tf_op | source)
XLA Modules:
  0.0 143.8 jit_solution(9876975297658022445)
XLA Ops:
  0.6 0.8 copy.19.owners
  1.4 1.6 %copy-done = f32[1,1,2,512,512]{4,3,2,1,0:T(8,128)S(1)} copy-done((f32[1,1,2,512,512]{4,3,2,1,0:T(8,128)S(1)}, f32[1,1,2,512,512]{4,3,2,1,0:T(8,128)}, u32[]{:S(2)}) %copy-start) | copy-done | bytes 2097176
  3.0 1.6 %copy-done.1 = f32[1,1,2,512,512]{4,3,2,1,0:T(8,128)S(1)} copy-done((f32[1,1,2,512,512]{4,3,2,1,0:T(8,128)S(1)}, f32[1,1,2,512,512]{4,3,2,1,0:T(8,128)}, u32[]{:S(2)}) %copy-start.1) | copy-done | bytes 2097176
  4.6 1.3 pack_old.1
  5.9 3.3 %collective-permute-start = (bf16[16,192,128]{2,1,0:T(8,128)(2,1)S(1)}, bf16[16,192,128]{2,1,0:T(8,128)(2,1)S(1)}, u32[]{:S(2)}, u32[]{:S(2)}) collective-permute-start(bf16[16,192,128]{2,1,0:T(8,128)(2,1)S(1)} %get-tuple-element.22), channel_id=1, source_target_pairs={{0,8},{8,0},{16,24},{24,16},{32,40},{40,32},{48,56},{56,48},{64,72... | collective-permute-start | bytes 2359304 | tf_op jit(solution)/shard_map/ppermute | solution.py:400
  9.9 2.9 %covariance_parts.1 = (bf16[16,96,128]{2,1,0:T(8,128)(2,1)S(1)}, bf16[16,96,128]{2,1,0:T(8,128)(2,1)S(1)}, bf16[512,1024]{1,0:T(8,128)(2,1)S(1)}) custom-call(s32[1]{0:T(128)S(6)} %copy.22.counts, bf16[1024,4096]{1,0:T(8,128)(2,1)} %refs_3_.5, bf16[1024,512]{1,0:T(8,128)(2,1)S(1)} %copy-done.2), custom_call_target="tpu_custom_call" | custom-call | flops 1073741824 | bytes 6291456 | tf_op jit(solution)/shard_map/covariance_parts/pallas_call | solution.py:425
  12.8 0.1 collective-permute-start.2
  12.9 0.7 choose_core.1
  13.6 1.3 collective-permute-start.1
  15.0 1.9 %collective-permute-start.3 = (bf16[8,96,128]{2,1,0:T(8,128)(2,1)S(1)}, bf16[8,96,128]{2,1,0:T(8,128)(2,1)S(1)}, u32[]{:S(2)}, u32[]{:S(2)}) collective-permute-start(bf16[8,96,128]{2,1,0:T(8,128)(2,1)S(1)} %get-tuple-element.28.refs_5_), channel_id=1, source_target_pairs={{0,128},{8,136},{16,144},{24,152},{32,160},{40,168},{48,176},{56,1... | collective-permute-start | bytes 589832 | tf_op jit(solution)/shard_map/ppermute | solution.py:403
  16.9 6.3 %gradient_send.1.unread = bf16[16,512,128]{2,1,0:T(8,128)(2,1)} custom-call(s32[2]{0:T(128)S(1)} %pad_add_fusion.scalars, bf16[512,1024]{1,0:T(8,128)(2,1)S(1)} %get-tuple-element.29.turned, bf16[1024,4096]{1,0:T(8,128)(2,1)} %refs_3_.5, bf16[1024,4096]{1,0:T(8,128)(2,1)} %refs_3_.5, bf16[1024,4096]{1,0:T(8,128)(2,1)} %refs_3_.5, ...), custom_call_target="tpu_custom_call" | custom-call | flops 2147483648 | bytes 8388608 | tf_op jit(solution)/shard_map/gradient_send/pallas_call | solution.py:453
  23.1 6.4 %collective-permute-done.3.arrived_sum = bf16[8,96,128]{2,1,0:T(8,128)(2,1)S(1)} collective-permute-done((bf16[8,96,128]{2,1,0:T(8,128)(2,1)S(1)}, bf16[8,96,128]{2,1,0:T(8,128)(2,1)S(1)}, u32[]{:S(2)}, u32[]{:S(2)}) %collective-permute-start.3) | collective-permute-done | bytes 196640 | tf_op jit(solution)/shard_map/ppermute | solution.py:403
  29.6 0.7 join_planes.1
  30.3 0.8 copy-done.3
  31.1 1.3 collective-permute-start.7
  32.4 6.4 %all-to-all-start = ((bf16[8,288,128]{2,1,0:T(8,128)(2,1)}), bf16[8,288,128]{2,1,0:T(8,128)(2,1)}, u32[]{:S(2)}, u32[]{:S(2)}) async-start(bf16[8,288,128]{2,1,0:T(8,128)(2,1)} %copy-done.3), calls=%async_computation | async-start | bytes 1179648 | tf_op jit(solution)/shard_map/all_to_all | solution.py:397
  38.9 4.1 %gradient_far.1 = bf16[8,512,128]{2,1,0:T(8,128)(2,1)} custom-call(s32[2]{0:T(128)S(1)} %pad_add_fusion.1.scalars, bf16[512,1024]{1,0:T(8,128)(2,1)S(1)} %get-tuple-element.29.turned, bf16[1024,4096]{1,0:T(8,128)(2,1)} %refs_3_.5, bf16[1024,4096]{1,0:T(8,128)(2,1)} %refs_3_.5, bf16[1024,4096]{1,0:T(8,128)(2,1)} %refs_3_.5, bf16[1024,4096]{1,0:T(8,128)(2,1)} %refs_3_.5, ...), custom_call_target="tpu_custom_call" | custom-call | flops 1073741824 | bytes 4194304 | tf_op jit(solution)/shard_map/gradient_far/pallas_call | solution.py:453
  43.0 2.9 %collective-permute-start.8 = (bf16[8,512,128]{2,1,0:T(8,128)(2,1)}, bf16[8,512,128]{2,1,0:T(8,128)(2,1)}, u32[]{:S(2)}, u32[]{:S(2)}) collective-permute-start(bf16[8,512,128]{2,1,0:T(8,128)(2,1)} %gradient_far.1), channel_id=1, source_target_pairs={{0,128},{8,136},{16,144},{24,152},{32,160},{40,168},{48,176},{56,1... | collective-permute-start | bytes 3145736 | tf_op jit(solution)/shard_map/ppermute | solution.py:403
  45.9 12.5 %all-to-all-done.arrived = bf16[8,288,128]{2,1,0:T(8,128)(2,1)} async-done(((bf16[8,288,128]{2,1,0:T(8,128)(2,1)}), bf16[8,288,128]{2,1,0:T(8,128)(2,1)}, u32[]{:S(2)}, u32[]{:S(2)}) %all-to-all-start) | async-done | bytes 589856 | tf_op jit(solution)/shard_map/all_to_all | solution.py:397
  58.4 1.1 make_shares.1
  59.5 0.7 copy-done.4
  60.3 3.4 %all-to-all-start.1 = ((bf16[8,160,128]{2,1,0:T(8,128)(2,1)}), bf16[8,160,128]{2,1,0:T(8,128)(2,1)S(1)}, u32[]{:S(2)}, u32[]{:S(2)}) async-start(bf16[8,160,128]{2,1,0:T(8,128)(2,1)} %copy-done.4), calls=%async_computation.1 | async-start | bytes 655360 | tf_op jit(solution)/shard_map/all_to_all | solution.py:397
  63.7 3.3 %gradient_near.1 = f32[8,512,128]{2,1,0:T(8,128)S(1)} custom-call(s32[2]{0:T(128)S(1)} %pad_add_fusion.1.scalars, bf16[512,1024]{1,0:T(8,128)(2,1)S(1)} %get-tuple-element.29.turned, bf16[1024,4096]{1,0:T(8,128)(2,1)} %refs_3_.5, bf16[1024,4096]{1,0:T(8,128)(2,1)} %refs_3_.5, bf16[1024,4096]{1,0:T(8,128)(2,1)} %refs_3_.5, bf16[1024,4096]{1,0:T(8,128)(2,1)} %refs_3_.5, ...), custom_call_target="tpu_custom_call" | custom-call | flops 1073741824 | bytes 4194304 | tf_op jit(solution)/shard_map/gradient_near/pallas_call | solution.py:453
  67.0 2.3 %collective-permute-done.8 = bf16[8,512,128]{2,1,0:T(8,128)(2,1)} collective-permute-done((bf16[8,512,128]{2,1,0:T(8,128)(2,1)}, bf16[8,512,128]{2,1,0:T(8,128)(2,1)}, u32[]{:S(2)}, u32[]{:S(2)}) %collective-permute-start.8) | collective-permute-done | bytes 1048608 | tf_op jit(solution)/shard_map/ppermute | solution.py:403
  69.3 2.4 %add_convert_fusion = bf16[8,512,128]{2,1,0:T(8,128)(2,1)} fusion(f32[8,512,128]{2,1,0:T(8,128)S(1)} %gradient_near.1, bf16[8,512,128]{2,1,0:T(8,128)(2,1)} %collective-permute-done.8), kind=kLoop, calls=%fused_computation | loop fusion | flops 1572864 | bytes 4194304 | tf_op jit(solution)/shard_map/convert_element_type | solution.py:555
  71.7 5.7 %all-to-all-done.1.mine = bf16[8,160,128]{2,1,0:T(8,128)(2,1)S(1)} async-done(((bf16[8,160,128]{2,1,0:T(8,128)(2,1)}), bf16[8,160,128]{2,1,0:T(8,128)(2,1)S(1)}, u32[]{:S(2)}, u32[]{:S(2)}) %all-to-all-start.1) | async-done | bytes 327712 | tf_op jit(solution)/shard_map/all_to_all | solution.py:397
  77.4 3.6 %all-to-all-start.2 = ((bf16[8,512,128]{2,1,0:T(8,128)(2,1)}), bf16[8,512,128]{2,1,0:T(8,128)(2,1)S(1)}, u32[]{:S(2)}, u32[]{:S(2)}) async-start(bf16[8,512,128]{2,1,0:T(8,128)(2,1)} %add_convert_fusion), calls=%async_computation.2 | async-start | bytes 2097152 | tf_op jit(solution)/shard_map/all_to_all | solution.py:397
  80.9 0.6 collective-permute-start.4
  81.5 1.3 collective-permute-done.4.other
  82.8 1.2 left_columns.1
  84.0 3.2 %collective-permute-start.9 = (bf16[512,128]{1,0:T(8,128)(2,1)S(1)}, bf16[512,128]{1,0:T(8,128)(2,1)S(1)}, u32[]{:S(2)}, u32[]{:S(2)}) collective-permute-start(bf16[512,128]{1,0:T(8,128)(2,1)S(1)} %left_columns.1), channel_id=1, source_target_pairs={{0,1},{8,9},{16,17},{24,25},{33,32},{41,40},{49,48},{57,56},{66,67... | collective-permute-start | bytes 393224 | tf_op jit(solution)/shard_map/ppermute | solution.py:524
  87.2 0.5 collective-permute-start.5
  87.7 2.0 %collective-permute-done.9 = bf16[512,128]{1,0:T(8,128)(2,1)S(1)} collective-permute-done((bf16[512,128]{1,0:T(8,128)(2,1)S(1)}, bf16[512,128]{1,0:T(8,128)(2,1)S(1)}, u32[]{:S(2)}, u32[]{:S(2)}) %collective-permute-start.9) | collective-permute-done | bytes 131104 | tf_op jit(solution)/shard_map/ppermute | solution.py:524
  89.7 1.3 collective-permute-start.10
  91.0 4.3 %collective-permute-start.11 = (bf16[512,128]{1,0:T(8,128)(2,1)S(1)}, bf16[512,128]{1,0:T(8,128)(2,1)S(1)}, u32[]{:S(2)}, u32[]{:S(2)}) collective-permute-start(bf16[512,128]{1,0:T(8,128)(2,1)S(1)} %broadcast_select_fusion), channel_id=1, source_target_pairs={{0,4},{1,5},{8,12},{9,13},{16,20},{17,21},{24,28},{25,29},{33,37},... | collective-permute-start | bytes 393224 | tf_op jit(solution)/shard_map/ppermute | solution.py:533
  95.3 1.3 collective-permute-start.12
  96.6 0.8 collective-permute-done.5.far_mine
  97.4 1.5 %collective-permute-start.6 = (bf16[8,160,128]{2,1,0:T(8,128)(2,1)S(1)}, bf16[8,160,128]{2,1,0:T(8,128)(2,1)S(1)}, u32[]{:S(2)}, u32[]{:S(2)}) collective-permute-start(bf16[8,160,128]{2,1,0:T(8,128)(2,1)S(1)} %collective-permute-done.5.far_mine), channel_id=1, source_target_pairs={{0,8},{8,0},{16,24},{24,16},{32,40},{40,32},{48,56},{56,48},{64,72... | collective-permute-start | bytes 983048 | tf_op jit(solution)/shard_map/ppermute | solution.py:400
  99.1 1.1 collective-permute-done.6.far_other
  100.2 4.0 %new_blocks.1 = (bf16[512,512]{1,0:T(8,128)(2,1)S(1)}, f32[512,512]{1,0:T(8,128)}, f32[512,512]{1,0:T(8,128)}) custom-call(s32[8,2]{1,0:T(8,128)S(1)} %copy.20.owners, bf16[8,160,128]{2,1,0:T(8,128)(2,1)S(1)} %all-to-all-done.1.mine, bf16[8,160,128]{2,1,0:T(8,128)(2,1)S(1)} %collective-permute-done.4.other, ...), custom_call_target="tpu_custom_call" | custom-call | flops 1073741824 | bytes 6291456 | tf_op jit(solution)/shard_map/new_blocks/pallas_call | solution.py:546
  104.2 5.9 %all-to-all-done.2 = bf16[8,512,128]{2,1,0:T(8,128)(2,1)S(1)} async-done(((bf16[8,512,128]{2,1,0:T(8,128)(2,1)}), bf16[8,512,128]{2,1,0:T(8,128)(2,1)S(1)}, u32[]{:S(2)}, u32[]{:S(2)}) %all-to-all-start.2) | async-done | bytes 1048608 | tf_op jit(solution)/shard_map/all_to_all | solution.py:397
  110.1 0.1 reduce_sum.30
  110.2 7.3 %all-gather = bf16[2048,128]{1,0:T(8,128)(2,1)S(1)} all-gather(bf16[512,128]{1,0:T(8,128)(2,1)S(1)} %reduce_sum.30), channel_id=2, replica_groups={{0,8,16,24},{32,40,48,56},{64,72,80,88},{96,104,112,120},{128,136,144,1..., dimensions={0}, use_global_device_ids=true | all-gather | bytes 655360 | tf_op jit(solution)/shard_map/all_gather | solution.py:558
  117.5 0.8 precondition.1
  118.3 10.7 %all_to_all.25 = f32[16,8,128]{2,1,0:T(8,128)S(1)} all-to-all(f32[16,8,128]{2,1,0:T(8,128)S(1)} %broadcast_in_dim.14), channel_id=1, replica_groups={{0,8,16,24,32,40,48,56,64,72,80,88,96,104,112,120},{128,136,144,152,160..., dimensions={0} | all-to-all | bytes 131072 | tf_op jit(solution)/shard_map/all_to_all | solution.py:568
  129.1 12.7 %all_to_all.26 = f32[16,8,128]{2,1,0:T(8,128)S(1)} all-to-all(f32[16,8,128]{2,1,0:T(8,128)S(1)} %broadcast_in_dim.15), channel_id=1, replica_groups={{0,1,2,3,4,5,6,7,128,129,130,131,132,133,134,135},{8,9,10,11,12,13,14,1..., dimensions={0} | all-to-all | bytes 131072 | tf_op jit(solution)/shard_map/all_to_all | solution.py:576
  141.8 0.5 slice.3
  143.1 0.7 broadcast_multiply_fusion
  (25 shorter events, 0.4 us)
Async XLA Ops:
  1.4 1.6 %copy-start = (f32[1,1,2,512,512]{4,3,2,1,0:T(8,128)S(1)}, f32[1,1,2,512,512]{4,3,2,1,0:T(8,128)}, u32[]{:S(2)}) copy-start(f32[1,1,2,512,512]{4,3,2,1,0:T(8,128)} %param.10) | copy-start | bytes 6291460
  3.0 1.6 %copy-start.1 = (f32[1,1,2,512,512]{4,3,2,1,0:T(8,128)S(1)}, f32[1,1,2,512,512]{4,3,2,1,0:T(8,128)}, u32[]{:S(2)}) copy-start(f32[1,1,2,512,512]{4,3,2,1,0:T(8,128)} %param.11) | copy-start | bytes 6291460
  4.6 5.3 %copy-start.2 = (bf16[1024,512]{1,0:T(8,128)(2,1)S(1)}, bf16[1024,512]{1,0:T(8,128)(2,1)}, u32[]{:S(2)}) copy-start(bf16[1024,512]{1,0:T(8,128)(2,1)} %out_grads.1) | copy-start | bytes 3145732
  5.9 7.0 %collective-permute-start = (bf16[16,192,128]{2,1,0:T(8,128)(2,1)S(1)}, bf16[16,192,128]{2,1,0:T(8,128)(2,1)S(1)}, u32[]{:S(2)}, u32[]{:S(2)}) collective-permute-start(bf16[16,192,128]{2,1,0:T(8,128)(2,1)S(1)} %get-tuple-element.22), channel_id=1, source_target_pairs={{0,8},{8,0},{16,24},{24,16},{32,40},{40,32},{48,56},{56,48},{64,72... | collective-permute-start | bytes 2359304 | tf_op jit(solution)/shard_map/ppermute | solution.py:400
  12.8 2.2 %collective-permute-start.2 = (bf16[16,96,128]{2,1,0:T(8,128)(2,1)S(1)}, bf16[16,96,128]{2,1,0:T(8,128)(2,1)S(1)}, u32[]{:S(2)}, u32[]{:S(2)}) collective-permute-start(bf16[16,96,128]{2,1,0:T(8,128)(2,1)S(1)} %get-tuple-element.26), channel_id=1, source_target_pairs={{0,8},{8,0},{16,24},{24,16},{32,40},{40,32},{48,56},{56,48},{64,72... | collective-permute-start | bytes 1179656 | tf_op jit(solution)/shard_map/ppermute | solution.py:400
  13.6 16.0 %collective-permute-start.1 = (bf16[8,192,128]{2,1,0:T(8,128)(2,1)S(1)}, bf16[8,192,128]{2,1,0:T(8,128)(2,1)S(1)}, u32[]{:S(2)}, u32[]{:S(2)}) collective-permute-start(bf16[8,192,128]{2,1,0:T(8,128)(2,1)S(1)} %get-tuple-element.24.refs_4_), channel_id=1, source_target_pairs={{0,128},{8,136},{16,144},{24,152},{32,160},{40,168},{48,176},{56,1... | collective-permute-start | bytes 1179656 | tf_op jit(solution)/shard_map/ppermute | solution.py:403
  15.0 14.6 %collective-permute-start.3 = (bf16[8,96,128]{2,1,0:T(8,128)(2,1)S(1)}, bf16[8,96,128]{2,1,0:T(8,128)(2,1)S(1)}, u32[]{:S(2)}, u32[]{:S(2)}) collective-permute-start(bf16[8,96,128]{2,1,0:T(8,128)(2,1)S(1)} %get-tuple-element.28.refs_5_), channel_id=1, source_target_pairs={{0,128},{8,136},{16,144},{24,152},{32,160},{40,168},{48,176},{56,1... | collective-permute-start | bytes 589832 | tf_op jit(solution)/shard_map/ppermute | solution.py:403
  30.3 0.8 copy-start.3
  31.1 7.9 %collective-permute-start.7 = (bf16[16,512,128]{2,1,0:T(8,128)(2,1)}, bf16[16,512,128]{2,1,0:T(8,128)(2,1)S(1)}, u32[]{:S(2)}, u32[]{:S(2)}) collective-permute-start(bf16[16,512,128]{2,1,0:T(8,128)(2,1)} %get-tuple-element.35), channel_id=1, source_target_pairs={{0,8},{8,0},{16,24},{24,16},{32,40},{40,32},{48,56},{56,48},{64,72... | collective-permute-start | bytes 6291464 | tf_op jit(solution)/shard_map/ppermute | solution.py:400
  32.4 26.0 %all-to-all-start = ((bf16[8,288,128]{2,1,0:T(8,128)(2,1)}), bf16[8,288,128]{2,1,0:T(8,128)(2,1)}, u32[]{:S(2)}, u32[]{:S(2)}) async-start(bf16[8,288,128]{2,1,0:T(8,128)(2,1)} %copy-done.3), calls=%async_computation | async-start | bytes 1179648 | tf_op jit(solution)/shard_map/all_to_all | solution.py:397
  43.0 26.3 %collective-permute-start.8 = (bf16[8,512,128]{2,1,0:T(8,128)(2,1)}, bf16[8,512,128]{2,1,0:T(8,128)(2,1)}, u32[]{:S(2)}, u32[]{:S(2)}) collective-permute-start(bf16[8,512,128]{2,1,0:T(8,128)(2,1)} %gradient_far.1), channel_id=1, source_target_pairs={{0,128},{8,136},{16,144},{24,152},{32,160},{40,168},{48,176},{56,1... | collective-permute-start | bytes 3145736 | tf_op jit(solution)/shard_map/ppermute | solution.py:403
  59.5 0.7 copy-start.4
  60.3 17.1 %all-to-all-start.1 = ((bf16[8,160,128]{2,1,0:T(8,128)(2,1)}), bf16[8,160,128]{2,1,0:T(8,128)(2,1)S(1)}, u32[]{:S(2)}, u32[]{:S(2)}) async-start(bf16[8,160,128]{2,1,0:T(8,128)(2,1)} %copy-done.4), calls=%async_computation.1 | async-start | bytes 655360 | tf_op jit(solution)/shard_map/all_to_all | solution.py:397
  71.7 27.2 %copy-start.5 = (s32[8,2]{0,1:T(2,128)S(1)}, s32[8,2]{0,1:T(2,128)}, u32[]{:S(2)}) copy-start(s32[8,2]{0,1:T(2,128)} %param.13) | copy-start | bytes 196
  77.4 32.7 %all-to-all-start.2 = ((bf16[8,512,128]{2,1,0:T(8,128)(2,1)}), bf16[8,512,128]{2,1,0:T(8,128)(2,1)S(1)}, u32[]{:S(2)}, u32[]{:S(2)}) async-start(bf16[8,512,128]{2,1,0:T(8,128)(2,1)} %add_convert_fusion), calls=%async_computation.2 | async-start | bytes 2097152 | tf_op jit(solution)/shard_map/all_to_all | solution.py:397
  80.9 1.8 %collective-permute-start.4 = (bf16[8,160,128]{2,1,0:T(8,128)(2,1)S(1)}, bf16[8,160,128]{2,1,0:T(8,128)(2,1)S(1)}, u32[]{:S(2)}, u32[]{:S(2)}) collective-permute-start(bf16[8,160,128]{2,1,0:T(8,128)(2,1)S(1)} %all-to-all-done.1.mine), channel_id=1, source_target_pairs={{0,8},{8,0},{16,24},{24,16},{32,40},{40,32},{48,56},{56,48},{64,72... | collective-permute-start | bytes 983048 | tf_op jit(solution)/shard_map/ppermute | solution.py:400
  84.0 5.7 %collective-permute-start.9 = (bf16[512,128]{1,0:T(8,128)(2,1)S(1)}, bf16[512,128]{1,0:T(8,128)(2,1)S(1)}, u32[]{:S(2)}, u32[]{:S(2)}) collective-permute-start(bf16[512,128]{1,0:T(8,128)(2,1)S(1)} %left_columns.1), channel_id=1, source_target_pairs={{0,1},{8,9},{16,17},{24,25},{33,32},{41,40},{49,48},{57,56},{66,67... | collective-permute-start | bytes 393224 | tf_op jit(solution)/shard_map/ppermute | solution.py:524
  87.2 10.2 %collective-permute-start.5 = (bf16[8,160,128]{2,1,0:T(8,128)(2,1)S(1)}, bf16[8,160,128]{2,1,0:T(8,128)(2,1)S(1)}, u32[]{:S(2)}, u32[]{:S(2)}) collective-permute-start(bf16[8,160,128]{2,1,0:T(8,128)(2,1)S(1)} %all-to-all-done.1.mine), channel_id=1, source_target_pairs={{0,128},{8,136},{16,144},{24,152},{32,160},{40,168},{48,176},{56,1... | collective-permute-start | bytes 983048 | tf_op jit(solution)/shard_map/ppermute | solution.py:403
  89.7 9.3 %collective-permute-start.10 = (bf16[512,128]{1,0:T(8,128)(2,1)S(1)}, bf16[512,128]{1,0:T(8,128)(2,1)S(1)}, u32[]{:S(2)}, u32[]{:S(2)}) collective-permute-start(bf16[512,128]{1,0:T(8,128)(2,1)S(1)} %broadcast_select_fusion), channel_id=1, source_target_pairs={{0,2},{1,3},{8,10},{9,11},{16,18},{17,19},{24,26},{25,27},{33,35},... | collective-permute-start | bytes 393224 | tf_op jit(solution)/shard_map/ppermute | solution.py:533
  91.0 8.0 %collective-permute-start.11 = (bf16[512,128]{1,0:T(8,128)(2,1)S(1)}, bf16[512,128]{1,0:T(8,128)(2,1)S(1)}, u32[]{:S(2)}, u32[]{:S(2)}) collective-permute-start(bf16[512,128]{1,0:T(8,128)(2,1)S(1)} %broadcast_select_fusion), channel_id=1, source_target_pairs={{0,4},{1,5},{8,12},{9,13},{16,20},{17,21},{24,28},{25,29},{33,37},... | collective-permute-start | bytes 393224 | tf_op jit(solution)/shard_map/ppermute | solution.py:533
  95.3 3.7 %collective-permute-start.12 = (bf16[512,128]{1,0:T(8,128)(2,1)S(1)}, bf16[512,128]{1,0:T(8,128)(2,1)S(1)}, u32[]{:S(2)}, u32[]{:S(2)}) collective-permute-start(bf16[512,128]{1,0:T(8,128)(2,1)S(1)} %broadcast_select_fusion), channel_id=1, source_target_pairs={{0,6},{1,7},{8,14},{9,15},{16,22},{17,23},{24,30},{25,31},{33,39},... | collective-permute-start | bytes 393224 | tf_op jit(solution)/shard_map/ppermute | solution.py:533
  97.4 2.8 %collective-permute-start.6 = (bf16[8,160,128]{2,1,0:T(8,128)(2,1)S(1)}, bf16[8,160,128]{2,1,0:T(8,128)(2,1)S(1)}, u32[]{:S(2)}, u32[]{:S(2)}) collective-permute-start(bf16[8,160,128]{2,1,0:T(8,128)(2,1)S(1)} %collective-permute-done.5.far_mine), channel_id=1, source_target_pairs={{0,8},{8,0},{16,24},{24,16},{32,40},{40,32},{48,56},{56,48},{64,72... | collective-permute-start | bytes 983048 | tf_op jit(solution)/shard_map/ppermute | solution.py:400

commit v6 on v5

--- a/solution.py
+++ b/solution.py
@@ -38,6 +38,7 @@
         chips = lax.axis_size("dp") // 2
         self.core = member & 1
         self.plane = jnp.where(member >= chips, 1, 0)
+        self.ring = lax.shift_right_logical(member & (chips - 1), 1)
         self.place = member & (lax.axis_size("dp") // lax.axis_size("mp") - 1)
         self.flip = jnp.where(self.column >= lax.axis_size("mp") // 2, 1, 0)
         self.own_kind = self.plane ^ self.flip
@@ -55,7 +56,7 @@
             ]
 
 
-def pack_old(owners, factors, inverses, keep, send, held, packed, diag, arrived):
+def pack_old(owners, factors, inverses, unread, keep, send, held, packed, diag, arrived):
     facts = Facts(owners)
     core, flip = facts.core, facts.flip
     tiles = held.shape[1] // TILE
@@ -177,46 +178,61 @@
         ref[...] = total.astype(ref.dtype)
 
 
-def join_planes(owners, near, arrived, near_sum, arrived_sum, unread, out, untouched):
+def join_planes(owners, near, arrived, near_sum, arrived_sum, *outs):
     facts = Facts(owners)
     first, second = facts.same_plane
-    own_kind = facts.own_kind
+    flag = jnp.where(facts.own_kind == 0, first, second)
     ring, rows = near.shape[0], near.shape[1]
     data = rows // 6 * 5
-    flag = jnp.where(own_kind == 0, first, second)
-
-    @pl.when(flag == 1)
-    def _():
-        out[:, :data, :] = near[:, :data, :]
-
-    @pl.when(flag == 0)
-    def _():
-        out[:, :data, :] = arrived[:, :data, :]
-
     words = merge_words(first, second, near[0, data:, :], arrived[0, data:, :]).astype(BF16)
-    for z in range(ring):
-        out[z, data:rows, :] = words
-    out[:, rows:, :] = (near_sum[...] + arrived_sum[...].astype(F32)).astype(BF16)
-
-
-def make_shares(owners, arrived, shares, diag):
+    for step, out in enumerate(outs):
+        at = (facts.ring + step) & (ring - 1)
+
+        @pl.when(flag == 1)
+        def _():
+            out[:data, :] = near[at, :data, :]
+
+        @pl.when(flag == 0)
+        def _():
+            out[:data, :] = arrived[at, :data, :]
+
+        out[data:rows, :] = words
+        out[rows:, :] = (near_sum[at] + arrived_sum[at].astype(F32)).astype(BF16)
+
+
+def make_shares(owners, *refs):
+    pieces, shares, diag, arrived = refs[:-3], refs[-3], refs[-2], refs[-1]
     facts = Facts(owners)
-    own_kind = facts.own_kind
-    first, second = facts.ring_at
-    ring, rows = shares.shape[0], shares.shape[1]
+    ring, rows = len(pieces), shares.shape[0]
     share = rows // 2
     words = rows // 5 + rows
-    owner = jnp.where(own_kind == 0, first, second)
+    first, second = [(facts.ring - at) & (ring - 1) for at in facts.ring_at]
+    for step, piece in enumerate(pieces):
+        arrived[step] = piece[...]
+    owner = jnp.where(facts.own_kind == 0, first, second)
     both = merge_words(1, 0, arrived[first, rows:words, :], arrived[second, rows:words, :])
     diag[...] = both[: diag.shape[0]] + both[diag.shape[0] :]
-    summed = sum(arrived[z, words:, :].astype(F32) for z in range(ring))
+    summed = sum(piece[words:, :].astype(F32) for piece in pieces)
     total = sum(summed[share + 4 * d : share + 4 * d + 1, :] * float(8**d) for d in range(4))
     factor = DECAY * arrived[owner, :share, :].astype(F32) + (1.0 - DECAY) * summed[:share] / total
-    factor = factor.astype(BF16)
-    inverse = arrived[owner, share:rows, :]
-    for z in range(ring):
-        shares[z, :share, :] = factor
-        shares[z, share:, :] = inverse
+    shares[:share, :] = factor.astype(BF16)
+    shares[share:, :] = arrived[owner, share:rows, :]
+
+
+def collect(*refs):
+    for step, piece in enumerate(refs[:-1]):
+        refs[-1][step] = piece[...]
+
+
+def add_planes(near, arrived, *outs):
+    position = Facts().ring
+    for step, out in enumerate(outs):
+        at = (position + step) & (near.shape[0] - 1)
+        out[...] = (near[at] + arrived[at].astype(F32)).astype(out.dtype)
+
+
+def add_ring(*refs):
+    refs[-1][...] = sum(piece[...].astype(F32) for piece in refs[:-1]).astype(BF16)
 
 
 def gradient_tiles(turned, tiles):
@@ -232,7 +248,8 @@
 
 
 def gradient_add(scalars, turned, *refs):
-    tiles, received, out = refs[:4], refs[4], refs[-1]
+    tiles, received = refs[:4], refs[4]
+    out = refs[5 + (len(refs) - 6) // 2]
     product = gradient_tiles(turned, tiles)
     for n in range(4):
         total = product[:, n * TILE : (n + 1) * TILE] + received[n].astype(F32)
@@ -241,12 +258,14 @@
 
 def unpack(mine, other, core, packed):
     share = mine.shape[1] // 2
-    for pair in range(mine.shape[0]):
+    position = Facts().ring
+    for step in range(mine.shape[0]):
+        pair = (position - step) & (mine.shape[0] - 1)
         for ref, parity in ((mine, core), (other, 1 - core)):
             start = pl.multiple_of((2 * pair + parity) * share, ROWS)
             for which in range(2):
                 packed[which, pl.ds(start, share), :] = ref[
-                    pair, which * share : (which + 1) * share, :
+                    step, which * share : (which + 1) * share, :
                 ]
 
 
@@ -393,8 +412,11 @@
     shape = jax.ShapeDtypeStruct
     megabyte = 2 * width * width * 2
 
-    def across_ring(parts):
-        return lax.all_to_all(parts, "dp", 0, 0, tiled=True, axis_index_groups=rings)
+    def along_ring(piece, step):
+        return lax.ppermute(piece, "dp", [(i, j) for r in rings for i, j in zip(r, r[step:] + r[:step])])
+
+    def around(pieces):
+        return [p if step == 0 else along_ring(p, step) for step, p in enumerate(pieces)]
 
     def swap_cores(send):
         return lax.ppermute(send, "dp", core_swap)
@@ -402,27 +424,8 @@
     def swap_planes(send):
         return lax.ppermute(send, "dp", plane_swap)
 
-    message = shape((chips, 2 * share + 8 * lanes, TILE), BF16)
-    keep, send = kernel_call(
-        pack_old,
-        (message, message),
-        [SCALARS, ANYWHERE, ANYWHERE],
-        [
-            pltpu.VMEM((4, width, width), F32),
-            pltpu.VMEM((2, 2, packed_rows, TILE), BF16),
-            pltpu.VMEM((4 * lanes, TILE), F32),
-            pltpu.SemaphoreType.DMA((4,)),
-        ],
-        moved=6 * megabyte,
-    )(old_owner, factor_old[0, 0], inverse_old[0, 0])
-    half_message = shape((ring,) + message.shape[1:], BF16)
-    near_old, far_old = kernel_call(
-        choose_core, (half_message, half_message), [SCALARS, WHOLE, WHOLE], moved=megabyte
-    )(old_owner, keep, swap_cores(send))
-    arrived_old = swap_planes(far_old)
-
     message = shape((chips, share + ROWS, TILE), BF16)
-    keep, send, turned = kernel_call(
+    cov_keep, cov_send, turned = kernel_call(
         covariance_parts,
         (message, message, shape((width, tok_rows), BF16)),
         [SCALARS, ANYWHERE, ANYWHERE],
@@ -437,12 +440,31 @@
         moved=6 * megabyte,
     )(counts, features, out_grads)
     half_shape = (ring,) + message.shape[1:]
+    message = shape((chips, 2 * share + 8 * lanes, TILE), BF16)
+    keep, send = kernel_call(
+        pack_old,
+        (message, message),
+        [SCALARS, ANYWHERE, ANYWHERE, ANYWHERE],
+        [
+            pltpu.VMEM((4, width, width), F32),
+            pltpu.VMEM((2, 2, packed_rows, TILE), BF16),
+            pltpu.VMEM((4 * lanes, TILE), F32),
+            pltpu.SemaphoreType.DMA((4,)),
+        ],
+        moved=6 * megabyte,
+    )(old_owner, factor_old[0, 0], inverse_old[0, 0], turned)
+    half_message = shape((ring,) + message.shape[1:], BF16)
+    near_old, far_old = kernel_call(
+        choose_core, (half_message, half_message), [SCALARS, WHOLE, WHOLE], moved=megabyte
+    )(old_owner, keep, swap_cores(send))
+    arrived_old = swap_planes(far_old)
+
     near_sum, far_sum = kernel_call(
         add_core, (shape(half_shape, F32), shape(half_shape, BF16)), [WHOLE, WHOLE], moved=megabyte
-    )(keep, swap_cores(send))
+    )(cov_keep, swap_cores(cov_send))
     arrived_sum = swap_planes(far_sum)
 
-    def gradient(body, tile_at, count, dtype, name, *others):
+    def gradient(body, tile_at, count, dtype, name, others, passed=()):
         def tile_spec(n):
             return pl.BlockSpec((tok_rows, TILE), lambda i, s: (0, 2 * tile_at(4 * i + n, s) + s[0]))
 
@@ -452,15 +474,17 @@
         parity = 1 - core if len(others) == 2 else core
         return pl.pallas_call(
             body,
-            out_shape=shape((count, width, TILE), dtype),
+            out_shape=(shape((count, width, TILE), dtype),) + tuple(shape(p.shape, p.dtype) for p in passed),
             grid_spec=pltpu.PrefetchScalarGridSpec(
                 num_scalar_prefetch=1,
                 grid=(count // 4,),
                 in_specs=[pl.BlockSpec((width, tok_rows), lambda i, s: (0, 0))]
                 + [tile_spec(n) for n in range(4)]
-                + other_specs,
-                out_specs=message_spec,
+                + other_specs
+                + [ANYWHERE] * len(passed),
+                out_specs=(message_spec,) + (ANYWHERE,) * len(passed),
             ),
+            input_output_aliases={6 + len(others) + n: 1 + n for n in range(len(passed))},
             compiler_params=PARAMS,
             cost_estimate=pl.CostEstimate(
                 flops=2 * tok_rows * width * TILE * count,
@@ -470,38 +494,44 @@
             name=name,
         )(
             jnp.stack([parity, jnp.where(member >= chips, 1, 0)]),
-            turned, features, features, features, features, *others,
+            turned, features, features, features, features, *others, *passed,
         )
 
-    send = gradient(gradient_send, lambda q, s: q, chips, BF16, "gradient_send", far_old, far_sum)
-    joined, send = kernel_call(
+    (send,) = gradient(
+        gradient_send, lambda q, s: q, chips, BF16, "gradient_send", (far_old, far_sum)
+    )
+    received = swap_cores(send)
+    joined = kernel_call(
         join_planes,
-        (
-            shape((ring, near_old.shape[1] + near_sum.shape[1], TILE), BF16),
-            shape(send.shape, send.dtype),
-        ),
-        [SCALARS] + [WHOLE] * 4 + [ANYWHERE],
-        out_specs=(WHOLE, ANYWHERE),
-        aliases={5: 1},
+        (shape((near_old.shape[1] + near_sum.shape[1], TILE), BF16),) * ring,
+        [SCALARS] + [WHOLE] * 4,
         moved=megabyte,
-    )(old_owner, near_old, arrived_old, near_sum, arrived_sum, send)
-    received = swap_cores(send)
-    far_grad = gradient(
-        gradient_add, lambda q, s: (1 - s[1]) * ring + q, ring, BF16, "gradient_far", received
+    )(old_owner, near_old, arrived_old, near_sum, arrived_sum)
+    far_grad, *joined = gradient(
+        gradient_add,
+        lambda q, s: (1 - s[1]) * ring + q,
+        ring,
+        BF16,
+        "gradient_far",
+        (received,),
+        joined,
     )
     arrived_grad = swap_planes(far_grad)
-    near_grad = gradient(
-        gradient_add, lambda q, s: s[1] * ring + q, ring, F32, "gradient_near", received
+    (near_grad,) = gradient(
+        gradient_add, lambda q, s: s[1] * ring + q, ring, F32, "gradient_near", (received,)
     )
 
     shares, diag = kernel_call(
         make_shares,
-        (shape((ring, 2 * share, TILE), BF16), shape((4 * lanes, TILE), F32)),
-        [SCALARS, WHOLE],
+        (shape((2 * share, TILE), BF16), shape((4 * lanes, TILE), F32)),
+        [SCALARS] + [WHOLE] * ring,
+        [pltpu.VMEM((ring,) + joined[0].shape, BF16)],
         moved=megabyte,
-    )(old_owner, across_ring(joined))
-
-    mine = across_ring(shares)
+    )(old_owner, *around(joined))
+
+    mine = kernel_call(
+        collect, shape((ring, 2 * share, TILE), BF16), [WHOLE] * ring, moved=megabyte
+    )(*around([shares] * ring))
     other = swap_cores(mine)
     far_mine = swap_planes(mine)
     far_other = swap_cores(far_mine)
@@ -552,8 +582,15 @@
         moved=6 * megabyte,
     )(new_owner, mine, other, far_mine, far_other, diag)
 
-    grad = across_ring((near_grad + arrived_grad.astype(F32)).astype(BF16))
-    grad = jnp.sum(grad.astype(F32), axis=0).astype(BF16)
+    parts = kernel_call(
+        add_planes,
+        tuple(shape((width, TILE), BF16 if step else F32) for step in range(ring)),
+        [WHOLE] * 2,
+        moved=4 * megabyte,
+    )(near_grad, arrived_grad)
+    grad = kernel_call(
+        add_ring, shape((width, TILE), BF16), [WHOLE] * ring, moved=megabyte
+    )(*around(parts))
     neighbours = [[holders * c + r for r in range(holders)] for c in range(columns)]
     grads = lax.all_gather(grad, "dp", axis=0, axis_index_groups=neighbours)
     result, curvature = kernel_call(

time: 145 us -> 182 us (1.26)
  starting transfers between devices: 36.9 us -> 60.3 us
  waiting for transfers between devices: 37.9 us -> 51.4 us
  Pallas kernels: 26.5 us -> 30.5 us
  local copies, waits for them, and re-layouts: 6.08 us -> 3.98 us
    ppermute x0 -> x21, starting transfers between devices: none -> 35.8 us  [along_ring(): lax.ppermute(piece, 'dp', [(i, j) for r in rings for i, j in zip(r, r[ste...]
    ppermute x0 -> x21, waiting for transfers between devices: none -> 30.2 us  [along_ring(): lax.ppermute(piece, 'dp', [(i, j) for r in rings for i, j in zip(r, r[ste...]
    all_to_all x3 -> x0, waiting for transfers between devices: 24 us -> none  [across_ring(): lax.all_to_all(parts, 'dp', 0, 0, tiled=True, axis_index_groups=rings)]
    all_to_all x3 -> x0, starting transfers between devices: 13.4 us -> none  [across_ring(): lax.all_to_all(parts, 'dp', 0, 0, tiled=True, axis_index_groups=rings)]
    ppermute x4, waiting for transfers between devices: 9.49 us -> 17.5 us  [swap_planes(): return lax.ppermute(send, 'dp', plane_swap)]
    all_to_all x1, blocking collectives: 12.7 us -> 9.18 us  [local(): lax.all_to_all(jnp.broadcast_to(curvature, (2 * columns, 8, TILE)), ('dp'...]
    convert_element_type x1 -> x0, other arithmetic: 2.4 us -> none  [local(): grad = across_ring((near_grad + arrived_grad.astype(F32)).astype(BF16))]
    pallas_call x6 -> x9, Pallas kernels: 16.8 us -> 19.1 us  [the longest x3 12.7 us: gradient(): pl.pallas_call(body, out_shape=(shape((count, width, TILE), dtype),) + tu...]
  transfers between devices with their start and end apart: 16 -> 34, of which waited for: 9 -> 15; matrix products, arithmetic and copies ran while one was open for 2% -> 2% of each run, Pallas kernels for 16% -> 7%
where the time goes in v6:
time: 182 us; the launch traced here: 181 us
  starting transfers between devices  60.3 us (33%)
  waiting for transfers between devices  51.4 us (28%)
  Pallas kernels  30.5 us (17%)
  blocking collectives  29.4 us (16%)
  local copies, waits for them, and re-layouts  3.98 us (2%)
  other arithmetic  3.61 us (2%)
  between operations  2.22 us (1%)
    ppermute x21, starting transfers between devices, along_ring(): lax.ppermute(piece, 'dp', [(i, j) for r in rings for i, j in zip(r, r[ste...  35.8 us
    ppermute x21, waiting for transfers between devices, along_ring(): lax.ppermute(piece, 'dp', [(i, j) for r in rings for i, j in zip(r, r[ste...  30.2 us
    ppermute x4, waiting for transfers between devices, swap_planes(): return lax.ppermute(send, 'dp', plane_swap)  17.5 us
    all_to_all x1, blocking collectives, local(): lax.all_to_all(jnp.broadcast_to(curvature, (chips, 8, TILE)), 'dp', 0, 0,...  13 us
    pallas_call x3, Pallas kernels, gradient(): pl.pallas_call(body, out_shape=(shape((count, width, TILE), dtype),) + tu...  12.7 us
    all_to_all x1, blocking collectives, local(): lax.all_to_all(jnp.broadcast_to(curvature, (2 * columns, 8, TILE)), ('dp'...  9.18 us
    ppermute x3, starting transfers between devices, local(): lax.ppermute(left, ('dp', 'mp'), [(i * columns + g, i * columns + (g + 2...  8.37 us
    ppermute x5, starting transfers between devices, swap_cores(): return lax.ppermute(send, 'dp', core_swap)  7.32 us
  transfers between devices with their start and end apart: 34, of which 15 were waited for; matrix products, arithmetic and copies ran while one was open for 2% of the time, Pallas kernels for 7%

profile of v6, /device:TPU:1, one launch (start us, length us, event | category | flops | bytes accessed | tf_op | source)
XLA Modules:
  0.0 181.4 jit_solution(12204285923220870543)
XLA Ops:
  2.0 1.2 copy-done.1
  3.3 3.8 %covariance_parts.1 = (bf16[16,96,128]{2,1,0:T(8,128)(2,1)S(1)}, bf16[16,96,128]{2,1,0:T(8,128)(2,1)}, bf16[512,1024]{1,0:T(8,128)(2,1)S(1)}) custom-call(s32[1]{0:T(128)S(6)} %copy.36.counts, bf16[1024,4096]{1,0:T(8,128)(2,1)} %refs_3_.5, bf16[1024,512]{1,0:T(8,128)(2,1)S(1)} %copy-done.1), custom_call_target="tpu_custom_call" | custom-call | flops 1073741824 | bytes 6291456 | tf_op jit(solution)/shard_map/covariance_parts/pallas_call | solution.py:428
  7.0 3.4 %pack_old.1 = (bf16[16,192,128]{2,1,0:T(8,128)(2,1)S(1)}, bf16[16,192,128]{2,1,0:T(8,128)(2,1)}) custom-call(s32[8,2]{1,0:T(8,128)S(1)} %copy.26.owners, f32[2,512,512]{2,1,0:T(8,128)S(1)} %bitcast.10, f32[2,512,512]{2,1,0:T(8,128)} %bitcast.11, bf16[512,1024]{1,0:T(8,128)(2,1)S(1)} %get-tuple-element.44.unread.turned), custom_call_target="tpu_custom_call" | custom-call | bytes 6291456 | tf_op jit(solution)/shard_map/pack_old/pallas_call | solution.py:444
  10.4 3.3 %collective-permute-start = (bf16[16,192,128]{2,1,0:T(8,128)(2,1)}, bf16[16,192,128]{2,1,0:T(8,128)(2,1)S(1)}, u32[]{:S(2)}, u32[]{:S(2)}) collective-permute-start(bf16[16,192,128]{2,1,0:T(8,128)(2,1)} %get-tuple-element.46), channel_id=1, source_target_pairs={{0,8},{8,0},{16,24},{24,16},{32,40},{40,32},{48,56},{56,48},{64,72... | collective-permute-start | bytes 2359304 | tf_op jit(solution)/shard_map/ppermute | solution.py:422
  13.9 2.5 %collective-permute-done.1.received = bf16[16,96,128]{2,1,0:T(8,128)(2,1)S(1)} collective-permute-done((bf16[16,96,128]{2,1,0:T(8,128)(2,1)}, bf16[16,96,128]{2,1,0:T(8,128)(2,1)S(1)}, u32[]{:S(2)}, u32[]{:S(2)}) %collective-permute-start.1) | collective-permute-done | bytes 393248 | tf_op jit(solution)/shard_map/ppermute | solution.py:422
  17.3 5.3 %gradient_send.1 = bf16[16,512,128]{2,1,0:T(8,128)(2,1)S(1)} custom-call(s32[2]{0:T(128)S(1)} %pad_add_fusion.1.scalars, bf16[512,1024]{1,0:T(8,128)(2,1)S(1)} %get-tuple-element.44.unread.turned, bf16[1024,4096]{1,0:T(8,128)(2,1)} %refs_3_.5, bf16[1024,4096]{1,0:T(8,128)(2,1)} %refs_3_.5, bf16[1024,4096]{1,0:T(8,128)(2,1)} %refs_3_.5, ...), custom_call_target="tpu_custom_call" | custom-call | flops 2147483648 | bytes 8388608 | tf_op jit(solution)/shard_map/gradient_send/pallas_call | solution.py:475
  23.0 1.2 collective-permute-start.3
  24.2 1.8 collective-permute-start.4
  26.1 13.3 %collective-permute-done.4.arrived_sum = bf16[8,96,128]{2,1,0:T(8,128)(2,1)S(1)} collective-permute-done((bf16[8,96,128]{2,1,0:T(8,128)(2,1)S(1)}, bf16[8,96,128]{2,1,0:T(8,128)(2,1)S(1)}, u32[]{:S(2)}, u32[]{:S(2)}) %collective-permute-start.4) | collective-permute-done | bytes 196640 | tf_op jit(solution)/shard_map/ppermute | solution.py:425
  40.1 4.1 %gradient_far.1 = (bf16[8,512,128]{2,1,0:T(8,128)(2,1)}, bf16[288,128]{1,0:T(8,128)(2,1)S(1)}, bf16[288,128]{1,0:T(8,128)(2,1)S(1)}, bf16[288,128]{1,0:T(8,128)(...) custom-call(s32[2]{0:T(128)S(1)} %pad_add_fusion.scalars, ...), custom_call_target="tpu_custom_call", output_to_operand_aliasing={{1}: (7, {}), {2}: (8, {}), {3}: (9, {}), {4}: (10, {}), {5... | custom-call | flops 1073741824 | bytes 4194304 | tf_op jit(solution)/shard_map/gradient_far/pallas_call | solution.py:475
  44.2 2.9 %collective-permute-start.6 = (bf16[288,128]{1,0:T(8,128)(2,1)S(1)}, bf16[288,128]{1,0:T(8,128)(2,1)S(1)}, u32[]{:S(2)}, u32[]{:S(2)}) collective-permute-start(bf16[288,128]{1,0:T(8,128)(2,1)S(1)} %get-tuple-element.63), channel_id=1, source_target_pairs={{0,32},{16,48},{32,64},{48,80},{64,96},{80,112},{96,0},{112,16},{8... | collective-permute-start | bytes 221192 | tf_op jit(solution)/shard_map/ppermute | solution.py:416
  47.1 3.8 %collective-permute-start.7 = (bf16[288,128]{1,0:T(8,128)(2,1)S(1)}, bf16[288,128]{1,0:T(8,128)(2,1)S(1)}, u32[]{:S(2)}, u32[]{:S(2)}) collective-permute-start(bf16[288,128]{1,0:T(8,128)(2,1)S(1)} %get-tuple-element.64), channel_id=1, source_target_pairs={{0,48},{16,64},{32,80},{48,96},{64,112},{80,0},{96,16},{112,32},{8... | collective-permute-start | bytes 221192 | tf_op jit(solution)/shard_map/ppermute | solution.py:416
  50.8 2.9 %collective-permute-start.22 = (bf16[8,512,128]{2,1,0:T(8,128)(2,1)}, bf16[8,512,128]{2,1,0:T(8,128)(2,1)}, u32[]{:S(2)}, u32[]{:S(2)}) collective-permute-start(bf16[8,512,128]{2,1,0:T(8,128)(2,1)} %get-tuple-element.73), channel_id=1, source_target_pairs={{0,128},{8,136},{16,144},{24,152},{32,160},{40,168},{48,176},{56,1... | collective-permute-start | bytes 3145736 | tf_op jit(solution)/shard_map/ppermute | solution.py:425
  54.2 4.5 %collective-permute-start.9 = (bf16[288,128]{1,0:T(8,128)(2,1)S(1)}, bf16[288,128]{1,0:T(8,128)(2,1)S(1)}, u32[]{:S(2)}, u32[]{:S(2)}) collective-permute-start(bf16[288,128]{1,0:T(8,128)(2,1)S(1)} %get-tuple-element.66), channel_id=1, source_target_pairs={{0,80},{16,96},{32,112},{48,0},{64,16},{80,32},{96,48},{112,64},{8... | collective-permute-start | bytes 221192 | tf_op jit(solution)/shard_map/ppermute | solution.py:416
  58.7 2.4 %collective-permute-start.10 = (bf16[288,128]{1,0:T(8,128)(2,1)S(1)}, bf16[288,128]{1,0:T(8,128)(2,1)S(1)}, u32[]{:S(2)}, u32[]{:S(2)}) collective-permute-start(bf16[288,128]{1,0:T(8,128)(2,1)S(1)} %get-tuple-element.67), channel_id=1, source_target_pairs={{0,96},{16,112},{32,0},{48,16},{64,32},{80,48},{96,64},{112,80},{8... | collective-permute-start | bytes 221192 | tf_op jit(solution)/shard_map/ppermute | solution.py:416
  61.8 1.3 collective-permute-done.9.refs_5_
  63.1 7.0 %collective-permute-done.10.refs_6_ = bf16[288,128]{1,0:T(8,128)(2,1)S(1)} collective-permute-done((bf16[288,128]{1,0:T(8,128)(2,1)S(1)}, bf16[288,128]{1,0:T(8,128)(2,1)S(1)}, u32[]{:S(2)}, u32[]{:S(2)}) %collective-permute-start.10) | collective-permute-done | bytes 73760 | tf_op jit(solution)/shard_map/ppermute | solution.py:416
  71.3 2.7 %collective-permute-start.18 = (bf16[160,128]{1,0:T(8,128)(2,1)S(1)}, bf16[160,128]{1,0:T(8,128)(2,1)S(1)}, u32[]{:S(2)}, u32[]{:S(2)}) collective-permute-start(bf16[160,128]{1,0:T(8,128)(2,1)S(1)} %get-tuple-element.69.refs_0_), channel_id=1, source_target_pairs={{0,112},{16,0},{32,16},{48,32},{64,48},{80,64},{96,80},{112,96},{8... | collective-permute-start | bytes 122888 | tf_op jit(solution)/shard_map/ppermute | solution.py:416
  74.0 2.3 %collective-permute-start.16 = (bf16[160,128]{1,0:T(8,128)(2,1)S(1)}, bf16[160,128]{1,0:T(8,128)(2,1)S(1)}, u32[]{:S(2)}, u32[]{:S(2)}) collective-permute-start(bf16[160,128]{1,0:T(8,128)(2,1)S(1)} %get-tuple-element.69.refs_0_), channel_id=1, source_target_pairs={{0,80},{16,96},{32,112},{48,0},{64,16},{80,32},{96,48},{112,64},{8... | collective-permute-start | bytes 122888 | tf_op jit(solution)/shard_map/ppermute | solution.py:416
  76.3 3.2 %collective-permute-start.15 = (bf16[160,128]{1,0:T(8,128)(2,1)S(1)}, bf16[160,128]{1,0:T(8,128)(2,1)S(1)}, u32[]{:S(2)}, u32[]{:S(2)}) collective-permute-start(bf16[160,128]{1,0:T(8,128)(2,1)S(1)} %get-tuple-element.69.refs_0_), channel_id=1, source_target_pairs={{0,64},{16,80},{32,96},{48,112},{64,0},{80,16},{96,32},{112,48},{8... | collective-permute-start | bytes 122888 | tf_op jit(solution)/shard_map/ppermute | solution.py:416
  79.5 2.1 %collective-permute-start.14 = (bf16[160,128]{1,0:T(8,128)(2,1)S(1)}, bf16[160,128]{1,0:T(8,128)(2,1)S(1)}, u32[]{:S(2)}, u32[]{:S(2)}) collective-permute-start(bf16[160,128]{1,0:T(8,128)(2,1)S(1)} %get-tuple-element.69.refs_0_), channel_id=1, source_target_pairs={{0,48},{16,64},{32,80},{48,96},{64,112},{80,0},{96,16},{112,32},{8... | collective-permute-start | bytes 122888 | tf_op jit(solution)/shard_map/ppermute | solution.py:416
  81.6 0.8 collective-permute-start.13
  83.0 2.3 %collective-permute-done.14.refs_3_ = bf16[160,128]{1,0:T(8,128)(2,1)S(1)} collective-permute-done((bf16[160,128]{1,0:T(8,128)(2,1)S(1)}, bf16[160,128]{1,0:T(8,128)(2,1)S(1)}, u32[]{:S(2)}, u32[]{:S(2)}) %collective-permute-start.14) | collective-permute-done | bytes 40992 | tf_op jit(solution)/shard_map/ppermute | solution.py:416
  85.3 2.1 %collective-permute-done.13.refs_2_ = bf16[160,128]{1,0:T(8,128)(2,1)S(1)} collective-permute-done((bf16[160,128]{1,0:T(8,128)(2,1)S(1)}, bf16[160,128]{1,0:T(8,128)(2,1)S(1)}, u32[]{:S(2)}, u32[]{:S(2)}) %collective-permute-start.13) | collective-permute-done | bytes 40992 | tf_op jit(solution)/shard_map/ppermute | solution.py:416
  87.5 1.0 collective-permute-done.12.refs_1_
  88.5 2.6 %collective-permute-start.19 = (bf16[8,160,128]{2,1,0:T(8,128)(2,1)S(1)}, bf16[8,160,128]{2,1,0:T(8,128)(2,1)S(1)}, u32[]{:S(2)}, u32[]{:S(2)}) collective-permute-start(bf16[8,160,128]{2,1,0:T(8,128)(2,1)S(1)} %collect.1.mine), channel_id=1, source_target_pairs={{0,8},{8,0},{16,24},{24,16},{32,40},{40,32},{48,56},{56,48},{64,72... | collective-permute-start | bytes 983048 | tf_op jit(solution)/shard_map/ppermute | solution.py:422
  91.1 1.2 collective-permute-done.19.other
  92.3 1.7 left_columns.1
  94.7 2.9 %collective-permute-start.30 = (bf16[512,128]{1,0:T(8,128)(2,1)}, bf16[512,128]{1,0:T(8,128)(2,1)}, u32[]{:S(2)}, u32[]{:S(2)}) collective-permute-start(bf16[512,128]{1,0:T(8,128)(2,1)} %left_columns.1), channel_id=1, source_target_pairs={{0,1},{8,9},{16,17},{24,25},{33,32},{41,40},{49,48},{57,56},{66,67... | collective-permute-start | bytes 393224 | tf_op jit(solution)/shard_map/ppermute | solution.py:554
  97.7 4.3 %collective-permute-done.20.far_mine = bf16[8,160,128]{2,1,0:T(8,128)(2,1)} collective-permute-done((bf16[8,160,128]{2,1,0:T(8,128)(2,1)S(1)}, bf16[8,160,128]{2,1,0:T(8,128)(2,1)}, u32[]{:S(2)}, u32[]{:S(2)}) %collective-permute-start.20) | collective-permute-done | bytes 327712 | tf_op jit(solution)/shard_map/ppermute | solution.py:425
  101.9 0.9 collective-permute-start.21
  102.8 1.6 broadcast_select_fusion
  104.4 4.4 %collective-permute-start.33 = (bf16[512,128]{1,0:T(8,128)(2,1)}, bf16[512,128]{1,0:T(8,128)(2,1)S(1)}, u32[]{:S(2)}, u32[]{:S(2)}) collective-permute-start(bf16[512,128]{1,0:T(8,128)(2,1)} %broadcast_select_fusion), channel_id=1, source_target_pairs={{0,6},{1,7},{8,14},{9,15},{16,22},{17,23},{24,30},{25,31},{33,39},... | collective-permute-start | bytes 393224 | tf_op jit(solution)/shard_map/ppermute | solution.py:563
  108.8 2.1 %collective-permute-start.32 = (bf16[512,128]{1,0:T(8,128)(2,1)}, bf16[512,128]{1,0:T(8,128)(2,1)}, u32[]{:S(2)}, u32[]{:S(2)}) collective-permute-start(bf16[512,128]{1,0:T(8,128)(2,1)} %broadcast_select_fusion), channel_id=1, source_target_pairs={{0,4},{1,5},{8,12},{9,13},{16,20},{17,21},{24,28},{25,29},{33,37},... | collective-permute-start | bytes 393224 | tf_op jit(solution)/shard_map/ppermute | solution.py:563
  110.8 1.9 %collective-permute-start.31 = (bf16[512,128]{1,0:T(8,128)(2,1)}, bf16[512,128]{1,0:T(8,128)(2,1)}, u32[]{:S(2)}, u32[]{:S(2)}) collective-permute-start(bf16[512,128]{1,0:T(8,128)(2,1)} %broadcast_select_fusion), channel_id=1, source_target_pairs={{0,2},{1,3},{8,10},{9,11},{16,18},{17,19},{24,26},{25,27},{33,35},... | collective-permute-start | bytes 393224 | tf_op jit(solution)/shard_map/ppermute | solution.py:563
  112.8 3.3 %gradient_near.1.near = f32[8,512,128]{2,1,0:T(8,128)S(1)} custom-call(s32[2]{0:T(128)S(1)} %pad_add_fusion.scalars, bf16[512,1024]{1,0:T(8,128)(2,1)S(1)} %get-tuple-element.44.unread.turned, bf16[1024,4096]{1,0:T(8,128)(2,1)} %refs_3_.5, bf16[1024,4096]{1,0:T(8,128)(2,1)} %refs_3_.5, bf16[1024,4096]{1,0:T(8,128)(2,1)} %refs_3_.5, ...), custom_call_target="tpu_custom_call" | custom-call | flops 1073741824 | bytes 4194304 | tf_op jit(solution)/shard_map/gradient_near/pallas_call | solution.py:475
  116.1 1.4 add_planes.1
  119.8 4.6 %collective-permute-start.26 = (bf16[512,128]{1,0:T(8,128)(2,1)S(1)}, bf16[512,128]{1,0:T(8,128)(2,1)S(1)}, u32[]{:S(2)}, u32[]{:S(2)}) collective-permute-start(bf16[512,128]{1,0:T(8,128)(2,1)S(1)} %get-tuple-element.78), channel_id=1, source_target_pairs={{0,64},{16,80},{32,96},{48,112},{64,0},{80,16},{96,32},{112,48},{8... | collective-permute-start | bytes 393224 | tf_op jit(solution)/shard_map/ppermute | solution.py:416
  124.4 3.5 %collective-permute-start.28 = (bf16[512,128]{1,0:T(8,128)(2,1)S(1)}, bf16[512,128]{1,0:T(8,128)(2,1)S(1)}, u32[]{:S(2)}, u32[]{:S(2)}) collective-permute-start(bf16[512,128]{1,0:T(8,128)(2,1)S(1)} %get-tuple-element.80), channel_id=1, source_target_pairs={{0,96},{16,112},{32,0},{48,16},{64,32},{80,48},{96,64},{112,80},{8... | collective-permute-start | bytes 393224 | tf_op jit(solution)/shard_map/ppermute | solution.py:416
  127.9 4.6 %collective-permute-done.24.refs_2_ = bf16[512,128]{1,0:T(8,128)(2,1)S(1)} collective-permute-done((bf16[512,128]{1,0:T(8,128)(2,1)S(1)}, bf16[512,128]{1,0:T(8,128)(2,1)S(1)}, u32[]{:S(2)}, u32[]{:S(2)}) %collective-permute-start.24) | collective-permute-done | bytes 131104 | tf_op jit(solution)/shard_map/ppermute | solution.py:416
  132.5 1.1 add_select_fusion.left
  133.6 4.3 %new_blocks.1 = (bf16[512,512]{1,0:T(8,128)(2,1)S(1)}, f32[512,512]{1,0:T(8,128)}, f32[512,512]{1,0:T(8,128)}) custom-call(s32[8,2]{1,0:T(8,128)S(1)} %copy.27.owners, bf16[8,160,128]{2,1,0:T(8,128)(2,1)S(1)} %collect.1.mine, bf16[8,160,128]{2,1,0:T(8,128)(2,1)S(1)} %copy-done.3, bf16[8,160,128]{2,1,0:T(8,128)(2,1)} %collective-permute-done.20.far_mine, ...), custom_call_target="tpu_custom_call" | custom-call | flops 1073741824 | bytes 6291456 | tf_op jit(solution)/shard_map/new_blocks/pallas_call | solution.py:576
  138.3 6.4 %collective-permute-done.28.refs_6_ = bf16[512,128]{1,0:T(8,128)(2,1)S(1)} collective-permute-done((bf16[512,128]{1,0:T(8,128)(2,1)S(1)}, bf16[512,128]{1,0:T(8,128)(2,1)S(1)}, u32[]{:S(2)}, u32[]{:S(2)}) %collective-permute-start.28) | collective-permute-done | bytes 131104 | tf_op jit(solution)/shard_map/ppermute | solution.py:416
  144.8 4.2 %collective-permute-done.29.refs_7_ = bf16[512,128]{1,0:T(8,128)(2,1)S(1)} collective-permute-done((bf16[512,128]{1,0:T(8,128)(2,1)S(1)}, bf16[512,128]{1,0:T(8,128)(2,1)S(1)}, u32[]{:S(2)}, u32[]{:S(2)}) %collective-permute-start.29) | collective-permute-done | bytes 131104 | tf_op jit(solution)/shard_map/ppermute | solution.py:416
  149.2 7.3 %all-gather = bf16[2048,128]{1,0:T(8,128)(2,1)S(1)} all-gather(bf16[512,128]{1,0:T(8,128)(2,1)S(1)} %add_ring.1), channel_id=2, replica_groups={{0,8,16,24},{32,40,48,56},{64,72,80,88},{96,104,112,120},{128,136,144,1..., dimensions={0}, use_global_device_ids=true | all-gather | bytes 655360 | tf_op jit(solution)/shard_map/all_gather | solution.py:595
  156.5 0.8 precondition.1
  157.3 13.0 %all_to_all.10 = f32[16,8,128]{2,1,0:T(8,128)S(1)} all-to-all(f32[16,8,128]{2,1,0:T(8,128)S(1)} %broadcast_in_dim.14), channel_id=1, replica_groups={{0,8,16,24,32,40,48,56,64,72,80,88,96,104,112,120},{128,136,144,152,160..., dimensions={0} | all-to-all | bytes 131072 | tf_op jit(solution)/shard_map/all_to_all | solution.py:605
  170.3 9.2 %all_to_all.11 = f32[16,8,128]{2,1,0:T(8,128)S(1)} all-to-all(f32[16,8,128]{2,1,0:T(8,128)S(1)} %broadcast_in_dim.15), channel_id=1, replica_groups={{0,1,2,3,4,5,6,7,128,129,130,131,132,133,134,135},{8,9,10,11,12,13,14,1..., dimensions={0} | all-to-all | bytes 131072 | tf_op jit(solution)/shard_map/all_to_all | solution.py:613
  (62 shorter events, 10.9 us)
Async XLA Ops:
  2.0 1.2 copy-start.1
  3.3 3.8 %copy-start = (f32[1,1,2,512,512]{4,3,2,1,0:T(8,128)S(1)}, f32[1,1,2,512,512]{4,3,2,1,0:T(8,128)}, u32[]{:S(2)}) copy-start(f32[1,1,2,512,512]{4,3,2,1,0:T(8,128)} %param.10) | copy-start | bytes 6291460
  10.4 6.1 %collective-permute-start = (bf16[16,192,128]{2,1,0:T(8,128)(2,1)}, bf16[16,192,128]{2,1,0:T(8,128)(2,1)S(1)}, u32[]{:S(2)}, u32[]{:S(2)}) collective-permute-start(bf16[16,192,128]{2,1,0:T(8,128)(2,1)} %get-tuple-element.46), channel_id=1, source_target_pairs={{0,8},{8,0},{16,24},{24,16},{32,40},{40,32},{48,56},{56,48},{64,72... | collective-permute-start | bytes 2359304 | tf_op jit(solution)/shard_map/ppermute | solution.py:422
  13.8 2.7 %collective-permute-start.1 = (bf16[16,96,128]{2,1,0:T(8,128)(2,1)}, bf16[16,96,128]{2,1,0:T(8,128)(2,1)S(1)}, u32[]{:S(2)}, u32[]{:S(2)}) collective-permute-start(bf16[16,96,128]{2,1,0:T(8,128)(2,1)} %get-tuple-element.49), channel_id=1, source_target_pairs={{0,8},{8,0},{16,24},{24,16},{32,40},{40,32},{48,56},{56,48},{64,72... | collective-permute-start | bytes 1179656 | tf_op jit(solution)/shard_map/ppermute | solution.py:422
  22.6 17.5 %collective-permute-start.2 = (bf16[16,512,128]{2,1,0:T(8,128)(2,1)S(1)}, bf16[16,512,128]{2,1,0:T(8,128)(2,1)S(1)}, u32[]{:S(2)}, u32[]{:S(2)}) collective-permute-start(bf16[16,512,128]{2,1,0:T(8,128)(2,1)S(1)} %gradient_send.1), channel_id=1, source_target_pairs={{0,8},{8,0},{16,24},{24,16},{32,40},{40,32},{48,56},{56,48},{64,72... | collective-permute-start | bytes 6291464 | tf_op jit(solution)/shard_map/ppermute | solution.py:422
  23.0 16.3 %collective-permute-start.3 = (bf16[8,192,128]{2,1,0:T(8,128)(2,1)S(1)}, bf16[8,192,128]{2,1,0:T(8,128)(2,1)S(1)}, u32[]{:S(2)}, u32[]{:S(2)}) collective-permute-start(bf16[8,192,128]{2,1,0:T(8,128)(2,1)S(1)} %get-tuple-element.47.refs_4_), channel_id=1, source_target_pairs={{0,128},{8,136},{16,144},{24,152},{32,160},{40,168},{48,176},{56,1... | collective-permute-start | bytes 1179656 | tf_op jit(solution)/shard_map/ppermute | solution.py:425
  24.2 15.1 %collective-permute-start.4 = (bf16[8,96,128]{2,1,0:T(8,128)(2,1)S(1)}, bf16[8,96,128]{2,1,0:T(8,128)(2,1)S(1)}, u32[]{:S(2)}, u32[]{:S(2)}) collective-permute-start(bf16[8,96,128]{2,1,0:T(8,128)(2,1)S(1)} %get-tuple-element.50.refs_5_), channel_id=1, source_target_pairs={{0,128},{8,136},{16,144},{24,152},{32,160},{40,168},{48,176},{56,1... | collective-permute-start | bytes 589832 | tf_op jit(solution)/shard_map/ppermute | solution.py:425
  44.2 10.0 %collective-permute-start.5 = (bf16[288,128]{1,0:T(8,128)(2,1)S(1)}, bf16[288,128]{1,0:T(8,128)(2,1)S(1)}, u32[]{:S(2)}, u32[]{:S(2)}) collective-permute-start(bf16[288,128]{1,0:T(8,128)(2,1)S(1)} %get-tuple-element.62), channel_id=1, source_target_pairs={{0,16},{16,32},{32,48},{48,64},{64,80},{80,96},{96,112},{112,0},{8... | collective-permute-start | bytes 221192 | tf_op jit(solution)/shard_map/ppermute | solution.py:416
  44.2 14.5 %collective-permute-start.6 = (bf16[288,128]{1,0:T(8,128)(2,1)S(1)}, bf16[288,128]{1,0:T(8,128)(2,1)S(1)}, u32[]{:S(2)}, u32[]{:S(2)}) collective-permute-start(bf16[288,128]{1,0:T(8,128)(2,1)S(1)} %get-tuple-element.63), channel_id=1, source_target_pairs={{0,32},{16,48},{32,64},{48,80},{64,96},{80,112},{96,0},{112,16},{8... | collective-permute-start | bytes 221192 | tf_op jit(solution)/shard_map/ppermute | solution.py:416
  47.1 14.0 %collective-permute-start.7 = (bf16[288,128]{1,0:T(8,128)(2,1)S(1)}, bf16[288,128]{1,0:T(8,128)(2,1)S(1)}, u32[]{:S(2)}, u32[]{:S(2)}) collective-permute-start(bf16[288,128]{1,0:T(8,128)(2,1)S(1)} %get-tuple-element.64), channel_id=1, source_target_pairs={{0,48},{16,64},{32,80},{48,96},{64,112},{80,0},{96,16},{112,32},{8... | collective-permute-start | bytes 221192 | tf_op jit(solution)/shard_map/ppermute | solution.py:416
  50.8 65.3 %collective-permute-start.22 = (bf16[8,512,128]{2,1,0:T(8,128)(2,1)}, bf16[8,512,128]{2,1,0:T(8,128)(2,1)}, u32[]{:S(2)}, u32[]{:S(2)}) collective-permute-start(bf16[8,512,128]{2,1,0:T(8,128)(2,1)} %get-tuple-element.73), channel_id=1, source_target_pairs={{0,128},{8,136},{16,144},{24,152},{32,160},{40,168},{48,176},{56,1... | collective-permute-start | bytes 3145736 | tf_op jit(solution)/shard_map/ppermute | solution.py:425
  53.7 8.1 %collective-permute-start.8 = (bf16[288,128]{1,0:T(8,128)(2,1)S(1)}, bf16[288,128]{1,0:T(8,128)(2,1)S(1)}, u32[]{:S(2)}, u32[]{:S(2)}) collective-permute-start(bf16[288,128]{1,0:T(8,128)(2,1)S(1)} %get-tuple-element.65), channel_id=1, source_target_pairs={{0,64},{16,80},{32,96},{48,112},{64,0},{80,16},{96,32},{112,48},{8... | collective-permute-start | bytes 221192 | tf_op jit(solution)/shard_map/ppermute | solution.py:416
  54.2 8.9 %collective-permute-start.9 = (bf16[288,128]{1,0:T(8,128)(2,1)S(1)}, bf16[288,128]{1,0:T(8,128)(2,1)S(1)}, u32[]{:S(2)}, u32[]{:S(2)}) collective-permute-start(bf16[288,128]{1,0:T(8,128)(2,1)S(1)} %get-tuple-element.66), channel_id=1, source_target_pairs={{0,80},{16,96},{32,112},{48,0},{64,16},{80,32},{96,48},{112,64},{8... | collective-permute-start | bytes 221192 | tf_op jit(solution)/shard_map/ppermute | solution.py:416
  58.7 11.5 %collective-permute-start.10 = (bf16[288,128]{1,0:T(8,128)(2,1)S(1)}, bf16[288,128]{1,0:T(8,128)(2,1)S(1)}, u32[]{:S(2)}, u32[]{:S(2)}) collective-permute-start(bf16[288,128]{1,0:T(8,128)(2,1)S(1)} %get-tuple-element.67), channel_id=1, source_target_pairs={{0,96},{16,112},{32,0},{48,16},{64,32},{80,48},{96,64},{112,80},{8... | collective-permute-start | bytes 221192 | tf_op jit(solution)/shard_map/ppermute | solution.py:416
  61.1 9.5 %collective-permute-start.11 = (bf16[288,128]{1,0:T(8,128)(2,1)S(1)}, bf16[288,128]{1,0:T(8,128)(2,1)S(1)}, u32[]{:S(2)}, u32[]{:S(2)}) collective-permute-start(bf16[288,128]{1,0:T(8,128)(2,1)S(1)} %get-tuple-element.68), channel_id=1, source_target_pairs={{0,112},{16,0},{32,16},{48,32},{64,48},{80,64},{96,80},{112,96},{8... | collective-permute-start | bytes 221192 | tf_op jit(solution)/shard_map/ppermute | solution.py:416
  71.3 8.2 %collective-permute-start.18 = (bf16[160,128]{1,0:T(8,128)(2,1)S(1)}, bf16[160,128]{1,0:T(8,128)(2,1)S(1)}, u32[]{:S(2)}, u32[]{:S(2)}) collective-permute-start(bf16[160,128]{1,0:T(8,128)(2,1)S(1)} %get-tuple-element.69.refs_0_), channel_id=1, source_target_pairs={{0,112},{16,0},{32,16},{48,32},{64,48},{80,64},{96,80},{112,96},{8... | collective-permute-start | bytes 122888 | tf_op jit(solution)/shard_map/ppermute | solution.py:416
  74.0 7.6 %collective-permute-start.17 = (bf16[160,128]{1,0:T(8,128)(2,1)S(1)}, bf16[160,128]{1,0:T(8,128)(2,1)S(1)}, u32[]{:S(2)}, u32[]{:S(2)}) collective-permute-start(bf16[160,128]{1,0:T(8,128)(2,1)S(1)} %get-tuple-element.69.refs_0_), channel_id=1, source_target_pairs={{0,96},{16,112},{32,0},{48,16},{64,32},{80,48},{96,64},{112,80},{8... | collective-permute-start | bytes 122888 | tf_op jit(solution)/shard_map/ppermute | solution.py:416
  74.0 8.4 %collective-permute-start.16 = (bf16[160,128]{1,0:T(8,128)(2,1)S(1)}, bf16[160,128]{1,0:T(8,128)(2,1)S(1)}, u32[]{:S(2)}, u32[]{:S(2)}) collective-permute-start(bf16[160,128]{1,0:T(8,128)(2,1)S(1)} %get-tuple-element.69.refs_0_), channel_id=1, source_target_pairs={{0,80},{16,96},{32,112},{48,0},{64,16},{80,32},{96,48},{112,64},{8... | collective-permute-start | bytes 122888 | tf_op jit(solution)/shard_map/ppermute | solution.py:416
  76.3 6.8 %collective-permute-start.15 = (bf16[160,128]{1,0:T(8,128)(2,1)S(1)}, bf16[160,128]{1,0:T(8,128)(2,1)S(1)}, u32[]{:S(2)}, u32[]{:S(2)}) collective-permute-start(bf16[160,128]{1,0:T(8,128)(2,1)S(1)} %get-tuple-element.69.refs_0_), channel_id=1, source_target_pairs={{0,64},{16,80},{32,96},{48,112},{64,0},{80,16},{96,32},{112,48},{8... | collective-permute-start | bytes 122888 | tf_op jit(solution)/shard_map/ppermute | solution.py:416
  79.5 5.9 %collective-permute-start.14 = (bf16[160,128]{1,0:T(8,128)(2,1)S(1)}, bf16[160,128]{1,0:T(8,128)(2,1)S(1)}, u32[]{:S(2)}, u32[]{:S(2)}) collective-permute-start(bf16[160,128]{1,0:T(8,128)(2,1)S(1)} %get-tuple-element.69.refs_0_), channel_id=1, source_target_pairs={{0,48},{16,64},{32,80},{48,96},{64,112},{80,0},{96,16},{112,32},{8... | collective-permute-start | bytes 122888 | tf_op jit(solution)/shard_map/ppermute | solution.py:416
  81.6 5.9 %collective-permute-start.13 = (bf16[160,128]{1,0:T(8,128)(2,1)S(1)}, bf16[160,128]{1,0:T(8,128)(2,1)S(1)}, u32[]{:S(2)}, u32[]{:S(2)}) collective-permute-start(bf16[160,128]{1,0:T(8,128)(2,1)S(1)} %get-tuple-element.69.refs_0_), channel_id=1, source_target_pairs={{0,32},{16,48},{32,64},{48,80},{64,96},{80,112},{96,0},{112,16},{8... | collective-permute-start | bytes 122888 | tf_op jit(solution)/shard_map/ppermute | solution.py:416
  82.4 6.1 %collective-permute-start.12 = (bf16[160,128]{1,0:T(8,128)(2,1)S(1)}, bf16[160,128]{1,0:T(8,128)(2,1)S(1)}, u32[]{:S(2)}, u32[]{:S(2)}) collective-permute-start(bf16[160,128]{1,0:T(8,128)(2,1)S(1)} %get-tuple-element.69.refs_0_), channel_id=1, source_target_pairs={{0,16},{16,32},{32,48},{48,64},{64,80},{80,96},{96,112},{112,0},{8... | collective-permute-start | bytes 122888 | tf_op jit(solution)/shard_map/ppermute | solution.py:416
  88.5 3.8 %collective-permute-start.19 = (bf16[8,160,128]{2,1,0:T(8,128)(2,1)S(1)}, bf16[8,160,128]{2,1,0:T(8,128)(2,1)S(1)}, u32[]{:S(2)}, u32[]{:S(2)}) collective-permute-start(bf16[8,160,128]{2,1,0:T(8,128)(2,1)S(1)} %collect.1.mine), channel_id=1, source_target_pairs={{0,8},{8,0},{16,24},{24,16},{32,40},{40,32},{48,56},{56,48},{64,72... | collective-permute-start | bytes 983048 | tf_op jit(solution)/shard_map/ppermute | solution.py:422
  91.1 10.9 %collective-permute-start.20 = (bf16[8,160,128]{2,1,0:T(8,128)(2,1)S(1)}, bf16[8,160,128]{2,1,0:T(8,128)(2,1)}, u32[]{:S(2)}, u32[]{:S(2)}) collective-permute-start(bf16[8,160,128]{2,1,0:T(8,128)(2,1)S(1)} %collect.1.mine), channel_id=1, source_target_pairs={{0,128},{8,136},{16,144},{24,152},{32,160},{40,168},{48,176},{56,1... | collective-permute-start | bytes 983048 | tf_op jit(solution)/shard_map/ppermute | solution.py:425
  94.0 0.7 copy-start.2
  94.7 8.1 %collective-permute-start.30 = (bf16[512,128]{1,0:T(8,128)(2,1)}, bf16[512,128]{1,0:T(8,128)(2,1)}, u32[]{:S(2)}, u32[]{:S(2)}) collective-permute-start(bf16[512,128]{1,0:T(8,128)(2,1)} %left_columns.1), channel_id=1, source_target_pairs={{0,1},{8,9},{16,17},{24,25},{33,32},{41,40},{49,48},{57,56},{66,67... | collective-permute-start | bytes 393224 | tf_op jit(solution)/shard_map/ppermute | solution.py:554
  101.9 22.5 %collective-permute-start.21 = (bf16[8,160,128]{2,1,0:T(8,128)(2,1)}, bf16[8,160,128]{2,1,0:T(8,128)(2,1)}, u32[]{:S(2)}, u32[]{:S(2)}) collective-permute-start(bf16[8,160,128]{2,1,0:T(8,128)(2,1)} %collective-permute-done.20.far_mine), channel_id=1, source_target_pairs={{0,8},{8,0},{16,24},{24,16},{32,40},{40,32},{48,56},{56,48},{64,72... | collective-permute-start | bytes 983048 | tf_op jit(solution)/shard_map/ppermute | solution.py:422
  104.4 13.9 %collective-permute-start.33 = (bf16[512,128]{1,0:T(8,128)(2,1)}, bf16[512,128]{1,0:T(8,128)(2,1)S(1)}, u32[]{:S(2)}, u32[]{:S(2)}) collective-permute-start(bf16[512,128]{1,0:T(8,128)(2,1)} %broadcast_select_fusion), channel_id=1, source_target_pairs={{0,6},{1,7},{8,14},{9,15},{16,22},{17,23},{24,30},{25,31},{33,39},... | collective-permute-start | bytes 393224 | tf_op jit(solution)/shard_map/ppermute | solution.py:563
  108.8 11.0 %collective-permute-start.32 = (bf16[512,128]{1,0:T(8,128)(2,1)}, bf16[512,128]{1,0:T(8,128)(2,1)}, u32[]{:S(2)}, u32[]{:S(2)}) collective-permute-start(bf16[512,128]{1,0:T(8,128)(2,1)} %broadcast_select_fusion), channel_id=1, source_target_pairs={{0,4},{1,5},{8,12},{9,13},{16,20},{17,21},{24,28},{25,29},{33,37},... | collective-permute-start | bytes 393224 | tf_op jit(solution)/shard_map/ppermute | solution.py:563
  110.8 8.9 %collective-permute-start.31 = (bf16[512,128]{1,0:T(8,128)(2,1)}, bf16[512,128]{1,0:T(8,128)(2,1)}, u32[]{:S(2)}, u32[]{:S(2)}) collective-permute-start(bf16[512,128]{1,0:T(8,128)(2,1)} %broadcast_select_fusion), channel_id=1, source_target_pairs={{0,2},{1,3},{8,10},{9,11},{16,18},{17,19},{24,26},{25,27},{33,35},... | collective-permute-start | bytes 393224 | tf_op jit(solution)/shard_map/ppermute | solution.py:563
  116.1 3.6 %copy-start.5 = (s32[8,2]{0,1:T(2,128)S(1)}, s32[8,2]{0,1:T(2,128)}, u32[]{:S(2)}) copy-start(s32[8,2]{0,1:T(2,128)} %param.13) | copy-start | bytes 196
  116.1 17.5 %copy-start.3 = (bf16[8,160,128]{2,1,0:T(8,128)(2,1)S(1)}, bf16[8,160,128]{2,1,0:T(8,128)(2,1)}, u32[]{:S(2)}) copy-start(bf16[8,160,128]{2,1,0:T(8,128)(2,1)} %copy-done.2) | copy-start | bytes 983044
  117.6 6.9 %collective-permute-start.23 = (bf16[512,128]{1,0:T(8,128)(2,1)S(1)}, bf16[512,128]{1,0:T(8,128)(2,1)S(1)}, u32[]{:S(2)}, u32[]{:S(2)}) collective-permute-start(bf16[512,128]{1,0:T(8,128)(2,1)S(1)} %get-tuple-element.75), channel_id=1, source_target_pairs={{0,16},{16,32},{32,48},{48,64},{64,80},{80,96},{96,112},{112,0},{8... | collective-permute-start | bytes 393224 | tf_op jit(solution)/shard_map/ppermute | solution.py:416
  118.3 0.7 copy-start.4
  118.9 13.6 %collective-permute-start.24 = (bf16[512,128]{1,0:T(8,128)(2,1)S(1)}, bf16[512,128]{1,0:T(8,128)(2,1)S(1)}, u32[]{:S(2)}, u32[]{:S(2)}) collective-permute-start(bf16[512,128]{1,0:T(8,128)(2,1)S(1)} %get-tuple-element.76), channel_id=1, source_target_pairs={{0,32},{16,48},{32,64},{48,80},{64,96},{80,112},{96,0},{112,16},{8... | collective-permute-start | bytes 393224 | tf_op jit(solution)/shard_map/ppermute | solution.py:416
  119.8 18.2 %collective-permute-start.25 = (bf16[512,128]{1,0:T(8,128)(2,1)S(1)}, bf16[512,128]{1,0:T(8,128)(2,1)S(1)}, u32[]{:S(2)}, u32[]{:S(2)}) collective-permute-start(bf16[512,128]{1,0:T(8,128)(2,1)S(1)} %get-tuple-element.77), channel_id=1, source_target_pairs={{0,48},{16,64},{32,80},{48,96},{64,112},{80,0},{96,16},{112,32},{8... | collective-permute-start | bytes 393224 | tf_op jit(solution)/shard_map/ppermute | solution.py:416
  119.8 18.5 %collective-permute-start.26 = (bf16[512,128]{1,0:T(8,128)(2,1)S(1)}, bf16[512,128]{1,0:T(8,128)(2,1)S(1)}, u32[]{:S(2)}, u32[]{:S(2)}) collective-permute-start(bf16[512,128]{1,0:T(8,128)(2,1)S(1)} %get-tuple-element.78), channel_id=1, source_target_pairs={{0,64},{16,80},{32,96},{48,112},{64,0},{80,16},{96,32},{112,48},{8... | collective-permute-start | bytes 393224 | tf_op jit(solution)/shard_map/ppermute | solution.py:416
  124.4 13.9 %collective-permute-start.27 = (bf16[512,128]{1,0:T(8,128)(2,1)S(1)}, bf16[512,128]{1,0:T(8,128)(2,1)S(1)}, u32[]{:S(2)}, u32[]{:S(2)}) collective-permute-start(bf16[512,128]{1,0:T(8,128)(2,1)S(1)} %get-tuple-element.79), channel_id=1, source_target_pairs={{0,80},{16,96},{32,112},{48,0},{64,16},{80,32},{96,48},{112,64},{8... | collective-permute-start | bytes 393224 | tf_op jit(solution)/shard_map/ppermute | solution.py:416
  124.4 20.3 %collective-permute-start.28 = (bf16[512,128]{1,0:T(8,128)(2,1)S(1)}, bf16[512,128]{1,0:T(8,128)(2,1)S(1)}, u32[]{:S(2)}, u32[]{:S(2)}) collective-permute-start(bf16[512,128]{1,0:T(8,128)(2,1)S(1)} %get-tuple-element.80), channel_id=1, source_target_pairs={{0,96},{16,112},{32,0},{48,16},{64,32},{80,48},{96,64},{112,80},{8... | collective-permute-start | bytes 393224 | tf_op jit(solution)/shard_map/ppermute | solution.py:416
  132.5 16.5 %collective-permute-start.29 = (bf16[512,128]{1,0:T(8,128)(2,1)S(1)}, bf16[512,128]{1,0:T(8,128)(2,1)S(1)}, u32[]{:S(2)}, u32[]{:S(2)}) collective-permute-start(bf16[512,128]{1,0:T(8,128)(2,1)S(1)} %get-tuple-element.81), channel_id=1, source_target_pairs={{0,112},{16,0},{32,16},{48,32},{64,48},{80,64},{96,80},{112,96},{8... | collective-permute-start | bytes 393224 | tf_op jit(solution)/shard_map/ppermute | solution.py:416

commit v7 on v5

--- a/solution.py
+++ b/solution.py
@@ -55,61 +55,31 @@
             ]
 
 
-def pack_old(owners, factors, inverses, keep, send, held, packed, diag, arrived):
+def first_parts(
+    owners, counts, features, out_grads, factors, inverses,
+    keep, send, turned,
+    own, grads, kept, held, packed, diag, arrived,
+):
     facts = Facts(owners)
-    core, flip = facts.core, facts.flip
-    tiles = held.shape[1] // TILE
+    core, flip, count = facts.core, facts.flip, counts[0]
+    rows, width = own.shape
+    tiles = width // TILE
     on_diagonal = diagonal_mask()
+    start = pl.multiple_of(facts.column * width, width)
     loads = [
+        pltpu.make_async_copy(features.at[:, pl.ds(start, width)], own, arrived.at[0]),
+        pltpu.make_async_copy(out_grads, grads, arrived.at[1]),
+    ] + [
         pltpu.make_async_copy(
-            source.at[facts.shared if kind else 0], held.at[which * 2 + kind], arrived.at[which * 2 + kind]
+            source.at[facts.shared if kind else 0],
+            held.at[which * 2 + kind],
+            arrived.at[2 + which * 2 + kind],
         )
         for which, source in enumerate((factors, inverses))
         for kind in range(2)
     ]
     for load in loads:
         load.start()
-    for which in range(2):
-        for kind in range(2):
-            loads[which * 2 + kind].wait()
-            for n, (a, b) in enumerate(upper_pairs(tiles)):
-                piece = held[(which * 2 + kind,) + tile_of(a, b)]
-                if a == b:
-                    row = (which * 2 + kind) * tiles + a
-                    diag[row : row + 1, :] = jnp.sum(
-                        jnp.where(on_diagonal, piece, 0.0), axis=0, keepdims=True
-                    )
-                    piece = jnp.where(on_diagonal, 0.0, piece)
-                packed[kind, which, n * TILE : (n + 1) * TILE, :] = piece.astype(BF16)
-    high = diag[...].astype(BF16)
-    low = (diag[...] - high.astype(F32)).astype(BF16)
-    words = jnp.concatenate([high, low], axis=0)
-    chips = keep.shape[0]
-    share = (keep.shape[1] - words.shape[0]) // 2
-    for q in range(chips):
-        plane, pair = divmod(q, chips // 2)
-        kind = flip if plane == 0 else 1 - flip
-        for ref, parity in ((keep, core), (send, 1 - core)):
-            start = pl.multiple_of((2 * pair + parity) * share, ROWS)
-            for which in range(2):
-                ref[q, which * share : (which + 1) * share, :] = packed[
-                    kind, which, pl.ds(start, share), :
-                ]
-            ref[q, 2 * share :, :] = words
-
-
-def covariance_parts(counts, features, out_grads, keep, send, turned, own, grads, kept, packed, arrived):
-    facts = Facts()
-    core, flip, count = facts.core, facts.flip, counts[0]
-    rows, width = own.shape
-    start = pl.multiple_of(facts.column * width, width)
-    loads = [
-        pltpu.make_async_copy(features.at[:, pl.ds(start, width)], own, arrived.at[0]),
-        pltpu.make_async_copy(out_grads, grads, arrived.at[1]),
-    ]
-    for load in loads:
-        load.start()
-    tiles = width // TILE
     valid = lax.broadcasted_iota(jnp.int32, (rows, width), 0) < count
     for kind, (block, left) in enumerate(((own, kept), (grads, turned))):
         loads[kind].wait()
@@ -124,19 +94,37 @@
                 for j in range(2):
                     if 2 * a + i <= 2 * b + j:
                         at = upper_pairs(tiles).index((2 * a + i, 2 * b + j))
-                        packed[kind, at * TILE : (at + 1) * TILE, :] = square[tile_of(i, j)]
+                        packed[kind, 2, at * TILE : (at + 1) * TILE, :] = square[tile_of(i, j)]
+    for which in range(2):
+        for kind in range(2):
+            loads[2 + which * 2 + kind].wait()
+            for n, (a, b) in enumerate(upper_pairs(tiles)):
+                piece = held[(which * 2 + kind,) + tile_of(a, b)]
+                if a == b:
+                    row = (which * 2 + kind) * tiles + a
+                    diag[row : row + 1, :] = jnp.sum(
+                        jnp.where(on_diagonal, piece, 0.0), axis=0, keepdims=True
+                    )
+                    piece = jnp.where(on_diagonal, 0.0, piece)
+                packed[kind, which, n * TILE : (n + 1) * TILE, :] = piece.astype(BF16)
+    high = diag[...].astype(BF16)
+    low = (diag[...] - high.astype(F32)).astype(BF16)
+    words = jnp.concatenate([high, low], axis=0)
     quarter = lax.broadcasted_iota(jnp.int32, (ROWS, TILE), 0) // 4
     digits = lax.shift_right_logical(jnp.full((ROWS, TILE), count), 3 * quarter) & 7
     digits = digits.astype(F32).astype(BF16)
     chips = keep.shape[0]
-    share = keep.shape[1] - ROWS
+    share = (keep.shape[1] - words.shape[0] - ROWS) // 3
+    sums = 2 * share + words.shape[0]
     for q in range(chips):
         plane, pair = divmod(q, chips // 2)
         kind = flip if plane == 0 else 1 - flip
         for ref, parity in ((keep, core), (send, 1 - core)):
             start = pl.multiple_of((2 * pair + parity) * share, ROWS)
-            ref[q, :share, :] = packed[kind, pl.ds(start, share), :]
-            ref[q, share:, :] = digits
+            for which, at in enumerate((0, share, sums)):
+                ref[q, at : at + share, :] = packed[kind, which, pl.ds(start, share), :]
+            ref[q, 2 * share : sums, :] = words
+            ref[q, sums + share :, :] = digits
 
 
 def merge_words(first_flag, second_flag, one, two):
@@ -146,57 +134,55 @@
     return jnp.where(flags == 1, one.astype(F32), two.astype(F32))
 
 
-def choose_core(owners, keep, received, near, far):
+def choose_core(owners, keep, received, unread, near_old, near_sum, far):
     facts = Facts(owners)
     first, second = facts.same_core
-    plane, own_kind = facts.plane, facts.own_kind
-    ring, rows = near.shape[0], near.shape[1]
+    ring, rows = near_old.shape[0], near_old.shape[1]
     data = rows // 6 * 5
-    words = merge_words(first, second, keep[0, data:, :], received[0, data:, :]).astype(BF16)
-    for ref, at, kind in ((near, plane, own_kind), (far, 1 - plane, 1 - own_kind)):
+    words = merge_words(first, second, keep[0, data:rows, :], received[0, data:rows, :]).astype(BF16)
+    for old, at, kind in (
+        (near_old, facts.plane, facts.own_kind),
+        (far, 1 - facts.plane, 1 - facts.own_kind),
+    ):
         flag = jnp.where(kind == 0, first, second)
 
         @pl.when(flag == 1)
         def _():
-            ref[:, :data, :] = keep[pl.ds(at * ring, ring), :data, :]
+            old[:, :data, :] = keep[pl.ds(at * ring, ring), :data, :]
 
         @pl.when(flag == 0)
         def _():
-            ref[:, :data, :] = received[pl.ds(at * ring, ring), :data, :]
+            old[:, :data, :] = received[pl.ds(at * ring, ring), :data, :]
 
         for z in range(ring):
-            ref[z, data:, :] = words
-
-
-def add_core(keep, received, near, far):
-    plane = Facts().plane
-    ring = near.shape[0]
-    for ref, at in ((near, plane), (far, 1 - plane)):
+            old[z, data:rows, :] = words
         chips = pl.ds(at * ring, ring)
-        total = keep[chips].astype(F32) + received[chips].astype(F32)
-        ref[...] = total.astype(ref.dtype)
-
-
-def join_planes(owners, near, arrived, near_sum, arrived_sum, unread, out, untouched):
+        total = keep[chips, rows:, :].astype(F32) + received[chips, rows:, :].astype(F32)
+        if old is far:
+            far[:, rows:, :] = total.astype(BF16)
+        else:
+            near_sum[...] = total
+
+
+def join_planes(owners, near_old, near_sum, arrived, unread, other_unread, out):
     facts = Facts(owners)
     first, second = facts.same_plane
-    own_kind = facts.own_kind
-    ring, rows = near.shape[0], near.shape[1]
+    flag = jnp.where(facts.own_kind == 0, first, second)
+    ring, rows = near_old.shape[0], near_old.shape[1]
     data = rows // 6 * 5
-    flag = jnp.where(own_kind == 0, first, second)
 
     @pl.when(flag == 1)
     def _():
-        out[:, :data, :] = near[:, :data, :]
+        out[:, :data, :] = near_old[:, :data, :]
 
     @pl.when(flag == 0)
     def _():
         out[:, :data, :] = arrived[:, :data, :]
 
-    words = merge_words(first, second, near[0, data:, :], arrived[0, data:, :]).astype(BF16)
+    words = merge_words(first, second, near_old[0, data:, :], arrived[0, data:rows, :]).astype(BF16)
     for z in range(ring):
         out[z, data:rows, :] = words
-    out[:, rows:, :] = (near_sum[...] + arrived_sum[...].astype(F32)).astype(BF16)
+    out[:, rows:, :] = (near_sum[...] + arrived[:, rows:, :].astype(F32)).astype(BF16)
 
 
 def make_shares(owners, arrived, shares, diag):
@@ -225,15 +211,14 @@
 
 
 def gradient_send(scalars, turned, *refs):
-    tiles, send = refs[:4], refs[-1]
-    product = gradient_tiles(turned, tiles)
+    product = gradient_tiles(turned, refs[:4])
     for n in range(4):
-        send[n] = product[:, n * TILE : (n + 1) * TILE].astype(send.dtype)
+        refs[-1][n] = product[:, n * TILE : (n + 1) * TILE].astype(BF16)
 
 
 def gradient_add(scalars, turned, *refs):
-    tiles, received, out = refs[:4], refs[4], refs[-1]
-    product = gradient_tiles(turned, tiles)
+    received, out = refs[4], refs[-1]
+    product = gradient_tiles(turned, refs[:4])
     for n in range(4):
         total = product[:, n * TILE : (n + 1) * TILE] + received[n].astype(F32)
         out[n] = total.astype(out.dtype)
@@ -402,98 +387,76 @@
     def swap_planes(send):
         return lax.ppermute(send, "dp", plane_swap)
 
-    message = shape((chips, 2 * share + 8 * lanes, TILE), BF16)
-    keep, send = kernel_call(
-        pack_old,
-        (message, message),
-        [SCALARS, ANYWHERE, ANYWHERE],
-        [
-            pltpu.VMEM((4, width, width), F32),
-            pltpu.VMEM((2, 2, packed_rows, TILE), BF16),
-            pltpu.VMEM((4 * lanes, TILE), F32),
-            pltpu.SemaphoreType.DMA((4,)),
-        ],
-        moved=6 * megabyte,
-    )(old_owner, factor_old[0, 0], inverse_old[0, 0])
-    half_message = shape((ring,) + message.shape[1:], BF16)
-    near_old, far_old = kernel_call(
-        choose_core, (half_message, half_message), [SCALARS, WHOLE, WHOLE], moved=megabyte
-    )(old_owner, keep, swap_cores(send))
-    arrived_old = swap_planes(far_old)
-
-    message = shape((chips, share + ROWS, TILE), BF16)
+    message = shape((chips, 3 * share + 8 * lanes + ROWS, TILE), BF16)
     keep, send, turned = kernel_call(
-        covariance_parts,
+        first_parts,
         (message, message, shape((width, tok_rows), BF16)),
-        [SCALARS, ANYWHERE, ANYWHERE],
+        [SCALARS, SCALARS] + [ANYWHERE] * 4,
         [
             pltpu.VMEM((tok_rows, width), BF16),
             pltpu.VMEM((tok_rows, width), BF16),
             pltpu.VMEM((width, tok_rows), BF16),
-            pltpu.VMEM((2, packed_rows, TILE), BF16),
-            pltpu.SemaphoreType.DMA((2,)),
+            pltpu.VMEM((4, width, width), F32),
+            pltpu.VMEM((2, 3, packed_rows, TILE), BF16),
+            pltpu.VMEM((4 * lanes, TILE), F32),
+            pltpu.SemaphoreType.DMA((6,)),
         ],
         flops=4 * tok_rows * width * width,
-        moved=6 * megabyte,
-    )(counts, features, out_grads)
-    half_shape = (ring,) + message.shape[1:]
-    near_sum, far_sum = kernel_call(
-        add_core, (shape(half_shape, F32), shape(half_shape, BF16)), [WHOLE, WHOLE], moved=megabyte
-    )(keep, swap_cores(send))
-    arrived_sum = swap_planes(far_sum)
-
-    def gradient(body, tile_at, count, dtype, name, *others):
+        moved=10 * megabyte,
+    )(old_owner, counts, features, out_grads, factor_old[0, 0], inverse_old[0, 0])
+    old_rows = 2 * share + 8 * lanes
+    far_shape = shape((ring,) + message.shape[1:], BF16)
+    def gradient(body, parity, which, dtype, name, other):
+        def chip_at(i, s):
+            return s[1] * ring + 4 * i
+
         def tile_spec(n):
-            return pl.BlockSpec((tok_rows, TILE), lambda i, s: (0, 2 * tile_at(4 * i + n, s) + s[0]))
-
-        message_spec = pl.BlockSpec((4, width, TILE), lambda i, s: (i, 0, 0))
-        received_spec = pl.BlockSpec((4, width, TILE), lambda i, s: (tile_at(4 * i, s) // 4, 0, 0))
-        other_specs = [received_spec] if len(others) == 1 else [ANYWHERE] * 2
-        parity = 1 - core if len(others) == 2 else core
+            return pl.BlockSpec((tok_rows, TILE), lambda i, s: (0, 2 * (chip_at(i, s) + n) + s[0]))
+
+        four_chips = pl.BlockSpec((4, width, TILE), lambda i, s: (i, 0, 0))
         return pl.pallas_call(
             body,
-            out_shape=shape((count, width, TILE), dtype),
+            out_shape=shape((ring, width, TILE), dtype),
             grid_spec=pltpu.PrefetchScalarGridSpec(
                 num_scalar_prefetch=1,
-                grid=(count // 4,),
+                grid=(ring // 4,),
                 in_specs=[pl.BlockSpec((width, tok_rows), lambda i, s: (0, 0))]
                 + [tile_spec(n) for n in range(4)]
-                + other_specs,
-                out_specs=message_spec,
+                + [four_chips if body is gradient_add else ANYWHERE],
+                out_specs=four_chips,
             ),
             compiler_params=PARAMS,
             cost_estimate=pl.CostEstimate(
-                flops=2 * tok_rows * width * TILE * count,
-                bytes_accessed=(count // 2) * megabyte,
+                flops=2 * ring * tok_rows * width * TILE,
+                bytes_accessed=ring * megabyte // 2,
                 transcendentals=0,
             ),
             name=name,
-        )(
-            jnp.stack([parity, jnp.where(member >= chips, 1, 0)]),
-            turned, features, features, features, features, *others,
-        )
-
-    send = gradient(gradient_send, lambda q, s: q, chips, BF16, "gradient_send", far_old, far_sum)
-    joined, send = kernel_call(
-        join_planes,
-        (
-            shape((ring, near_old.shape[1] + near_sum.shape[1], TILE), BF16),
-            shape(send.shape, send.dtype),
-        ),
-        [SCALARS] + [WHOLE] * 4 + [ANYWHERE],
-        out_specs=(WHOLE, ANYWHERE),
-        aliases={5: 1},
-        moved=megabyte,
-    )(old_owner, near_old, arrived_old, near_sum, arrived_sum, send)
-    received = swap_cores(send)
-    far_grad = gradient(
-        gradient_add, lambda q, s: (1 - s[1]) * ring + q, ring, BF16, "gradient_far", received
-    )
+        )(jnp.stack([parity, which]), turned, features, features, features, features, other)
+
+    plane = jnp.where(member >= chips, 1, 0)
+    send_far = gradient(gradient_send, 1 - core, 1 - plane, BF16, "send_far", counts)
+    received_far = swap_cores(send_far)
+    near_old, near_sum, far = kernel_call(
+        choose_core,
+        (shape((ring, old_rows, TILE), BF16), shape((ring, share + ROWS, TILE), F32), far_shape),
+        [SCALARS, WHOLE, WHOLE, ANYWHERE],
+        moved=2 * megabyte,
+    )(old_owner, keep, swap_cores(send), send_far)
+    arrived = swap_planes(far)
+
+    send_near = gradient(gradient_send, 1 - core, plane, BF16, "send_near", far)
+    far_grad = gradient(gradient_add, core, 1 - plane, BF16, "gradient_far", received_far)
     arrived_grad = swap_planes(far_grad)
     near_grad = gradient(
-        gradient_add, lambda q, s: s[1] * ring + q, ring, F32, "gradient_near", received
-    )
-
+        gradient_add, core, plane, F32, "gradient_near", swap_cores(send_near)
+    )
+    joined = kernel_call(
+        join_planes,
+        far_shape,
+        [SCALARS] + [WHOLE] * 3 + [ANYWHERE] * 2,
+        moved=megabyte,
+    )(old_owner, near_old, near_sum, arrived, far_grad, send_near)
     shares, diag = kernel_call(
         make_shares,
         (shape((ring, 2 * share, TILE), BF16), shape((4 * lanes, TILE), F32)),

time: 145 us -> 142 us (0.979)
  waiting for transfers between devices: 37.9 us -> 32.6 us
  blocking collectives: 30.8 us -> 33.7 us
  local copies, waits for them, and re-layouts: 6.08 us -> 4.12 us
    all_to_all x3, waiting for transfers between devices: 24 us -> 18.2 us  [across_ring(): lax.all_to_all(parts, 'dp', 0, 0, tiled=True, axis_index_groups=rings)]
    ppermute x5, starting transfers between devices: 6.85 us -> 9.73 us  [swap_cores(): return lax.ppermute(send, 'dp', core_swap)]
    unnamed x14 -> x10, local copies, waits for them, and re-layouts: 5.55 us -> 3.59 us
    ppermute x4 -> x3, starting transfers between devices: 6.52 us -> 4.61 us  [swap_planes(): return lax.ppermute(send, 'dp', plane_swap)]
    all_gather x1, blocking collectives: 7.29 us -> 9.2 us  [local(): grads = lax.all_gather(grad, 'dp', axis=0, axis_index_groups=neighbours)]
    pallas_call x8 -> x7, Pallas kernels: 19.3 us -> 19.7 us  [the longest x4 13.4 us: gradient(): pl.pallas_call(body, out_shape=shape((ring, width, TILE), dtype), grid_sp...]
    ppermute x4 -> x3, waiting for transfers between devices: 9.49 us -> 9.49 us  [swap_planes(): return lax.ppermute(send, 'dp', plane_swap)]
  transfers between devices with their start and end apart: 16 -> 15, of which waited for: 9 -> 11; matrix products, arithmetic and copies ran while one was open for 2% -> 2% of each run, Pallas kernels for 16% -> 15%
where the time goes in v7:
time: 142 us; the launch traced here: 141 us
  starting transfers between devices  37.8 us (27%)
  blocking collectives  33.7 us (24%)
  waiting for transfers between devices  32.6 us (23%)
  Pallas kernels  26.9 us (19%)
  local copies, waits for them, and re-layouts  4.12 us (3%)
  other arithmetic  3.68 us (3%)
  between operations  2.19 us (2%)
    all_to_all x3, waiting for transfers between devices, across_ring(): lax.all_to_all(parts, 'dp', 0, 0, tiled=True, axis_index_groups=rings)  18.2 us
    all_to_all x1, blocking collectives, local(): lax.all_to_all(jnp.broadcast_to(curvature, (2 * columns, 8, TILE)), ('dp'...  14.1 us
    all_to_all x3, starting transfers between devices, across_ring(): lax.all_to_all(parts, 'dp', 0, 0, tiled=True, axis_index_groups=rings)  13.5 us
    pallas_call x4, Pallas kernels, gradient(): pl.pallas_call(body, out_shape=shape((ring, width, TILE), dtype), grid_sp...  13.4 us
    all_to_all x1, blocking collectives, local(): lax.all_to_all(jnp.broadcast_to(curvature, (chips, 8, TILE)), 'dp', 0, 0,...  10.4 us
    ppermute x5, starting transfers between devices, swap_cores(): return lax.ppermute(send, 'dp', core_swap)  9.73 us
    ppermute x3, waiting for transfers between devices, swap_planes(): return lax.ppermute(send, 'dp', plane_swap)  9.49 us
    all_gather x1, blocking collectives, local(): grads = lax.all_gather(grad, 'dp', axis=0, axis_index_groups=neighbours)  9.2 us
  transfers between devices with their start and end apart: 15, of which 11 were waited for; matrix products, arithmetic and copies ran while one was open for 2% of the time, Pallas kernels for 15%

profile of v7, /device:TPU:1, one launch (start us, length us, event | category | flops | bytes accessed | tf_op | source)
XLA Modules:
  0.0 141.0 jit_solution(4873682797018056702)
XLA Ops:
  1.3 0.8 copy.18.owners
  2.0 1.2 copy-done.1
  3.3 4.9 %first_parts.1 = (bf16[16,288,128]{2,1,0:T(8,128)(2,1)S(1)}, bf16[16,288,128]{2,1,0:T(8,128)(2,1)}, bf16[512,1024]{1,0:T(8,128)(2,1)S(1)}) custom-call(s32[8,2]{1,0:T(8,128)S(1)} %copy.18.owners, s32[1]{0:T(128)S(6)} %copy.20.counts.refs_4_, bf16[1024,4096]{1,0:T(8,128)(2,1)} %refs_3_.7, bf16[1024,512]{1,0:T(8,128)(2,1)S(1)} %copy-done.1, ...), custom_call_target="tpu_custom_call" | custom-call | flops 1073741824 | bytes 10485760 | tf_op jit(solution)/shard_map/first_parts/pallas_call | solution.py:391
  8.2 3.3 %collective-permute-start = (bf16[16,288,128]{2,1,0:T(8,128)(2,1)}, bf16[16,288,128]{2,1,0:T(8,128)(2,1)S(1)}, u32[]{:S(2)}, u32[]{:S(2)}) collective-permute-start(bf16[16,288,128]{2,1,0:T(8,128)(2,1)} %get-tuple-element.17), channel_id=1, source_target_pairs={{0,8},{8,0},{16,24},{24,16},{32,40},{40,32},{48,56},{56,48},{64,72... | collective-permute-start | bytes 3538952 | tf_op jit(solution)/shard_map/ppermute | solution.py:385
  11.6 3.3 %send_far.1.unread = bf16[8,512,128]{2,1,0:T(8,128)(2,1)S(1)} custom-call(s32[2]{0:T(128)S(1)} %pad_add_fusion.1.scalars, bf16[512,1024]{1,0:T(8,128)(2,1)S(1)} %get-tuple-element.18.turned, bf16[1024,4096]{1,0:T(8,128)(2,1)} %refs_3_.7, bf16[1024,4096]{1,0:T(8,128)(2,1)} %refs_3_.7, bf16[1024,4096]{1,0:T(8,128)(2,1)} %refs_3_.7, ...), custom_call_target="tpu_custom_call" | custom-call | flops 1073741824 | bytes 4194304 | tf_op jit(solution)/shard_map/send_far/pallas_call | solution.py:417
  14.9 0.1 collective-permute-start.2
  15.0 0.8 choose_core.1
  15.7 1.3 collective-permute-start.1
  17.1 0.5 collective-permute-done.2.refs_4_
  17.6 3.3 %gradient_far.1.unread = bf16[8,512,128]{2,1,0:T(8,128)(2,1)S(1)} custom-call(s32[2]{0:T(128)S(1)} %pad_add_fusion.scalars, bf16[512,1024]{1,0:T(8,128)(2,1)S(1)} %get-tuple-element.18.turned, bf16[1024,4096]{1,0:T(8,128)(2,1)} %refs_3_.7, bf16[1024,4096]{1,0:T(8,128)(2,1)} %refs_3_.7, bf16[1024,4096]{1,0:T(8,128)(2,1)} %refs_3_.7, ...), custom_call_target="tpu_custom_call" | custom-call | flops 1073741824 | bytes 4194304 | tf_op jit(solution)/shard_map/gradient_far/pallas_call | solution.py:417
  20.9 3.3 %send_near.1.other_unread = bf16[8,512,128]{2,1,0:T(8,128)(2,1)S(1)} custom-call(s32[2]{0:T(128)S(1)} %pad_add_fusion.2.scalars, bf16[512,1024]{1,0:T(8,128)(2,1)S(1)} %get-tuple-element.18.turned, bf16[1024,4096]{1,0:T(8,128)(2,1)} %refs_3_.7, bf16[1024,4096]{1,0:T(8,128)(2,1)} %refs_3_.7, bf16[1024,4096]{1,0:T(8,128)(2,1)} %refs_3_.7, ...), custom_call_target="tpu_custom_call" | custom-call | flops 1073741824 | bytes 4194304 | tf_op jit(solution)/shard_map/send_near/pallas_call | solution.py:417
  24.2 7.5 %collective-permute-done.1.arrived = bf16[8,288,128]{2,1,0:T(8,128)(2,1)S(1)} collective-permute-done((bf16[8,288,128]{2,1,0:T(8,128)(2,1)S(1)}, bf16[8,288,128]{2,1,0:T(8,128)(2,1)S(1)}, u32[]{:S(2)}, u32[]{:S(2)}) %collective-permute-start.1) | collective-permute-done | bytes 589856 | tf_op jit(solution)/shard_map/ppermute | solution.py:388
  31.7 0.7 join_planes.1
  32.4 0.8 copy-done
  33.3 6.5 %all-to-all-start = ((bf16[8,288,128]{2,1,0:T(8,128)(2,1)}), bf16[8,288,128]{2,1,0:T(8,128)(2,1)}, u32[]{:S(2)}, u32[]{:S(2)}) async-start(bf16[8,288,128]{2,1,0:T(8,128)(2,1)} %copy-done), calls=%async_computation | async-start | bytes 1179648 | tf_op jit(solution)/shard_map/all_to_all | solution.py:382
  39.7 1.6 %collective-permute-start.6 = (bf16[8,512,128]{2,1,0:T(8,128)(2,1)S(1)}, bf16[8,512,128]{2,1,0:T(8,128)(2,1)}, u32[]{:S(2)}, u32[]{:S(2)}) collective-permute-start(bf16[8,512,128]{2,1,0:T(8,128)(2,1)S(1)} %send_near.1.other_unread), channel_id=1, source_target_pairs={{0,8},{8,0},{16,24},{24,16},{32,40},{40,32},{48,56},{56,48},{64,72... | collective-permute-start | bytes 3145736 | tf_op jit(solution)/shard_map/ppermute | solution.py:385
  41.3 2.9 %collective-permute-start.7 = (bf16[8,512,128]{2,1,0:T(8,128)(2,1)S(1)}, bf16[8,512,128]{2,1,0:T(8,128)(2,1)}, u32[]{:S(2)}, u32[]{:S(2)}) collective-permute-start(bf16[8,512,128]{2,1,0:T(8,128)(2,1)S(1)} %gradient_far.1.unread), channel_id=1, source_target_pairs={{0,128},{8,136},{16,144},{24,152},{32,160},{40,168},{48,176},{56,1... | collective-permute-start | bytes 3145736 | tf_op jit(solution)/shard_map/ppermute | solution.py:388
  44.2 13.4 %all-to-all-done.arrived = bf16[8,288,128]{2,1,0:T(8,128)(2,1)} async-done(((bf16[8,288,128]{2,1,0:T(8,128)(2,1)}), bf16[8,288,128]{2,1,0:T(8,128)(2,1)}, u32[]{:S(2)}, u32[]{:S(2)}) %all-to-all-start) | async-done | bytes 589856 | tf_op jit(solution)/shard_map/all_to_all | solution.py:382
  57.7 1.1 make_shares.1
  58.8 0.7 copy-done.2
  59.5 3.4 %all-to-all-start.1 = ((bf16[8,160,128]{2,1,0:T(8,128)(2,1)}), bf16[8,160,128]{2,1,0:T(8,128)(2,1)S(1)}, u32[]{:S(2)}, u32[]{:S(2)}) async-start(bf16[8,160,128]{2,1,0:T(8,128)(2,1)} %copy-done.2), calls=%async_computation.1 | async-start | bytes 655360 | tf_op jit(solution)/shard_map/all_to_all | solution.py:382
  63.0 3.5 %gradient_near.1 = f32[8,512,128]{2,1,0:T(8,128)S(1)} custom-call(s32[2]{0:T(128)S(1)} %pad_add_fusion.3.scalars, bf16[512,1024]{1,0:T(8,128)(2,1)S(1)} %get-tuple-element.18.turned, bf16[1024,4096]{1,0:T(8,128)(2,1)} %refs_3_.7, bf16[1024,4096]{1,0:T(8,128)(2,1)} %refs_3_.7, bf16[1024,4096]{1,0:T(8,128)(2,1)} %refs_3_.7, bf16[1024,4096]{1,0:T(8,128)(2,1)} %refs_3_.7, ...), custom_call_target="tpu_custom_call" | custom-call | flops 1073741824 | bytes 4194304 | tf_op jit(solution)/shard_map/gradient_near/pallas_call | solution.py:417
  66.5 1.1 collective-permute-done.7
  67.7 2.4 %add_convert_fusion = bf16[8,512,128]{2,1,0:T(8,128)(2,1)} fusion(f32[8,512,128]{2,1,0:T(8,128)S(1)} %gradient_near.1, bf16[8,512,128]{2,1,0:T(8,128)(2,1)} %collective-permute-done.7), kind=kLoop, calls=%fused_computation | loop fusion | flops 1572864 | bytes 4194304 | tf_op jit(solution)/shard_map/convert_element_type | solution.py:518
  70.1 3.9 %all-to-all-done.1.mine = bf16[8,160,128]{2,1,0:T(8,128)(2,1)S(1)} async-done(((bf16[8,160,128]{2,1,0:T(8,128)(2,1)}), bf16[8,160,128]{2,1,0:T(8,128)(2,1)S(1)}, u32[]{:S(2)}, u32[]{:S(2)}) %all-to-all-start.1) | async-done | bytes 327712 | tf_op jit(solution)/shard_map/all_to_all | solution.py:382
  74.0 3.6 %all-to-all-start.2 = ((bf16[8,512,128]{2,1,0:T(8,128)(2,1)}), bf16[8,512,128]{2,1,0:T(8,128)(2,1)S(1)}, u32[]{:S(2)}, u32[]{:S(2)}) async-start(bf16[8,512,128]{2,1,0:T(8,128)(2,1)} %add_convert_fusion), calls=%async_computation.2 | async-start | bytes 2097152 | tf_op jit(solution)/shard_map/all_to_all | solution.py:382
  77.6 3.2 %collective-permute-start.3 = (bf16[8,160,128]{2,1,0:T(8,128)(2,1)S(1)}, bf16[8,160,128]{2,1,0:T(8,128)(2,1)S(1)}, u32[]{:S(2)}, u32[]{:S(2)}) collective-permute-start(bf16[8,160,128]{2,1,0:T(8,128)(2,1)S(1)} %all-to-all-done.1.mine), channel_id=1, source_target_pairs={{0,8},{8,0},{16,24},{24,16},{32,40},{40,32},{48,56},{56,48},{64,72... | collective-permute-start | bytes 983048 | tf_op jit(solution)/shard_map/ppermute | solution.py:385
  80.8 1.3 collective-permute-done.3.other
  82.0 1.2 left_columns.1
  83.3 3.2 %collective-permute-start.8 = (bf16[512,128]{1,0:T(8,128)(2,1)S(1)}, bf16[512,128]{1,0:T(8,128)(2,1)S(1)}, u32[]{:S(2)}, u32[]{:S(2)}) collective-permute-start(bf16[512,128]{1,0:T(8,128)(2,1)S(1)} %left_columns.1), channel_id=1, source_target_pairs={{0,1},{8,9},{16,17},{24,25},{33,32},{41,40},{49,48},{57,56},{66,67... | collective-permute-start | bytes 393224 | tf_op jit(solution)/shard_map/ppermute | solution.py:487
  86.5 0.4 collective-permute-start.4
  86.9 2.0 %collective-permute-done.8 = bf16[512,128]{1,0:T(8,128)(2,1)S(1)} collective-permute-done((bf16[512,128]{1,0:T(8,128)(2,1)S(1)}, bf16[512,128]{1,0:T(8,128)(2,1)S(1)}, u32[]{:S(2)}, u32[]{:S(2)}) %collective-permute-start.8) | collective-permute-done | bytes 131104 | tf_op jit(solution)/shard_map/ppermute | solution.py:487
  89.0 2.4 %collective-permute-start.11 = (bf16[512,128]{1,0:T(8,128)(2,1)S(1)}, bf16[512,128]{1,0:T(8,128)(2,1)S(1)}, u32[]{:S(2)}, u32[]{:S(2)}) collective-permute-start(bf16[512,128]{1,0:T(8,128)(2,1)S(1)} %broadcast_select_fusion), channel_id=1, source_target_pairs={{0,6},{1,7},{8,14},{9,15},{16,22},{17,23},{24,30},{25,31},{33,39},... | collective-permute-start | bytes 393224 | tf_op jit(solution)/shard_map/ppermute | solution.py:496
  91.4 3.2 %collective-permute-start.10 = (bf16[512,128]{1,0:T(8,128)(2,1)S(1)}, bf16[512,128]{1,0:T(8,128)(2,1)S(1)}, u32[]{:S(2)}, u32[]{:S(2)}) collective-permute-start(bf16[512,128]{1,0:T(8,128)(2,1)S(1)} %broadcast_select_fusion), channel_id=1, source_target_pairs={{0,4},{1,5},{8,12},{9,13},{16,20},{17,21},{24,28},{25,29},{33,37},... | collective-permute-start | bytes 393224 | tf_op jit(solution)/shard_map/ppermute | solution.py:496
  94.5 1.3 collective-permute-start.9
  95.8 0.8 collective-permute-done.4.far_mine
  96.7 1.5 %collective-permute-start.5 = (bf16[8,160,128]{2,1,0:T(8,128)(2,1)S(1)}, bf16[8,160,128]{2,1,0:T(8,128)(2,1)S(1)}, u32[]{:S(2)}, u32[]{:S(2)}) collective-permute-start(bf16[8,160,128]{2,1,0:T(8,128)(2,1)S(1)} %collective-permute-done.4.far_mine), channel_id=1, source_target_pairs={{0,8},{8,0},{16,24},{24,16},{32,40},{40,32},{48,56},{56,48},{64,72... | collective-permute-start | bytes 983048 | tf_op jit(solution)/shard_map/ppermute | solution.py:385
  98.3 0.9 collective-permute-done.9
  99.2 0.2 collective-permute-done.5.far_other
  99.4 4.0 %new_blocks.1 = (bf16[512,512]{1,0:T(8,128)(2,1)S(1)}, f32[512,512]{1,0:T(8,128)}, f32[512,512]{1,0:T(8,128)}) custom-call(s32[8,2]{1,0:T(8,128)S(1)} %copy.19.owners, bf16[8,160,128]{2,1,0:T(8,128)(2,1)S(1)} %all-to-all-done.1.mine, bf16[8,160,128]{2,1,0:T(8,128)(2,1)S(1)} %collective-permute-done.3.other, ...), custom_call_target="tpu_custom_call" | custom-call | flops 1073741824 | bytes 6291456 | tf_op jit(solution)/shard_map/new_blocks/pallas_call | solution.py:509
  103.4 0.9 all-to-all-done.2
  104.4 0.1 reduce_sum.30
  104.5 9.2 %all-gather = bf16[2048,128]{1,0:T(8,128)(2,1)S(1)} all-gather(bf16[512,128]{1,0:T(8,128)(2,1)S(1)} %reduce_sum.30), channel_id=2, replica_groups={{0,8,16,24},{32,40,48,56},{64,72,80,88},{96,104,112,120},{128,136,144,1..., dimensions={0}, use_global_device_ids=true | all-gather | bytes 655360 | tf_op jit(solution)/shard_map/all_gather | solution.py:521
  113.7 0.8 precondition.1
  114.5 10.4 %all_to_all.25 = f32[16,8,128]{2,1,0:T(8,128)S(1)} all-to-all(f32[16,8,128]{2,1,0:T(8,128)S(1)} %broadcast_in_dim.14), channel_id=1, replica_groups={{0,8,16,24,32,40,48,56,64,72,80,88,96,104,112,120},{128,136,144,152,160..., dimensions={0} | all-to-all | bytes 131072 | tf_op jit(solution)/shard_map/all_to_all | solution.py:531
  125.0 14.1 %all_to_all.26 = f32[16,8,128]{2,1,0:T(8,128)S(1)} all-to-all(f32[16,8,128]{2,1,0:T(8,128)S(1)} %broadcast_in_dim.15), channel_id=1, replica_groups={{0,1,2,3,4,5,6,7,128,129,130,131,132,133,134,135},{8,9,10,11,12,13,14,1..., dimensions={0} | all-to-all | bytes 131072 | tf_op jit(solution)/shard_map/all_to_all | solution.py:539
  139.0 0.5 slice.3
  140.3 0.7 broadcast_multiply_fusion
  (20 shorter events, 0.5 us)
Async XLA Ops:
  2.0 1.2 copy-start.1
  8.2 6.8 %collective-permute-start = (bf16[16,288,128]{2,1,0:T(8,128)(2,1)}, bf16[16,288,128]{2,1,0:T(8,128)(2,1)S(1)}, u32[]{:S(2)}, u32[]{:S(2)}) collective-permute-start(bf16[16,288,128]{2,1,0:T(8,128)(2,1)} %get-tuple-element.17), channel_id=1, source_target_pairs={{0,8},{8,0},{16,24},{24,16},{32,40},{40,32},{48,56},{56,48},{64,72... | collective-permute-start | bytes 3538952 | tf_op jit(solution)/shard_map/ppermute | solution.py:385
  14.9 2.7 %collective-permute-start.2 = (bf16[8,512,128]{2,1,0:T(8,128)(2,1)S(1)}, bf16[8,512,128]{2,1,0:T(8,128)(2,1)S(1)}, u32[]{:S(2)}, u32[]{:S(2)}) collective-permute-start(bf16[8,512,128]{2,1,0:T(8,128)(2,1)S(1)} %send_far.1.unread), channel_id=1, source_target_pairs={{0,8},{8,0},{16,24},{24,16},{32,40},{40,32},{48,56},{56,48},{64,72... | collective-permute-start | bytes 3145736 | tf_op jit(solution)/shard_map/ppermute | solution.py:385
  15.7 16.0 %collective-permute-start.1 = (bf16[8,288,128]{2,1,0:T(8,128)(2,1)S(1)}, bf16[8,288,128]{2,1,0:T(8,128)(2,1)S(1)}, u32[]{:S(2)}, u32[]{:S(2)}) collective-permute-start(bf16[8,288,128]{2,1,0:T(8,128)(2,1)S(1)} %get-tuple-element.21.refs_4_), channel_id=1, source_target_pairs={{0,128},{8,136},{16,144},{24,152},{32,160},{40,168},{48,176},{56,1... | collective-permute-start | bytes 1769480 | tf_op jit(solution)/shard_map/ppermute | solution.py:388
  32.4 0.8 copy-start
  33.3 24.4 %all-to-all-start = ((bf16[8,288,128]{2,1,0:T(8,128)(2,1)}), bf16[8,288,128]{2,1,0:T(8,128)(2,1)}, u32[]{:S(2)}, u32[]{:S(2)}) async-start(bf16[8,288,128]{2,1,0:T(8,128)(2,1)} %copy-done), calls=%async_computation | async-start | bytes 1179648 | tf_op jit(solution)/shard_map/all_to_all | solution.py:382
  39.7 23.3 %collective-permute-start.6 = (bf16[8,512,128]{2,1,0:T(8,128)(2,1)S(1)}, bf16[8,512,128]{2,1,0:T(8,128)(2,1)}, u32[]{:S(2)}, u32[]{:S(2)}) collective-permute-start(bf16[8,512,128]{2,1,0:T(8,128)(2,1)S(1)} %send_near.1.other_unread), channel_id=1, source_target_pairs={{0,8},{8,0},{16,24},{24,16},{32,40},{40,32},{48,56},{56,48},{64,72... | collective-permute-start | bytes 3145736 | tf_op jit(solution)/shard_map/ppermute | solution.py:385
  41.3 26.3 %collective-permute-start.7 = (bf16[8,512,128]{2,1,0:T(8,128)(2,1)S(1)}, bf16[8,512,128]{2,1,0:T(8,128)(2,1)}, u32[]{:S(2)}, u32[]{:S(2)}) collective-permute-start(bf16[8,512,128]{2,1,0:T(8,128)(2,1)S(1)} %gradient_far.1.unread), channel_id=1, source_target_pairs={{0,128},{8,136},{16,144},{24,152},{32,160},{40,168},{48,176},{56,1... | collective-permute-start | bytes 3145736 | tf_op jit(solution)/shard_map/ppermute | solution.py:388
  58.8 0.7 copy-start.2
  59.5 14.5 %all-to-all-start.1 = ((bf16[8,160,128]{2,1,0:T(8,128)(2,1)}), bf16[8,160,128]{2,1,0:T(8,128)(2,1)S(1)}, u32[]{:S(2)}, u32[]{:S(2)}) async-start(bf16[8,160,128]{2,1,0:T(8,128)(2,1)} %copy-done.2), calls=%async_computation.1 | async-start | bytes 655360 | tf_op jit(solution)/shard_map/all_to_all | solution.py:382
  70.1 28.1 %copy-start.3 = (s32[8,2]{0,1:T(2,128)S(1)}, s32[8,2]{0,1:T(2,128)}, u32[]{:S(2)}) copy-start(s32[8,2]{0,1:T(2,128)} %param.13) | copy-start | bytes 196
  74.0 30.4 %all-to-all-start.2 = ((bf16[8,512,128]{2,1,0:T(8,128)(2,1)}), bf16[8,512,128]{2,1,0:T(8,128)(2,1)S(1)}, u32[]{:S(2)}, u32[]{:S(2)}) async-start(bf16[8,512,128]{2,1,0:T(8,128)(2,1)} %add_convert_fusion), calls=%async_computation.2 | async-start | bytes 2097152 | tf_op jit(solution)/shard_map/all_to_all | solution.py:382
  77.6 4.4 %collective-permute-start.3 = (bf16[8,160,128]{2,1,0:T(8,128)(2,1)S(1)}, bf16[8,160,128]{2,1,0:T(8,128)(2,1)S(1)}, u32[]{:S(2)}, u32[]{:S(2)}) collective-permute-start(bf16[8,160,128]{2,1,0:T(8,128)(2,1)S(1)} %all-to-all-done.1.mine), channel_id=1, source_target_pairs={{0,8},{8,0},{16,24},{24,16},{32,40},{40,32},{48,56},{56,48},{64,72... | collective-permute-start | bytes 983048 | tf_op jit(solution)/shard_map/ppermute | solution.py:385
  83.3 5.7 %collective-permute-start.8 = (bf16[512,128]{1,0:T(8,128)(2,1)S(1)}, bf16[512,128]{1,0:T(8,128)(2,1)S(1)}, u32[]{:S(2)}, u32[]{:S(2)}) collective-permute-start(bf16[512,128]{1,0:T(8,128)(2,1)S(1)} %left_columns.1), channel_id=1, source_target_pairs={{0,1},{8,9},{16,17},{24,25},{33,32},{41,40},{49,48},{57,56},{66,67... | collective-permute-start | bytes 393224 | tf_op jit(solution)/shard_map/ppermute | solution.py:487
  86.5 10.2 %collective-permute-start.4 = (bf16[8,160,128]{2,1,0:T(8,128)(2,1)S(1)}, bf16[8,160,128]{2,1,0:T(8,128)(2,1)S(1)}, u32[]{:S(2)}, u32[]{:S(2)}) collective-permute-start(bf16[8,160,128]{2,1,0:T(8,128)(2,1)S(1)} %all-to-all-done.1.mine), channel_id=1, source_target_pairs={{0,128},{8,136},{16,144},{24,152},{32,160},{40,168},{48,176},{56,1... | collective-permute-start | bytes 983048 | tf_op jit(solution)/shard_map/ppermute | solution.py:388
  89.0 9.3 %collective-permute-start.11 = (bf16[512,128]{1,0:T(8,128)(2,1)S(1)}, bf16[512,128]{1,0:T(8,128)(2,1)S(1)}, u32[]{:S(2)}, u32[]{:S(2)}) collective-permute-start(bf16[512,128]{1,0:T(8,128)(2,1)S(1)} %broadcast_select_fusion), channel_id=1, source_target_pairs={{0,6},{1,7},{8,14},{9,15},{16,22},{17,23},{24,30},{25,31},{33,39},... | collective-permute-start | bytes 393224 | tf_op jit(solution)/shard_map/ppermute | solution.py:496
  91.4 6.9 %collective-permute-start.10 = (bf16[512,128]{1,0:T(8,128)(2,1)S(1)}, bf16[512,128]{1,0:T(8,128)(2,1)S(1)}, u32[]{:S(2)}, u32[]{:S(2)}) collective-permute-start(bf16[512,128]{1,0:T(8,128)(2,1)S(1)} %broadcast_select_fusion), channel_id=1, source_target_pairs={{0,4},{1,5},{8,12},{9,13},{16,20},{17,21},{24,28},{25,29},{33,37},... | collective-permute-start | bytes 393224 | tf_op jit(solution)/shard_map/ppermute | solution.py:496
  94.5 4.7 %collective-permute-start.9 = (bf16[512,128]{1,0:T(8,128)(2,1)S(1)}, bf16[512,128]{1,0:T(8,128)(2,1)S(1)}, u32[]{:S(2)}, u32[]{:S(2)}) collective-permute-start(bf16[512,128]{1,0:T(8,128)(2,1)S(1)} %broadcast_select_fusion), channel_id=1, source_target_pairs={{0,2},{1,3},{8,10},{9,11},{16,18},{17,19},{24,26},{25,27},{33,35},... | collective-permute-start | bytes 393224 | tf_op jit(solution)/shard_map/ppermute | solution.py:496
  96.7 2.8 %collective-permute-start.5 = (bf16[8,160,128]{2,1,0:T(8,128)(2,1)S(1)}, bf16[8,160,128]{2,1,0:T(8,128)(2,1)S(1)}, u32[]{:S(2)}, u32[]{:S(2)}) collective-permute-start(bf16[8,160,128]{2,1,0:T(8,128)(2,1)S(1)} %collective-permute-done.4.far_mine), channel_id=1, source_target_pairs={{0,8},{8,0},{16,24},{24,16},{32,40},{40,32},{48,56},{56,48},{64,72... | collective-permute-start | bytes 983048 | tf_op jit(solution)/shard_map/ppermute | solution.py:385

commit v8 on v7

--- a/solution.py
+++ b/solution.py
@@ -38,6 +38,7 @@
         chips = lax.axis_size("dp") // 2
         self.core = member & 1
         self.plane = jnp.where(member >= chips, 1, 0)
+        self.ring = lax.shift_right_logical(member & (chips - 1), 1)
         self.place = member & (lax.axis_size("dp") // lax.axis_size("mp") - 1)
         self.flip = jnp.where(self.column >= lax.axis_size("mp") // 2, 1, 0)
         self.own_kind = self.plane ^ self.flip
@@ -224,6 +225,18 @@
         out[n] = total.astype(out.dtype)
 
 
+def add_planes(near, arrived, keep, send):
+    parity = Facts().ring & 1
+    for pair in range(keep.shape[0]):
+        for out, which in ((keep, parity), (send, 1 - parity)):
+            at = 2 * pair + which
+            out[pair] = (near[at] + arrived[at].astype(F32)).astype(out.dtype)
+
+
+def add_pair(keep, received, out):
+    out[...] = (keep[...] + received[...].astype(F32)).astype(BF16)
+
+
 def unpack(mine, other, core, packed):
     share = mine.shape[1] // 2
     for pair in range(mine.shape[0]):
@@ -434,6 +447,9 @@
             name=name,
         )(jnp.stack([parity, which]), turned, features, features, features, features, other)
 
+    def plane_shape(count, dtype):
+        return shape((count, width, TILE), dtype)
+
     plane = jnp.where(member >= chips, 1, 0)
     send_far = gradient(gradient_send, 1 - core, 1 - plane, BF16, "send_far", counts)
     received_far = swap_cores(send_far)
@@ -515,7 +531,19 @@
         moved=6 * megabyte,
     )(new_owner, mine, other, far_mine, far_other, diag)
 
-    grad = across_ring((near_grad + arrived_grad.astype(F32)).astype(BF16))
+    pairs = ring // 2
+    keep, send = kernel_call(
+        add_planes,
+        (plane_shape(pairs, F32), plane_shape(pairs, BF16)),
+        [WHOLE] * 2,
+        moved=4 * megabyte,
+    )(near_grad, arrived_grad)
+    received = lax.ppermute(send, "dp", [(i, i ^ 2) for i in range(members)])
+    grad = kernel_call(add_pair, plane_shape(pairs, BF16), [WHOLE] * 2, moved=2 * megabyte)(
+        keep, received
+    )
+    halves = [[r[z] for z in range(parity, ring, 2)] for r in rings for parity in range(2)]
+    grad = lax.all_to_all(grad, "dp", 0, 0, tiled=True, axis_index_groups=halves)
     grad = jnp.sum(grad.astype(F32), axis=0).astype(BF16)
     neighbours = [[holders * c + r for r in range(holders)] for c in range(columns)]
     grads = lax.all_gather(grad, "dp", axis=0, axis_index_groups=neighbours)
@@ -533,12 +561,12 @@
         "dp", 0, 0, tiled=True, axis_index_groups=planes,
     )
     curvature = jnp.sum(curvature, axis=0)
-    rings = [
+    across = [
         [(y * chips + i) * columns + c for y in range(2) for c in range(columns)] for i in range(chips)
     ]
     curvature = lax.all_to_all(
         jnp.broadcast_to(curvature, (2 * columns, 8, TILE)),
-        ("dp", "mp"), 0, 0, tiled=True, axis_index_groups=rings,
+        ("dp", "mp"), 0, 0, tiled=True, axis_index_groups=across,
     )
     curvature = jnp.sum(curvature, axis=0)[0, 0]
     entries = float(feature_count * width * columns)

time: 142 us -> 152 us (1.070)
  waiting for transfers between devices: 32.6 us -> 39.9 us
  starting transfers between devices: 37.8 us -> 42.3 us
  other arithmetic: 3.68 us -> 1.18 us
  Pallas kernels: 26.9 us -> 29 us
    ppermute x0 -> x1, waiting for transfers between devices: none -> 13.5 us  [local(): received = lax.ppermute(send, 'dp', [(i, i ^ 2) for i in range(members)])]
    all_to_all x0 -> x1, starting transfers between devices: none -> 4.87 us  [local(): lax.all_to_all(grad, 'dp', 0, 0, tiled=True, axis_index_groups=halves)]
    all_to_all x3 -> x2, starting transfers between devices: 13.5 us -> 9.91 us  [across_ring(): lax.all_to_all(parts, 'dp', 0, 0, tiled=True, axis_index_groups=rings)]
    all_to_all x3 -> x2, waiting for transfers between devices: 18.2 us -> 15 us  [across_ring(): lax.all_to_all(parts, 'dp', 0, 0, tiled=True, axis_index_groups=rings)]
    convert_element_type x1 -> x0, other arithmetic: 2.43 us -> none  [local(): grad = across_ring((near_grad + arrived_grad.astype(F32)).astype(BF16))]
    ppermute x3, starting transfers between devices: 4.61 us -> 7.03 us  [swap_planes(): return lax.ppermute(send, 'dp', plane_swap)]
    pallas_call x0 -> x2, Pallas kernels: none -> 2.27 us  [the longest x1 1.39 us: local(): kernel_call(add_planes, (plane_shape(pairs, F32), plane_shape(pairs, BF16...]
    ppermute x1, waiting for transfers between devices: 2.04 us -> 0.01 us  [local(): lax.ppermute(left, ('dp', 'mp'), [(i * columns + g, i * columns + (g ^ 1)...]
  transfers between devices with their start and end apart: 15 -> 16, of which waited for: 11 -> 5; matrix products, arithmetic and copies ran while one was open for 2% -> 0% of each run, Pallas kernels for 15% -> 13%
where the time goes in v8:
time: 152 us
  starting transfers between devices  42.3 us (28%)
  waiting for transfers between devices  39.9 us (26%)
  blocking collectives  33 us (22%)
  Pallas kernels  29 us (19%)
  local copies, waits for them, and re-layouts  4.12 us (3%)
  between operations  2.26 us (1%)
    all_to_all x2, waiting for transfers between devices, across_ring(): lax.all_to_all(parts, 'dp', 0, 0, tiled=True, axis_index_groups=rings)  15 us
    all_to_all x1, blocking collectives, local(): lax.all_to_all(jnp.broadcast_to(curvature, (2 * columns, 8, TILE)), ('dp'...  13.6 us
    ppermute x1, waiting for transfers between devices, local(): received = lax.ppermute(send, 'dp', [(i, i ^ 2) for i in range(members)])  13.5 us
    pallas_call x4, Pallas kernels, gradient(): pl.pallas_call(body, out_shape=shape((ring, width, TILE), dtype), grid_sp...  13.4 us
    all_to_all x1, blocking collectives, local(): lax.all_to_all(jnp.broadcast_to(curvature, (chips, 8, TILE)), 'dp', 0, 0,...  11.2 us
    ppermute x3, waiting for transfers between devices, swap_planes(): return lax.ppermute(send, 'dp', plane_swap)  10.9 us
    ppermute x5, starting transfers between devices, swap_cores(): return lax.ppermute(send, 'dp', core_swap)  10.1 us
    all_to_all x2, starting transfers between devices, across_ring(): lax.all_to_all(parts, 'dp', 0, 0, tiled=True, axis_index_groups=rings)  9.91 us
  transfers between devices with their start and end apart: 16, of which 5 were waited for; matrix products, arithmetic and copies ran while one was open for 0% of the time, Pallas kernels for 13%

profile of v8, /device:TPU:1, one launch (start us, length us, event | category | flops | bytes accessed | tf_op | source)
XLA Modules:
  0.0 151.7 jit_solution(14349311572183376765)
XLA Ops:
  0.6 0.8 copy.18.owners
  2.0 1.2 copy-done.1
  3.3 4.9 %first_parts.1 = (bf16[16,288,128]{2,1,0:T(8,128)(2,1)S(1)}, bf16[16,288,128]{2,1,0:T(8,128)(2,1)}, bf16[512,1024]{1,0:T(8,128)(2,1)S(1)}) custom-call(s32[8,2]{1,0:T(8,128)S(1)} %copy.18.owners, s32[1]{0:T(128)S(6)} %copy.20.counts.refs_4_, bf16[1024,4096]{1,0:T(8,128)(2,1)} %refs_3_.7, bf16[1024,512]{1,0:T(8,128)(2,1)S(1)} %copy-done.1, ...), custom_call_target="tpu_custom_call" | custom-call | flops 1073741824 | bytes 10485760 | tf_op jit(solution)/shard_map/first_parts/pallas_call | solution.py:404
  8.2 3.3 %collective-permute-start = (bf16[16,288,128]{2,1,0:T(8,128)(2,1)}, bf16[16,288,128]{2,1,0:T(8,128)(2,1)S(1)}, u32[]{:S(2)}, u32[]{:S(2)}) collective-permute-start(bf16[16,288,128]{2,1,0:T(8,128)(2,1)} %get-tuple-element.19), channel_id=1, source_target_pairs={{0,8},{8,0},{16,24},{24,16},{32,40},{40,32},{48,56},{56,48},{64,72... | collective-permute-start | bytes 3538952 | tf_op jit(solution)/shard_map/ppermute | solution.py:398
  11.5 0.1 pad_add_fusion.1.scalars
  11.6 3.3 %send_far.1.unread = bf16[8,512,128]{2,1,0:T(8,128)(2,1)S(1)} custom-call(s32[2]{0:T(128)S(1)} %pad_add_fusion.1.scalars, bf16[512,1024]{1,0:T(8,128)(2,1)S(1)} %get-tuple-element.20.turned, bf16[1024,4096]{1,0:T(8,128)(2,1)} %refs_3_.7, bf16[1024,4096]{1,0:T(8,128)(2,1)} %refs_3_.7, bf16[1024,4096]{1,0:T(8,128)(2,1)} %refs_3_.7, ...), custom_call_target="tpu_custom_call" | custom-call | flops 1073741824 | bytes 4194304 | tf_op jit(solution)/shard_map/send_far/pallas_call | solution.py:430
  14.8 0.1 collective-permute-start.2
  15.0 0.8 choose_core.1
  15.7 1.3 collective-permute-start.1
  17.0 0.1 pad_add_fusion.2.scalars
  17.1 0.1 pad_add_fusion.scalars
  17.1 3.3 %send_near.1.other_unread = bf16[8,512,128]{2,1,0:T(8,128)(2,1)S(1)} custom-call(s32[2]{0:T(128)S(1)} %pad_add_fusion.2.scalars, bf16[512,1024]{1,0:T(8,128)(2,1)S(1)} %get-tuple-element.20.turned, bf16[1024,4096]{1,0:T(8,128)(2,1)} %refs_3_.7, bf16[1024,4096]{1,0:T(8,128)(2,1)} %refs_3_.7, bf16[1024,4096]{1,0:T(8,128)(2,1)} %refs_3_.7, ...), custom_call_target="tpu_custom_call" | custom-call | flops 1073741824 | bytes 4194304 | tf_op jit(solution)/shard_map/send_near/pallas_call | solution.py:430
  20.4 0.9 collective-permute-start.6
  21.3 3.3 %gradient_far.1.unread = bf16[8,512,128]{2,1,0:T(8,128)(2,1)S(1)} custom-call(s32[2]{0:T(128)S(1)} %pad_add_fusion.scalars, bf16[512,1024]{1,0:T(8,128)(2,1)S(1)} %get-tuple-element.20.turned, bf16[1024,4096]{1,0:T(8,128)(2,1)} %refs_3_.7, bf16[1024,4096]{1,0:T(8,128)(2,1)} %refs_3_.7, bf16[1024,4096]{1,0:T(8,128)(2,1)} %refs_3_.7, ...), custom_call_target="tpu_custom_call" | custom-call | flops 1073741824 | bytes 4194304 | tf_op jit(solution)/shard_map/gradient_far/pallas_call | solution.py:430
  24.6 7.1 %collective-permute-done.1.arrived = bf16[8,288,128]{2,1,0:T(8,128)(2,1)S(1)} collective-permute-done((bf16[8,288,128]{2,1,0:T(8,128)(2,1)S(1)}, bf16[8,288,128]{2,1,0:T(8,128)(2,1)S(1)}, u32[]{:S(2)}, u32[]{:S(2)}) %collective-permute-start.1) | collective-permute-done | bytes 589856 | tf_op jit(solution)/shard_map/ppermute | solution.py:401
  31.7 0.7 join_planes.1
  32.4 0.8 copy-done
  33.2 6.5 %all-to-all-start = ((bf16[8,288,128]{2,1,0:T(8,128)(2,1)}), bf16[8,288,128]{2,1,0:T(8,128)(2,1)}, u32[]{:S(2)}, u32[]{:S(2)}) async-start(bf16[8,288,128]{2,1,0:T(8,128)(2,1)} %copy-done), calls=%async_computation | async-start | bytes 1179648 | tf_op jit(solution)/shard_map/all_to_all | solution.py:395
  39.7 2.9 %collective-permute-start.7 = (bf16[8,512,128]{2,1,0:T(8,128)(2,1)S(1)}, bf16[8,512,128]{2,1,0:T(8,128)(2,1)}, u32[]{:S(2)}, u32[]{:S(2)}) collective-permute-start(bf16[8,512,128]{2,1,0:T(8,128)(2,1)S(1)} %gradient_far.1.unread), channel_id=1, source_target_pairs={{0,128},{8,136},{16,144},{24,152},{32,160},{40,168},{48,176},{56,1... | collective-permute-start | bytes 3145736 | tf_op jit(solution)/shard_map/ppermute | solution.py:401
  42.7 15.0 %all-to-all-done.arrived = bf16[8,288,128]{2,1,0:T(8,128)(2,1)} async-done(((bf16[8,288,128]{2,1,0:T(8,128)(2,1)}), bf16[8,288,128]{2,1,0:T(8,128)(2,1)}, u32[]{:S(2)}, u32[]{:S(2)}) %all-to-all-start) | async-done | bytes 589856 | tf_op jit(solution)/shard_map/all_to_all | solution.py:395
  57.7 1.1 make_shares.1
  58.8 0.7 copy-done.2
  59.5 3.4 %all-to-all-start.1 = ((bf16[8,160,128]{2,1,0:T(8,128)(2,1)}), bf16[8,160,128]{2,1,0:T(8,128)(2,1)S(1)}, u32[]{:S(2)}, u32[]{:S(2)}) async-start(bf16[8,160,128]{2,1,0:T(8,128)(2,1)} %copy-done.2), calls=%async_computation.1 | async-start | bytes 655360 | tf_op jit(solution)/shard_map/all_to_all | solution.py:395
  63.0 3.5 %gradient_near.1.near = f32[8,512,128]{2,1,0:T(8,128)S(1)} custom-call(s32[2]{0:T(128)S(1)} %pad_add_fusion.3.scalars, bf16[512,1024]{1,0:T(8,128)(2,1)S(1)} %get-tuple-element.20.turned, bf16[1024,4096]{1,0:T(8,128)(2,1)} %refs_3_.7, bf16[1024,4096]{1,0:T(8,128)(2,1)} %refs_3_.7, bf16[1024,4096]{1,0:T(8,128)(2,1)} %refs_3_.7, bf16[1024,4096]{1,0:T(8,128)(2,1)} %refs_3_.7, ...), custom_call_target="tpu_custom_call" | custom-call | flops 1073741824 | bytes 4194304 | tf_op jit(solution)/shard_map/gradient_near/pallas_call | solution.py:430
  66.5 1.4 add_planes.1
  67.9 1.4 collective-permute-start.8
  69.3 13.5 %collective-permute-done.8.received = bf16[4,512,128]{2,1,0:T(8,128)(2,1)S(1)} collective-permute-done((bf16[4,512,128]{2,1,0:T(8,128)(2,1)S(1)}, bf16[4,512,128]{2,1,0:T(8,128)(2,1)S(1)}, u32[]{:S(2)}, u32[]{:S(2)}) %collective-permute-start.8) | collective-permute-done | bytes 524320 | tf_op jit(solution)/shard_map/ppermute | solution.py:541
  82.9 0.9 add_pair.1
  83.8 4.9 %all-to-all-start.2 = ((bf16[4,512,128]{2,1,0:T(8,128)(2,1)}), bf16[4,512,128]{2,1,0:T(8,128)(2,1)S(1)}, u32[]{:S(2)}, u32[]{:S(2)}) async-start(bf16[4,512,128]{2,1,0:T(8,128)(2,1)} %add_pair.1), calls=%async_computation.2 | async-start | bytes 1048576 | tf_op jit(solution)/shard_map/all_to_all | solution.py:546
  88.6 2.5 %collective-permute-start.3 = (bf16[8,160,128]{2,1,0:T(8,128)(2,1)S(1)}, bf16[8,160,128]{2,1,0:T(8,128)(2,1)S(1)}, u32[]{:S(2)}, u32[]{:S(2)}) collective-permute-start(bf16[8,160,128]{2,1,0:T(8,128)(2,1)S(1)} %all-to-all-done.1.mine), channel_id=1, source_target_pairs={{0,8},{8,0},{16,24},{24,16},{32,40},{40,32},{48,56},{56,48},{64,72... | collective-permute-start | bytes 983048 | tf_op jit(solution)/shard_map/ppermute | solution.py:398
  91.1 2.9 %collective-permute-start.4 = (bf16[8,160,128]{2,1,0:T(8,128)(2,1)S(1)}, bf16[8,160,128]{2,1,0:T(8,128)(2,1)S(1)}, u32[]{:S(2)}, u32[]{:S(2)}) collective-permute-start(bf16[8,160,128]{2,1,0:T(8,128)(2,1)S(1)} %all-to-all-done.1.mine), channel_id=1, source_target_pairs={{0,128},{8,136},{16,144},{24,152},{32,160},{40,168},{48,176},{56,1... | collective-permute-start | bytes 983048 | tf_op jit(solution)/shard_map/ppermute | solution.py:401
  94.0 1.2 left_columns.1
  95.2 2.3 %collective-permute-start.9 = (bf16[512,128]{1,0:T(8,128)(2,1)S(1)}, bf16[512,128]{1,0:T(8,128)(2,1)S(1)}, u32[]{:S(2)}, u32[]{:S(2)}) collective-permute-start(bf16[512,128]{1,0:T(8,128)(2,1)S(1)} %left_columns.1), channel_id=1, source_target_pairs={{0,1},{8,9},{16,17},{24,25},{33,32},{41,40},{49,48},{57,56},{66,67... | collective-permute-start | bytes 393224 | tf_op jit(solution)/shard_map/ppermute | solution.py:503
  97.6 0.1 copy.19.owners
  97.6 0.4 all-to-all-done.2
  98.1 0.1 reduce_sum.30
  98.2 3.8 %collective-permute-done.4.far_mine = bf16[8,160,128]{2,1,0:T(8,128)(2,1)S(1)} collective-permute-done((bf16[8,160,128]{2,1,0:T(8,128)(2,1)S(1)}, bf16[8,160,128]{2,1,0:T(8,128)(2,1)S(1)}, u32[]{:S(2)}, u32[]{:S(2)}) %collective-permute-start.4) | collective-permute-done | bytes 327712 | tf_op jit(solution)/shard_map/ppermute | solution.py:401
  101.9 3.4 %collective-permute-start.5 = (bf16[8,160,128]{2,1,0:T(8,128)(2,1)S(1)}, bf16[8,160,128]{2,1,0:T(8,128)(2,1)S(1)}, u32[]{:S(2)}, u32[]{:S(2)}) collective-permute-start(bf16[8,160,128]{2,1,0:T(8,128)(2,1)S(1)} %collective-permute-done.4.far_mine), channel_id=1, source_target_pairs={{0,8},{8,0},{16,24},{24,16},{32,40},{40,32},{48,56},{56,48},{64,72... | collective-permute-start | bytes 983048 | tf_op jit(solution)/shard_map/ppermute | solution.py:398
  105.4 3.1 %collective-permute-start.10 = (bf16[512,128]{1,0:T(8,128)(2,1)S(1)}, bf16[512,128]{1,0:T(8,128)(2,1)S(1)}, u32[]{:S(2)}, u32[]{:S(2)}) collective-permute-start(bf16[512,128]{1,0:T(8,128)(2,1)S(1)} %broadcast_select_fusion), channel_id=1, source_target_pairs={{0,2},{1,3},{8,10},{9,11},{16,18},{17,19},{24,26},{25,27},{33,35},... | collective-permute-start | bytes 393224 | tf_op jit(solution)/shard_map/ppermute | solution.py:512
  108.5 2.2 %collective-permute-start.11 = (bf16[512,128]{1,0:T(8,128)(2,1)S(1)}, bf16[512,128]{1,0:T(8,128)(2,1)S(1)}, u32[]{:S(2)}, u32[]{:S(2)}) collective-permute-start(bf16[512,128]{1,0:T(8,128)(2,1)S(1)} %broadcast_select_fusion), channel_id=1, source_target_pairs={{0,4},{1,5},{8,12},{9,13},{16,20},{17,21},{24,28},{25,29},{33,37},... | collective-permute-start | bytes 393224 | tf_op jit(solution)/shard_map/ppermute | solution.py:512
  110.7 1.3 collective-permute-start.12
  112.0 8.2 %all-gather = bf16[2048,128]{1,0:T(8,128)(2,1)S(1)} all-gather(bf16[512,128]{1,0:T(8,128)(2,1)S(1)} %reduce_sum.30), channel_id=2, replica_groups={{0,8,16,24},{32,40,48,56},{64,72,80,88},{96,104,112,120},{128,136,144,1..., dimensions={0}, use_global_device_ids=true | all-gather | bytes 655360 | tf_op jit(solution)/shard_map/all_gather | solution.py:549
  120.2 3.8 %new_blocks.1 = (bf16[512,512]{1,0:T(8,128)(2,1)S(1)}, f32[512,512]{1,0:T(8,128)}, f32[512,512]{1,0:T(8,128)}) custom-call(s32[8,2]{1,0:T(8,128)S(1)} %copy.19.owners, bf16[8,160,128]{2,1,0:T(8,128)(2,1)S(1)} %all-to-all-done.1.mine, bf16[8,160,128]{2,1,0:T(8,128)(2,1)S(1)} %collective-permute-done.3.other, ...), custom_call_target="tpu_custom_call" | custom-call | flops 1073741824 | bytes 6291456 | tf_op jit(solution)/shard_map/new_blocks/pallas_call | solution.py:525
  124.0 0.8 precondition.1
  124.8 11.2 %all_to_all.25 = f32[16,8,128]{2,1,0:T(8,128)S(1)} all-to-all(f32[16,8,128]{2,1,0:T(8,128)S(1)} %broadcast_in_dim.14), channel_id=1, replica_groups={{0,8,16,24,32,40,48,56,64,72,80,88,96,104,112,120},{128,136,144,152,160..., dimensions={0} | all-to-all | bytes 131072 | tf_op jit(solution)/shard_map/all_to_all | solution.py:559
  136.0 13.6 %all_to_all.26 = f32[16,8,128]{2,1,0:T(8,128)S(1)} all-to-all(f32[16,8,128]{2,1,0:T(8,128)S(1)} %broadcast_in_dim.15), channel_id=1, replica_groups={{0,1,2,3,4,5,6,7,128,129,130,131,132,133,134,135},{8,9,10,11,12,13,14,1..., dimensions={0} | all-to-all | bytes 131072 | tf_op jit(solution)/shard_map/all_to_all | solution.py:567
  149.7 0.5 slice.3
  150.9 0.7 broadcast_multiply_fusion
  (23 shorter events, 0.2 us)
Async XLA Ops:
  2.0 1.2 copy-start.1
  8.2 6.8 %collective-permute-start = (bf16[16,288,128]{2,1,0:T(8,128)(2,1)}, bf16[16,288,128]{2,1,0:T(8,128)(2,1)S(1)}, u32[]{:S(2)}, u32[]{:S(2)}) collective-permute-start(bf16[16,288,128]{2,1,0:T(8,128)(2,1)} %get-tuple-element.19), channel_id=1, source_target_pairs={{0,8},{8,0},{16,24},{24,16},{32,40},{40,32},{48,56},{56,48},{64,72... | collective-permute-start | bytes 3538952 | tf_op jit(solution)/shard_map/ppermute | solution.py:398
  14.8 6.4 %collective-permute-start.2 = (bf16[8,512,128]{2,1,0:T(8,128)(2,1)S(1)}, bf16[8,512,128]{2,1,0:T(8,128)(2,1)S(1)}, u32[]{:S(2)}, u32[]{:S(2)}) collective-permute-start(bf16[8,512,128]{2,1,0:T(8,128)(2,1)S(1)} %send_far.1.unread), channel_id=1, source_target_pairs={{0,8},{8,0},{16,24},{24,16},{32,40},{40,32},{48,56},{56,48},{64,72... | collective-permute-start | bytes 3145736 | tf_op jit(solution)/shard_map/ppermute | solution.py:398
  15.7 16.0 %collective-permute-start.1 = (bf16[8,288,128]{2,1,0:T(8,128)(2,1)S(1)}, bf16[8,288,128]{2,1,0:T(8,128)(2,1)S(1)}, u32[]{:S(2)}, u32[]{:S(2)}) collective-permute-start(bf16[8,288,128]{2,1,0:T(8,128)(2,1)S(1)} %get-tuple-element.23.refs_4_), channel_id=1, source_target_pairs={{0,128},{8,136},{16,144},{24,152},{32,160},{40,168},{48,176},{56,1... | collective-permute-start | bytes 1769480 | tf_op jit(solution)/shard_map/ppermute | solution.py:401
  20.4 42.5 %collective-permute-start.6 = (bf16[8,512,128]{2,1,0:T(8,128)(2,1)S(1)}, bf16[8,512,128]{2,1,0:T(8,128)(2,1)}, u32[]{:S(2)}, u32[]{:S(2)}) collective-permute-start(bf16[8,512,128]{2,1,0:T(8,128)(2,1)S(1)} %send_near.1.other_unread), channel_id=1, source_target_pairs={{0,8},{8,0},{16,24},{24,16},{32,40},{40,32},{48,56},{56,48},{64,72... | collective-permute-start | bytes 3145736 | tf_op jit(solution)/shard_map/ppermute | solution.py:398
  32.4 0.8 copy-start
  33.2 24.4 %all-to-all-start = ((bf16[8,288,128]{2,1,0:T(8,128)(2,1)}), bf16[8,288,128]{2,1,0:T(8,128)(2,1)}, u32[]{:S(2)}, u32[]{:S(2)}) async-start(bf16[8,288,128]{2,1,0:T(8,128)(2,1)} %copy-done), calls=%async_computation | async-start | bytes 1179648 | tf_op jit(solution)/shard_map/all_to_all | solution.py:395
  39.7 26.8 %collective-permute-start.7 = (bf16[8,512,128]{2,1,0:T(8,128)(2,1)S(1)}, bf16[8,512,128]{2,1,0:T(8,128)(2,1)}, u32[]{:S(2)}, u32[]{:S(2)}) collective-permute-start(bf16[8,512,128]{2,1,0:T(8,128)(2,1)S(1)} %gradient_far.1.unread), channel_id=1, source_target_pairs={{0,128},{8,136},{16,144},{24,152},{32,160},{40,168},{48,176},{56,1... | collective-permute-start | bytes 3145736 | tf_op jit(solution)/shard_map/ppermute | solution.py:401
  58.8 0.7 copy-start.2
  59.5 24.2 %all-to-all-start.1 = ((bf16[8,160,128]{2,1,0:T(8,128)(2,1)}), bf16[8,160,128]{2,1,0:T(8,128)(2,1)S(1)}, u32[]{:S(2)}, u32[]{:S(2)}) async-start(bf16[8,160,128]{2,1,0:T(8,128)(2,1)} %copy-done.2), calls=%async_computation.1 | async-start | bytes 655360 | tf_op jit(solution)/shard_map/all_to_all | solution.py:395
  67.9 29.6 %copy-start.3 = (s32[8,2]{0,1:T(2,128)S(1)}, s32[8,2]{0,1:T(2,128)}, u32[]{:S(2)}) copy-start(s32[8,2]{0,1:T(2,128)} %param.13) | copy-start | bytes 196
  67.9 15.0 %collective-permute-start.8 = (bf16[4,512,128]{2,1,0:T(8,128)(2,1)S(1)}, bf16[4,512,128]{2,1,0:T(8,128)(2,1)S(1)}, u32[]{:S(2)}, u32[]{:S(2)}) collective-permute-start(bf16[4,512,128]{2,1,0:T(8,128)(2,1)S(1)} %get-tuple-element.29), channel_id=1, source_target_pairs={{0,16},{8,24},{16,0},{24,8},{32,48},{40,56},{48,32},{56,40},{64,80... | collective-permute-start | bytes 1572872 | tf_op jit(solution)/shard_map/ppermute | solution.py:541
  83.8 14.3 %all-to-all-start.2 = ((bf16[4,512,128]{2,1,0:T(8,128)(2,1)}), bf16[4,512,128]{2,1,0:T(8,128)(2,1)S(1)}, u32[]{:S(2)}, u32[]{:S(2)}) async-start(bf16[4,512,128]{2,1,0:T(8,128)(2,1)} %add_pair.1), calls=%async_computation.2 | async-start | bytes 1048576 | tf_op jit(solution)/shard_map/all_to_all | solution.py:546
  88.6 5.3 %collective-permute-start.3 = (bf16[8,160,128]{2,1,0:T(8,128)(2,1)S(1)}, bf16[8,160,128]{2,1,0:T(8,128)(2,1)S(1)}, u32[]{:S(2)}, u32[]{:S(2)}) collective-permute-start(bf16[8,160,128]{2,1,0:T(8,128)(2,1)S(1)} %all-to-all-done.1.mine), channel_id=1, source_target_pairs={{0,8},{8,0},{16,24},{24,16},{32,40},{40,32},{48,56},{56,48},{64,72... | collective-permute-start | bytes 983048 | tf_op jit(solution)/shard_map/ppermute | solution.py:398
  91.1 10.8 %collective-permute-start.4 = (bf16[8,160,128]{2,1,0:T(8,128)(2,1)S(1)}, bf16[8,160,128]{2,1,0:T(8,128)(2,1)S(1)}, u32[]{:S(2)}, u32[]{:S(2)}) collective-permute-start(bf16[8,160,128]{2,1,0:T(8,128)(2,1)S(1)} %all-to-all-done.1.mine), channel_id=1, source_target_pairs={{0,128},{8,136},{16,144},{24,152},{32,160},{40,168},{48,176},{56,1... | collective-permute-start | bytes 983048 | tf_op jit(solution)/shard_map/ppermute | solution.py:401
  95.2 10.1 %collective-permute-start.9 = (bf16[512,128]{1,0:T(8,128)(2,1)S(1)}, bf16[512,128]{1,0:T(8,128)(2,1)S(1)}, u32[]{:S(2)}, u32[]{:S(2)}) collective-permute-start(bf16[512,128]{1,0:T(8,128)(2,1)S(1)} %left_columns.1), channel_id=1, source_target_pairs={{0,1},{8,9},{16,17},{24,25},{33,32},{41,40},{49,48},{57,56},{66,67... | collective-permute-start | bytes 393224 | tf_op jit(solution)/shard_map/ppermute | solution.py:503
  101.9 18.3 %collective-permute-start.5 = (bf16[8,160,128]{2,1,0:T(8,128)(2,1)S(1)}, bf16[8,160,128]{2,1,0:T(8,128)(2,1)S(1)}, u32[]{:S(2)}, u32[]{:S(2)}) collective-permute-start(bf16[8,160,128]{2,1,0:T(8,128)(2,1)S(1)} %collective-permute-done.4.far_mine), channel_id=1, source_target_pairs={{0,8},{8,0},{16,24},{24,16},{32,40},{40,32},{48,56},{56,48},{64,72... | collective-permute-start | bytes 983048 | tf_op jit(solution)/shard_map/ppermute | solution.py:398
  105.4 14.8 %collective-permute-start.10 = (bf16[512,128]{1,0:T(8,128)(2,1)S(1)}, bf16[512,128]{1,0:T(8,128)(2,1)S(1)}, u32[]{:S(2)}, u32[]{:S(2)}) collective-permute-start(bf16[512,128]{1,0:T(8,128)(2,1)S(1)} %broadcast_select_fusion), channel_id=1, source_target_pairs={{0,2},{1,3},{8,10},{9,11},{16,18},{17,19},{24,26},{25,27},{33,35},... | collective-permute-start | bytes 393224 | tf_op jit(solution)/shard_map/ppermute | solution.py:512
  108.5 11.7 %collective-permute-start.11 = (bf16[512,128]{1,0:T(8,128)(2,1)S(1)}, bf16[512,128]{1,0:T(8,128)(2,1)S(1)}, u32[]{:S(2)}, u32[]{:S(2)}) collective-permute-start(bf16[512,128]{1,0:T(8,128)(2,1)S(1)} %broadcast_select_fusion), channel_id=1, source_target_pairs={{0,4},{1,5},{8,12},{9,13},{16,20},{17,21},{24,28},{25,29},{33,37},... | collective-permute-start | bytes 393224 | tf_op jit(solution)/shard_map/ppermute | solution.py:512
  110.7 9.5 %collective-permute-start.12 = (bf16[512,128]{1,0:T(8,128)(2,1)S(1)}, bf16[512,128]{1,0:T(8,128)(2,1)S(1)}, u32[]{:S(2)}, u32[]{:S(2)}) collective-permute-start(bf16[512,128]{1,0:T(8,128)(2,1)S(1)} %broadcast_select_fusion), channel_id=1, source_target_pairs={{0,6},{1,7},{8,14},{9,15},{16,22},{17,23},{24,30},{25,31},{33,39},... | collective-permute-start | bytes 393224 | tf_op jit(solution)/shard_map/ppermute | solution.py:512

commit v9 on v7

--- a/solution.py
+++ b/solution.py
@@ -31,6 +31,10 @@
     return (slice(a * TILE, (a + 1) * TILE), slice(b * TILE, (b + 1) * TILE))
 
 
+def turn_of(core):
+    return core * (lax.axis_size("dp") // 8)
+
+
 class Facts:
     def __init__(self, old_owner=None, new_owner=None):
         member = lax.axis_index("dp")
@@ -38,6 +42,7 @@
         chips = lax.axis_size("dp") // 2
         self.core = member & 1
         self.plane = jnp.where(member >= chips, 1, 0)
+        self.turn = turn_of(self.core)
         self.place = member & (lax.axis_size("dp") // lax.axis_size("mp") - 1)
         self.flip = jnp.where(self.column >= lax.axis_size("mp") // 2, 1, 0)
         self.own_kind = self.plane ^ self.flip
@@ -48,7 +53,7 @@
             self.same_plane = [
                 jnp.where(jnp.where(o >= chips, 1, 0) == self.plane, 1, 0) for o in owners
             ]
-            self.ring_at = [lax.shift_right_logical(o & (chips - 1), 1) for o in owners]
+            self.slots = [lax.shift_right_logical(o & (chips - 1), 1) ^ self.turn for o in owners]
         if new_owner is not None:
             self.keeps = [
                 jnp.where(new_owner[self.column, kind] == member, 1, 0) for kind in range(2)
@@ -171,24 +176,26 @@
     ring, rows = near_old.shape[0], near_old.shape[1]
     data = rows // 6 * 5
 
-    @pl.when(flag == 1)
-    def _():
-        out[:, :data, :] = near_old[:, :data, :]
-
-    @pl.when(flag == 0)
-    def _():
-        out[:, :data, :] = arrived[:, :data, :]
-
     words = merge_words(first, second, near_old[0, data:, :], arrived[0, data:rows, :]).astype(BF16)
-    for z in range(ring):
-        out[z, data:rows, :] = words
-    out[:, rows:, :] = (near_sum[...] + arrived[:, rows:, :].astype(F32)).astype(BF16)
+    for slot in range(ring):
+        z = slot ^ facts.turn
+
+        @pl.when(flag == 1)
+        def _():
+            out[slot, :data, :] = near_old[z, :data, :]
+
+        @pl.when(flag == 0)
+        def _():
+            out[slot, :data, :] = arrived[z, :data, :]
+
+        out[slot, data:rows, :] = words
+        out[slot, rows:, :] = (near_sum[z] + arrived[z, rows:, :].astype(F32)).astype(BF16)
 
 
 def make_shares(owners, arrived, shares, diag):
     facts = Facts(owners)
     own_kind = facts.own_kind
-    first, second = facts.ring_at
+    first, second = facts.slots
     ring, rows = shares.shape[0], shares.shape[1]
     share = rows // 2
     words = rows // 5 + rows
@@ -224,14 +231,22 @@
         out[n] = total.astype(out.dtype)
 
 
+def add_planes(near, arrived, out):
+    turn = Facts().turn
+    for slot in range(out.shape[0]):
+        z = slot ^ turn
+        out[slot] = (near[z] + arrived[z].astype(F32)).astype(BF16)
+
+
 def unpack(mine, other, core, packed):
     share = mine.shape[1] // 2
-    for pair in range(mine.shape[0]):
+    for slot in range(mine.shape[0]):
         for ref, parity in ((mine, core), (other, 1 - core)):
+            pair = slot ^ turn_of(parity)
             start = pl.multiple_of((2 * pair + parity) * share, ROWS)
             for which in range(2):
                 packed[which, pl.ds(start, share), :] = ref[
-                    pair, which * share : (which + 1) * share, :
+                    slot, which * share : (which + 1) * share, :
                 ]
 
 
@@ -370,7 +385,9 @@
     core = member & 1
     core_swap = [(i, i ^ 1) for i in range(members)]
     plane_swap = [(i, (i + chips) % members) for i in range(members)]
-    rings = [[y * chips + 2 * z + c for z in range(ring)] for y in range(2) for c in range(2)]
+    rings = [
+        [y * chips + 2 * (z ^ turn_of(c)) + c for z in range(ring)] for y in range(2) for c in range(2)
+    ]
     packed_rows = width * (width + TILE) // 2 // TILE
     share = 2 * packed_rows // members
     lanes = width // TILE
@@ -515,7 +532,11 @@
         moved=6 * megabyte,
     )(new_owner, mine, other, far_mine, far_other, diag)
 
-    grad = across_ring((near_grad + arrived_grad.astype(F32)).astype(BF16))
+    grad = across_ring(
+        kernel_call(add_planes, shape(far_grad.shape, BF16), [WHOLE] * 2, moved=4 * megabyte)(
+            near_grad, arrived_grad
+        )
+    )
     grad = jnp.sum(grad.astype(F32), axis=0).astype(BF16)
     neighbours = [[holders * c + r for r in range(holders)] for c in range(columns)]
     grads = lax.all_gather(grad, "dp", axis=0, axis_index_groups=neighbours)

time: 142 us -> 143 us (level)
  starting transfers between devices: 37.8 us -> 45.7 us
  waiting for transfers between devices: 32.6 us -> 25.9 us
  other arithmetic: 3.68 us -> 1.25 us
  Pallas kernels: 26.9 us -> 29.2 us
    all_to_all x3, starting transfers between devices: 13.5 us -> 26.6 us  [across_ring(): lax.all_to_all(parts, 'dp', 0, 0, tiled=True, axis_index_groups=rings)]
    all_to_all x3, waiting for transfers between devices: 18.2 us -> 11.7 us  [across_ring(): lax.all_to_all(parts, 'dp', 0, 0, tiled=True, axis_index_groups=rings)]
    ppermute x5, starting transfers between devices: 9.73 us -> 4.7 us  [swap_cores(): return lax.ppermute(send, 'dp', core_swap)]
    convert_element_type x1 -> x0, other arithmetic: 2.43 us -> none  [local(): grad = across_ring((near_grad + arrived_grad.astype(F32)).astype(BF16))]
    pallas_call x0 -> x1, Pallas kernels: none -> 2.4 us  [local(): kernel_call(add_planes, shape(far_grad.shape, BF16), [WHOLE] * 2, moved=4...]
    all_to_all x1, blocking collectives: 10.4 us -> 12.6 us  [local(): lax.all_to_all(jnp.broadcast_to(curvature, (chips, 8, TILE)), 'dp', 0, 0,...]
  transfers between devices with their start and end apart: 15 -> 15, of which waited for: 11 -> 8; matrix products, arithmetic and copies ran while one was open for 2% -> 0% of each run, Pallas kernels for 15% -> 16%
where the time goes in v9:
time: 143 us; the launch traced here: 142 us
  starting transfers between devices  45.7 us (32%)
  blocking collectives  33.7 us (24%)
  Pallas kernels  29.2 us (20%)
  waiting for transfers between devices  25.9 us (18%)
  local copies, waits for them, and re-layouts  4.12 us (3%)
  between operations  2.18 us (2%)
    all_to_all x3, starting transfers between devices, across_ring(): lax.all_to_all(parts, 'dp', 0, 0, tiled=True, axis_index_groups=rings)  26.6 us
    pallas_call x4, Pallas kernels, gradient(): pl.pallas_call(body, out_shape=shape((ring, width, TILE), dtype), grid_sp...  13.4 us
    all_to_all x1, blocking collectives, local(): lax.all_to_all(jnp.broadcast_to(curvature, (2 * columns, 8, TILE)), ('dp'...  13 us
    all_to_all x1, blocking collectives, local(): lax.all_to_all(jnp.broadcast_to(curvature, (chips, 8, TILE)), 'dp', 0, 0,...  12.6 us
    all_to_all x3, waiting for transfers between devices, across_ring(): lax.all_to_all(parts, 'dp', 0, 0, tiled=True, axis_index_groups=rings)  11.7 us
    ppermute x3, waiting for transfers between devices, swap_planes(): return lax.ppermute(send, 'dp', plane_swap)  8.63 us
    all_gather x1, blocking collectives, local(): grads = lax.all_gather(grad, 'dp', axis=0, axis_index_groups=neighbours)  8.05 us
    ppermute x3, starting transfers between devices, local(): lax.ppermute(left, ('dp', 'mp'), [(i * columns + g, i * columns + (g + 2...  6.57 us
  transfers between devices with their start and end apart: 15, of which 8 were waited for; matrix products, arithmetic and copies ran while one was open for 0% of the time, Pallas kernels for 16%

profile of v9, /device:TPU:1, one launch (start us, length us, event | category | flops | bytes accessed | tf_op | source)
XLA Modules:
  0.0 141.9 jit_solution(8422327622062591321)
XLA Ops:
  1.3 0.8 copy.18.owners
  2.0 1.2 copy-done.1
  3.3 4.9 %first_parts.1 = (bf16[16,288,128]{2,1,0:T(8,128)(2,1)S(1)}, bf16[16,288,128]{2,1,0:T(8,128)(2,1)}, bf16[512,1024]{1,0:T(8,128)(2,1)S(1)}) custom-call(s32[8,2]{1,0:T(8,128)S(1)} %copy.18.owners, s32[1]{0:T(128)S(6)} %copy.20.counts.refs_4_, bf16[1024,4096]{1,0:T(8,128)(2,1)} %refs_3_.7, bf16[1024,512]{1,0:T(8,128)(2,1)S(1)} %copy-done.1, ...), custom_call_target="tpu_custom_call" | custom-call | flops 1073741824 | bytes 10485760 | tf_op jit(solution)/shard_map/first_parts/pallas_call | solution.py:408
  8.2 3.3 %collective-permute-start = (bf16[16,288,128]{2,1,0:T(8,128)(2,1)}, bf16[16,288,128]{2,1,0:T(8,128)(2,1)S(1)}, u32[]{:S(2)}, u32[]{:S(2)}) collective-permute-start(bf16[16,288,128]{2,1,0:T(8,128)(2,1)} %get-tuple-element.17), channel_id=1, source_target_pairs={{0,8},{8,0},{16,24},{24,16},{32,40},{40,32},{48,56},{56,48},{64,72... | collective-permute-start | bytes 3538952 | tf_op jit(solution)/shard_map/ppermute | solution.py:402
  11.5 0.1 pad_add_fusion.1.scalars
  11.6 3.3 %send_far.1.unread = bf16[8,512,128]{2,1,0:T(8,128)(2,1)S(1)} custom-call(s32[2]{0:T(128)S(1)} %pad_add_fusion.1.scalars, bf16[512,1024]{1,0:T(8,128)(2,1)S(1)} %get-tuple-element.18.turned, bf16[1024,4096]{1,0:T(8,128)(2,1)} %refs_3_.7, bf16[1024,4096]{1,0:T(8,128)(2,1)} %refs_3_.7, bf16[1024,4096]{1,0:T(8,128)(2,1)} %refs_3_.7, ...), custom_call_target="tpu_custom_call" | custom-call | flops 1073741824 | bytes 4194304 | tf_op jit(solution)/shard_map/send_far/pallas_call | solution.py:434
  14.9 0.1 collective-permute-start.2
  15.0 0.8 choose_core.1
  15.7 1.3 collective-permute-start.1
  17.0 0.1 pad_add_fusion.2.scalars
  17.1 0.1 pad_add_fusion.scalars
  17.1 0.5 collective-permute-done.2.refs_4_
  17.6 3.3 %gradient_far.1.unread = bf16[8,512,128]{2,1,0:T(8,128)(2,1)S(1)} custom-call(s32[2]{0:T(128)S(1)} %pad_add_fusion.scalars, bf16[512,1024]{1,0:T(8,128)(2,1)S(1)} %get-tuple-element.18.turned, bf16[1024,4096]{1,0:T(8,128)(2,1)} %refs_3_.7, bf16[1024,4096]{1,0:T(8,128)(2,1)} %refs_3_.7, bf16[1024,4096]{1,0:T(8,128)(2,1)} %refs_3_.7, ...), custom_call_target="tpu_custom_call" | custom-call | flops 1073741824 | bytes 4194304 | tf_op jit(solution)/shard_map/gradient_far/pallas_call | solution.py:434
  20.9 3.3 %send_near.1.other_unread = bf16[8,512,128]{2,1,0:T(8,128)(2,1)S(1)} custom-call(s32[2]{0:T(128)S(1)} %pad_add_fusion.2.scalars, bf16[512,1024]{1,0:T(8,128)(2,1)S(1)} %get-tuple-element.18.turned, bf16[1024,4096]{1,0:T(8,128)(2,1)} %refs_3_.7, bf16[1024,4096]{1,0:T(8,128)(2,1)} %refs_3_.7, bf16[1024,4096]{1,0:T(8,128)(2,1)} %refs_3_.7, ...), custom_call_target="tpu_custom_call" | custom-call | flops 1073741824 | bytes 4194304 | tf_op jit(solution)/shard_map/send_near/pallas_call | solution.py:434
  24.2 7.5 %collective-permute-done.1.arrived = bf16[8,288,128]{2,1,0:T(8,128)(2,1)S(1)} collective-permute-done((bf16[8,288,128]{2,1,0:T(8,128)(2,1)S(1)}, bf16[8,288,128]{2,1,0:T(8,128)(2,1)S(1)}, u32[]{:S(2)}, u32[]{:S(2)}) %collective-permute-start.1) | collective-permute-done | bytes 589856 | tf_op jit(solution)/shard_map/ppermute | solution.py:405
  31.7 0.7 join_planes.1
  32.5 0.8 copy-done
  33.3 9.3 %all-to-all-start = ((bf16[8,288,128]{2,1,0:T(8,128)(2,1)}), bf16[8,288,128]{2,1,0:T(8,128)(2,1)}, u32[]{:S(2)}, u32[]{:S(2)}) async-start(bf16[8,288,128]{2,1,0:T(8,128)(2,1)} %copy-done), calls=%async_computation | async-start | bytes 1179648 | tf_op jit(solution)/shard_map/all_to_all | solution.py:399
  42.6 2.9 %collective-permute-start.7 = (bf16[8,512,128]{2,1,0:T(8,128)(2,1)S(1)}, bf16[8,512,128]{2,1,0:T(8,128)(2,1)}, u32[]{:S(2)}, u32[]{:S(2)}) collective-permute-start(bf16[8,512,128]{2,1,0:T(8,128)(2,1)S(1)} %gradient_far.1.unread), channel_id=1, source_target_pairs={{0,128},{8,136},{16,144},{24,152},{32,160},{40,168},{48,176},{56,1... | collective-permute-start | bytes 3145736 | tf_op jit(solution)/shard_map/ppermute | solution.py:405
  45.5 10.0 %all-to-all-done.arrived = bf16[8,288,128]{2,1,0:T(8,128)(2,1)} async-done(((bf16[8,288,128]{2,1,0:T(8,128)(2,1)}), bf16[8,288,128]{2,1,0:T(8,128)(2,1)}, u32[]{:S(2)}, u32[]{:S(2)}) %all-to-all-start) | async-done | bytes 589856 | tf_op jit(solution)/shard_map/all_to_all | solution.py:399
  55.5 1.1 make_shares.1
  56.7 0.7 copy-done.2
  57.4 7.7 %all-to-all-start.1 = ((bf16[8,160,128]{2,1,0:T(8,128)(2,1)}), bf16[8,160,128]{2,1,0:T(8,128)(2,1)S(1)}, u32[]{:S(2)}, u32[]{:S(2)}) async-start(bf16[8,160,128]{2,1,0:T(8,128)(2,1)} %copy-done.2), calls=%async_computation.1 | async-start | bytes 655360 | tf_op jit(solution)/shard_map/all_to_all | solution.py:399
  65.1 0.1 pad_add_fusion.3.scalars
  65.1 3.5 %gradient_near.1.near = f32[8,512,128]{2,1,0:T(8,128)S(1)} custom-call(s32[2]{0:T(128)S(1)} %pad_add_fusion.3.scalars, bf16[512,1024]{1,0:T(8,128)(2,1)S(1)} %get-tuple-element.18.turned, bf16[1024,4096]{1,0:T(8,128)(2,1)} %refs_3_.7, bf16[1024,4096]{1,0:T(8,128)(2,1)} %refs_3_.7, bf16[1024,4096]{1,0:T(8,128)(2,1)} %refs_3_.7, bf16[1024,4096]{1,0:T(8,128)(2,1)} %refs_3_.7, ...), custom_call_target="tpu_custom_call" | custom-call | flops 1073741824 | bytes 4194304 | tf_op jit(solution)/shard_map/gradient_near/pallas_call | solution.py:434
  68.7 2.4 %add_planes.1 = bf16[8,512,128]{2,1,0:T(8,128)(2,1)} custom-call(f32[8,512,128]{2,1,0:T(8,128)S(1)} %gradient_near.1.near, bf16[8,512,128]{2,1,0:T(8,128)(2,1)} %collective-permute-done.7.arrived), custom_call_target="tpu_custom_call" | custom-call | bytes 4194304 | tf_op jit(solution)/shard_map/add_planes/pallas_call | solution.py:536
  71.1 1.7 %all-to-all-done.1.mine = bf16[8,160,128]{2,1,0:T(8,128)(2,1)S(1)} async-done(((bf16[8,160,128]{2,1,0:T(8,128)(2,1)}), bf16[8,160,128]{2,1,0:T(8,128)(2,1)S(1)}, u32[]{:S(2)}, u32[]{:S(2)}) %all-to-all-start.1) | async-done | bytes 327712 | tf_op jit(solution)/shard_map/all_to_all | solution.py:399
  72.7 9.6 %all-to-all-start.2 = ((bf16[8,512,128]{2,1,0:T(8,128)(2,1)}), bf16[8,512,128]{2,1,0:T(8,128)(2,1)S(1)}, u32[]{:S(2)}, u32[]{:S(2)}) async-start(bf16[8,512,128]{2,1,0:T(8,128)(2,1)} %add_planes.1), calls=%async_computation.2 | async-start | bytes 2097152 | tf_op jit(solution)/shard_map/all_to_all | solution.py:399
  82.4 1.6 %collective-permute-done.3.other = bf16[8,160,128]{2,1,0:T(8,128)(2,1)S(1)} collective-permute-done((bf16[8,160,128]{2,1,0:T(8,128)(2,1)S(1)}, bf16[8,160,128]{2,1,0:T(8,128)(2,1)S(1)}, u32[]{:S(2)}, u32[]{:S(2)}) %collective-permute-start.3) | collective-permute-done | bytes 327712 | tf_op jit(solution)/shard_map/ppermute | solution.py:402
  84.0 1.0 left_columns.1
  85.0 3.2 %collective-permute-start.8 = (bf16[512,128]{1,0:T(8,128)(2,1)S(1)}, bf16[512,128]{1,0:T(8,128)(2,1)S(1)}, u32[]{:S(2)}, u32[]{:S(2)}) collective-permute-start(bf16[512,128]{1,0:T(8,128)(2,1)S(1)} %left_columns.1), channel_id=1, source_target_pairs={{0,1},{8,9},{16,17},{24,25},{33,32},{41,40},{49,48},{57,56},{66,67... | collective-permute-start | bytes 393224 | tf_op jit(solution)/shard_map/ppermute | solution.py:504
  88.2 0.4 collective-permute-start.4
  88.7 2.3 %collective-permute-done.8 = bf16[512,128]{1,0:T(8,128)(2,1)S(1)} collective-permute-done((bf16[512,128]{1,0:T(8,128)(2,1)S(1)}, bf16[512,128]{1,0:T(8,128)(2,1)S(1)}, u32[]{:S(2)}, u32[]{:S(2)}) %collective-permute-start.8) | collective-permute-done | bytes 131104 | tf_op jit(solution)/shard_map/ppermute | solution.py:504
  91.0 2.1 %collective-permute-start.11 = (bf16[512,128]{1,0:T(8,128)(2,1)S(1)}, bf16[512,128]{1,0:T(8,128)(2,1)S(1)}, u32[]{:S(2)}, u32[]{:S(2)}) collective-permute-start(bf16[512,128]{1,0:T(8,128)(2,1)S(1)} %broadcast_select_fusion), channel_id=1, source_target_pairs={{0,6},{1,7},{8,14},{9,15},{16,22},{17,23},{24,30},{25,31},{33,39},... | collective-permute-start | bytes 393224 | tf_op jit(solution)/shard_map/ppermute | solution.py:513
  93.1 3.1 %collective-permute-start.10 = (bf16[512,128]{1,0:T(8,128)(2,1)S(1)}, bf16[512,128]{1,0:T(8,128)(2,1)S(1)}, u32[]{:S(2)}, u32[]{:S(2)}) collective-permute-start(bf16[512,128]{1,0:T(8,128)(2,1)S(1)} %broadcast_select_fusion), channel_id=1, source_target_pairs={{0,4},{1,5},{8,12},{9,13},{16,20},{17,21},{24,28},{25,29},{33,37},... | collective-permute-start | bytes 393224 | tf_op jit(solution)/shard_map/ppermute | solution.py:513
  96.3 1.3 collective-permute-start.9
  97.6 1.1 collective-permute-done.4.far_mine
  98.7 1.3 collective-permute-start.5
  100.0 0.1 copy.19.owners
  100.1 1.1 collective-permute-done.9
  101.2 4.0 %new_blocks.1 = (bf16[512,512]{1,0:T(8,128)(2,1)S(1)}, f32[512,512]{1,0:T(8,128)}, f32[512,512]{1,0:T(8,128)}) custom-call(s32[8,2]{1,0:T(8,128)S(1)} %copy.19.owners, bf16[8,160,128]{2,1,0:T(8,128)(2,1)S(1)} %all-to-all-done.1.mine, bf16[8,160,128]{2,1,0:T(8,128)(2,1)S(1)} %collective-permute-done.3.other, ...), custom_call_target="tpu_custom_call" | custom-call | flops 1073741824 | bytes 6291456 | tf_op jit(solution)/shard_map/new_blocks/pallas_call | solution.py:526
  105.3 0.1 reduce_sum.30
  105.4 8.1 %all-gather = bf16[2048,128]{1,0:T(8,128)(2,1)S(1)} all-gather(bf16[512,128]{1,0:T(8,128)(2,1)S(1)} %reduce_sum.30), channel_id=2, replica_groups={{0,8,16,24},{32,40,48,56},{64,72,80,88},{96,104,112,120},{128,136,144,1..., dimensions={0}, use_global_device_ids=true | all-gather | bytes 655360 | tf_op jit(solution)/shard_map/all_gather | solution.py:542
  113.5 0.8 precondition.1
  114.3 12.6 %all_to_all.25 = f32[16,8,128]{2,1,0:T(8,128)S(1)} all-to-all(f32[16,8,128]{2,1,0:T(8,128)S(1)} %broadcast_in_dim.14), channel_id=1, replica_groups={{0,8,16,24,32,40,48,56,64,72,80,88,96,104,112,120},{128,136,144,152,160..., dimensions={0} | all-to-all | bytes 131072 | tf_op jit(solution)/shard_map/all_to_all | solution.py:552
  126.9 13.0 %all_to_all.26 = f32[16,8,128]{2,1,0:T(8,128)S(1)} all-to-all(f32[16,8,128]{2,1,0:T(8,128)S(1)} %broadcast_in_dim.15), channel_id=1, replica_groups={{0,1,2,3,4,5,6,7,128,129,130,131,132,133,134,135},{8,9,10,11,12,13,14,1..., dimensions={0} | all-to-all | bytes 131072 | tf_op jit(solution)/shard_map/all_to_all | solution.py:560
  140.0 0.5 slice.3
  141.2 0.7 broadcast_multiply_fusion
  (20 shorter events, 0.1 us)
Async XLA Ops:
  2.0 1.2 copy-start.1
  8.2 6.8 %collective-permute-start = (bf16[16,288,128]{2,1,0:T(8,128)(2,1)}, bf16[16,288,128]{2,1,0:T(8,128)(2,1)S(1)}, u32[]{:S(2)}, u32[]{:S(2)}) collective-permute-start(bf16[16,288,128]{2,1,0:T(8,128)(2,1)} %get-tuple-element.17), channel_id=1, source_target_pairs={{0,8},{8,0},{16,24},{24,16},{32,40},{40,32},{48,56},{56,48},{64,72... | collective-permute-start | bytes 3538952 | tf_op jit(solution)/shard_map/ppermute | solution.py:402
  14.9 2.7 %collective-permute-start.2 = (bf16[8,512,128]{2,1,0:T(8,128)(2,1)S(1)}, bf16[8,512,128]{2,1,0:T(8,128)(2,1)S(1)}, u32[]{:S(2)}, u32[]{:S(2)}) collective-permute-start(bf16[8,512,128]{2,1,0:T(8,128)(2,1)S(1)} %send_far.1.unread), channel_id=1, source_target_pairs={{0,8},{8,0},{16,24},{24,16},{32,40},{40,32},{48,56},{56,48},{64,72... | collective-permute-start | bytes 3145736 | tf_op jit(solution)/shard_map/ppermute | solution.py:402
  15.7 16.0 %collective-permute-start.1 = (bf16[8,288,128]{2,1,0:T(8,128)(2,1)S(1)}, bf16[8,288,128]{2,1,0:T(8,128)(2,1)S(1)}, u32[]{:S(2)}, u32[]{:S(2)}) collective-permute-start(bf16[8,288,128]{2,1,0:T(8,128)(2,1)S(1)} %get-tuple-element.21.refs_4_), channel_id=1, source_target_pairs={{0,128},{8,136},{16,144},{24,152},{32,160},{40,168},{48,176},{56,1... | collective-permute-start | bytes 1769480 | tf_op jit(solution)/shard_map/ppermute | solution.py:405
  32.5 0.8 copy-start
  33.3 22.2 %all-to-all-start = ((bf16[8,288,128]{2,1,0:T(8,128)(2,1)}), bf16[8,288,128]{2,1,0:T(8,128)(2,1)}, u32[]{:S(2)}, u32[]{:S(2)}) async-start(bf16[8,288,128]{2,1,0:T(8,128)(2,1)} %copy-done), calls=%async_computation | async-start | bytes 1179648 | tf_op jit(solution)/shard_map/all_to_all | solution.py:399
  42.6 22.6 %collective-permute-start.6 = (bf16[8,512,128]{2,1,0:T(8,128)(2,1)S(1)}, bf16[8,512,128]{2,1,0:T(8,128)(2,1)}, u32[]{:S(2)}, u32[]{:S(2)}) collective-permute-start(bf16[8,512,128]{2,1,0:T(8,128)(2,1)S(1)} %send_near.1.other_unread), channel_id=1, source_target_pairs={{0,8},{8,0},{16,24},{24,16},{32,40},{40,32},{48,56},{56,48},{64,72... | collective-permute-start | bytes 3145736 | tf_op jit(solution)/shard_map/ppermute | solution.py:402
  42.6 26.1 %collective-permute-start.7 = (bf16[8,512,128]{2,1,0:T(8,128)(2,1)S(1)}, bf16[8,512,128]{2,1,0:T(8,128)(2,1)}, u32[]{:S(2)}, u32[]{:S(2)}) collective-permute-start(bf16[8,512,128]{2,1,0:T(8,128)(2,1)S(1)} %gradient_far.1.unread), channel_id=1, source_target_pairs={{0,128},{8,136},{16,144},{24,152},{32,160},{40,168},{48,176},{56,1... | collective-permute-start | bytes 3145736 | tf_op jit(solution)/shard_map/ppermute | solution.py:405
  56.6 0.7 copy-start.2
  57.4 15.4 %all-to-all-start.1 = ((bf16[8,160,128]{2,1,0:T(8,128)(2,1)}), bf16[8,160,128]{2,1,0:T(8,128)(2,1)S(1)}, u32[]{:S(2)}, u32[]{:S(2)}) async-start(bf16[8,160,128]{2,1,0:T(8,128)(2,1)} %copy-done.2), calls=%async_computation.1 | async-start | bytes 655360 | tf_op jit(solution)/shard_map/all_to_all | solution.py:399
  71.1 28.9 %copy-start.3 = (s32[8,2]{0,1:T(2,128)S(1)}, s32[8,2]{0,1:T(2,128)}, u32[]{:S(2)}) copy-start(s32[8,2]{0,1:T(2,128)} %param.13) | copy-start | bytes 196
  72.7 32.5 %all-to-all-start.2 = ((bf16[8,512,128]{2,1,0:T(8,128)(2,1)}), bf16[8,512,128]{2,1,0:T(8,128)(2,1)S(1)}, u32[]{:S(2)}, u32[]{:S(2)}) async-start(bf16[8,512,128]{2,1,0:T(8,128)(2,1)} %add_planes.1), calls=%async_computation.2 | async-start | bytes 2097152 | tf_op jit(solution)/shard_map/all_to_all | solution.py:399
  82.4 1.6 %collective-permute-start.3 = (bf16[8,160,128]{2,1,0:T(8,128)(2,1)S(1)}, bf16[8,160,128]{2,1,0:T(8,128)(2,1)S(1)}, u32[]{:S(2)}, u32[]{:S(2)}) collective-permute-start(bf16[8,160,128]{2,1,0:T(8,128)(2,1)S(1)} %all-to-all-done.1.mine), channel_id=1, source_target_pairs={{0,8},{8,0},{16,24},{24,16},{32,40},{40,32},{48,56},{56,48},{64,72... | collective-permute-start | bytes 983048 | tf_op jit(solution)/shard_map/ppermute | solution.py:402
  85.0 5.9 %collective-permute-start.8 = (bf16[512,128]{1,0:T(8,128)(2,1)S(1)}, bf16[512,128]{1,0:T(8,128)(2,1)S(1)}, u32[]{:S(2)}, u32[]{:S(2)}) collective-permute-start(bf16[512,128]{1,0:T(8,128)(2,1)S(1)} %left_columns.1), channel_id=1, source_target_pairs={{0,1},{8,9},{16,17},{24,25},{33,32},{41,40},{49,48},{57,56},{66,67... | collective-permute-start | bytes 393224 | tf_op jit(solution)/shard_map/ppermute | solution.py:504
  88.2 10.4 %collective-permute-start.4 = (bf16[8,160,128]{2,1,0:T(8,128)(2,1)S(1)}, bf16[8,160,128]{2,1,0:T(8,128)(2,1)S(1)}, u32[]{:S(2)}, u32[]{:S(2)}) collective-permute-start(bf16[8,160,128]{2,1,0:T(8,128)(2,1)S(1)} %all-to-all-done.1.mine), channel_id=1, source_target_pairs={{0,128},{8,136},{16,144},{24,152},{32,160},{40,168},{48,176},{56,1... | collective-permute-start | bytes 983048 | tf_op jit(solution)/shard_map/ppermute | solution.py:405
  91.0 9.1 %collective-permute-start.11 = (bf16[512,128]{1,0:T(8,128)(2,1)S(1)}, bf16[512,128]{1,0:T(8,128)(2,1)S(1)}, u32[]{:S(2)}, u32[]{:S(2)}) collective-permute-start(bf16[512,128]{1,0:T(8,128)(2,1)S(1)} %broadcast_select_fusion), channel_id=1, source_target_pairs={{0,6},{1,7},{8,14},{9,15},{16,22},{17,23},{24,30},{25,31},{33,39},... | collective-permute-start | bytes 393224 | tf_op jit(solution)/shard_map/ppermute | solution.py:513
  93.1 6.9 %collective-permute-start.10 = (bf16[512,128]{1,0:T(8,128)(2,1)S(1)}, bf16[512,128]{1,0:T(8,128)(2,1)S(1)}, u32[]{:S(2)}, u32[]{:S(2)}) collective-permute-start(bf16[512,128]{1,0:T(8,128)(2,1)S(1)} %broadcast_select_fusion), channel_id=1, source_target_pairs={{0,4},{1,5},{8,12},{9,13},{16,20},{17,21},{24,28},{25,29},{33,37},... | collective-permute-start | bytes 393224 | tf_op jit(solution)/shard_map/ppermute | solution.py:513
  96.3 4.9 %collective-permute-start.9 = (bf16[512,128]{1,0:T(8,128)(2,1)S(1)}, bf16[512,128]{1,0:T(8,128)(2,1)S(1)}, u32[]{:S(2)}, u32[]{:S(2)}) collective-permute-start(bf16[512,128]{1,0:T(8,128)(2,1)S(1)} %broadcast_select_fusion), channel_id=1, source_target_pairs={{0,2},{1,3},{8,10},{9,11},{16,18},{17,19},{24,26},{25,27},{33,35},... | collective-permute-start | bytes 393224 | tf_op jit(solution)/shard_map/ppermute | solution.py:513
  98.7 2.5 %collective-permute-start.5 = (bf16[8,160,128]{2,1,0:T(8,128)(2,1)S(1)}, bf16[8,160,128]{2,1,0:T(8,128)(2,1)S(1)}, u32[]{:S(2)}, u32[]{:S(2)}) collective-permute-start(bf16[8,160,128]{2,1,0:T(8,128)(2,1)S(1)} %collective-permute-done.4.far_mine), channel_id=1, source_target_pairs={{0,8},{8,0},{16,24},{24,16},{32,40},{40,32},{48,56},{56,48},{64,72... | collective-permute-start | bytes 983048 | tf_op jit(solution)/shard_map/ppermute | solution.py:402

commit v10 on v7

--- a/solution.py
+++ b/solution.py
@@ -1,3 +1,5 @@
+import functools
+
 import jax
 import jax.numpy as jnp
 from jax import lax
@@ -29,6 +31,12 @@
 
 def tile_of(a, b):
     return (slice(a * TILE, (a + 1) * TILE), slice(b * TILE, (b + 1) * TILE))
+
+
+def clip(entries, result, partials, update):
+    curvature = jnp.sum(partials[...], axis=0)[:1, :1]
+    scale = jnp.minimum(1.0, jnp.sqrt(entries / jnp.abs(curvature)))
+    update[...] = scale * result[...]
 
 
 class Facts:
@@ -109,13 +117,19 @@
                 packed[kind, which, n * TILE : (n + 1) * TILE, :] = piece.astype(BF16)
     high = diag[...].astype(BF16)
     low = (diag[...] - high.astype(F32)).astype(BF16)
-    words = jnp.concatenate([high, low], axis=0)
+    words = []
+    for kind in range(2):
+        ends = [((which * 2 + kind) * tiles, (which * 2 + kind + 1) * tiles) for which in range(2)]
+        words.append(jnp.concatenate([w[a:b].astype(F32) for w in (high, low) for a, b in ends], axis=0))
     quarter = lax.broadcasted_iota(jnp.int32, (ROWS, TILE), 0) // 4
     digits = lax.shift_right_logical(jnp.full((ROWS, TILE), count), 3 * quarter) & 7
     digits = digits.astype(F32).astype(BF16)
     chips = keep.shape[0]
-    share = (keep.shape[1] - words.shape[0] - ROWS) // 3
-    sums = 2 * share + words.shape[0]
+    share = (keep.shape[1] - 4 * tiles - ROWS) // 3
+    sums = 2 * share + 4 * tiles
+    of_plane = [
+        jnp.where(flip == first, words[0], words[1]).astype(BF16) for first in range(2)
+    ]
     for q in range(chips):
         plane, pair = divmod(q, chips // 2)
         kind = flip if plane == 0 else 1 - flip
@@ -123,40 +137,29 @@
             start = pl.multiple_of((2 * pair + parity) * share, ROWS)
             for which, at in enumerate((0, share, sums)):
                 ref[q, at : at + share, :] = packed[kind, which, pl.ds(start, share), :]
-            ref[q, 2 * share : sums, :] = words
+            ref[q, 2 * share : sums, :] = of_plane[plane]
             ref[q, sums + share :, :] = digits
-
-
-def merge_words(first_flag, second_flag, one, two):
-    lanes = one.shape[0] // 8
-    kinds = (lax.broadcasted_iota(jnp.int32, one.shape, 0) // lanes) % 2
-    flags = jnp.where(kinds == 0, first_flag, second_flag)
-    return jnp.where(flags == 1, one.astype(F32), two.astype(F32))
 
 
 def choose_core(owners, keep, received, unread, near_old, near_sum, far):
     facts = Facts(owners)
     first, second = facts.same_core
     ring, rows = near_old.shape[0], near_old.shape[1]
-    data = rows // 6 * 5
-    words = merge_words(first, second, keep[0, data:rows, :], received[0, data:rows, :]).astype(BF16)
     for old, at, kind in (
         (near_old, facts.plane, facts.own_kind),
         (far, 1 - facts.plane, 1 - facts.own_kind),
     ):
         flag = jnp.where(kind == 0, first, second)
+        chips = pl.ds(at * ring, ring)
 
         @pl.when(flag == 1)
         def _():
-            old[:, :data, :] = keep[pl.ds(at * ring, ring), :data, :]
+            old[:, :rows, :] = keep[chips, :rows, :]
 
         @pl.when(flag == 0)
         def _():
-            old[:, :data, :] = received[pl.ds(at * ring, ring), :data, :]
-
-        for z in range(ring):
-            old[z, data:rows, :] = words
-        chips = pl.ds(at * ring, ring)
+            old[:, :rows, :] = received[chips, :rows, :]
+
         total = keep[chips, rows:, :].astype(F32) + received[chips, rows:, :].astype(F32)
         if old is far:
             far[:, rows:, :] = total.astype(BF16)
@@ -168,34 +171,28 @@
     facts = Facts(owners)
     first, second = facts.same_plane
     flag = jnp.where(facts.own_kind == 0, first, second)
-    ring, rows = near_old.shape[0], near_old.shape[1]
-    data = rows // 6 * 5
+    rows = near_old.shape[1]
 
     @pl.when(flag == 1)
     def _():
-        out[:, :data, :] = near_old[:, :data, :]
+        out[:, :rows, :] = near_old[...]
 
     @pl.when(flag == 0)
     def _():
-        out[:, :data, :] = arrived[:, :data, :]
-
-    words = merge_words(first, second, near_old[0, data:, :], arrived[0, data:rows, :]).astype(BF16)
-    for z in range(ring):
-        out[z, data:rows, :] = words
+        out[:, :rows, :] = arrived[:, :rows, :]
+
     out[:, rows:, :] = (near_sum[...] + arrived[:, rows:, :].astype(F32)).astype(BF16)
 
 
 def make_shares(owners, arrived, shares, diag):
     facts = Facts(owners)
-    own_kind = facts.own_kind
-    first, second = facts.ring_at
     ring, rows = shares.shape[0], shares.shape[1]
-    share = rows // 2
-    words = rows // 5 + rows
-    owner = jnp.where(own_kind == 0, first, second)
-    both = merge_words(1, 0, arrived[first, rows:words, :], arrived[second, rows:words, :])
-    diag[...] = both[: diag.shape[0]] + both[diag.shape[0] :]
-    summed = sum(arrived[z, words:, :].astype(F32) for z in range(ring))
+    share, lanes = rows // 2, diag.shape[0]
+    sums = rows + 2 * lanes
+    owner = jnp.where(facts.own_kind == 0, facts.ring_at[0], facts.ring_at[1])
+    words = arrived[owner, rows:sums, :].astype(F32)
+    diag[...] = words[:lanes] + words[lanes:]
+    summed = sum(arrived[z, sums:, :].astype(F32) for z in range(ring))
     total = sum(summed[share + 4 * d : share + 4 * d + 1, :] * float(8**d) for d in range(4))
     factor = DECAY * arrived[owner, :share, :].astype(F32) + (1.0 - DECAY) * summed[:share] / total
     factor = factor.astype(BF16)
@@ -251,10 +248,9 @@
             high[tile_of(b, a)] = piece.T.astype(BF16)
 
 
-def fill_blocks(kind, packed, diag, factor, factor_low, inverse, inverse_low):
-    tiles = factor.shape[0] // TILE
-    spread(packed, 0, diag, kind * tiles, DECAY, factor, factor_low)
-    spread(packed, 1, diag, (2 + kind) * tiles, 1.0, inverse, inverse_low)
+def fill_blocks(packed, diag, factor, factor_low, inverse, inverse_low):
+    spread(packed, 0, diag, 0, DECAY, factor, factor_low)
+    spread(packed, 1, diag, factor.shape[0] // TILE, 1.0, inverse, inverse_low)
 
 
 def times(high, low, right):
@@ -280,7 +276,7 @@
     facts = Facts()
     core, place = facts.core, facts.place
     unpack(mine, other, core, packed)
-    fill_blocks(0, packed, diag, factor, factor_low, inverse, inverse_low)
+    fill_blocks(packed, diag, factor, factor_low, inverse, inverse_low)
     start = pl.multiple_of(place * TILE, TILE)
     part = inverse[:, pl.ds(start, TILE)].astype(F32)
     rows = lax.broadcasted_iota(jnp.int32, part.shape, 0) - start
@@ -291,8 +287,8 @@
 
 
 def new_blocks(
-    owners, mine, other, far_mine, far_other, diag, right, factor_out, inverse_out,
-    packed, factor, factor_low, inverse, inverse_low,
+    owners, mine, other, far_mine, far_other, diag, far_diag, right, factor_out, inverse_out,
+    packed, factor, factor_low, inverse, inverse_low, lanes,
 ):
     facts = Facts(new_owner=owners)
     core, own_kind = facts.core, facts.own_kind
@@ -303,12 +299,14 @@
         @pl.when(own_kind == kind)
         def _():
             unpack(mine, other, core, packed)
+            lanes[...] = diag[...]
 
         @pl.when(own_kind != kind)
         def _():
             unpack(far_mine, far_other, core, packed)
-
-        fill_blocks(kind, packed, diag, *blocks)
+            lanes[...] = far_diag[...]
+
+        fill_blocks(packed, lanes, *blocks)
 
     load_blocks(1)
     fresh = refine(*blocks, exact_block(inverse, inverse_low))
@@ -342,7 +340,7 @@
     curvature[...] = jnp.full(curvature.shape, jnp.sum(product * grad[own].astype(F32).T))
 
 
-def kernel_call(body, out_shape, in_specs, scratch=(), out_specs=None, aliases=None, flops=0, moved=0):
+def kernel_call(body, out_shape, in_specs, scratch=(), out_specs=None, aliases=None, flops=0, moved=0, name=None):
     if out_specs is None:
         out_specs = (WHOLE,) * len(out_shape) if isinstance(out_shape, tuple) else WHOLE
     return pl.pallas_call(
@@ -354,7 +352,7 @@
         scratch_shapes=list(scratch),
         compiler_params=PARAMS,
         cost_estimate=pl.CostEstimate(flops=flops, bytes_accessed=moved, transcendentals=0),
-        name=body.__name__,
+        name=name or body.__name__,
     )
 
 
@@ -387,7 +385,7 @@
     def swap_planes(send):
         return lax.ppermute(send, "dp", plane_swap)
 
-    message = shape((chips, 3 * share + 8 * lanes + ROWS, TILE), BF16)
+    message = shape((chips, 3 * share + 4 * lanes + ROWS, TILE), BF16)
     keep, send, turned = kernel_call(
         first_parts,
         (message, message, shape((width, tok_rows), BF16)),
@@ -404,7 +402,7 @@
         flops=4 * tok_rows * width * width,
         moved=10 * megabyte,
     )(old_owner, counts, features, out_grads, factor_old[0, 0], inverse_old[0, 0])
-    old_rows = 2 * share + 8 * lanes
+    old_rows = 2 * share + 4 * lanes
     far_shape = shape((ring,) + message.shape[1:], BF16)
     def gradient(body, parity, which, dtype, name, other):
         def chip_at(i, s):
@@ -459,7 +457,7 @@
     )(old_owner, near_old, near_sum, arrived, far_grad, send_near)
     shares, diag = kernel_call(
         make_shares,
-        (shape((ring, 2 * share, TILE), BF16), shape((4 * lanes, TILE), F32)),
+        (shape((ring, 2 * share, TILE), BF16), shape((2 * lanes, TILE), F32)),
         [SCALARS, WHOLE],
         moved=megabyte,
     )(old_owner, across_ring(joined))
@@ -509,11 +507,11 @@
     right, factor_out, inverse_out = kernel_call(
         new_blocks,
         (shape((width, width), BF16), square, square),
-        [SCALARS] + [WHOLE] * 5,
-        unpacked,
+        [SCALARS] + [WHOLE] * 6,
+        unpacked + [pltpu.VMEM((2 * lanes, TILE), F32)],
         flops=8 * width * width * width,
         moved=6 * megabyte,
-    )(new_owner, mine, other, far_mine, far_other, diag)
+    )(new_owner, mine, other, far_mine, far_other, diag, swap_planes(diag))
 
     grad = across_ring((near_grad + arrived_grad.astype(F32)).astype(BF16))
     grad = jnp.sum(grad.astype(F32), axis=0).astype(BF16)
@@ -540,10 +538,11 @@
         jnp.broadcast_to(curvature, (2 * columns, 8, TILE)),
         ("dp", "mp"), 0, 0, tiled=True, axis_index_groups=rings,
     )
-    curvature = jnp.sum(curvature, axis=0)[0, 0]
     entries = float(feature_count * width * columns)
-    clip_scale = jnp.minimum(1.0, jnp.sqrt(entries / jnp.abs(curvature)))
-    return (factor_out[None, None], inverse_out[None, None], clip_scale * result)
+    update = kernel_call(
+        functools.partial(clip, entries), shape((TILE, width), F32), [WHOLE] * 2, name="clip"
+    )(result, curvature)
+    return (factor_out[None, None], inverse_out[None, None], update)
 
 
 def solution(mesh):

time: 142 us -> 142 us (level)
  starting transfers between devices: 37.8 us -> 40.8 us
  waiting for transfers between devices: 32.6 us -> 30.1 us
    all_to_all x3, waiting for transfers between devices: 18.2 us -> 15.5 us  [across_ring(): lax.all_to_all(parts, 'dp', 0, 0, tiled=True, axis_index_groups=rings)]
    ppermute x3 -> x4, starting transfers between devices: 4.61 us -> 7.32 us  [swap_planes(): return lax.ppermute(send, 'dp', plane_swap)]
    all_to_all x1, blocking collectives: 10.4 us -> 12.5 us  [local(): lax.all_to_all(jnp.broadcast_to(curvature, (chips, 8, TILE)), 'dp', 0, 0,...]
    ppermute x3 -> x4, waiting for transfers between devices: 9.49 us -> 10.8 us  [swap_planes(): return lax.ppermute(send, 'dp', plane_swap)]
  transfers between devices with their start and end apart: 15 -> 16, of which waited for: 11 -> 9; matrix products, arithmetic and copies ran while one was open for 2% -> 2% of each run, Pallas kernels for 15% -> 15%
where the time goes in v10:
time: 142 us; the launch traced here: 141 us
  starting transfers between devices  40.8 us (29%)
  blocking collectives  34.8 us (25%)
  waiting for transfers between devices  30.1 us (21%)
  Pallas kernels  27.6 us (19%)
  local copies, waits for them, and re-layouts  3.59 us (3%)
  other arithmetic  2.91 us (2%)
  between operations  1.47 us (1%)
    all_to_all x3, waiting for transfers between devices, across_ring(): lax.all_to_all(parts, 'dp', 0, 0, tiled=True, axis_index_groups=rings)  15.5 us
    all_to_all x3, starting transfers between devices, across_ring(): lax.all_to_all(parts, 'dp', 0, 0, tiled=True, axis_index_groups=rings)  14.2 us
    all_to_all x1, blocking collectives, local(): lax.all_to_all(jnp.broadcast_to(curvature, (2 * columns, 8, TILE)), ('dp'...  13.7 us
    pallas_call x4, Pallas kernels, gradient(): pl.pallas_call(body, out_shape=shape((ring, width, TILE), dtype), grid_sp...  13.4 us
    all_to_all x1, blocking collectives, local(): lax.all_to_all(jnp.broadcast_to(curvature, (chips, 8, TILE)), 'dp', 0, 0,...  12.5 us
    ppermute x4, waiting for transfers between devices, swap_planes(): return lax.ppermute(send, 'dp', plane_swap)  10.8 us
    ppermute x5, starting transfers between devices, swap_cores(): return lax.ppermute(send, 'dp', core_swap)  9.33 us
    all_gather x1, blocking collectives, local(): grads = lax.all_gather(grad, 'dp', axis=0, axis_index_groups=neighbours)  8.51 us
  transfers between devices with their start and end apart: 16, of which 9 were waited for; matrix products, arithmetic and copies ran while one was open for 2% of the time, Pallas kernels for 15%

profile of v10, /device:TPU:1, one launch (start us, length us, event | category | flops | bytes accessed | tf_op | source)
XLA Modules:
  0.0 141.3 jit_solution(1507936336528000496)
XLA Ops:
  0.6 0.8 copy.18.owners
  2.0 1.2 copy-done.1
  3.3 4.9 %first_parts.1 = (bf16[16,272,128]{2,1,0:T(8,128)(2,1)S(1)}, bf16[16,272,128]{2,1,0:T(8,128)(2,1)}, bf16[512,1024]{1,0:T(8,128)(2,1)S(1)}) custom-call(s32[8,2]{1,0:T(8,128)S(1)} %copy.18.owners, s32[1]{0:T(128)S(6)} %copy.20.counts.refs_4_, bf16[1024,4096]{1,0:T(8,128)(2,1)} %refs_3_.7, bf16[1024,512]{1,0:T(8,128)(2,1)S(1)} %copy-done.1, ...), custom_call_target="tpu_custom_call" | custom-call | flops 1073741824 | bytes 10485760 | tf_op jit(solution)/shard_map/first_parts/pallas_call | solution.py:389
  8.2 3.3 %collective-permute-start = (bf16[16,272,128]{2,1,0:T(8,128)(2,1)}, bf16[16,272,128]{2,1,0:T(8,128)(2,1)S(1)}, u32[]{:S(2)}, u32[]{:S(2)}) collective-permute-start(bf16[16,272,128]{2,1,0:T(8,128)(2,1)} %get-tuple-element.17), channel_id=1, source_target_pairs={{0,8},{8,0},{16,24},{24,16},{32,40},{40,32},{48,56},{56,48},{64,72... | collective-permute-start | bytes 3342344 | tf_op jit(solution)/shard_map/ppermute | solution.py:383
  11.5 3.3 %send_far.1.unread = bf16[8,512,128]{2,1,0:T(8,128)(2,1)S(1)} custom-call(s32[2]{0:T(128)S(1)} %pad_add_fusion.1.scalars, bf16[512,1024]{1,0:T(8,128)(2,1)S(1)} %get-tuple-element.18.turned, bf16[1024,4096]{1,0:T(8,128)(2,1)} %refs_3_.7, bf16[1024,4096]{1,0:T(8,128)(2,1)} %refs_3_.7, bf16[1024,4096]{1,0:T(8,128)(2,1)} %refs_3_.7, ...), custom_call_target="tpu_custom_call" | custom-call | flops 1073741824 | bytes 4194304 | tf_op jit(solution)/shard_map/send_far/pallas_call | solution.py:415
  14.8 0.1 collective-permute-start.2
  14.9 0.8 choose_core.1
  15.7 1.3 collective-permute-start.1
  17.1 0.5 collective-permute-done.2.refs_4_
  17.6 3.3 %gradient_far.1.unread = bf16[8,512,128]{2,1,0:T(8,128)(2,1)S(1)} custom-call(s32[2]{0:T(128)S(1)} %pad_add_fusion.scalars, bf16[512,1024]{1,0:T(8,128)(2,1)S(1)} %get-tuple-element.18.turned, bf16[1024,4096]{1,0:T(8,128)(2,1)} %refs_3_.7, bf16[1024,4096]{1,0:T(8,128)(2,1)} %refs_3_.7, bf16[1024,4096]{1,0:T(8,128)(2,1)} %refs_3_.7, ...), custom_call_target="tpu_custom_call" | custom-call | flops 1073741824 | bytes 4194304 | tf_op jit(solution)/shard_map/gradient_far/pallas_call | solution.py:415
  20.9 3.3 %send_near.1.other_unread = bf16[8,512,128]{2,1,0:T(8,128)(2,1)S(1)} custom-call(s32[2]{0:T(128)S(1)} %pad_add_fusion.2.scalars, bf16[512,1024]{1,0:T(8,128)(2,1)S(1)} %get-tuple-element.18.turned, bf16[1024,4096]{1,0:T(8,128)(2,1)} %refs_3_.7, bf16[1024,4096]{1,0:T(8,128)(2,1)} %refs_3_.7, bf16[1024,4096]{1,0:T(8,128)(2,1)} %refs_3_.7, ...), custom_call_target="tpu_custom_call" | custom-call | flops 1073741824 | bytes 4194304 | tf_op jit(solution)/shard_map/send_near/pallas_call | solution.py:415
  24.2 6.8 %collective-permute-done.1.arrived = bf16[8,272,128]{2,1,0:T(8,128)(2,1)S(1)} collective-permute-done((bf16[8,272,128]{2,1,0:T(8,128)(2,1)S(1)}, bf16[8,272,128]{2,1,0:T(8,128)(2,1)S(1)}, u32[]{:S(2)}, u32[]{:S(2)}) %collective-permute-start.1) | collective-permute-done | bytes 557088 | tf_op jit(solution)/shard_map/ppermute | solution.py:386
  31.0 0.7 join_planes.1
  31.7 0.8 copy-done
  32.5 6.5 %all-to-all-start = ((bf16[8,272,128]{2,1,0:T(8,128)(2,1)}), bf16[8,272,128]{2,1,0:T(8,128)(2,1)}, u32[]{:S(2)}, u32[]{:S(2)}) async-start(bf16[8,272,128]{2,1,0:T(8,128)(2,1)} %copy-done), calls=%async_computation | async-start | bytes 1114112 | tf_op jit(solution)/shard_map/all_to_all | solution.py:380
  39.0 1.6 %collective-permute-start.7 = (bf16[8,512,128]{2,1,0:T(8,128)(2,1)S(1)}, bf16[8,512,128]{2,1,0:T(8,128)(2,1)}, u32[]{:S(2)}, u32[]{:S(2)}) collective-permute-start(bf16[8,512,128]{2,1,0:T(8,128)(2,1)S(1)} %send_near.1.other_unread), channel_id=1, source_target_pairs={{0,8},{8,0},{16,24},{24,16},{32,40},{40,32},{48,56},{56,48},{64,72... | collective-permute-start | bytes 3145736 | tf_op jit(solution)/shard_map/ppermute | solution.py:383
  40.6 2.9 %collective-permute-start.8 = (bf16[8,512,128]{2,1,0:T(8,128)(2,1)S(1)}, bf16[8,512,128]{2,1,0:T(8,128)(2,1)}, u32[]{:S(2)}, u32[]{:S(2)}) collective-permute-start(bf16[8,512,128]{2,1,0:T(8,128)(2,1)S(1)} %gradient_far.1.unread), channel_id=1, source_target_pairs={{0,128},{8,136},{16,144},{24,152},{32,160},{40,168},{48,176},{56,1... | collective-permute-start | bytes 3145736 | tf_op jit(solution)/shard_map/ppermute | solution.py:386
  43.5 12.6 %all-to-all-done.arrived = bf16[8,272,128]{2,1,0:T(8,128)(2,1)} async-done(((bf16[8,272,128]{2,1,0:T(8,128)(2,1)}), bf16[8,272,128]{2,1,0:T(8,128)(2,1)}, u32[]{:S(2)}, u32[]{:S(2)}) %all-to-all-start) | async-done | bytes 557088 | tf_op jit(solution)/shard_map/all_to_all | solution.py:380
  56.2 1.1 make_shares.1
  57.3 0.7 copy-done.2
  58.0 3.4 %all-to-all-start.1 = ((bf16[8,160,128]{2,1,0:T(8,128)(2,1)}), bf16[8,160,128]{2,1,0:T(8,128)(2,1)S(1)}, u32[]{:S(2)}, u32[]{:S(2)}) async-start(bf16[8,160,128]{2,1,0:T(8,128)(2,1)} %copy-done.2), calls=%async_computation.1 | async-start | bytes 655360 | tf_op jit(solution)/shard_map/all_to_all | solution.py:380
  61.4 0.1 pad_add_fusion.3.scalars
  61.5 3.5 %gradient_near.1 = f32[8,512,128]{2,1,0:T(8,128)S(1)} custom-call(s32[2]{0:T(128)S(1)} %pad_add_fusion.3.scalars, bf16[512,1024]{1,0:T(8,128)(2,1)S(1)} %get-tuple-element.18.turned, bf16[1024,4096]{1,0:T(8,128)(2,1)} %refs_3_.7, bf16[1024,4096]{1,0:T(8,128)(2,1)} %refs_3_.7, bf16[1024,4096]{1,0:T(8,128)(2,1)} %refs_3_.7, bf16[1024,4096]{1,0:T(8,128)(2,1)} %refs_3_.7, ...), custom_call_target="tpu_custom_call" | custom-call | flops 1073741824 | bytes 4194304 | tf_op jit(solution)/shard_map/gradient_near/pallas_call | solution.py:415
  65.0 1.9 %collective-permute-done.8 = bf16[8,512,128]{2,1,0:T(8,128)(2,1)} collective-permute-done((bf16[8,512,128]{2,1,0:T(8,128)(2,1)S(1)}, bf16[8,512,128]{2,1,0:T(8,128)(2,1)}, u32[]{:S(2)}, u32[]{:S(2)}) %collective-permute-start.8) | collective-permute-done | bytes 1048608 | tf_op jit(solution)/shard_map/ppermute | solution.py:386
  66.9 2.4 %add_convert_fusion = bf16[8,512,128]{2,1,0:T(8,128)(2,1)} fusion(f32[8,512,128]{2,1,0:T(8,128)S(1)} %gradient_near.1, bf16[8,512,128]{2,1,0:T(8,128)(2,1)} %collective-permute-done.8), kind=kLoop, calls=%fused_computation | loop fusion | flops 1572864 | bytes 4194304 | tf_op jit(solution)/shard_map/convert_element_type | solution.py:516
  69.3 2.9 %all-to-all-done.1.mine = bf16[8,160,128]{2,1,0:T(8,128)(2,1)S(1)} async-done(((bf16[8,160,128]{2,1,0:T(8,128)(2,1)}), bf16[8,160,128]{2,1,0:T(8,128)(2,1)S(1)}, u32[]{:S(2)}, u32[]{:S(2)}) %all-to-all-start.1) | async-done | bytes 327712 | tf_op jit(solution)/shard_map/all_to_all | solution.py:380
  72.2 4.3 %all-to-all-start.2 = ((bf16[8,512,128]{2,1,0:T(8,128)(2,1)}), bf16[8,512,128]{2,1,0:T(8,128)(2,1)S(1)}, u32[]{:S(2)}, u32[]{:S(2)}) async-start(bf16[8,512,128]{2,1,0:T(8,128)(2,1)} %add_convert_fusion), calls=%async_computation.2 | async-start | bytes 2097152 | tf_op jit(solution)/shard_map/all_to_all | solution.py:380
  76.5 2.8 %collective-permute-start.3 = (bf16[8,160,128]{2,1,0:T(8,128)(2,1)S(1)}, bf16[8,160,128]{2,1,0:T(8,128)(2,1)S(1)}, u32[]{:S(2)}, u32[]{:S(2)}) collective-permute-start(bf16[8,160,128]{2,1,0:T(8,128)(2,1)S(1)} %all-to-all-done.1.mine), channel_id=1, source_target_pairs={{0,8},{8,0},{16,24},{24,16},{32,40},{40,32},{48,56},{56,48},{64,72... | collective-permute-start | bytes 983048 | tf_op jit(solution)/shard_map/ppermute | solution.py:383
  79.2 1.3 collective-permute-done.3.other
  80.5 1.2 left_columns.1
  81.7 3.2 %collective-permute-start.9 = (bf16[512,128]{1,0:T(8,128)(2,1)S(1)}, bf16[512,128]{1,0:T(8,128)(2,1)S(1)}, u32[]{:S(2)}, u32[]{:S(2)}) collective-permute-start(bf16[512,128]{1,0:T(8,128)(2,1)S(1)} %left_columns.1), channel_id=1, source_target_pairs={{0,1},{8,9},{16,17},{24,25},{33,32},{41,40},{49,48},{57,56},{66,67... | collective-permute-start | bytes 393224 | tf_op jit(solution)/shard_map/ppermute | solution.py:485
  85.0 0.4 collective-permute-start.4
  85.4 2.0 %collective-permute-done.9 = bf16[512,128]{1,0:T(8,128)(2,1)S(1)} collective-permute-done((bf16[512,128]{1,0:T(8,128)(2,1)S(1)}, bf16[512,128]{1,0:T(8,128)(2,1)S(1)}, u32[]{:S(2)}, u32[]{:S(2)}) %collective-permute-start.9) | collective-permute-done | bytes 131104 | tf_op jit(solution)/shard_map/ppermute | solution.py:485
  87.5 1.3 collective-permute-start.10
  88.8 4.2 %collective-permute-start.11 = (bf16[512,128]{1,0:T(8,128)(2,1)S(1)}, bf16[512,128]{1,0:T(8,128)(2,1)S(1)}, u32[]{:S(2)}, u32[]{:S(2)}) collective-permute-start(bf16[512,128]{1,0:T(8,128)(2,1)S(1)} %broadcast_select_fusion), channel_id=1, source_target_pairs={{0,4},{1,5},{8,12},{9,13},{16,20},{17,21},{24,28},{25,29},{33,37},... | collective-permute-start | bytes 393224 | tf_op jit(solution)/shard_map/ppermute | solution.py:494
  93.0 1.3 collective-permute-start.12
  94.3 0.8 collective-permute-done.4.far_mine
  95.1 1.5 %collective-permute-start.5 = (bf16[8,160,128]{2,1,0:T(8,128)(2,1)S(1)}, bf16[8,160,128]{2,1,0:T(8,128)(2,1)S(1)}, u32[]{:S(2)}, u32[]{:S(2)}) collective-permute-start(bf16[8,160,128]{2,1,0:T(8,128)(2,1)S(1)} %collective-permute-done.4.far_mine), channel_id=1, source_target_pairs={{0,8},{8,0},{16,24},{24,16},{32,40},{40,32},{48,56},{56,48},{64,72... | collective-permute-start | bytes 983048 | tf_op jit(solution)/shard_map/ppermute | solution.py:383
  96.7 0.1 copy.19.owners
  96.8 2.7 %collective-permute-start.6 = (f32[8,128]{1,0:T(8,128)S(1)}, f32[8,128]{1,0:T(8,128)S(1)}, u32[]{:S(2)}, u32[]{:S(2)}) collective-permute-start(f32[8,128]{1,0:T(8,128)S(1)} %get-tuple-element.23.diag), channel_id=1, source_target_pairs={{0,128},{8,136},{16,144},{24,152},{32,160},{40,168},{48,176},{56,1... | collective-permute-start | bytes 12296 | tf_op jit(solution)/shard_map/ppermute | solution.py:386
  99.5 1.2 collective-permute-done.6.far_diag
  100.7 4.0 %new_blocks.1 = (bf16[512,512]{1,0:T(8,128)(2,1)S(1)}, f32[512,512]{1,0:T(8,128)}, f32[512,512]{1,0:T(8,128)}) custom-call(s32[8,2]{1,0:T(8,128)S(1)} %copy.19.owners, bf16[8,160,128]{2,1,0:T(8,128)(2,1)S(1)} %all-to-all-done.1.mine, bf16[8,160,128]{2,1,0:T(8,128)(2,1)S(1)} %collective-permute-done.3.other, ...), custom_call_target="tpu_custom_call" | custom-call | flops 1073741824 | bytes 6291456 | tf_op jit(solution)/shard_map/new_blocks/pallas_call | solution.py:507
  104.7 0.1 reduce_sum.21
  104.9 8.5 %all-gather = bf16[2048,128]{1,0:T(8,128)(2,1)S(1)} all-gather(bf16[512,128]{1,0:T(8,128)(2,1)S(1)} %reduce_sum.21), channel_id=2, replica_groups={{0,8,16,24},{32,40,48,56},{64,72,80,88},{96,104,112,120},{128,136,144,1..., dimensions={0}, use_global_device_ids=true | all-gather | bytes 655360 | tf_op jit(solution)/shard_map/all_gather | solution.py:519
  113.4 0.8 precondition.1
  114.2 12.5 %all_to_all.25 = f32[16,8,128]{2,1,0:T(8,128)S(1)} all-to-all(f32[16,8,128]{2,1,0:T(8,128)S(1)} %broadcast_in_dim.14), channel_id=1, replica_groups={{0,8,16,24,32,40,48,56,64,72,80,88,96,104,112,120},{128,136,144,152,160..., dimensions={0} | all-to-all | bytes 131072 | tf_op jit(solution)/shard_map/all_to_all | solution.py:529
  126.7 13.7 %all_to_all.26.partials = f32[16,8,128]{2,1,0:T(8,128)S(1)} all-to-all(f32[16,8,128]{2,1,0:T(8,128)S(1)} %broadcast_in_dim.15), channel_id=1, replica_groups={{0,1,2,3,4,5,6,7,128,129,130,131,132,133,134,135},{8,9,10,11,12,13,14,1..., dimensions={0} | all-to-all | bytes 131072 | tf_op jit(solution)/shard_map/all_to_all | solution.py:537
  140.5 0.8 clip.1
  (20 shorter events, 0.3 us)
Async XLA Ops:
  2.0 1.2 copy-start.1
  8.2 6.8 %collective-permute-start = (bf16[16,272,128]{2,1,0:T(8,128)(2,1)}, bf16[16,272,128]{2,1,0:T(8,128)(2,1)S(1)}, u32[]{:S(2)}, u32[]{:S(2)}) collective-permute-start(bf16[16,272,128]{2,1,0:T(8,128)(2,1)} %get-tuple-element.17), channel_id=1, source_target_pairs={{0,8},{8,0},{16,24},{24,16},{32,40},{40,32},{48,56},{56,48},{64,72... | collective-permute-start | bytes 3342344 | tf_op jit(solution)/shard_map/ppermute | solution.py:383
  14.8 2.7 %collective-permute-start.2 = (bf16[8,512,128]{2,1,0:T(8,128)(2,1)S(1)}, bf16[8,512,128]{2,1,0:T(8,128)(2,1)S(1)}, u32[]{:S(2)}, u32[]{:S(2)}) collective-permute-start(bf16[8,512,128]{2,1,0:T(8,128)(2,1)S(1)} %send_far.1.unread), channel_id=1, source_target_pairs={{0,8},{8,0},{16,24},{24,16},{32,40},{40,32},{48,56},{56,48},{64,72... | collective-permute-start | bytes 3145736 | tf_op jit(solution)/shard_map/ppermute | solution.py:383
  15.7 15.3 %collective-permute-start.1 = (bf16[8,272,128]{2,1,0:T(8,128)(2,1)S(1)}, bf16[8,272,128]{2,1,0:T(8,128)(2,1)S(1)}, u32[]{:S(2)}, u32[]{:S(2)}) collective-permute-start(bf16[8,272,128]{2,1,0:T(8,128)(2,1)S(1)} %get-tuple-element.21.refs_4_), channel_id=1, source_target_pairs={{0,128},{8,136},{16,144},{24,152},{32,160},{40,168},{48,176},{56,1... | collective-permute-start | bytes 1671176 | tf_op jit(solution)/shard_map/ppermute | solution.py:386
  31.7 0.8 copy-start
  32.5 23.6 %all-to-all-start = ((bf16[8,272,128]{2,1,0:T(8,128)(2,1)}), bf16[8,272,128]{2,1,0:T(8,128)(2,1)}, u32[]{:S(2)}, u32[]{:S(2)}) async-start(bf16[8,272,128]{2,1,0:T(8,128)(2,1)} %copy-done), calls=%async_computation | async-start | bytes 1114112 | tf_op jit(solution)/shard_map/all_to_all | solution.py:380
  39.0 22.5 %collective-permute-start.7 = (bf16[8,512,128]{2,1,0:T(8,128)(2,1)S(1)}, bf16[8,512,128]{2,1,0:T(8,128)(2,1)}, u32[]{:S(2)}, u32[]{:S(2)}) collective-permute-start(bf16[8,512,128]{2,1,0:T(8,128)(2,1)S(1)} %send_near.1.other_unread), channel_id=1, source_target_pairs={{0,8},{8,0},{16,24},{24,16},{32,40},{40,32},{48,56},{56,48},{64,72... | collective-permute-start | bytes 3145736 | tf_op jit(solution)/shard_map/ppermute | solution.py:383
  40.6 26.3 %collective-permute-start.8 = (bf16[8,512,128]{2,1,0:T(8,128)(2,1)S(1)}, bf16[8,512,128]{2,1,0:T(8,128)(2,1)}, u32[]{:S(2)}, u32[]{:S(2)}) collective-permute-start(bf16[8,512,128]{2,1,0:T(8,128)(2,1)S(1)} %gradient_far.1.unread), channel_id=1, source_target_pairs={{0,128},{8,136},{16,144},{24,152},{32,160},{40,168},{48,176},{56,1... | collective-permute-start | bytes 3145736 | tf_op jit(solution)/shard_map/ppermute | solution.py:386
  57.3 0.7 copy-start.2
  58.0 14.2 %all-to-all-start.1 = ((bf16[8,160,128]{2,1,0:T(8,128)(2,1)}), bf16[8,160,128]{2,1,0:T(8,128)(2,1)S(1)}, u32[]{:S(2)}, u32[]{:S(2)}) async-start(bf16[8,160,128]{2,1,0:T(8,128)(2,1)} %copy-done.2), calls=%async_computation.1 | async-start | bytes 655360 | tf_op jit(solution)/shard_map/all_to_all | solution.py:380
  69.3 27.3 %copy-start.3 = (s32[8,2]{0,1:T(2,128)S(1)}, s32[8,2]{0,1:T(2,128)}, u32[]{:S(2)}) copy-start(s32[8,2]{0,1:T(2,128)} %param.13) | copy-start | bytes 196
  72.2 32.5 %all-to-all-start.2 = ((bf16[8,512,128]{2,1,0:T(8,128)(2,1)}), bf16[8,512,128]{2,1,0:T(8,128)(2,1)S(1)}, u32[]{:S(2)}, u32[]{:S(2)}) async-start(bf16[8,512,128]{2,1,0:T(8,128)(2,1)} %add_convert_fusion), calls=%async_computation.2 | async-start | bytes 2097152 | tf_op jit(solution)/shard_map/all_to_all | solution.py:380
  76.5 4.0 %collective-permute-start.3 = (bf16[8,160,128]{2,1,0:T(8,128)(2,1)S(1)}, bf16[8,160,128]{2,1,0:T(8,128)(2,1)S(1)}, u32[]{:S(2)}, u32[]{:S(2)}) collective-permute-start(bf16[8,160,128]{2,1,0:T(8,128)(2,1)S(1)} %all-to-all-done.1.mine), channel_id=1, source_target_pairs={{0,8},{8,0},{16,24},{24,16},{32,40},{40,32},{48,56},{56,48},{64,72... | collective-permute-start | bytes 983048 | tf_op jit(solution)/shard_map/ppermute | solution.py:383
  81.7 5.7 %collective-permute-start.9 = (bf16[512,128]{1,0:T(8,128)(2,1)S(1)}, bf16[512,128]{1,0:T(8,128)(2,1)S(1)}, u32[]{:S(2)}, u32[]{:S(2)}) collective-permute-start(bf16[512,128]{1,0:T(8,128)(2,1)S(1)} %left_columns.1), channel_id=1, source_target_pairs={{0,1},{8,9},{16,17},{24,25},{33,32},{41,40},{49,48},{57,56},{66,67... | collective-permute-start | bytes 393224 | tf_op jit(solution)/shard_map/ppermute | solution.py:485
  85.0 10.2 %collective-permute-start.4 = (bf16[8,160,128]{2,1,0:T(8,128)(2,1)S(1)}, bf16[8,160,128]{2,1,0:T(8,128)(2,1)S(1)}, u32[]{:S(2)}, u32[]{:S(2)}) collective-permute-start(bf16[8,160,128]{2,1,0:T(8,128)(2,1)S(1)} %all-to-all-done.1.mine), channel_id=1, source_target_pairs={{0,128},{8,136},{16,144},{24,152},{32,160},{40,168},{48,176},{56,1... | collective-permute-start | bytes 983048 | tf_op jit(solution)/shard_map/ppermute | solution.py:386
  87.5 12.0 %collective-permute-start.10 = (bf16[512,128]{1,0:T(8,128)(2,1)S(1)}, bf16[512,128]{1,0:T(8,128)(2,1)S(1)}, u32[]{:S(2)}, u32[]{:S(2)}) collective-permute-start(bf16[512,128]{1,0:T(8,128)(2,1)S(1)} %broadcast_select_fusion), channel_id=1, source_target_pairs={{0,2},{1,3},{8,10},{9,11},{16,18},{17,19},{24,26},{25,27},{33,35},... | collective-permute-start | bytes 393224 | tf_op jit(solution)/shard_map/ppermute | solution.py:494
  88.8 10.7 %collective-permute-start.11 = (bf16[512,128]{1,0:T(8,128)(2,1)S(1)}, bf16[512,128]{1,0:T(8,128)(2,1)S(1)}, u32[]{:S(2)}, u32[]{:S(2)}) collective-permute-start(bf16[512,128]{1,0:T(8,128)(2,1)S(1)} %broadcast_select_fusion), channel_id=1, source_target_pairs={{0,4},{1,5},{8,12},{9,13},{16,20},{17,21},{24,28},{25,29},{33,37},... | collective-permute-start | bytes 393224 | tf_op jit(solution)/shard_map/ppermute | solution.py:494
  93.0 6.5 %collective-permute-start.12 = (bf16[512,128]{1,0:T(8,128)(2,1)S(1)}, bf16[512,128]{1,0:T(8,128)(2,1)S(1)}, u32[]{:S(2)}, u32[]{:S(2)}) collective-permute-start(bf16[512,128]{1,0:T(8,128)(2,1)S(1)} %broadcast_select_fusion), channel_id=1, source_target_pairs={{0,6},{1,7},{8,14},{9,15},{16,22},{17,23},{24,30},{25,31},{33,39},... | collective-permute-start | bytes 393224 | tf_op jit(solution)/shard_map/ppermute | solution.py:494
  95.1 5.6 %collective-permute-start.5 = (bf16[8,160,128]{2,1,0:T(8,128)(2,1)S(1)}, bf16[8,160,128]{2,1,0:T(8,128)(2,1)S(1)}, u32[]{:S(2)}, u32[]{:S(2)}) collective-permute-start(bf16[8,160,128]{2,1,0:T(8,128)(2,1)S(1)} %collective-permute-done.4.far_mine), channel_id=1, source_target_pairs={{0,8},{8,0},{16,24},{24,16},{32,40},{40,32},{48,56},{56,48},{64,72... | collective-permute-start | bytes 983048 | tf_op jit(solution)/shard_map/ppermute | solution.py:383
  96.8 4.0 %collective-permute-start.6 = (f32[8,128]{1,0:T(8,128)S(1)}, f32[8,128]{1,0:T(8,128)S(1)}, u32[]{:S(2)}, u32[]{:S(2)}) collective-permute-start(f32[8,128]{1,0:T(8,128)S(1)} %get-tuple-element.23.diag), channel_id=1, source_target_pairs={{0,128},{8,136},{16,144},{24,152},{32,160},{40,168},{48,176},{56,1... | collective-permute-start | bytes 12296 | tf_op jit(solution)/shard_map/ppermute | solution.py:386

commit v11 on v7

--- a/solution.py
+++ b/solution.py
@@ -1,3 +1,5 @@
+import functools
+
 import jax
 import jax.numpy as jnp
 from jax import lax
@@ -29,6 +31,12 @@
 
 def tile_of(a, b):
     return (slice(a * TILE, (a + 1) * TILE), slice(b * TILE, (b + 1) * TILE))
+
+
+def clip(entries, result, partials, update):
+    curvature = jnp.sum(partials[...], axis=0)[:1, :1]
+    scale = jnp.minimum(1.0, jnp.sqrt(entries / jnp.abs(curvature)))
+    update[...] = scale * result[...]
 
 
 class Facts:
@@ -342,7 +350,7 @@
     curvature[...] = jnp.full(curvature.shape, jnp.sum(product * grad[own].astype(F32).T))
 
 
-def kernel_call(body, out_shape, in_specs, scratch=(), out_specs=None, aliases=None, flops=0, moved=0):
+def kernel_call(body, out_shape, in_specs, scratch=(), out_specs=None, aliases=None, flops=0, moved=0, name=None):
     if out_specs is None:
         out_specs = (WHOLE,) * len(out_shape) if isinstance(out_shape, tuple) else WHOLE
     return pl.pallas_call(
@@ -354,7 +362,7 @@
         scratch_shapes=list(scratch),
         compiler_params=PARAMS,
         cost_estimate=pl.CostEstimate(flops=flops, bytes_accessed=moved, transcendentals=0),
-        name=body.__name__,
+        name=name or body.__name__,
     )
 
 
@@ -540,10 +548,11 @@
         jnp.broadcast_to(curvature, (2 * columns, 8, TILE)),
         ("dp", "mp"), 0, 0, tiled=True, axis_index_groups=rings,
     )
-    curvature = jnp.sum(curvature, axis=0)[0, 0]
     entries = float(feature_count * width * columns)
-    clip_scale = jnp.minimum(1.0, jnp.sqrt(entries / jnp.abs(curvature)))
-    return (factor_out[None, None], inverse_out[None, None], clip_scale * result)
+    update = kernel_call(
+        functools.partial(clip, entries), shape((TILE, width), F32), [WHOLE] * 2, name="clip"
+    )(result, curvature)
+    return (factor_out[None, None], inverse_out[None, None], update)
 
 
 def solution(mesh):

time: 142 us -> 140 us (0.986)
    all_to_all x1, blocking collectives: 14.1 us -> 11.4 us  [local(): lax.all_to_all(jnp.broadcast_to(curvature, (2 * columns, 8, TILE)), ('dp'...]
    all_to_all x1, blocking collectives: 10.4 us -> 13 us  [local(): lax.all_to_all(jnp.broadcast_to(curvature, (chips, 8, TILE)), 'dp', 0, 0,...]
where the time goes in v11:
time: 140 us
  starting transfers between devices  38.5 us (28%)
  blocking collectives  33.6 us (24%)
  waiting for transfers between devices  32 us (23%)
  Pallas kernels  27.7 us (20%)
  local copies, waits for them, and re-layouts  3.6 us (3%)
  other arithmetic  2.91 us (2%)
  between operations  1.47 us (1%)
    all_to_all x3, waiting for transfers between devices, across_ring(): lax.all_to_all(parts, 'dp', 0, 0, tiled=True, axis_index_groups=rings)  18.3 us
    all_to_all x3, starting transfers between devices, across_ring(): lax.all_to_all(parts, 'dp', 0, 0, tiled=True, axis_index_groups=rings)  13.5 us
    pallas_call x4, Pallas kernels, gradient(): pl.pallas_call(body, out_shape=shape((ring, width, TILE), dtype), grid_sp...  13.4 us
    all_to_all x1, blocking collectives, local(): lax.all_to_all(jnp.broadcast_to(curvature, (chips, 8, TILE)), 'dp', 0, 0,...  13 us
    all_to_all x1, blocking collectives, local(): lax.all_to_all(jnp.broadcast_to(curvature, (2 * columns, 8, TILE)), ('dp'...  11.4 us
    ppermute x5, starting transfers between devices, swap_cores(): return lax.ppermute(send, 'dp', core_swap)  9.73 us
    all_gather x1, blocking collectives, local(): grads = lax.all_gather(grad, 'dp', axis=0, axis_index_groups=neighbours)  9.2 us
    ppermute x3, waiting for transfers between devices, swap_planes(): return lax.ppermute(send, 'dp', plane_swap)  8.86 us
  transfers between devices with their start and end apart: 15, of which 11 were waited for; matrix products, arithmetic and copies ran while one was open for 2% of the time, Pallas kernels for 15%

profile of v11, /device:TPU:1, one launch (start us, length us, event | category | flops | bytes accessed | tf_op | source)
XLA Modules:
  0.0 139.8 jit_solution(12332657808656239474)
XLA Ops:
  0.6 0.8 copy.18.owners
  2.0 1.2 copy-done.1
  3.3 4.9 %first_parts.1 = (bf16[16,288,128]{2,1,0:T(8,128)(2,1)S(1)}, bf16[16,288,128]{2,1,0:T(8,128)(2,1)}, bf16[512,1024]{1,0:T(8,128)(2,1)S(1)}) custom-call(s32[8,2]{1,0:T(8,128)S(1)} %copy.18.owners, s32[1]{0:T(128)S(6)} %copy.20.counts.refs_4_, bf16[1024,4096]{1,0:T(8,128)(2,1)} %refs_3_.7, bf16[1024,512]{1,0:T(8,128)(2,1)S(1)} %copy-done.1, ...), custom_call_target="tpu_custom_call" | custom-call | flops 1073741824 | bytes 10485760 | tf_op jit(solution)/shard_map/first_parts/pallas_call | solution.py:399
  8.2 3.3 %collective-permute-start = (bf16[16,288,128]{2,1,0:T(8,128)(2,1)}, bf16[16,288,128]{2,1,0:T(8,128)(2,1)S(1)}, u32[]{:S(2)}, u32[]{:S(2)}) collective-permute-start(bf16[16,288,128]{2,1,0:T(8,128)(2,1)} %get-tuple-element.17), channel_id=1, source_target_pairs={{0,8},{8,0},{16,24},{24,16},{32,40},{40,32},{48,56},{56,48},{64,72... | collective-permute-start | bytes 3538952 | tf_op jit(solution)/shard_map/ppermute | solution.py:393
  11.5 3.3 %send_far.1.unread = bf16[8,512,128]{2,1,0:T(8,128)(2,1)S(1)} custom-call(s32[2]{0:T(128)S(1)} %pad_add_fusion.1.scalars, bf16[512,1024]{1,0:T(8,128)(2,1)S(1)} %get-tuple-element.18.turned, bf16[1024,4096]{1,0:T(8,128)(2,1)} %refs_3_.7, bf16[1024,4096]{1,0:T(8,128)(2,1)} %refs_3_.7, bf16[1024,4096]{1,0:T(8,128)(2,1)} %refs_3_.7, ...), custom_call_target="tpu_custom_call" | custom-call | flops 1073741824 | bytes 4194304 | tf_op jit(solution)/shard_map/send_far/pallas_call | solution.py:425
  14.8 0.1 collective-permute-start.2
  15.0 0.8 choose_core.1
  15.7 1.3 collective-permute-start.1
  17.1 0.5 collective-permute-done.2.refs_4_
  17.6 3.3 %gradient_far.1.unread = bf16[8,512,128]{2,1,0:T(8,128)(2,1)S(1)} custom-call(s32[2]{0:T(128)S(1)} %pad_add_fusion.scalars, bf16[512,1024]{1,0:T(8,128)(2,1)S(1)} %get-tuple-element.18.turned, bf16[1024,4096]{1,0:T(8,128)(2,1)} %refs_3_.7, bf16[1024,4096]{1,0:T(8,128)(2,1)} %refs_3_.7, bf16[1024,4096]{1,0:T(8,128)(2,1)} %refs_3_.7, ...), custom_call_target="tpu_custom_call" | custom-call | flops 1073741824 | bytes 4194304 | tf_op jit(solution)/shard_map/gradient_far/pallas_call | solution.py:425
  20.9 3.3 %send_near.1.other_unread = bf16[8,512,128]{2,1,0:T(8,128)(2,1)S(1)} custom-call(s32[2]{0:T(128)S(1)} %pad_add_fusion.2.scalars, bf16[512,1024]{1,0:T(8,128)(2,1)S(1)} %get-tuple-element.18.turned, bf16[1024,4096]{1,0:T(8,128)(2,1)} %refs_3_.7, bf16[1024,4096]{1,0:T(8,128)(2,1)} %refs_3_.7, bf16[1024,4096]{1,0:T(8,128)(2,1)} %refs_3_.7, ...), custom_call_target="tpu_custom_call" | custom-call | flops 1073741824 | bytes 4194304 | tf_op jit(solution)/shard_map/send_near/pallas_call | solution.py:425
  24.2 7.5 %collective-permute-done.1.arrived = bf16[8,288,128]{2,1,0:T(8,128)(2,1)S(1)} collective-permute-done((bf16[8,288,128]{2,1,0:T(8,128)(2,1)S(1)}, bf16[8,288,128]{2,1,0:T(8,128)(2,1)S(1)}, u32[]{:S(2)}, u32[]{:S(2)}) %collective-permute-start.1) | collective-permute-done | bytes 589856 | tf_op jit(solution)/shard_map/ppermute | solution.py:396
  31.7 0.7 join_planes.1
  32.4 0.8 copy-done
  33.2 6.5 %all-to-all-start = ((bf16[8,288,128]{2,1,0:T(8,128)(2,1)}), bf16[8,288,128]{2,1,0:T(8,128)(2,1)}, u32[]{:S(2)}, u32[]{:S(2)}) async-start(bf16[8,288,128]{2,1,0:T(8,128)(2,1)} %copy-done), calls=%async_computation | async-start | bytes 1179648 | tf_op jit(solution)/shard_map/all_to_all | solution.py:390
  39.7 1.6 %collective-permute-start.6 = (bf16[8,512,128]{2,1,0:T(8,128)(2,1)S(1)}, bf16[8,512,128]{2,1,0:T(8,128)(2,1)}, u32[]{:S(2)}, u32[]{:S(2)}) collective-permute-start(bf16[8,512,128]{2,1,0:T(8,128)(2,1)S(1)} %send_near.1.other_unread), channel_id=1, source_target_pairs={{0,8},{8,0},{16,24},{24,16},{32,40},{40,32},{48,56},{56,48},{64,72... | collective-permute-start | bytes 3145736 | tf_op jit(solution)/shard_map/ppermute | solution.py:393
  41.3 2.9 %collective-permute-start.7 = (bf16[8,512,128]{2,1,0:T(8,128)(2,1)S(1)}, bf16[8,512,128]{2,1,0:T(8,128)(2,1)}, u32[]{:S(2)}, u32[]{:S(2)}) collective-permute-start(bf16[8,512,128]{2,1,0:T(8,128)(2,1)S(1)} %gradient_far.1.unread), channel_id=1, source_target_pairs={{0,128},{8,136},{16,144},{24,152},{32,160},{40,168},{48,176},{56,1... | collective-permute-start | bytes 3145736 | tf_op jit(solution)/shard_map/ppermute | solution.py:396
  44.2 13.4 %all-to-all-done.arrived = bf16[8,288,128]{2,1,0:T(8,128)(2,1)} async-done(((bf16[8,288,128]{2,1,0:T(8,128)(2,1)}), bf16[8,288,128]{2,1,0:T(8,128)(2,1)}, u32[]{:S(2)}, u32[]{:S(2)}) %all-to-all-start) | async-done | bytes 589856 | tf_op jit(solution)/shard_map/all_to_all | solution.py:390
  57.6 1.1 make_shares.1
  58.8 0.7 copy-done.2
  59.5 3.4 %all-to-all-start.1 = ((bf16[8,160,128]{2,1,0:T(8,128)(2,1)}), bf16[8,160,128]{2,1,0:T(8,128)(2,1)S(1)}, u32[]{:S(2)}, u32[]{:S(2)}) async-start(bf16[8,160,128]{2,1,0:T(8,128)(2,1)} %copy-done.2), calls=%async_computation.1 | async-start | bytes 655360 | tf_op jit(solution)/shard_map/all_to_all | solution.py:390
  63.0 3.5 %gradient_near.1 = f32[8,512,128]{2,1,0:T(8,128)S(1)} custom-call(s32[2]{0:T(128)S(1)} %pad_add_fusion.3.scalars, bf16[512,1024]{1,0:T(8,128)(2,1)S(1)} %get-tuple-element.18.turned, bf16[1024,4096]{1,0:T(8,128)(2,1)} %refs_3_.7, bf16[1024,4096]{1,0:T(8,128)(2,1)} %refs_3_.7, bf16[1024,4096]{1,0:T(8,128)(2,1)} %refs_3_.7, bf16[1024,4096]{1,0:T(8,128)(2,1)} %refs_3_.7, ...), custom_call_target="tpu_custom_call" | custom-call | flops 1073741824 | bytes 4194304 | tf_op jit(solution)/shard_map/gradient_near/pallas_call | solution.py:425
  66.5 1.1 collective-permute-done.7
  67.7 2.4 %add_convert_fusion = bf16[8,512,128]{2,1,0:T(8,128)(2,1)} fusion(f32[8,512,128]{2,1,0:T(8,128)S(1)} %gradient_near.1, bf16[8,512,128]{2,1,0:T(8,128)(2,1)} %collective-permute-done.7), kind=kLoop, calls=%fused_computation | loop fusion | flops 1572864 | bytes 4194304 | tf_op jit(solution)/shard_map/convert_element_type | solution.py:526
  70.1 3.9 %all-to-all-done.1.mine = bf16[8,160,128]{2,1,0:T(8,128)(2,1)S(1)} async-done(((bf16[8,160,128]{2,1,0:T(8,128)(2,1)}), bf16[8,160,128]{2,1,0:T(8,128)(2,1)S(1)}, u32[]{:S(2)}, u32[]{:S(2)}) %all-to-all-start.1) | async-done | bytes 327712 | tf_op jit(solution)/shard_map/all_to_all | solution.py:390
  74.0 3.6 %all-to-all-start.2 = ((bf16[8,512,128]{2,1,0:T(8,128)(2,1)}), bf16[8,512,128]{2,1,0:T(8,128)(2,1)S(1)}, u32[]{:S(2)}, u32[]{:S(2)}) async-start(bf16[8,512,128]{2,1,0:T(8,128)(2,1)} %add_convert_fusion), calls=%async_computation.2 | async-start | bytes 2097152 | tf_op jit(solution)/shard_map/all_to_all | solution.py:390
  77.6 3.2 %collective-permute-start.3 = (bf16[8,160,128]{2,1,0:T(8,128)(2,1)S(1)}, bf16[8,160,128]{2,1,0:T(8,128)(2,1)S(1)}, u32[]{:S(2)}, u32[]{:S(2)}) collective-permute-start(bf16[8,160,128]{2,1,0:T(8,128)(2,1)S(1)} %all-to-all-done.1.mine), channel_id=1, source_target_pairs={{0,8},{8,0},{16,24},{24,16},{32,40},{40,32},{48,56},{56,48},{64,72... | collective-permute-start | bytes 983048 | tf_op jit(solution)/shard_map/ppermute | solution.py:393
  80.8 1.3 collective-permute-done.3.other
  82.0 1.2 left_columns.1
  83.2 3.2 %collective-permute-start.8 = (bf16[512,128]{1,0:T(8,128)(2,1)S(1)}, bf16[512,128]{1,0:T(8,128)(2,1)S(1)}, u32[]{:S(2)}, u32[]{:S(2)}) collective-permute-start(bf16[512,128]{1,0:T(8,128)(2,1)S(1)} %left_columns.1), channel_id=1, source_target_pairs={{0,1},{8,9},{16,17},{24,25},{33,32},{41,40},{49,48},{57,56},{66,67... | collective-permute-start | bytes 393224 | tf_op jit(solution)/shard_map/ppermute | solution.py:495
  86.5 0.4 collective-permute-start.4
  86.9 2.0 %collective-permute-done.8 = bf16[512,128]{1,0:T(8,128)(2,1)S(1)} collective-permute-done((bf16[512,128]{1,0:T(8,128)(2,1)S(1)}, bf16[512,128]{1,0:T(8,128)(2,1)S(1)}, u32[]{:S(2)}, u32[]{:S(2)}) %collective-permute-start.8) | collective-permute-done | bytes 131104 | tf_op jit(solution)/shard_map/ppermute | solution.py:495
  89.0 4.9 %collective-permute-start.10 = (bf16[512,128]{1,0:T(8,128)(2,1)S(1)}, bf16[512,128]{1,0:T(8,128)(2,1)S(1)}, u32[]{:S(2)}, u32[]{:S(2)}) collective-permute-start(bf16[512,128]{1,0:T(8,128)(2,1)S(1)} %broadcast_select_fusion), channel_id=1, source_target_pairs={{0,4},{1,5},{8,12},{9,13},{16,20},{17,21},{24,28},{25,29},{33,37},... | collective-permute-start | bytes 393224 | tf_op jit(solution)/shard_map/ppermute | solution.py:504
  93.8 1.3 collective-permute-start.11
  95.1 1.3 collective-permute-start.9
  96.4 0.2 collective-permute-done.4.far_mine
  96.7 1.5 %collective-permute-start.5 = (bf16[8,160,128]{2,1,0:T(8,128)(2,1)S(1)}, bf16[8,160,128]{2,1,0:T(8,128)(2,1)S(1)}, u32[]{:S(2)}, u32[]{:S(2)}) collective-permute-start(bf16[8,160,128]{2,1,0:T(8,128)(2,1)S(1)} %collective-permute-done.4.far_mine), channel_id=1, source_target_pairs={{0,8},{8,0},{16,24},{24,16},{32,40},{40,32},{48,56},{56,48},{64,72... | collective-permute-start | bytes 983048 | tf_op jit(solution)/shard_map/ppermute | solution.py:393
  98.2 0.1 copy.19.owners
  98.3 0.3 collective-permute-done.9
  98.6 0.9 collective-permute-done.5.far_other
  99.4 4.0 %new_blocks.1 = (bf16[512,512]{1,0:T(8,128)(2,1)S(1)}, f32[512,512]{1,0:T(8,128)}, f32[512,512]{1,0:T(8,128)}) custom-call(s32[8,2]{1,0:T(8,128)S(1)} %copy.19.owners, bf16[8,160,128]{2,1,0:T(8,128)(2,1)S(1)} %all-to-all-done.1.mine, bf16[8,160,128]{2,1,0:T(8,128)(2,1)S(1)} %collective-permute-done.3.other, ...), custom_call_target="tpu_custom_call" | custom-call | flops 1073741824 | bytes 6291456 | tf_op jit(solution)/shard_map/new_blocks/pallas_call | solution.py:517
  103.4 0.9 all-to-all-done.2
  104.4 0.1 reduce_sum.21
  104.5 9.2 %all-gather = bf16[2048,128]{1,0:T(8,128)(2,1)S(1)} all-gather(bf16[512,128]{1,0:T(8,128)(2,1)S(1)} %reduce_sum.21), channel_id=2, replica_groups={{0,8,16,24},{32,40,48,56},{64,72,80,88},{96,104,112,120},{128,136,144,1..., dimensions={0}, use_global_device_ids=true | all-gather | bytes 655360 | tf_op jit(solution)/shard_map/all_gather | solution.py:529
  113.7 0.8 precondition.1
  114.5 13.0 %all_to_all.25 = f32[16,8,128]{2,1,0:T(8,128)S(1)} all-to-all(f32[16,8,128]{2,1,0:T(8,128)S(1)} %broadcast_in_dim.14), channel_id=1, replica_groups={{0,8,16,24,32,40,48,56,64,72,80,88,96,104,112,120},{128,136,144,152,160..., dimensions={0} | all-to-all | bytes 131072 | tf_op jit(solution)/shard_map/all_to_all | solution.py:539
  127.6 11.4 %all_to_all.26.partials = f32[16,8,128]{2,1,0:T(8,128)S(1)} all-to-all(f32[16,8,128]{2,1,0:T(8,128)S(1)} %broadcast_in_dim.15), channel_id=1, replica_groups={{0,1,2,3,4,5,6,7,128,129,130,131,132,133,134,135},{8,9,10,11,12,13,14,1..., dimensions={0} | all-to-all | bytes 131072 | tf_op jit(solution)/shard_map/all_to_all | solution.py:547
  139.0 0.8 clip.1
  (18 shorter events, 0.4 us)
Async XLA Ops:
  2.0 1.2 copy-start.1
  8.2 6.8 %collective-permute-start = (bf16[16,288,128]{2,1,0:T(8,128)(2,1)}, bf16[16,288,128]{2,1,0:T(8,128)(2,1)S(1)}, u32[]{:S(2)}, u32[]{:S(2)}) collective-permute-start(bf16[16,288,128]{2,1,0:T(8,128)(2,1)} %get-tuple-element.17), channel_id=1, source_target_pairs={{0,8},{8,0},{16,24},{24,16},{32,40},{40,32},{48,56},{56,48},{64,72... | collective-permute-start | bytes 3538952 | tf_op jit(solution)/shard_map/ppermute | solution.py:393
  14.8 2.7 %collective-permute-start.2 = (bf16[8,512,128]{2,1,0:T(8,128)(2,1)S(1)}, bf16[8,512,128]{2,1,0:T(8,128)(2,1)S(1)}, u32[]{:S(2)}, u32[]{:S(2)}) collective-permute-start(bf16[8,512,128]{2,1,0:T(8,128)(2,1)S(1)} %send_far.1.unread), channel_id=1, source_target_pairs={{0,8},{8,0},{16,24},{24,16},{32,40},{40,32},{48,56},{56,48},{64,72... | collective-permute-start | bytes 3145736 | tf_op jit(solution)/shard_map/ppermute | solution.py:393
  15.7 16.0 %collective-permute-start.1 = (bf16[8,288,128]{2,1,0:T(8,128)(2,1)S(1)}, bf16[8,288,128]{2,1,0:T(8,128)(2,1)S(1)}, u32[]{:S(2)}, u32[]{:S(2)}) collective-permute-start(bf16[8,288,128]{2,1,0:T(8,128)(2,1)S(1)} %get-tuple-element.21.refs_4_), channel_id=1, source_target_pairs={{0,128},{8,136},{16,144},{24,152},{32,160},{40,168},{48,176},{56,1... | collective-permute-start | bytes 1769480 | tf_op jit(solution)/shard_map/ppermute | solution.py:396
  32.4 0.8 copy-start
  33.2 24.4 %all-to-all-start = ((bf16[8,288,128]{2,1,0:T(8,128)(2,1)}), bf16[8,288,128]{2,1,0:T(8,128)(2,1)}, u32[]{:S(2)}, u32[]{:S(2)}) async-start(bf16[8,288,128]{2,1,0:T(8,128)(2,1)} %copy-done), calls=%async_computation | async-start | bytes 1179648 | tf_op jit(solution)/shard_map/all_to_all | solution.py:390
  39.7 23.3 %collective-permute-start.6 = (bf16[8,512,128]{2,1,0:T(8,128)(2,1)S(1)}, bf16[8,512,128]{2,1,0:T(8,128)(2,1)}, u32[]{:S(2)}, u32[]{:S(2)}) collective-permute-start(bf16[8,512,128]{2,1,0:T(8,128)(2,1)S(1)} %send_near.1.other_unread), channel_id=1, source_target_pairs={{0,8},{8,0},{16,24},{24,16},{32,40},{40,32},{48,56},{56,48},{64,72... | collective-permute-start | bytes 3145736 | tf_op jit(solution)/shard_map/ppermute | solution.py:393
  41.3 26.3 %collective-permute-start.7 = (bf16[8,512,128]{2,1,0:T(8,128)(2,1)S(1)}, bf16[8,512,128]{2,1,0:T(8,128)(2,1)}, u32[]{:S(2)}, u32[]{:S(2)}) collective-permute-start(bf16[8,512,128]{2,1,0:T(8,128)(2,1)S(1)} %gradient_far.1.unread), channel_id=1, source_target_pairs={{0,128},{8,136},{16,144},{24,152},{32,160},{40,168},{48,176},{56,1... | collective-permute-start | bytes 3145736 | tf_op jit(solution)/shard_map/ppermute | solution.py:396
  58.8 0.7 copy-start.2
  59.5 14.5 %all-to-all-start.1 = ((bf16[8,160,128]{2,1,0:T(8,128)(2,1)}), bf16[8,160,128]{2,1,0:T(8,128)(2,1)S(1)}, u32[]{:S(2)}, u32[]{:S(2)}) async-start(bf16[8,160,128]{2,1,0:T(8,128)(2,1)} %copy-done.2), calls=%async_computation.1 | async-start | bytes 655360 | tf_op jit(solution)/shard_map/all_to_all | solution.py:390
  70.1 28.1 %copy-start.3 = (s32[8,2]{0,1:T(2,128)S(1)}, s32[8,2]{0,1:T(2,128)}, u32[]{:S(2)}) copy-start(s32[8,2]{0,1:T(2,128)} %param.13) | copy-start | bytes 196
  74.0 30.4 %all-to-all-start.2 = ((bf16[8,512,128]{2,1,0:T(8,128)(2,1)}), bf16[8,512,128]{2,1,0:T(8,128)(2,1)S(1)}, u32[]{:S(2)}, u32[]{:S(2)}) async-start(bf16[8,512,128]{2,1,0:T(8,128)(2,1)} %add_convert_fusion), calls=%async_computation.2 | async-start | bytes 2097152 | tf_op jit(solution)/shard_map/all_to_all | solution.py:390
  77.6 4.4 %collective-permute-start.3 = (bf16[8,160,128]{2,1,0:T(8,128)(2,1)S(1)}, bf16[8,160,128]{2,1,0:T(8,128)(2,1)S(1)}, u32[]{:S(2)}, u32[]{:S(2)}) collective-permute-start(bf16[8,160,128]{2,1,0:T(8,128)(2,1)S(1)} %all-to-all-done.1.mine), channel_id=1, source_target_pairs={{0,8},{8,0},{16,24},{24,16},{32,40},{40,32},{48,56},{56,48},{64,72... | collective-permute-start | bytes 983048 | tf_op jit(solution)/shard_map/ppermute | solution.py:393
  83.2 5.7 %collective-permute-start.8 = (bf16[512,128]{1,0:T(8,128)(2,1)S(1)}, bf16[512,128]{1,0:T(8,128)(2,1)S(1)}, u32[]{:S(2)}, u32[]{:S(2)}) collective-permute-start(bf16[512,128]{1,0:T(8,128)(2,1)S(1)} %left_columns.1), channel_id=1, source_target_pairs={{0,1},{8,9},{16,17},{24,25},{33,32},{41,40},{49,48},{57,56},{66,67... | collective-permute-start | bytes 393224 | tf_op jit(solution)/shard_map/ppermute | solution.py:495
  86.5 10.2 %collective-permute-start.4 = (bf16[8,160,128]{2,1,0:T(8,128)(2,1)S(1)}, bf16[8,160,128]{2,1,0:T(8,128)(2,1)S(1)}, u32[]{:S(2)}, u32[]{:S(2)}) collective-permute-start(bf16[8,160,128]{2,1,0:T(8,128)(2,1)S(1)} %all-to-all-done.1.mine), channel_id=1, source_target_pairs={{0,128},{8,136},{16,144},{24,152},{32,160},{40,168},{48,176},{56,1... | collective-permute-start | bytes 983048 | tf_op jit(solution)/shard_map/ppermute | solution.py:396
  89.0 9.3 %collective-permute-start.10 = (bf16[512,128]{1,0:T(8,128)(2,1)S(1)}, bf16[512,128]{1,0:T(8,128)(2,1)S(1)}, u32[]{:S(2)}, u32[]{:S(2)}) collective-permute-start(bf16[512,128]{1,0:T(8,128)(2,1)S(1)} %broadcast_select_fusion), channel_id=1, source_target_pairs={{0,4},{1,5},{8,12},{9,13},{16,20},{17,21},{24,28},{25,29},{33,37},... | collective-permute-start | bytes 393224 | tf_op jit(solution)/shard_map/ppermute | solution.py:504
  93.8 4.4 %collective-permute-start.11 = (bf16[512,128]{1,0:T(8,128)(2,1)S(1)}, bf16[512,128]{1,0:T(8,128)(2,1)S(1)}, u32[]{:S(2)}, u32[]{:S(2)}) collective-permute-start(bf16[512,128]{1,0:T(8,128)(2,1)S(1)} %broadcast_select_fusion), channel_id=1, source_target_pairs={{0,6},{1,7},{8,14},{9,15},{16,22},{17,23},{24,30},{25,31},{33,39},... | collective-permute-start | bytes 393224 | tf_op jit(solution)/shard_map/ppermute | solution.py:504
  95.1 3.4 %collective-permute-start.9 = (bf16[512,128]{1,0:T(8,128)(2,1)S(1)}, bf16[512,128]{1,0:T(8,128)(2,1)S(1)}, u32[]{:S(2)}, u32[]{:S(2)}) collective-permute-start(bf16[512,128]{1,0:T(8,128)(2,1)S(1)} %broadcast_select_fusion), channel_id=1, source_target_pairs={{0,2},{1,3},{8,10},{9,11},{16,18},{17,19},{24,26},{25,27},{33,35},... | collective-permute-start | bytes 393224 | tf_op jit(solution)/shard_map/ppermute | solution.py:504
  96.7 2.8 %collective-permute-start.5 = (bf16[8,160,128]{2,1,0:T(8,128)(2,1)S(1)}, bf16[8,160,128]{2,1,0:T(8,128)(2,1)S(1)}, u32[]{:S(2)}, u32[]{:S(2)}) collective-permute-start(bf16[8,160,128]{2,1,0:T(8,128)(2,1)S(1)} %collective-permute-done.4.far_mine), channel_id=1, source_target_pairs={{0,8},{8,0},{16,24},{24,16},{32,40},{40,32},{48,56},{56,48},{64,72... | collective-permute-start | bytes 983048 | tf_op jit(solution)/shard_map/ppermute | solution.py:393

commit v12 on v11

--- a/solution.py
+++ b/solution.py
@@ -172,7 +172,8 @@
             near_sum[...] = total
 
 
-def join_planes(owners, near_old, near_sum, arrived, unread, other_unread, out):
+def join_planes(owners, near_old, near_sum, arrived, *refs):
+    out = refs[-1]
     facts = Facts(owners)
     first, second = facts.same_plane
     flag = jnp.where(facts.own_kind == 0, first, second)
@@ -298,9 +299,19 @@
     left[...] = refine(factor, factor_low, inverse, inverse_low, part).astype(BF16)
 
 
+def blank(unread, first, second, zeros, sent):
+    zeros[...] = jnp.zeros_like(zeros)
+    copies = [pltpu.make_async_copy(zeros, out, sent.at[n]) for n, out in enumerate((first, second))]
+    for copy in copies:
+        copy.start()
+    for copy in copies:
+        copy.wait()
+
+
 def new_blocks(
-    owners, mine, other, far_mine, far_other, diag, right, factor_out, inverse_out,
-    packed, factor, factor_low, inverse, inverse_low,
+    owners, mine, other, far_mine, far_other, diag, blank_factor, blank_inverse,
+    right, factor_out, inverse_out,
+    packed, factor, factor_low, inverse, inverse_low, new_factor, new_inverse, sent,
 ):
     facts = Facts(new_owner=owners)
     core, own_kind = facts.core, facts.own_kind
@@ -324,19 +335,25 @@
 
     @pl.when(second == 1)
     def _():
-        factor_out[...] = exact_block(factor, factor_low)
-        inverse_out[...] = fresh
-
-    @pl.when(second == 0)
-    def _():
-        factor_out[...] = jnp.zeros_like(factor_out)
-        inverse_out[...] = jnp.zeros_like(inverse_out)
+        new_factor[...] = exact_block(factor, factor_low)
+        new_inverse[...] = fresh
 
     @pl.when(first == 1)
     def _():
         load_blocks(0)
-        factor_out[...] = exact_block(factor, factor_low)
-        inverse_out[...] = refine(*blocks, exact_block(inverse, inverse_low))
+        new_factor[...] = exact_block(factor, factor_low)
+        new_inverse[...] = refine(*blocks, exact_block(inverse, inverse_low))
+
+    @pl.when(first + second > 0)
+    def _():
+        copies = [
+            pltpu.make_async_copy(new_factor, factor_out, sent.at[0]),
+            pltpu.make_async_copy(new_inverse, inverse_out, sent.at[1]),
+        ]
+        for copy in copies:
+            copy.start()
+        for copy in copies:
+            copy.wait()
 
 
 def precondition(grad, left, right, result, curvature):
@@ -459,12 +476,21 @@
     near_grad = gradient(
         gradient_add, core, plane, F32, "gradient_near", swap_cores(send_near)
     )
+    square = shape((width, width), F32)
+    blanks = kernel_call(
+        blank,
+        (square, square),
+        [ANYWHERE],
+        [pltpu.VMEM((width, width), F32), pltpu.SemaphoreType.DMA((2,))],
+        out_specs=(ANYWHERE, ANYWHERE),
+        moved=2 * megabyte,
+    )(far)
     joined = kernel_call(
         join_planes,
         far_shape,
-        [SCALARS] + [WHOLE] * 3 + [ANYWHERE] * 2,
+        [SCALARS] + [WHOLE] * 3 + [ANYWHERE] * 4,
         moved=megabyte,
-    )(old_owner, near_old, near_sum, arrived, far_grad, send_near)
+    )(old_owner, near_old, near_sum, arrived, far_grad, send_near, *blanks)
     shares, diag = kernel_call(
         make_shares,
         (shape((ring, 2 * share, TILE), BF16), shape((4 * lanes, TILE), F32)),
@@ -513,15 +539,18 @@
             for step in range(1, columns // 2)
         ),
     )
-    square = shape((width, width), F32)
     right, factor_out, inverse_out = kernel_call(
         new_blocks,
         (shape((width, width), BF16), square, square),
-        [SCALARS] + [WHOLE] * 5,
-        unpacked,
+        [SCALARS] + [WHOLE] * 5 + [ANYWHERE] * 2,
+        unpacked
+        + [pltpu.VMEM((width, width), F32)] * 2
+        + [pltpu.SemaphoreType.DMA((2,))],
+        out_specs=(WHOLE, ANYWHERE, ANYWHERE),
+        aliases={6: 1, 7: 2},
         flops=8 * width * width * width,
         moved=6 * megabyte,
-    )(new_owner, mine, other, far_mine, far_other, diag)
+    )(new_owner, mine, other, far_mine, far_other, diag, *blanks)
 
     grad = across_ring((near_grad + arrived_grad.astype(F32)).astype(BF16))
     grad = jnp.sum(grad.astype(F32), axis=0).astype(BF16)

time: 140 us -> 140 us (level)
    ppermute x3, waiting for transfers between devices: 8.86 us -> 7.4 us  [swap_planes(): return lax.ppermute(send, 'dp', plane_swap)]
    pallas_call x1, Pallas kernels: 4.01 us -> 2.58 us  [local(): kernel_call(new_blocks, (shape((width, width), BF16), square, square), [S...]
    all_to_all x3, waiting for transfers between devices: 18.3 us -> 19.7 us  [across_ring(): lax.all_to_all(parts, 'dp', 0, 0, tiled=True, axis_index_groups=rings)]
    unnamed x10 -> x14, local copies, waits for them, and re-layouts: 3.59 us -> 3.6 us
where the time goes in v12:
time: 140 us; the launch traced here: 139 us
  starting transfers between devices  38.5 us (28%)
  blocking collectives  33.1 us (24%)
  waiting for transfers between devices  32 us (23%)
  Pallas kernels  27.7 us (20%)
  local copies, waits for them, and re-layouts  3.62 us (3%)
  other arithmetic  2.91 us (2%)
  between operations  1.5 us (1%)
    all_to_all x3, waiting for transfers between devices, across_ring(): lax.all_to_all(parts, 'dp', 0, 0, tiled=True, axis_index_groups=rings)  19.7 us
    all_to_all x3, starting transfers between devices, across_ring(): lax.all_to_all(parts, 'dp', 0, 0, tiled=True, axis_index_groups=rings)  13.5 us
    pallas_call x4, Pallas kernels, gradient(): pl.pallas_call(body, out_shape=shape((ring, width, TILE), dtype), grid_sp...  13.4 us
    all_to_all x1, blocking collectives, local(): lax.all_to_all(jnp.broadcast_to(curvature, (2 * columns, 8, TILE)), ('dp'...  12.2 us
    all_to_all x1, blocking collectives, local(): lax.all_to_all(jnp.broadcast_to(curvature, (chips, 8, TILE)), 'dp', 0, 0,...  11.6 us
    ppermute x5, starting transfers between devices, swap_cores(): return lax.ppermute(send, 'dp', core_swap)  9.73 us
    all_gather x1, blocking collectives, local(): grads = lax.all_gather(grad, 'dp', axis=0, axis_index_groups=neighbours)  9.2 us
    ppermute x3, starting transfers between devices, local(): lax.ppermute(left, ('dp', 'mp'), [(i * columns + g, i * columns + (g + 2...  7.46 us
  transfers between devices with their start and end apart: 15, of which 11 were waited for; matrix products, arithmetic and copies ran while one was open for 2% of the time, Pallas kernels for 15%

profile of v12, /device:TPU:1, one launch (start us, length us, event | category | flops | bytes accessed | tf_op | source)
XLA Modules:
  0.0 139.2 jit_solution(7723436750020563880)
XLA Ops:
  0.6 0.8 copy.20.owners
  2.0 1.2 copy-done.1
  3.3 4.9 %first_parts.1 = (bf16[16,288,128]{2,1,0:T(8,128)(2,1)S(1)}, bf16[16,288,128]{2,1,0:T(8,128)(2,1)}, bf16[512,1024]{1,0:T(8,128)(2,1)S(1)}) custom-call(s32[8,2]{1,0:T(8,128)S(1)} %copy.20.owners, s32[1]{0:T(128)S(6)} %copy.24.counts.refs_4_, bf16[1024,4096]{1,0:T(8,128)(2,1)} %refs_3_.7, bf16[1024,512]{1,0:T(8,128)(2,1)S(1)} %copy-done.1, ...), custom_call_target="tpu_custom_call" | custom-call | flops 1073741824 | bytes 10485760 | tf_op jit(solution)/shard_map/first_parts/pallas_call | solution.py:416
  8.2 3.3 %collective-permute-start = (bf16[16,288,128]{2,1,0:T(8,128)(2,1)}, bf16[16,288,128]{2,1,0:T(8,128)(2,1)S(1)}, u32[]{:S(2)}, u32[]{:S(2)}) collective-permute-start(bf16[16,288,128]{2,1,0:T(8,128)(2,1)} %get-tuple-element.19), channel_id=1, source_target_pairs={{0,8},{8,0},{16,24},{24,16},{32,40},{40,32},{48,56},{56,48},{64,72... | collective-permute-start | bytes 3538952 | tf_op jit(solution)/shard_map/ppermute | solution.py:410
  11.5 3.3 %send_far.1.unread = bf16[8,512,128]{2,1,0:T(8,128)(2,1)S(1)} custom-call(s32[2]{0:T(128)S(1)} %pad_add_fusion.1.scalars, bf16[512,1024]{1,0:T(8,128)(2,1)S(1)} %get-tuple-element.20.turned, bf16[1024,4096]{1,0:T(8,128)(2,1)} %refs_3_.7, bf16[1024,4096]{1,0:T(8,128)(2,1)} %refs_3_.7, bf16[1024,4096]{1,0:T(8,128)(2,1)} %refs_3_.7, ...), custom_call_target="tpu_custom_call" | custom-call | flops 1073741824 | bytes 4194304 | tf_op jit(solution)/shard_map/send_far/pallas_call | solution.py:442
  14.8 0.1 collective-permute-start.2
  14.9 0.8 choose_core.1
  15.7 1.3 collective-permute-start.1
  17.1 0.5 collective-permute-done.2.refs_4_
  17.6 3.3 %gradient_far.1.refs_0_ = bf16[8,512,128]{2,1,0:T(8,128)(2,1)S(1)} custom-call(s32[2]{0:T(128)S(1)} %pad_add_fusion.scalars, bf16[512,1024]{1,0:T(8,128)(2,1)S(1)} %get-tuple-element.20.turned, bf16[1024,4096]{1,0:T(8,128)(2,1)} %refs_3_.7, bf16[1024,4096]{1,0:T(8,128)(2,1)} %refs_3_.7, bf16[1024,4096]{1,0:T(8,128)(2,1)} %refs_3_.7, ...), custom_call_target="tpu_custom_call" | custom-call | flops 1073741824 | bytes 4194304 | tf_op jit(solution)/shard_map/gradient_far/pallas_call | solution.py:442
  20.9 1.4 %blank.1 = (f32[512,512]{1,0:T(8,128)}, f32[512,512]{1,0:T(8,128)}) custom-call(bf16[8,288,128]{2,1,0:T(8,128)(2,1)S(1)} %get-tuple-element.23.refs_4_.unread), custom_call_target="tpu_custom_call" | custom-call | bytes 2097152 | tf_op jit(solution)/shard_map/blank/pallas_call | solution.py:480
  22.3 3.3 %send_near.1.refs_1_ = bf16[8,512,128]{2,1,0:T(8,128)(2,1)S(1)} custom-call(s32[2]{0:T(128)S(1)} %pad_add_fusion.2.scalars, bf16[512,1024]{1,0:T(8,128)(2,1)S(1)} %get-tuple-element.20.turned, bf16[1024,4096]{1,0:T(8,128)(2,1)} %refs_3_.7, bf16[1024,4096]{1,0:T(8,128)(2,1)} %refs_3_.7, bf16[1024,4096]{1,0:T(8,128)(2,1)} %refs_3_.7, ...), custom_call_target="tpu_custom_call" | custom-call | flops 1073741824 | bytes 4194304 | tf_op jit(solution)/shard_map/send_near/pallas_call | solution.py:442
  25.7 6.1 %collective-permute-done.1.arrived = bf16[8,288,128]{2,1,0:T(8,128)(2,1)S(1)} collective-permute-done((bf16[8,288,128]{2,1,0:T(8,128)(2,1)S(1)}, bf16[8,288,128]{2,1,0:T(8,128)(2,1)S(1)}, u32[]{:S(2)}, u32[]{:S(2)}) %collective-permute-start.1) | collective-permute-done | bytes 589856 | tf_op jit(solution)/shard_map/ppermute | solution.py:413
  31.7 0.7 join_planes.1
  32.4 0.8 copy-done
  33.3 6.5 %all-to-all-start = ((bf16[8,288,128]{2,1,0:T(8,128)(2,1)}), bf16[8,288,128]{2,1,0:T(8,128)(2,1)}, u32[]{:S(2)}, u32[]{:S(2)}) async-start(bf16[8,288,128]{2,1,0:T(8,128)(2,1)} %copy-done), calls=%async_computation | async-start | bytes 1179648 | tf_op jit(solution)/shard_map/all_to_all | solution.py:407
  39.7 1.6 %collective-permute-start.6 = (bf16[8,512,128]{2,1,0:T(8,128)(2,1)S(1)}, bf16[8,512,128]{2,1,0:T(8,128)(2,1)}, u32[]{:S(2)}, u32[]{:S(2)}) collective-permute-start(bf16[8,512,128]{2,1,0:T(8,128)(2,1)S(1)} %send_near.1.refs_1_), channel_id=1, source_target_pairs={{0,8},{8,0},{16,24},{24,16},{32,40},{40,32},{48,56},{56,48},{64,72... | collective-permute-start | bytes 3145736 | tf_op jit(solution)/shard_map/ppermute | solution.py:410
  41.3 2.9 %collective-permute-start.7 = (bf16[8,512,128]{2,1,0:T(8,128)(2,1)S(1)}, bf16[8,512,128]{2,1,0:T(8,128)(2,1)}, u32[]{:S(2)}, u32[]{:S(2)}) collective-permute-start(bf16[8,512,128]{2,1,0:T(8,128)(2,1)S(1)} %gradient_far.1.refs_0_), channel_id=1, source_target_pairs={{0,128},{8,136},{16,144},{24,152},{32,160},{40,168},{48,176},{56,1... | collective-permute-start | bytes 3145736 | tf_op jit(solution)/shard_map/ppermute | solution.py:413
  44.2 13.4 %all-to-all-done.arrived = bf16[8,288,128]{2,1,0:T(8,128)(2,1)} async-done(((bf16[8,288,128]{2,1,0:T(8,128)(2,1)}), bf16[8,288,128]{2,1,0:T(8,128)(2,1)}, u32[]{:S(2)}, u32[]{:S(2)}) %all-to-all-start) | async-done | bytes 589856 | tf_op jit(solution)/shard_map/all_to_all | solution.py:407
  57.6 1.1 make_shares.1
  58.8 0.7 copy-done.4
  59.5 3.4 %all-to-all-start.1 = ((bf16[8,160,128]{2,1,0:T(8,128)(2,1)}), bf16[8,160,128]{2,1,0:T(8,128)(2,1)S(1)}, u32[]{:S(2)}, u32[]{:S(2)}) async-start(bf16[8,160,128]{2,1,0:T(8,128)(2,1)} %copy-done.4), calls=%async_computation.1 | async-start | bytes 655360 | tf_op jit(solution)/shard_map/all_to_all | solution.py:407
  63.0 3.5 %gradient_near.1 = f32[8,512,128]{2,1,0:T(8,128)S(1)} custom-call(s32[2]{0:T(128)S(1)} %pad_add_fusion.3.scalars, bf16[512,1024]{1,0:T(8,128)(2,1)S(1)} %get-tuple-element.20.turned, bf16[1024,4096]{1,0:T(8,128)(2,1)} %refs_3_.7, bf16[1024,4096]{1,0:T(8,128)(2,1)} %refs_3_.7, bf16[1024,4096]{1,0:T(8,128)(2,1)} %refs_3_.7, bf16[1024,4096]{1,0:T(8,128)(2,1)} %refs_3_.7, ...), custom_call_target="tpu_custom_call" | custom-call | flops 1073741824 | bytes 4194304 | tf_op jit(solution)/shard_map/gradient_near/pallas_call | solution.py:442
  66.5 1.1 collective-permute-done.7
  67.7 2.4 %add_convert_fusion = bf16[8,512,128]{2,1,0:T(8,128)(2,1)} fusion(f32[8,512,128]{2,1,0:T(8,128)S(1)} %gradient_near.1, bf16[8,512,128]{2,1,0:T(8,128)(2,1)} %collective-permute-done.7), kind=kLoop, calls=%fused_computation | loop fusion | flops 1572864 | bytes 4194304 | tf_op jit(solution)/shard_map/convert_element_type | solution.py:555
  70.1 3.9 %all-to-all-done.1.mine = bf16[8,160,128]{2,1,0:T(8,128)(2,1)S(1)} async-done(((bf16[8,160,128]{2,1,0:T(8,128)(2,1)}), bf16[8,160,128]{2,1,0:T(8,128)(2,1)S(1)}, u32[]{:S(2)}, u32[]{:S(2)}) %all-to-all-start.1) | async-done | bytes 327712 | tf_op jit(solution)/shard_map/all_to_all | solution.py:407
  74.0 3.6 %all-to-all-start.2 = ((bf16[8,512,128]{2,1,0:T(8,128)(2,1)}), bf16[8,512,128]{2,1,0:T(8,128)(2,1)S(1)}, u32[]{:S(2)}, u32[]{:S(2)}) async-start(bf16[8,512,128]{2,1,0:T(8,128)(2,1)} %add_convert_fusion), calls=%async_computation.2 | async-start | bytes 2097152 | tf_op jit(solution)/shard_map/all_to_all | solution.py:407
  77.6 3.2 %collective-permute-start.3 = (bf16[8,160,128]{2,1,0:T(8,128)(2,1)S(1)}, bf16[8,160,128]{2,1,0:T(8,128)(2,1)S(1)}, u32[]{:S(2)}, u32[]{:S(2)}) collective-permute-start(bf16[8,160,128]{2,1,0:T(8,128)(2,1)S(1)} %all-to-all-done.1.mine), channel_id=1, source_target_pairs={{0,8},{8,0},{16,24},{24,16},{32,40},{40,32},{48,56},{56,48},{64,72... | collective-permute-start | bytes 983048 | tf_op jit(solution)/shard_map/ppermute | solution.py:410
  80.7 1.3 collective-permute-done.3.other
  82.0 1.2 left_columns.1
  83.2 3.2 %collective-permute-start.8 = (bf16[512,128]{1,0:T(8,128)(2,1)S(1)}, bf16[512,128]{1,0:T(8,128)(2,1)S(1)}, u32[]{:S(2)}, u32[]{:S(2)}) collective-permute-start(bf16[512,128]{1,0:T(8,128)(2,1)S(1)} %left_columns.1), channel_id=1, source_target_pairs={{0,1},{8,9},{16,17},{24,25},{33,32},{41,40},{49,48},{57,56},{66,67... | collective-permute-start | bytes 393224 | tf_op jit(solution)/shard_map/ppermute | solution.py:521
  86.5 0.5 collective-permute-start.4
  86.9 2.0 %collective-permute-done.8 = bf16[512,128]{1,0:T(8,128)(2,1)S(1)} collective-permute-done((bf16[512,128]{1,0:T(8,128)(2,1)S(1)}, bf16[512,128]{1,0:T(8,128)(2,1)S(1)}, u32[]{:S(2)}, u32[]{:S(2)}) %collective-permute-start.8) | collective-permute-done | bytes 131104 | tf_op jit(solution)/shard_map/ppermute | solution.py:521
  89.0 4.9 %collective-permute-start.10 = (bf16[512,128]{1,0:T(8,128)(2,1)S(1)}, bf16[512,128]{1,0:T(8,128)(2,1)S(1)}, u32[]{:S(2)}, u32[]{:S(2)}) collective-permute-start(bf16[512,128]{1,0:T(8,128)(2,1)S(1)} %broadcast_select_fusion), channel_id=1, source_target_pairs={{0,4},{1,5},{8,12},{9,13},{16,20},{17,21},{24,28},{25,29},{33,37},... | collective-permute-start | bytes 393224 | tf_op jit(solution)/shard_map/ppermute | solution.py:530
  93.8 1.3 collective-permute-start.11
  95.1 1.3 collective-permute-start.9
  96.4 0.2 collective-permute-done.4.far_mine
  96.7 1.5 %collective-permute-start.5 = (bf16[8,160,128]{2,1,0:T(8,128)(2,1)S(1)}, bf16[8,160,128]{2,1,0:T(8,128)(2,1)S(1)}, u32[]{:S(2)}, u32[]{:S(2)}) collective-permute-start(bf16[8,160,128]{2,1,0:T(8,128)(2,1)S(1)} %collective-permute-done.4.far_mine), channel_id=1, source_target_pairs={{0,8},{8,0},{16,24},{24,16},{32,40},{40,32},{48,56},{56,48},{64,72... | collective-permute-start | bytes 983048 | tf_op jit(solution)/shard_map/ppermute | solution.py:410
  98.3 0.3 collective-permute-done.9
  98.6 0.9 collective-permute-done.5.far_other
  99.4 2.6 %new_blocks.1 = (bf16[512,512]{1,0:T(8,128)(2,1)S(1)}, f32[512,512]{1,0:T(8,128)}, f32[512,512]{1,0:T(8,128)}) custom-call(s32[8,2]{1,0:T(8,128)S(1)} %copy.21.owners, bf16[8,160,128]{2,1,0:T(8,128)(2,1)S(1)} %all-to-all-done.1.mine, bf16[8,160,128]{2,1,0:T(8,128)(2,1)S(1)} %collective-permute-done.3.other, ...), custom_call_target="tpu_custom_call", output_to_operand_aliasing={{1}: (6, {}), {2}: (7, {})} | custom-call | flops 1073741824 | bytes 6291456 | tf_op jit(solution)/shard_map/new_blocks/pallas_call | solution.py:542
  102.0 2.3 %all-to-all-done.2 = bf16[8,512,128]{2,1,0:T(8,128)(2,1)S(1)} async-done(((bf16[8,512,128]{2,1,0:T(8,128)(2,1)}), bf16[8,512,128]{2,1,0:T(8,128)(2,1)S(1)}, u32[]{:S(2)}, u32[]{:S(2)}) %all-to-all-start.2) | async-done | bytes 1048608 | tf_op jit(solution)/shard_map/all_to_all | solution.py:407
  104.4 0.1 reduce_sum.21
  104.5 9.2 %all-gather = bf16[2048,128]{1,0:T(8,128)(2,1)S(1)} all-gather(bf16[512,128]{1,0:T(8,128)(2,1)S(1)} %reduce_sum.21), channel_id=2, replica_groups={{0,8,16,24},{32,40,48,56},{64,72,80,88},{96,104,112,120},{128,136,144,1..., dimensions={0}, use_global_device_ids=true | all-gather | bytes 655360 | tf_op jit(solution)/shard_map/all_gather | solution.py:558
  113.7 0.8 precondition.1
  114.5 11.6 %all_to_all.25 = f32[16,8,128]{2,1,0:T(8,128)S(1)} all-to-all(f32[16,8,128]{2,1,0:T(8,128)S(1)} %broadcast_in_dim.14), channel_id=1, replica_groups={{0,8,16,24,32,40,48,56,64,72,80,88,96,104,112,120},{128,136,144,152,160..., dimensions={0} | all-to-all | bytes 131072 | tf_op jit(solution)/shard_map/all_to_all | solution.py:568
  126.2 12.2 %all_to_all.26.partials = f32[16,8,128]{2,1,0:T(8,128)S(1)} all-to-all(f32[16,8,128]{2,1,0:T(8,128)S(1)} %broadcast_in_dim.15), channel_id=1, replica_groups={{0,1,2,3,4,5,6,7,128,129,130,131,132,133,134,135},{8,9,10,11,12,13,14,1..., dimensions={0} | all-to-all | bytes 131072 | tf_op jit(solution)/shard_map/all_to_all | solution.py:576
  138.4 0.8 clip.1
  (23 shorter events, 0.5 us)
Async XLA Ops:
  2.0 1.2 copy-start.1
  8.2 6.8 %collective-permute-start = (bf16[16,288,128]{2,1,0:T(8,128)(2,1)}, bf16[16,288,128]{2,1,0:T(8,128)(2,1)S(1)}, u32[]{:S(2)}, u32[]{:S(2)}) collective-permute-start(bf16[16,288,128]{2,1,0:T(8,128)(2,1)} %get-tuple-element.19), channel_id=1, source_target_pairs={{0,8},{8,0},{16,24},{24,16},{32,40},{40,32},{48,56},{56,48},{64,72... | collective-permute-start | bytes 3538952 | tf_op jit(solution)/shard_map/ppermute | solution.py:410
  14.8 2.7 %collective-permute-start.2 = (bf16[8,512,128]{2,1,0:T(8,128)(2,1)S(1)}, bf16[8,512,128]{2,1,0:T(8,128)(2,1)S(1)}, u32[]{:S(2)}, u32[]{:S(2)}) collective-permute-start(bf16[8,512,128]{2,1,0:T(8,128)(2,1)S(1)} %send_far.1.unread), channel_id=1, source_target_pairs={{0,8},{8,0},{16,24},{24,16},{32,40},{40,32},{48,56},{56,48},{64,72... | collective-permute-start | bytes 3145736 | tf_op jit(solution)/shard_map/ppermute | solution.py:410
  15.7 16.0 %collective-permute-start.1 = (bf16[8,288,128]{2,1,0:T(8,128)(2,1)S(1)}, bf16[8,288,128]{2,1,0:T(8,128)(2,1)S(1)}, u32[]{:S(2)}, u32[]{:S(2)}) collective-permute-start(bf16[8,288,128]{2,1,0:T(8,128)(2,1)S(1)} %get-tuple-element.23.refs_4_.unread), channel_id=1, source_target_pairs={{0,128},{8,136},{16,144},{24,152},{32,160},{40,168},{48,176},{56,1... | collective-permute-start | bytes 1769480 | tf_op jit(solution)/shard_map/ppermute | solution.py:413
  22.3 9.4 %copy-start.2 = (f32[512,512]{1,0:T(8,128)S(1)}, f32[512,512]{1,0:T(8,128)}, u32[]{:S(2)}) copy-start(f32[512,512]{1,0:T(8,128)} %get-tuple-element.24.refs_2_.blank_factor) | copy-start | bytes 3145732
  22.3 9.4 %copy-start.3 = (f32[512,512]{1,0:T(8,128)S(1)}, f32[512,512]{1,0:T(8,128)}, u32[]{:S(2)}) copy-start(f32[512,512]{1,0:T(8,128)} %get-tuple-element.25.refs_3_.blank_inverse) | copy-start | bytes 3145732
  32.4 0.8 copy-start
  33.3 24.4 %all-to-all-start = ((bf16[8,288,128]{2,1,0:T(8,128)(2,1)}), bf16[8,288,128]{2,1,0:T(8,128)(2,1)}, u32[]{:S(2)}, u32[]{:S(2)}) async-start(bf16[8,288,128]{2,1,0:T(8,128)(2,1)} %copy-done), calls=%async_computation | async-start | bytes 1179648 | tf_op jit(solution)/shard_map/all_to_all | solution.py:407
  39.7 23.3 %collective-permute-start.6 = (bf16[8,512,128]{2,1,0:T(8,128)(2,1)S(1)}, bf16[8,512,128]{2,1,0:T(8,128)(2,1)}, u32[]{:S(2)}, u32[]{:S(2)}) collective-permute-start(bf16[8,512,128]{2,1,0:T(8,128)(2,1)S(1)} %send_near.1.refs_1_), channel_id=1, source_target_pairs={{0,8},{8,0},{16,24},{24,16},{32,40},{40,32},{48,56},{56,48},{64,72... | collective-permute-start | bytes 3145736 | tf_op jit(solution)/shard_map/ppermute | solution.py:410
  41.3 26.3 %collective-permute-start.7 = (bf16[8,512,128]{2,1,0:T(8,128)(2,1)S(1)}, bf16[8,512,128]{2,1,0:T(8,128)(2,1)}, u32[]{:S(2)}, u32[]{:S(2)}) collective-permute-start(bf16[8,512,128]{2,1,0:T(8,128)(2,1)S(1)} %gradient_far.1.refs_0_), channel_id=1, source_target_pairs={{0,128},{8,136},{16,144},{24,152},{32,160},{40,168},{48,176},{56,1... | collective-permute-start | bytes 3145736 | tf_op jit(solution)/shard_map/ppermute | solution.py:413
  58.8 0.7 copy-start.4
  59.5 14.5 %all-to-all-start.1 = ((bf16[8,160,128]{2,1,0:T(8,128)(2,1)}), bf16[8,160,128]{2,1,0:T(8,128)(2,1)S(1)}, u32[]{:S(2)}, u32[]{:S(2)}) async-start(bf16[8,160,128]{2,1,0:T(8,128)(2,1)} %copy-done.4), calls=%async_computation.1 | async-start | bytes 655360 | tf_op jit(solution)/shard_map/all_to_all | solution.py:407
  70.1 28.1 %copy-start.5 = (s32[8,2]{0,1:T(2,128)S(1)}, s32[8,2]{0,1:T(2,128)}, u32[]{:S(2)}) copy-start(s32[8,2]{0,1:T(2,128)} %param.13) | copy-start | bytes 196
  74.0 30.4 %all-to-all-start.2 = ((bf16[8,512,128]{2,1,0:T(8,128)(2,1)}), bf16[8,512,128]{2,1,0:T(8,128)(2,1)S(1)}, u32[]{:S(2)}, u32[]{:S(2)}) async-start(bf16[8,512,128]{2,1,0:T(8,128)(2,1)} %add_convert_fusion), calls=%async_computation.2 | async-start | bytes 2097152 | tf_op jit(solution)/shard_map/all_to_all | solution.py:407
  77.6 4.4 %collective-permute-start.3 = (bf16[8,160,128]{2,1,0:T(8,128)(2,1)S(1)}, bf16[8,160,128]{2,1,0:T(8,128)(2,1)S(1)}, u32[]{:S(2)}, u32[]{:S(2)}) collective-permute-start(bf16[8,160,128]{2,1,0:T(8,128)(2,1)S(1)} %all-to-all-done.1.mine), channel_id=1, source_target_pairs={{0,8},{8,0},{16,24},{24,16},{32,40},{40,32},{48,56},{56,48},{64,72... | collective-permute-start | bytes 983048 | tf_op jit(solution)/shard_map/ppermute | solution.py:410
  83.2 5.7 %collective-permute-start.8 = (bf16[512,128]{1,0:T(8,128)(2,1)S(1)}, bf16[512,128]{1,0:T(8,128)(2,1)S(1)}, u32[]{:S(2)}, u32[]{:S(2)}) collective-permute-start(bf16[512,128]{1,0:T(8,128)(2,1)S(1)} %left_columns.1), channel_id=1, source_target_pairs={{0,1},{8,9},{16,17},{24,25},{33,32},{41,40},{49,48},{57,56},{66,67... | collective-permute-start | bytes 393224 | tf_op jit(solution)/shard_map/ppermute | solution.py:521
  86.5 10.2 %collective-permute-start.4 = (bf16[8,160,128]{2,1,0:T(8,128)(2,1)S(1)}, bf16[8,160,128]{2,1,0:T(8,128)(2,1)S(1)}, u32[]{:S(2)}, u32[]{:S(2)}) collective-permute-start(bf16[8,160,128]{2,1,0:T(8,128)(2,1)S(1)} %all-to-all-done.1.mine), channel_id=1, source_target_pairs={{0,128},{8,136},{16,144},{24,152},{32,160},{40,168},{48,176},{56,1... | collective-permute-start | bytes 983048 | tf_op jit(solution)/shard_map/ppermute | solution.py:413
  89.0 9.3 %collective-permute-start.10 = (bf16[512,128]{1,0:T(8,128)(2,1)S(1)}, bf16[512,128]{1,0:T(8,128)(2,1)S(1)}, u32[]{:S(2)}, u32[]{:S(2)}) collective-permute-start(bf16[512,128]{1,0:T(8,128)(2,1)S(1)} %broadcast_select_fusion), channel_id=1, source_target_pairs={{0,4},{1,5},{8,12},{9,13},{16,20},{17,21},{24,28},{25,29},{33,37},... | collective-permute-start | bytes 393224 | tf_op jit(solution)/shard_map/ppermute | solution.py:530
  93.8 4.4 %collective-permute-start.11 = (bf16[512,128]{1,0:T(8,128)(2,1)S(1)}, bf16[512,128]{1,0:T(8,128)(2,1)S(1)}, u32[]{:S(2)}, u32[]{:S(2)}) collective-permute-start(bf16[512,128]{1,0:T(8,128)(2,1)S(1)} %broadcast_select_fusion), channel_id=1, source_target_pairs={{0,6},{1,7},{8,14},{9,15},{16,22},{17,23},{24,30},{25,31},{33,39},... | collective-permute-start | bytes 393224 | tf_op jit(solution)/shard_map/ppermute | solution.py:530
  95.1 3.4 %collective-permute-start.9 = (bf16[512,128]{1,0:T(8,128)(2,1)S(1)}, bf16[512,128]{1,0:T(8,128)(2,1)S(1)}, u32[]{:S(2)}, u32[]{:S(2)}) collective-permute-start(bf16[512,128]{1,0:T(8,128)(2,1)S(1)} %broadcast_select_fusion), channel_id=1, source_target_pairs={{0,2},{1,3},{8,10},{9,11},{16,18},{17,19},{24,26},{25,27},{33,35},... | collective-permute-start | bytes 393224 | tf_op jit(solution)/shard_map/ppermute | solution.py:530
  96.7 2.8 %collective-permute-start.5 = (bf16[8,160,128]{2,1,0:T(8,128)(2,1)S(1)}, bf16[8,160,128]{2,1,0:T(8,128)(2,1)S(1)}, u32[]{:S(2)}, u32[]{:S(2)}) collective-permute-start(bf16[8,160,128]{2,1,0:T(8,128)(2,1)S(1)} %collective-permute-done.4.far_mine), channel_id=1, source_target_pairs={{0,8},{8,0},{16,24},{24,16},{32,40},{40,32},{48,56},{56,48},{64,72... | collective-permute-start | bytes 983048 | tf_op jit(solution)/shard_map/ppermute | solution.py:410
